TPU v7x, 32 devices: a whole 2x2x4 slice. The times are simulated.
32 devices in a mesh: fsdp: 32 (over z, y, x, core).
Axes of the slice: x: 2, y: 2, z: 4, core: 2. Of those that a mesh axis runs over, the one named last changes fastest.
Arguments:
- tokens: bfloat16 [8192, 2048], P('fsdp'), may hold values from -6 to 6
- cotangent: bfloat16 [8192, 2048], P('fsdp'), may hold values from -6 to 6
- dealt_lengths: int32 [96], replicated, may hold values from 16 to 128, as said below
- deal: int32 [96], replicated, may hold values from 0 to 95, each once
- norm_gain: bfloat16 [2048], P('fsdp'), may hold values from 0.5 to 1.5
- mixer_in: bfloat16 [2048, 6144], P('fsdp'), may hold values from -0.125 to 0.125
- forget_floor: bfloat16 [2048], P('fsdp'), may hold values from 0.099609375 to 0.96875
- group_gain: bfloat16 [2048], P('fsdp'), may hold values from 0.25 to 1.75
- out_proj: bfloat16 [2048, 2048], P('fsdp'), may hold values from -0.125 to 0.125
- ffn_gain: bfloat16 [2048], P('fsdp'), may hold values from 0.5 to 1.5
- gate_up: bfloat16 [2048, 11264], P('fsdp'), may hold values from -0.125 to 0.125
- down_proj: bfloat16 [2048, 5632], P('fsdp'), may hold values from -0.078125 to 0.078125
Outputs:
- layer_out: float32 [8192, 2048], P('fsdp')
- input_grad: float32 [8192, 2048], P('fsdp')
- d_norm_gain: float32 [2048], P('fsdp')
- d_mixer_in: float32 [2048, 6144], P('fsdp')
- d_forget_floor: float32 [2048], P('fsdp')
- d_group_gain: float32 [2048], P('fsdp')
- d_out_proj: float32 [2048, 2048], P('fsdp')
- d_ffn_gain: float32 [2048], P('fsdp')
- d_gate_up: float32 [2048, 11264], P('fsdp')
- d_down_proj: float32 [2048, 5632], P('fsdp')
Inputs may be any that keep to these rules, and one draw needn't show every extreme that they name: The 3 entries dealt_lengths[d * 3] onward of each device d sum to 256, and exactly one of them is 128. `deal`: each sequence is dealt once.
All inputs are finite; a program needn't handle non-finite values.
Results may differ from a plain program's by a relative error of at most 0.009.
Values may be sent and summed in bfloat16 or wider, within the bound.
A program may use at most 448 MiB of HBM per device.

v0:
```python
import jax
import jax.numpy as jnp
from jax import lax
from jax.sharding import PartitionSpec as P

HEADS = 16
BLOCK = 32


norm_eps = 1e-05


def rounded(values):
    return lax.optimization_barrier(values.astype(jnp.bfloat16)).astype(jnp.float32)


def rms_scaled(values):
    inverse = lax.rsqrt(jnp.mean(values * values, axis=-1, keepdims=True) + norm_eps)
    return (values * inverse, inverse)


def rms_back(grad_scaled, scaled, inverse):
    return inverse * (grad_scaled - scaled * jnp.mean(grad_scaled * scaled, axis=-1, keepdims=True))


def silu_slope(values, sigmoid_values):
    return sigmoid_values * (1.0 + values * (1.0 - sigmoid_values))


def exact_einsum(pattern, left_side, right_side):
    return jnp.einsum(
        pattern,
        left_side,
        right_side,
        precision=lax.Precision.HIGHEST,
        preferred_element_type=jnp.float32,
    )


def transposed_rows(left_side, right_side):
    return lax.dot_general(
        left_side, right_side, (((0,), (0,)), ((), ())), preferred_element_type=jnp.float32
    )


def against_rows(left_side, weight_piece):
    return lax.dot_general(
        left_side, weight_piece, (((1,), (1,)), ((), ())), preferred_element_type=jnp.float32
    )


def padded_take(values, table):
    padding = jnp.zeros((1,) + values.shape[1:], values.dtype)
    return jnp.take(jnp.concatenate([values, padding], axis=0), table, axis=0)


def carry_in(first_part, second_part):
    return (
        lax.all_to_all(first_part, "fsdp", split_axis=1, concat_axis=1, tiled=True),
        lax.all_to_all(second_part, "fsdp", split_axis=1, concat_axis=1, tiled=True),
    )


def carry_out(first_part, second_part):
    return (
        lax.all_to_all(
            first_part.astype(jnp.bfloat16), "fsdp", split_axis=1, concat_axis=1, tiled=True
        ).astype(first_part.dtype),
        lax.all_to_all(
            second_part.astype(jnp.bfloat16), "fsdp", split_axis=1, concat_axis=1, tiled=True
        ).astype(second_part.dtype),
    )


def deal_tables(dealt_lengths, deal, row_count, device_count):
    own_index = lax.axis_index("fsdp")
    seq_count = deal.shape[0]
    seq_dev = seq_count // device_count
    per_peer = row_count // device_count
    peer_room = per_peer + seq_dev - 1
    seq_ids = jnp.arange(seq_count, dtype=jnp.int32)
    matches = deal[:, None] == seq_ids[None, :]
    given_lengths = jnp.sum(jnp.where(matches, dealt_lengths[:, None], 0), axis=0)
    given_starts = jnp.cumsum(given_lengths) - given_lengths
    dealt_starts = jnp.cumsum(dealt_lengths) - dealt_lengths
    dealt_place = jnp.sum(jnp.where(matches, seq_ids[:, None], 0), axis=0)
    held_rows = jnp.arange(row_count, dtype=jnp.int32)
    peer_ids = jnp.arange(device_count, dtype=jnp.int32)
    global_rows = own_index + device_count * held_rows
    owner_seq = (
        jnp.sum((given_starts[None, :] <= global_rows[:, None]).astype(jnp.int32), axis=1) - 1
    )
    owner_slot = dealt_place[owner_seq]
    target_device = owner_slot // seq_dev
    hits = (target_device[:, None] == peer_ids[None, :]).astype(jnp.int32)
    earlier_hits = jnp.cumsum(hits, axis=0) - hits
    send_rank = jnp.sum(earlier_hits * hits, axis=1)
    send_flat = send_rank * device_count + target_device
    arrived_flat = held_rows % per_peer * device_count + held_rows // per_peer
    send_table = (
        jnp.full((peer_room * device_count,), per_peer * device_count, jnp.int32)
        .at[send_flat]
        .set(arrived_flat)
    )
    home_grid = peer_ids[None, :] * per_peer + jnp.arange(per_peer, dtype=jnp.int32)[:, None]
    home_table = send_flat[home_grid.reshape(-1)]
    local_starts = (
        lax.dynamic_slice_in_dim(dealt_starts, own_index * seq_dev, seq_dev, 0)
        - own_index * row_count
    )
    local_seqs = lax.dynamic_slice_in_dim(deal, own_index * seq_dev, seq_dev, 0)
    segment_ids = (
        jnp.sum((local_starts[None, :] <= held_rows[:, None]).astype(jnp.int32), axis=1) - 1
    )
    given_rows = given_starts[local_seqs[segment_ids]] + held_rows - local_starts[segment_ids]
    via_device = given_rows % device_count
    via_lane = given_rows // device_count
    ahead = (via_device[:, None] == via_device[None, :]) & (via_lane[None, :] < via_lane[:, None])
    recv_rank = jnp.sum(ahead.astype(jnp.int32), axis=1)
    recv_index = recv_rank * device_count + via_device
    back_table = (
        jnp.full((peer_room * device_count,), row_count, jnp.int32).at[recv_index].set(held_rows)
    )
    return (send_table, recv_index, back_table, home_table, segment_ids, peer_room)


def block_parts(query, key_gate, decay_log, segment_ids):
    block_total = query.shape[0] // BLOCK
    shaped = (block_total, BLOCK) + query.shape[1:]
    query_blocks = query.reshape(shaped)
    key_blocks = key_gate.reshape(shaped)
    decay_sum = jnp.cumsum(decay_log.reshape(shaped), axis=1)
    final_sum = decay_sum[:, -1]
    block_segs = segment_ids.reshape(block_total, BLOCK)
    prior_seg = jnp.concatenate([jnp.full((1,), -1, jnp.int32), block_segs[:-1, -1]])
    carried = (block_segs == prior_seg[:, None]).astype(jnp.float32)[:, :, None, None]
    tail_mask = (block_segs == block_segs[:, -1:]).astype(jnp.float32)[:, :, None, None]
    passing = (block_segs[:, -1] == prior_seg).astype(jnp.float32)[:, None, None]
    positions = jnp.arange(BLOCK)
    within = (positions[:, None] >= positions[None, :])[None, None] & (
        block_segs[:, None, :, None] == block_segs[:, None, None, :]
    )
    query_scaled = query_blocks * jnp.exp(decay_sum)
    key_scaled = key_blocks * jnp.exp(-decay_sum)
    key_tail = key_blocks * jnp.exp(final_sum[:, None] - decay_sum) * tail_mask
    final_fade = jnp.exp(final_sum) * passing
    return (
        query_scaled,
        key_scaled,
        key_tail,
        decay_sum,
        final_sum,
        final_fade,
        carried,
        tail_mask,
        within,
    )


def recurrence_forward(parts, value_blocks):
    (
        query_scaled,
        key_scaled,
        key_tail,
        decay_sum,
        final_sum,
        final_fade,
        carried,
        tail_mask,
        within,
    ) = parts
    scores = jnp.where(within, exact_einsum("nihc,njhc->nhij", query_scaled, key_scaled), 0.0)
    inner_part = exact_einsum("nhij,njhe->nihe", scores, value_blocks)
    update = exact_einsum("njhc,njhe->nhce", key_tail, value_blocks)

    def advance(state_now, step_items):
        change, keep_rate = step_items
        return (state_now * keep_rate[:, :, None] + change, state_now)

    _, entering = lax.scan(advance, jnp.zeros(update.shape[1:], jnp.float32), (update, final_fade))
    outer_part = exact_einsum("nihc,nhce->nihe", query_scaled * carried, entering)
    return (inner_part + outer_part, scores, entering)


def recurrence_backward(parts, value_blocks, scores, entering, grad_blocks):
    (
        query_scaled,
        key_scaled,
        key_tail,
        decay_sum,
        final_sum,
        final_fade,
        carried,
        tail_mask,
        within,
    ) = parts
    d_scores = jnp.where(within, exact_einsum("nihe,njhe->nhij", grad_blocks, value_blocks), 0.0)
    local_grad = exact_einsum("nihc,nihe->nhce", query_scaled * carried, grad_blocks)

    def retreat(later_grad, step_items):
        here_grad, keep_rate = step_items
        return (here_grad + later_grad * keep_rate[:, :, None], later_grad)

    _, after_grad = lax.scan(
        retreat,
        jnp.zeros(local_grad.shape[1:], jnp.float32),
        (local_grad, final_fade),
        reverse=True,
    )
    d_value = exact_einsum("nhij,nihe->njhe", scores, grad_blocks) + exact_einsum(
        "njhc,nhce->njhe", key_tail, after_grad
    )
    d_qscaled = exact_einsum("nhij,njhc->nihc", d_scores, key_scaled) + carried * exact_einsum(
        "nhce,nihe->nihc", entering, grad_blocks
    )
    d_kscaled = exact_einsum("nhij,nihc->njhc", d_scores, query_scaled)
    d_ktail = tail_mask * exact_einsum("njhe,nhce->njhc", value_blocks, after_grad)
    d_query = d_qscaled * jnp.exp(decay_sum)
    d_key = d_kscaled * jnp.exp(-decay_sum) + d_ktail * jnp.exp(final_sum[:, None] - decay_sum)
    d_decay = d_qscaled * query_scaled - d_kscaled * key_scaled - d_ktail * key_tail
    d_final = jnp.sum(d_ktail * key_tail, axis=1) + final_fade * jnp.sum(
        entering * after_grad, axis=-1
    )
    d_decay = d_decay.at[:, -1].add(d_final)
    d_log = jnp.flip(jnp.cumsum(jnp.flip(d_decay, 1), axis=1), 1)
    return (d_query, d_key, d_value, d_log)


def body(
    tokens,
    cotangent,
    dealt_lengths,
    deal,
    norm_gain,
    mixer_in,
    forget_floor,
    group_gain,
    out_proj,
    ffn_gain,
    gate_up,
    down_proj,
):
    row_count, model_width = tokens.shape
    device_count = lax.axis_size("fsdp")
    per_peer = row_count // device_count
    ffn_width = down_proj.shape[1]
    head_dim = model_width // HEADS
    send_table, recv_index, back_table, home_table, segment_ids, peer_room = deal_tables(
        dealt_lengths, deal, row_count, device_count
    )
    spread_shape = (per_peer, device_count, model_width)
    room_shape = (peer_room, device_count, model_width)
    hop_tokens, hop_cotangent = carry_in(
        tokens.reshape(spread_shape), cotangent.reshape(spread_shape)
    )
    routed_tokens = padded_take(hop_tokens.reshape(row_count, model_width), send_table).reshape(
        room_shape
    )
    routed_cotangent = padded_take(
        hop_cotangent.reshape(row_count, model_width), send_table
    ).reshape(room_shape)
    got_tokens, got_cotangent = carry_in(routed_tokens, routed_cotangent)
    dealt = jnp.take(got_tokens.reshape(peer_room * device_count, model_width), recv_index, axis=0)
    cot_dealt = jnp.take(
        got_cotangent.reshape(peer_room * device_count, model_width), recv_index, axis=0
    )
    inputs = dealt.astype(jnp.float32)
    first_scaled, first_inverse = rms_scaled(inputs)
    gain_piece = lax.all_gather(norm_gain, "fsdp", axis=0, tiled=True)
    floor_piece = lax.all_gather(forget_floor, "fsdp", axis=0, tiled=True)
    weight_piece = lax.all_gather(mixer_in, "fsdp", axis=0, tiled=True)
    normed_part = (first_scaled * gain_piece.astype(jnp.float32)).astype(jnp.bfloat16)
    running = jnp.dot(normed_part, weight_piece, preferred_element_type=jnp.float32)
    normed_rows = normed_part
    gain_rows = gain_piece
    projected = running
    first_normed = normed_rows
    first_gain = gain_rows
    q_pre = projected[:, :model_width]
    f_pre = projected[:, model_width : 2 * model_width]
    q_sigmoid = jax.nn.sigmoid(q_pre)
    query = rounded(q_pre * q_sigmoid)
    floor_values = floor_piece.astype(jnp.float32)
    f_sigmoid = jax.nn.sigmoid(f_pre)
    forget = floor_values + (1.0 - floor_values) * f_sigmoid
    key_gate = rounded(1.0 - forget)
    value = rounded(projected[:, 2 * model_width :])
    head_shape = (row_count, HEADS, head_dim)
    block_shape = (row_count // BLOCK, BLOCK, HEADS, head_dim)
    parts = block_parts(
        query.reshape(head_shape),
        key_gate.reshape(head_shape),
        jnp.log(forget).reshape(head_shape),
        segment_ids,
    )
    value_blocks = value.reshape(block_shape)
    state_blocks, scores, entering = recurrence_forward(parts, value_blocks)
    group_scaled, group_inverse = rms_scaled(state_blocks.reshape(head_shape))
    group_normed = group_scaled.reshape(row_count, model_width)
    gain_piece = lax.all_gather(group_gain, "fsdp", axis=0, tiled=True)
    weight_piece = lax.all_gather(out_proj, "fsdp", axis=0, tiled=True)
    input_part = (group_normed * gain_piece.astype(jnp.float32)).astype(jnp.bfloat16)
    running = jnp.dot(input_part, weight_piece, preferred_element_type=jnp.float32)
    gain_rows = gain_piece
    mixed = running
    group_whole = gain_rows
    residual = inputs + mixed
    second_scaled, second_inverse = rms_scaled(residual)
    gain_piece = lax.all_gather(ffn_gain, "fsdp", axis=0, tiled=True)
    weight_piece = lax.all_gather(gate_up, "fsdp", axis=0, tiled=True)
    normed_part = (second_scaled * gain_piece.astype(jnp.float32)).astype(jnp.bfloat16)
    running = jnp.dot(normed_part, weight_piece, preferred_element_type=jnp.float32)
    normed_rows = normed_part
    gain_rows = gain_piece
    gate_part = running[:, :ffn_width]
    up_part = running[:, ffn_width:]
    gate_sigmoid = jax.nn.sigmoid(gate_part)
    gate_act = gate_part * gate_sigmoid
    hidden_act = (gate_act * up_part).astype(jnp.bfloat16)
    ffn_out = against_rows(hidden_act, lax.all_gather(down_proj, "fsdp", axis=0, tiled=True))
    dealt_out = residual + ffn_out
    out_grad = cot_dealt.astype(jnp.float32)
    d_hidden = jnp.dot(
        cot_dealt,
        lax.all_gather(down_proj, "fsdp", axis=0, tiled=True),
        preferred_element_type=jnp.float32,
    )
    d_gate_pre = jnp.concatenate(
        [d_hidden * up_part * silu_slope(gate_part, gate_sigmoid), d_hidden * gate_act], axis=1
    ).astype(jnp.bfloat16)
    d_second = against_rows(d_gate_pre, lax.all_gather(gate_up, "fsdp", axis=0, tiled=True))
    d_residual = out_grad + rms_back(
        d_second * gain_rows.astype(jnp.float32), second_scaled, second_inverse
    )
    d_mix_out = d_residual.astype(jnp.bfloat16)
    d_mixer_input = against_rows(d_mix_out, lax.all_gather(out_proj, "fsdp", axis=0, tiled=True))
    d_group = (d_mixer_input * group_whole.astype(jnp.float32)).reshape(head_shape)
    d_state = rms_back(d_group, group_scaled, group_inverse)
    d_query, d_key, d_value, d_log = recurrence_backward(
        parts, value_blocks, scores, entering, d_state.reshape(block_shape)
    )
    d_query = d_query.reshape(row_count, model_width)
    d_key = d_key.reshape(row_count, model_width)
    d_value = d_value.reshape(row_count, model_width)
    d_log = d_log.reshape(row_count, model_width)
    d_forget = d_log / forget - d_key
    d_f_pre = d_forget * (1.0 - floor_values) * f_sigmoid * (1.0 - f_sigmoid)
    d_projected = jnp.concatenate(
        [d_query * silu_slope(q_pre, q_sigmoid), d_f_pre, d_value], axis=1
    ).astype(jnp.bfloat16)
    d_first = against_rows(d_projected, lax.all_gather(mixer_in, "fsdp", axis=0, tiled=True))
    d_dealt = d_residual + rms_back(
        d_first * first_gain.astype(jnp.float32), first_scaled, first_inverse
    )
    first_gain_grad = jnp.sum(d_first * first_scaled, axis=0)
    floor_grad = jnp.sum(d_forget * (1.0 - f_sigmoid), axis=0)
    group_gain_grad = jnp.sum(d_mixer_input * group_normed, axis=0)
    second_gain_grad = jnp.sum(d_second * second_scaled, axis=0)
    feed_grads = lax.psum_scatter(
        (
            transposed_rows(normed_rows, d_gate_pre),
            transposed_rows(cot_dealt, hidden_act),
            second_gain_grad,
        ),
        "fsdp",
        scatter_dimension=0,
        tiled=True,
    )
    attention_grads = lax.psum_scatter(
        (
            transposed_rows(first_normed, d_projected),
            transposed_rows(input_part, d_mix_out),
            first_gain_grad,
            floor_grad,
            group_gain_grad,
        ),
        "fsdp",
        scatter_dimension=0,
        tiled=True,
    )
    sent_out = padded_take(dealt_out, back_table).reshape(room_shape)
    sent_grad = padded_take(d_dealt, back_table).reshape(room_shape)
    came_out, came_grad = carry_out(sent_out, sent_grad)
    home_out = jnp.take(
        came_out.reshape(peer_room * device_count, model_width), home_table, axis=0
    ).reshape(spread_shape)
    home_grad = jnp.take(
        came_grad.reshape(peer_room * device_count, model_width), home_table, axis=0
    ).reshape(spread_shape)
    final_out, final_grad = carry_out(home_out, home_grad)
    layer_out = final_out.reshape(row_count, model_width)
    input_grad = final_grad.reshape(row_count, model_width)
    return (
        layer_out,
        input_grad,
        attention_grads[2],
        attention_grads[0],
        attention_grads[3],
        attention_grads[4],
        attention_grads[1],
        feed_grads[2],
        feed_grads[0],
        feed_grads[1],
    )


def solution(mesh):
    placed = (
        P("fsdp", None),
        P("fsdp", None),
        P(),
        P(),
        P("fsdp"),
        P("fsdp", None),
        P("fsdp"),
        P("fsdp"),
        P("fsdp", None),
        P("fsdp"),
        P("fsdp", None),
        P("fsdp", None),
    )
    return jax.shard_map(
        body,
        mesh=mesh,
        in_specs=placed,
        out_specs=(
            P("fsdp", None),
            P("fsdp", None),
            P("fsdp"),
            P("fsdp", None),
            P("fsdp"),
            P("fsdp"),
            P("fsdp", None),
            P("fsdp"),
            P("fsdp", None),
            P("fsdp", None),
        ),
        check_vma=False,
    )
```

profile of v0, /device:TPU:0, one launch (start us, length us, event | category | flops | bytes accessed | tf_op | source)
XLA Modules:
  0.0 3013.2 jit_solution(163646904831446319)
XLA Ops:
  21.1 40.9 %all-to-all-done.4 = bf16[8,32,2048]{2,0,1:T(8,128)(2,1)S(1)} async-done(((bf16[8,32,2048]{2,0,1:T(8,128)(2,1)}), bf16[8,32,2048]{2,0,1:T(8,128)(2,1)S(1)}, u32[]{:S(2)}, u32[]{:S(2)}) %all-to-all-start.4) | async-done | bytes 1048608 | tf_op jit(solution)/shard_map/all_to_all | solution.py:60
  73.7 46.1 %all-to-all-done = bf16[8,32,2048]{2,0,1:T(8,128)(2,1)} async-done(((bf16[8,32,2048]{2,0,1:T(8,128)(2,1)}), bf16[8,32,2048]{2,0,1:T(8,128)(2,1)}, u32[]{:S(2)}, u32[]{:S(2)}) %all-to-all-start) | async-done | bytes 1048608 | tf_op jit(solution)/shard_map/all_to_all | solution.py:59
  133.5 122.9 %all-reduce.13 = (bf16[2048]{0:T(1024)(128)(2,1)S(1)}, bf16[2048]{0:T(1024)(128)(2,1)S(1)}, bf16[2048]{0:T(1024)(128)(2,1)S(1)}, bf16[2048]{0:T(1024)(128)(2,1)S(1)}) all-reduce(bf16[2048]{0:T(1024)(128)(2,1)S(1)} %dynamic-update-slice.5, bf16[2048]{0:T(1024)(128)(2,1)S(1)} %dynamic-update-slice.4, ...), channel_id=1, replica_groups=mesh['fsdp'=32] {'fsdp'}, use_global_device_ids=true, to_apply=%add.6 | all-reduce | flops 8192 | bytes 32768
  279.8 66.2 %all-to-all-done.5 = bf16[10,32,2048]{2,0,1:T(8,128)(2,1)} async-done(((bf16[10,32,2048]{2,0,1:T(8,128)(2,1)}), bf16[10,32,2048]{2,0,1:T(8,128)(2,1)}, u32[]{:S(2)}, u32[]{:S(2)}) %all-to-all-start.5) | async-done | bytes 1310752 | tf_op jit(solution)/shard_map/all_to_all | solution.py:60
  351.1 12.3 fusion.66
  378.7 9.4 fusion.58
  392.3 23.2 while.31
  415.5 10.3 fusion.32
  443.1 167.1 %all-gather.9.cloned.1.call-done = bf16[2048,11264]{1,0:T(8,128)(2,1)} async-done(((bf16[64,11264]{1,0:T(8,128)(2,1)}), bf16[2048,11264]{1,0:T(8,128)(2,1)}) %all-gather.9.cloned.1.call-update) | async-done | bytes 46137360 | tf_op jit(solution)/shard_map/all_gather | solution.py:310
  610.3 24.9 fusion.94
  635.2 120.6 %all-gather.11.cloned.1.call-done = bf16[2048,5632]{1,0:T(8,128)(2,1)} async-done(((bf16[64,5632]{1,0:T(8,128)(2,1)}), bf16[2048,5632]{1,0:T(8,128)(2,1)}) %all-gather.11.cloned.1.call-update) | async-done | bytes 23068688 | tf_op jit(solution)/shard_map/all_gather | solution.py:320
  755.8 20.4 multiply_convert_fusion.1
  776.1 22.3 multiply_reduce_fusion.1
  802.8 8.2 fusion.61
  813.9 8.5 multiply_reduce_fusion.2
  833.1 15.6 fusion.30
  853.0 23.3 while.32
  876.3 10.4 fusion.40
  904.2 15.0 bitcast_add_fusion.2
  928.9 8.3 multiply_reduce_fusion
  958.6 21.8 fusion.41
  981.6 19.9 fusion.92
  1003.1 56.4 %fusion.1 = f32[2048,11264]{1,0:T(8,128)} fusion(bf16[256,5632]{1,0:T(8,128)(2,1)} %get-tuple-element.234, bf16[256,5632]{1,0:T(8,128)(2,1)} %get-tuple-element.233, f32[256,2048]{1,0:T(8,128)S(1)} %copy-done.31, f32[2048]{0:T(1024)S(1)} %convert_element_type.129, f32[256]{0:T(256)S(1)} %add_rsqrt_fusion.1), kind=kOutput, calls=%fused_computation.26 | convolution fusion | flops 11824267264 | bytes 100148224 | tf_op jit(solution)/shard_map/dot_general | solution.py:41
  1061.7 16.3 fusion.12
  1084.1 12.5 convolution_add_fusion
  1111.5 95.8 %all-to-all-done.6 = bf16[10,32,2048]{2,0,1:T(8,128)(2,1)S(1)} async-done(((bf16[10,32,2048]{2,0,1:T(8,128)(2,1)}), bf16[10,32,2048]{2,0,1:T(8,128)(2,1)S(1)}, u32[]{:S(2)}, u32[]{:S(2)}) %all-to-all-start.6) | async-done | bytes 1310752 | tf_op jit(solution)/shard_map/all_to_all | solution.py:69
  1215.2 89.5 %all-to-all-done.2 = bf16[10,32,2048]{2,0,1:T(8,128)(2,1)} async-done(((bf16[10,32,2048]{2,0,1:T(8,128)(2,1)}), bf16[10,32,2048]{2,0,1:T(8,128)(2,1)}, u32[]{:S(2)}, u32[]{:S(2)}) %all-to-all-start.2) | async-done | bytes 1310752 | tf_op jit(solution)/shard_map/all_to_all | solution.py:66
  1315.4 24.7 all-to-all-done.3
  1343.7 49.1 %all-reduce.12 = (f32[2048]{0:T(1024)S(1)}, f32[2048]{0:T(1024)S(1)}, f32[2048]{0:T(1024)S(1)}, f32[2048]{0:T(1024)S(1)}) all-reduce(f32[2048]{0:T(1024)S(1)} %get-tuple-element.196, f32[2048]{0:T(1024)S(1)} %copy-done.58, f32[2048]{0:T(1024)S(1)} %copy-done.57, f32[2048]{0:T(1024)S(1)} %copy-done.65), channel_id=2, replica_groups=mesh['fsdp'=32] {'fsdp'}, use_global_device_ids=true, to_apply=%region_27.32.clone | all-reduce | flops 8192 | bytes 65536
  1399.6 144.7 %reduce-scatter.5.cloned.1.call-done = f32[64,6144]{1,0:T(8,128)} async-done(((f32[2048,6144]{1,0:T(8,128)}), f32[64,6144]{1,0:T(8,128)}) %reduce-scatter.5.cloned.1.call-update) | async-done | bytes 1572880 | tf_op jit(solution)/shard_map/reduce_scatter | solution.py:369
  1544.4 486.9 %reduce-scatter.11.cloned.1.call-done = f32[64,5632]{1,0:T(8,128)} async-done(((f32[2048,5632]{1,0:T(8,128)}), f32[64,5632]{1,0:T(8,128)}) %reduce-scatter.11.cloned.1.call-update) | async-done | bytes 1441808 | tf_op jit(solution)/shard_map/reduce_scatter | solution.py:359
  2031.3 974.9 %reduce-scatter.9.cloned.1.call-done = f32[64,11264]{1,0:T(8,128)} async-done(((f32[2048,11264]{1,0:T(8,128)}), f32[64,11264]{1,0:T(8,128)}) %reduce-scatter.9.cloned.1.call-update) | async-done | bytes 2883600 | tf_op jit(solution)/shard_map/reduce_scatter | solution.py:359
  (407 shorter events, 274.7 us)
Async XLA Ops:
  7.2 343.9 %all-gather.5.cloned.1.call-start = ((), (), s32[]{:S(2)}) async-start(), calls=%async_computation.12 | async-start | bytes 25952256 | tf_op jit(solution)/shard_map/all_gather | solution.py:271
  7.9 427.7 %all-gather.7.cloned.1.call-start = ((), (), s32[]{:S(2)}) async-start(), calls=%async_computation.13 | async-start | bytes 8650752 | tf_op jit(solution)/shard_map/all_gather | solution.py:301
  8.7 601.6 %all-gather.9.cloned.1.call-start = ((), (), s32[]{:S(2)}) async-start(), calls=%async_computation.14 | async-start | bytes 47579136 | tf_op jit(solution)/shard_map/all_gather | solution.py:310
  9.4 746.4 %all-gather.11.cloned.1.call-start = ((), (), s32[]{:S(2)}) async-start(), calls=%async_computation.15 | async-start | bytes 23789568 | tf_op jit(solution)/shard_map/all_gather | solution.py:320
  11.6 50.4 %all-to-all-start.4 = ((bf16[8,32,2048]{2,0,1:T(8,128)(2,1)}), bf16[8,32,2048]{2,0,1:T(8,128)(2,1)S(1)}, u32[]{:S(2)}, u32[]{:S(2)}) async-start(bf16[8,32,2048]{2,0,1:T(8,128)(2,1)} %copy.247), calls=%async_computation.4 | async-start | bytes 2097152 | tf_op jit(solution)/shard_map/all_to_all | solution.py:60
  62.0 57.9 %all-to-all-start = ((bf16[8,32,2048]{2,0,1:T(8,128)(2,1)}), bf16[8,32,2048]{2,0,1:T(8,128)(2,1)}, u32[]{:S(2)}, u32[]{:S(2)}) async-start(bf16[8,32,2048]{2,0,1:T(8,128)(2,1)} %copy.227), calls=%async_computation | async-start | bytes 2097152 | tf_op jit(solution)/shard_map/all_to_all | solution.py:59
  129.5 131.1 %all-to-all-start.1 = ((bf16[10,32,2048]{2,0,1:T(8,128)(2,1)}), bf16[10,32,2048]{2,0,1:T(8,128)(2,1)S(1)}, u32[]{:S(2)}, u32[]{:S(2)}) async-start(bf16[10,32,2048]{2,0,1:T(8,128)(2,1)} %copy.229), calls=%async_computation.1 | async-start | bytes 4194304 | tf_op jit(solution)/shard_map/all_to_all | solution.py:59
  256.4 107.2 %copy-start.49 = (f32[2048]{0:T(1024)}, f32[2048]{0:T(1024)S(1)}, u32[]{:S(2)}) copy-start(f32[2048]{0:T(1024)S(1)} %convert_element_type.122) | copy-start | bytes 24580
  256.4 94.7 %copy-start.47 = (f32[2048]{0:T(1024)}, f32[2048]{0:T(1024)S(1)}, u32[]{:S(2)}) copy-start(f32[2048]{0:T(1024)S(1)} %convert_element_type.119) | copy-start | bytes 24580
  261.9 84.0 %all-to-all-start.5 = ((bf16[10,32,2048]{2,0,1:T(8,128)(2,1)}), bf16[10,32,2048]{2,0,1:T(8,128)(2,1)}, u32[]{:S(2)}, u32[]{:S(2)}) async-start(bf16[10,32,2048]{2,0,1:T(8,128)(2,1)} %copy.249), calls=%async_computation.5 | async-start | bytes 4194304 | tf_op jit(solution)/shard_map/all_to_all | solution.py:60
  267.5 1132.1 %reduce-scatter.7.cloned.1.call-start = ((), (), s32[]{:S(2)}) async-start(), calls=%async_computation.17 | async-start | bytes 17301504 | tf_op jit(solution)/shard_map/reduce_scatter | solution.py:369
  275.9 93.9 %copy-start.66 = (f32[8]{0:T(128)}, f32[8]{0:T(128)S(1)}, u32[]{:S(2)}) copy-start(f32[8]{0:T(128)S(1)} %compare_convert_fusion.2) | copy-start | bytes 100
  275.9 87.7 %copy-start.51 = (f32[2048]{0:T(1024)}, f32[2048]{0:T(1024)S(1)}, u32[]{:S(2)}) copy-start(f32[2048]{0:T(1024)S(1)} %broadcast_subtract_fusion) | copy-start | bytes 24580
  276.0 93.8 %copy-start.55 = (f32[8,32]{1,0:T(8,128)}, f32[8,32]{1,0:T(8,128)S(1)}, u32[]{:S(2)}) copy-start(f32[8,32]{1,0:T(8,128)S(1)} %get-tuple-element.251) | copy-start | bytes 3076
  279.8 71.4 %copy-start.24 = (bf16[256,2048]{1,0:T(8,128)(2,1)}, bf16[256,2048]{1,0:T(8,128)(2,1)S(1)}, u32[]{:S(2)}) copy-start(bf16[256,2048]{1,0:T(8,128)(2,1)S(1)} %gather_fusion.4) | copy-start | bytes 3145732
  610.3 145.5 %copy-start.28 = (bf16[256,2048]{1,0:T(8,128)(2,1)S(1)}, bf16[256,2048]{1,0:T(8,128)(2,1)}, u32[]{:S(2)}) copy-start(bf16[256,2048]{1,0:T(8,128)(2,1)} %gather_fusion.8) | copy-start | bytes 3145732
  811.0 733.4 %reduce-scatter.5.cloned.1.call-start = ((), (), s32[]{:S(2)}) async-start(), calls=%async_computation.16 | async-start | bytes 51904512 | tf_op jit(solution)/shard_map/reduce_scatter | solution.py:369
  904.1 15.1 copy-start.14
  904.1 15.1 copy-start.23
  904.1 15.1 copy-start.34
  958.5 21.8 copy-start.40
  980.4 1050.9 %reduce-scatter.11.cloned.1.call-start = ((), (), s32[]{:S(2)}) async-start(), calls=%async_computation.19 | async-start | bytes 47579136 | tf_op jit(solution)/shard_map/reduce_scatter | solution.py:359
  1001.5 2004.6 %reduce-scatter.9.cloned.1.call-start = ((), (), s32[]{:S(2)}) async-start(), calls=%async_computation.18 | async-start | bytes 95158272 | tf_op jit(solution)/shard_map/reduce_scatter | solution.py:359
  1061.7 16.3 copy-start.10
  1106.2 101.2 %all-to-all-start.6 = ((bf16[10,32,2048]{2,0,1:T(8,128)(2,1)}), bf16[10,32,2048]{2,0,1:T(8,128)(2,1)S(1)}, u32[]{:S(2)}, u32[]{:S(2)}) async-start(bf16[10,32,2048]{2,0,1:T(8,128)(2,1)} %copy.263), calls=%async_computation.6 | async-start | bytes 4194304 | tf_op jit(solution)/shard_map/all_to_all | solution.py:69
  1111.5 99.7 %copy-start = (s32[256]{0:T(256)S(1)}, s32[256]{0:T(256)}, u32[]{:S(2)}) copy-start(s32[256]{0:T(256)} %get-tuple-element.256) | copy-start | bytes 3076
  1207.3 97.4 %all-to-all-start.2 = ((bf16[10,32,2048]{2,0,1:T(8,128)(2,1)}), bf16[10,32,2048]{2,0,1:T(8,128)(2,1)}, u32[]{:S(2)}, u32[]{:S(2)}) async-start(bf16[10,32,2048]{2,0,1:T(8,128)(2,1)} %copy.243), calls=%async_computation.2 | async-start | bytes 4194304 | tf_op jit(solution)/shard_map/all_to_all | solution.py:66
  1310.6 29.4 all-to-all-start.3
  1313.8 29.9 copy-start.57
  1313.8 29.9 copy-start.58
  1313.8 29.9 copy-start.65
  1340.0 55.7 %all-to-all-start.7 = ((bf16[8,32,2048]{2,0,1:T(8,128)(2,1)}), bf16[8,32,2048]{2,0,1:T(8,128)(2,1)S(1)}, u32[]{:S(2)}, u32[]{:S(2)}) async-start(bf16[8,32,2048]{2,0,1:T(8,128)(2,1)} %copy.265), calls=%async_computation.7 | async-start | bytes 2097152 | tf_op jit(solution)/shard_map/all_to_all | solution.py:69
  (62 other events, 335.6 us)
Sparse Core Ops, SparseCore 0:
  10.9 238.3 all-gather.4
  252.2 100.8 all-gather.6
  356.0 254.2 all-gather.8
  612.9 142.7 all-gather.10
  811.1 181.0 reduce-scatter.6
  999.1 545.2 reduce-scatter.4
  1547.2 484.0 reduce-scatter.10
  2034.2 971.9 reduce-scatter.8
where the time goes:
time: 3030 us; the launch traced here: 3010 us
  waiting for transfers between devices  2260 us (75%)
  matrix products  327 us (11%)
  blocking collectives  172 us (6%)
  local copies, waits for them, and re-layouts  102 us (3%)
  other arithmetic  102 us (3%)
  starting transfers between devices  33.7 us (1%)
    reduce_scatter x2, waiting for transfers between devices, body(): lax.psum_scatter((transposed_rows(normed_rows, d_gate_pre), transposed_ro...  1460 us
    unnamed x2, blocking collectives  172 us
    all_gather x1, waiting for transfers between devices, body(): weight_piece = lax.all_gather(gate_up, 'fsdp', axis=0, tiled=True)  167 us
    reduce_scatter x2, waiting for transfers between devices, body(): lax.psum_scatter((transposed_rows(first_normed, d_projected), transposed_...  145 us
    all_gather x1, waiting for transfers between devices, body(): lax.all_gather(down_proj, 'fsdp', axis=0, tiled=True)  121 us
    all_to_all x2, waiting for transfers between devices, carry_out(): lax.all_to_all(first_part.astype(jnp.bfloat16), 'fsdp', split_axis=1, con...  114 us
    all_to_all x2, waiting for transfers between devices, carry_in(): lax.all_to_all(second_part, 'fsdp', split_axis=1, concat_axis=1, tiled=True)  107 us
    dot_general x4, matrix products, transposed_rows(): lax.dot_general(left_side, right_side, (((0,), (0,)), ((), ())), preferre...  106 us
  transfers between devices with their start and end apart: 16, of which 11 were waited for; matrix products, arithmetic and copies ran while one was open for 15% of the time, Pallas kernels for 0%

commit v1 on v0

v1 whole, which is shorter than its diff:
```python
import functools

import jax
import jax.numpy as jnp
from jax import lax
from jax.experimental import pallas as pl
from jax.experimental.pallas import tpu as pltpu
from jax.sharding import PartitionSpec as P

HEADS = 16
CHUNK = 64
HALF = 32
MAXLEN = 128
GROUP = 8
MESH_ID = pl.DeviceIdType.MESH
VMEM = pl.BlockSpec(memory_space=pltpu.VMEM)
SMEM = pl.BlockSpec(memory_space=pltpu.SMEM)
ANY = pl.BlockSpec(memory_space=pl.ANY)

norm_eps = 1e-05
f32 = jnp.float32
bf16 = jnp.bfloat16


def inverse_rms(values):
    return lax.rsqrt(jnp.mean(values * values, axis=-1, keepdims=True) + norm_eps)


def rms_back(grad_scaled, scaled, inverse):
    return inverse * (grad_scaled - scaled * jnp.mean(grad_scaled * scaled, axis=-1, keepdims=True))


def dot_nt(left, right):
    return lax.dot_general(left, right, (((1,), (1,)), ((), ())), preferred_element_type=f32)


def dot_nn(left, right):
    return lax.dot_general(left, right, (((1,), (0,)), ((), ())), preferred_element_type=f32)


def dot_tn(left, right):
    return lax.dot_general(left, right, (((0,), (0,)), ((), ())), preferred_element_type=f32)


def places():
    me = lax.axis_index("fsdp")
    slot = lax.rem(me, GROUP)
    core = lax.rem(slot, 2)
    step_low = 2 - 4 * lax.rem(slot // 2, 2)
    step_high = 4 - 8 * (slot // 4)
    step_core = 1 - 2 * core
    first_step = (1 - core) * step_low + core * step_high
    second_step = core * step_low + (1 - core) * step_high
    return me, slot, step_core, first_step, second_step


def greet(others):
    barrier = pltpu.get_barrier_semaphore()
    for other in others:
        pl.semaphore_signal(barrier, inc=1, device_id=(other,), device_id_type=MESH_ID)
    pl.semaphore_wait(barrier, len(others))


def remote(source, target, send_sem, recv_sem, device):
    return pltpu.make_async_remote_copy(
        src_ref=source,
        dst_ref=target,
        send_sem=send_sem,
        recv_sem=recv_sem,
        device_id=(device,),
        device_id_type=MESH_ID,
    )


def group_gather_kernel(x_ref, out_ref, send_sem, recv_sem, own_sem):
    me, slot, step_core, first_step, second_step = places()
    first, second, mate = me + first_step, me + second_step, me + step_core
    greet((first, second, mate))

    def block(place):
        return out_ref.at[:, place]

    own = pltpu.make_async_copy(x_ref, block(slot), own_sem)
    sent = []

    def send(source, place, number, target):
        copy = remote(source, block(place), send_sem.at[number], recv_sem.at[number], target)
        copy.start()
        sent.append(copy)

    def arrived(place, number, source):
        remote(
            block(place), block(place), send_sem.at[number], recv_sem.at[number], source
        ).wait_recv()

    from_first, from_second = slot + first_step, slot + second_step
    corner = slot + first_step + second_step
    send(x_ref, slot, 0, first)
    send(x_ref, slot, 1, second)
    send(x_ref, slot, 2, mate)
    own.start()
    arrived(from_first, 0, first)
    send(block(from_first), from_first, 3, second)
    send(block(from_first), from_first, 4, mate)
    arrived(from_second, 1, second)
    send(block(from_second), from_second, 5, mate)
    arrived(corner, 3, second)
    send(block(corner), corner, 6, mate)
    arrived(slot + step_core, 2, mate)
    arrived(slot + step_core + second_step, 4, mate)
    arrived(slot + step_core + first_step, 5, mate)
    arrived(corner + step_core, 6, mate)
    for copy in sent:
        copy.wait_send()
    own.wait()


def group_gather(x, number):
    parts, rows, columns = x.shape
    return pl.pallas_call(
        group_gather_kernel,
        out_shape=jax.ShapeDtypeStruct((parts, GROUP, rows, columns), x.dtype),
        in_specs=[ANY],
        out_specs=ANY,
        scratch_shapes=[
            pltpu.SemaphoreType.DMA((7,)),
            pltpu.SemaphoreType.DMA((7,)),
            pltpu.SemaphoreType.DMA,
        ],
        compiler_params=pltpu.CompilerParams(collective_id=number, has_side_effects=True),
        cost_estimate=pl.CostEstimate(flops=0, transcendentals=0, bytes_accessed=150_000_000),
    )(x)


def group_scatter_kernel(slab_rows, x_ref, out_ref, near, far, going, send_sem, recv_sem):
    me, slot, step_core, first_step, second_step = places()
    first, second, mate = me + first_step, me + second_step, me + step_core
    greet((first, second, mate))
    parts, rows, _ = out_ref.shape
    corner_step = first_step + second_step
    steps = (corner_step, first_step, second_step, corner_step * 0)
    mate_steps = (corner_step, second_step, first_step, corner_step * 0)
    sent = []

    def send(source, target, number, device):
        copy = remote(source, target, send_sem.at[number], recv_sem.at[number], device)
        copy.start()
        sent.append(copy)

    def arrived(ref, number, source):
        remote(ref, ref, send_sem.at[number], recv_sem.at[number], source).wait_recv()

    def add(kind, extra, target):
        place = slot + steps[kind]

        def slab(i, _):
            part = i // (rows // slab_rows)
            at = pl.ds(
                pl.multiple_of(lax.rem(i, rows // slab_rows) * slab_rows, slab_rows), slab_rows
            )
            total = x_ref[part, place, at, :].astype(f32) + near[kind, part, at, :].astype(f32)
            for ref in extra:
                total = total + ref[part, at, :].astype(f32)
            target[part, at, :] = total.astype(target.dtype)
            return 0

        lax.fori_loop(0, parts * (rows // slab_rows), slab, 0)

    for kind in (0, 2, 1, 3):
        send(x_ref.at[:, slot + step_core + mate_steps[kind]], near.at[kind], kind, mate)
    arrived(near.at[0], 0, mate)
    add(0, (), going.at[0])
    send(going.at[0], far.at[0], 4, second)
    arrived(near.at[2], 2, mate)
    add(2, (), going.at[2])
    send(going.at[2], far.at[2], 5, second)
    arrived(near.at[1], 1, mate)
    arrived(far.at[0], 4, second)
    add(1, (far.at[0],), going.at[1])
    send(going.at[1], far.at[1], 6, first)
    arrived(near.at[3], 3, mate)
    arrived(far.at[2], 5, second)
    arrived(far.at[1], 6, first)
    add(3, (far.at[1], far.at[2]), out_ref)
    for copy in sent:
        copy.wait_send()


def group_scatter(x, number, out_type):
    parts, _, rows, columns = x.shape
    return pl.pallas_call(
        functools.partial(group_scatter_kernel, min(32, rows)),
        out_shape=jax.ShapeDtypeStruct((parts, rows, columns), out_type),
        in_specs=[VMEM],
        out_specs=VMEM,
        scratch_shapes=[
            pltpu.VMEM((4, parts, rows, columns), x.dtype),
            pltpu.VMEM((3, parts, rows, columns), x.dtype),
            pltpu.VMEM((3, parts, rows, columns), x.dtype),
            pltpu.SemaphoreType.DMA((7,)),
            pltpu.SemaphoreType.DMA((7,)),
        ],
        compiler_params=pltpu.CompilerParams(
            collective_id=number, has_side_effects=True, vmem_limit_bytes=48 * 2**20
        ),
        cost_estimate=pl.CostEstimate(flops=0, transcendentals=0, bytes_accessed=130_000_000),
    )(x)


def low(values):
    return values.astype(bf16).astype(f32)


def gates(proj_ref, floor_ref, rows, head, heads):
    dim = floor_ref.shape[1] // heads
    wide = heads * dim
    lo = head * dim
    q_pre = proj_ref[rows, lo : lo + dim]
    f_pre = proj_ref[rows, wide + lo : wide + lo + dim]
    value = proj_ref[rows, 2 * wide + lo : 2 * wide + lo + dim].astype(bf16)
    floor = floor_ref[:, lo : lo + dim]
    q_sigmoid = jax.nn.sigmoid(q_pre)
    query = low(q_pre * q_sigmoid)
    f_sigmoid = jax.nn.sigmoid(f_pre)
    forget = floor + (1.0 - floor) * f_sigmoid
    key = low(1.0 - forget)
    row = lax.broadcasted_iota(jnp.int32, (CHUNK, dim), 0)
    in_half = lax.rem(row, HALF)
    product = forget
    step = 1
    while step < HALF:
        product = jnp.where(in_half >= step, product * pltpu.roll(product, step, 0), product)
        step *= 2
    middle = product[HALF - 1 : HALF, :]
    end = product[CHUNK - 1 : CHUNK, :]
    ratio = jnp.where(row < HALF, product / middle, product)
    inverse = 1.0 / ratio
    return {
        "q_pre": q_pre,
        "q_sigmoid": q_sigmoid,
        "f_sigmoid": f_sigmoid,
        "forget": forget,
        "value": value,
        "floor": floor,
        "middle": middle,
        "end": end,
        "ratio": ratio,
        "inverse": inverse,
        "row": row,
        "query_mid": query * ratio,
        "key_mid": key * inverse,
    }


def whole_fade(g, last):
    return g["middle"] * g["end"] * jnp.where(last < 0, 1.0, 0.0)


def tail_keys(g, last):
    return jnp.where(g["row"] >= last, g["key_mid"] * g["end"], 0.0).astype(bf16)


def entry_queries(g, carried):
    return jnp.where(carried, g["query_mid"] * g["middle"], 0.0).astype(bf16)


def next_state(g, last, state):
    return state * whole_fade(g, last) + dot_tn(g["value"], tail_keys(g, last))


def forward_kernel(
    heads, last_ref, proj_ref, start_ref, floor_ref, gain_ref, in_ref, mix_ref, out_ref, enter_ref, state
):
    dim = floor_ref.shape[1] // heads
    state[...] = in_ref[...]

    def step(n, _):
        base = pl.multiple_of(n * CHUNK, CHUNK)
        rows = pl.ds(base, CHUNK)
        starts = start_ref[rows, :] - base
        last = last_ref[n] - base
        column = lax.broadcasted_iota(jnp.int32, (CHUNK, CHUNK), 1)
        line = lax.broadcasted_iota(jnp.int32, (CHUNK, CHUNK), 0)
        within = (column <= line) & (column >= starts)
        carried = starts < 0
        for head in range(heads):
            lo = head * dim
            g = gates(proj_ref, floor_ref, rows, head, heads)
            now = state[head]
            enter_ref[n, head] = now
            scores = dot_nt(g["query_mid"].astype(bf16), g["key_mid"].astype(bf16))
            scores = jnp.where(within, scores, 0.0).astype(bf16)
            out = dot_nn(scores, g["value"]) + dot_nt(entry_queries(g, carried), now.astype(bf16))
            state[head] = next_state(g, last, now)
            out_ref[rows, lo : lo + dim] = out
            mix_ref[rows, lo : lo + dim] = (
                out * inverse_rms(out) * gain_ref[:, lo : lo + dim]
            ).astype(bf16)
        return 0

    lax.fori_loop(0, proj_ref.shape[0] // CHUNK, step, 0)


def last_state_kernel(heads, last_ref, proj_ref, floor_ref, out_ref):
    for head in range(heads):
        state = jnp.zeros(out_ref.shape[1:], f32)
        for n in range(proj_ref.shape[0] // CHUNK):
            g = gates(proj_ref, floor_ref, pl.ds(n * CHUNK, CHUNK), head, heads)
            state = next_state(g, last_ref[n] - n * CHUNK, state)
        out_ref[head] = state


def state_grad(out_ref, dmix_ref, gain_ref, rows, lo, dim):
    out = out_ref[rows, lo : lo + dim]
    inverse = inverse_rms(out)
    scaled = out * inverse
    dmix = dmix_ref[rows, lo : lo + dim].astype(f32)
    grad = rms_back(dmix * gain_ref[:, lo : lo + dim], scaled, inverse)
    return grad, jnp.sum(dmix * scaled, axis=0, keepdims=True)


def backward_kernel(
    heads,
    last_ref,
    proj_ref,
    start_ref,
    floor_ref,
    gain_ref,
    out_ref,
    dmix_ref,
    enter_ref,
    in_ref,
    dproj_ref,
    dfloor_ref,
    dgain_ref,
    later,
):
    dim = floor_ref.shape[1] // heads
    wide = heads * dim
    chunks = proj_ref.shape[0] // CHUNK
    later[...] = in_ref[...]
    dfloor_ref[...] = jnp.zeros_like(dfloor_ref)
    dgain_ref[...] = jnp.zeros_like(dgain_ref)

    def step(i, _):
        n = chunks - 1 - i
        base = pl.multiple_of(n * CHUNK, CHUNK)
        rows = pl.ds(base, CHUNK)
        starts = start_ref[rows, :] - base
        last = last_ref[n] - base
        column = lax.broadcasted_iota(jnp.int32, (CHUNK, CHUNK), 1)
        line = lax.broadcasted_iota(jnp.int32, (CHUNK, CHUNK), 0)
        within = (column <= line) & (column >= starts)
        carried = starts < 0
        for head in range(heads):
            lo = head * dim
            g = gates(proj_ref, floor_ref, rows, head, heads)
            grad, dgain = state_grad(out_ref, dmix_ref, gain_ref, rows, lo, dim)
            grad_hi = grad.astype(bf16)
            grad_lo = (grad - grad_hi.astype(f32)).astype(bf16)
            state = enter_ref[n, head]
            after = later[head]
            after_low = after.astype(bf16)
            query_mid = g["query_mid"].astype(bf16)
            key_mid = g["key_mid"].astype(bf16)
            scores = jnp.where(within, dot_nt(query_mid, key_mid), 0.0).astype(bf16)
            d_scores = dot_nt(grad_hi, g["value"]) + dot_nt(grad_lo, g["value"])
            d_scores = jnp.where(within, d_scores, 0.0).astype(bf16)
            query_in = entry_queries(g, carried)
            key_out = tail_keys(g, last)
            d_query_mid = dot_nn(d_scores, key_mid)
            d_query_in = jnp.where(carried, dot_nn(grad_hi, state.astype(bf16)), 0.0)
            d_key_mid = dot_tn(d_scores, query_mid)
            d_key_out = jnp.where(g["row"] >= last, dot_nn(g["value"], after_low), 0.0)
            d_value = dot_tn(scores, grad_hi) + dot_nt(key_out, after_low)
            d_query = (d_query_mid + d_query_in * g["middle"]) * g["ratio"]
            d_key = (d_key_mid + d_key_out * g["end"]) * g["inverse"]
            tail = d_key_out * key_out.astype(f32)
            term = (
                d_query_mid * query_mid.astype(f32)
                + d_query_in * query_in.astype(f32)
                - d_key_mid * key_mid.astype(f32)
                - tail
            )
            fade = whole_fade(g, last)
            final = jnp.sum(tail, axis=0, keepdims=True) + fade * jnp.sum(
                state * after, axis=0, keepdims=True
            )
            step_rows = 1
            while step_rows < CHUNK:
                term = jnp.where(
                    g["row"] < CHUNK - step_rows,
                    term + pltpu.roll(term, CHUNK - step_rows, 0),
                    term,
                )
                step_rows *= 2
            d_forget = (term + final) / g["forget"] - d_key
            q_sigmoid, f_sigmoid = g["q_sigmoid"], g["f_sigmoid"]
            d_q_pre = d_query * q_sigmoid * (1.0 + g["q_pre"] * (1.0 - q_sigmoid))
            d_floor = d_forget * (1.0 - f_sigmoid)
            d_f_pre = d_floor * (1.0 - g["floor"]) * f_sigmoid
            dproj_ref[rows, lo : lo + dim] = d_q_pre.astype(bf16)
            dproj_ref[rows, wide + lo : wide + lo + dim] = d_f_pre.astype(bf16)
            dproj_ref[rows, 2 * wide + lo : 2 * wide + lo + dim] = d_value.astype(bf16)
            dfloor_ref[:, lo : lo + dim] += jnp.sum(d_floor, axis=0, keepdims=True)
            dgain_ref[:, lo : lo + dim] += dgain
            later[head] = after * fade + dot_tn(grad_hi, query_in)
        return 0

    lax.fori_loop(0, chunks, step, 0)


def first_grad_kernel(
    heads, last_ref, proj_ref, start_ref, floor_ref, gain_ref, out_ref, dmix_ref, grad_ref
):
    dim = floor_ref.shape[1] // heads
    for head in range(heads):
        after = jnp.zeros((dim, dim), f32)
        for n in range(proj_ref.shape[0] // CHUNK - 1, -1, -1):
            rows = pl.ds(n * CHUNK, CHUNK)
            g = gates(proj_ref, floor_ref, rows, head, heads)
            grad, _ = state_grad(out_ref, dmix_ref, gain_ref, rows, head * dim, dim)
            queries = entry_queries(g, start_ref[rows, :] < n * CHUNK)
            after = after * whole_fade(g, last_ref[n] - n * CHUNK) + dot_tn(
                grad.astype(bf16), queries
            )
        grad_ref[head] = after


def local_call(kernel, heads, out_shape, scratch, *operands):
    return pl.pallas_call(
        functools.partial(kernel, heads),
        out_shape=out_shape,
        in_specs=[SMEM] + [VMEM] * (len(operands) - 1),
        out_specs=jax.tree.map(lambda _: VMEM, out_shape),
        scratch_shapes=scratch,
        compiler_params=pltpu.CompilerParams(vmem_limit_bytes=48 * 2**20),
    )(*operands)


def body(
    tokens,
    cotangent,
    dealt_lengths,
    deal,
    norm_gain,
    mixer_in,
    forget_floor,
    group_gain,
    out_proj,
    ffn_gain,
    gate_up,
    down_proj,
):
    row_count, width = tokens.shape
    weight_rows = mixer_in.shape[0]
    device_count = lax.axis_size("fsdp")
    groups = device_count // GROUP
    own_index = lax.axis_index("fsdp")
    slot = lax.rem(own_index, GROUP)
    group = own_index // GROUP
    group_rows = GROUP * row_count
    heads = HEADS // GROUP
    own_width = width // GROUP
    dim = width // HEADS
    ffn_width = down_proj.shape[1]
    own_ffn = ffn_width // GROUP
    planes = [[g * GROUP + s for s in range(GROUP)] for g in range(groups)]
    lines = [[g * GROUP + s for g in range(groups)] for s in range(GROUP)]

    def swap(x):
        return lax.all_to_all(x, "fsdp", 0, 0, axis_index_groups=planes, tiled=True)

    def line_gather(x):
        return lax.all_gather(x, "fsdp", axis=0, axis_index_groups=lines, tiled=True)

    def line_scatter(x):
        return lax.psum_scatter(
            x, "fsdp", scatter_dimension=0, axis_index_groups=lines, tiled=True
        )

    def own_columns(weight, pieces):
        columns = weight.shape[1] // (pieces * GROUP)
        parted = weight.reshape(weight_rows, pieces, GROUP, columns).transpose(2, 0, 1, 3)
        swapped = swap(parted.reshape(GROUP, weight_rows, pieces * columns))
        return line_gather(swapped.reshape(GROUP * weight_rows, pieces * columns))

    def home_rows(grad, pieces):
        columns = grad.shape[1] // pieces
        summed = line_scatter(grad.astype(bf16)).reshape(GROUP, weight_rows, pieces * columns)
        swapped = swap(summed).reshape(GROUP, weight_rows, pieces, columns)
        return swapped.transpose(1, 2, 0, 3).reshape(weight_rows, -1).astype(f32)

    seq_count = deal.shape[0]
    seq_ids = jnp.arange(seq_count, dtype=jnp.int32)
    matches = deal[:, None] == seq_ids[None, :]
    lengths = jnp.sum(jnp.where(matches, dealt_lengths[:, None], 0), axis=0)
    seq_starts = jnp.sum(
        jnp.where(seq_ids[:, None] < seq_ids[None, :], lengths[:, None], 0), axis=0
    )
    group_start = group * group_rows
    rows_here = group_start + jnp.arange(group_rows, dtype=jnp.int32)
    starts = (
        jnp.max(jnp.where(seq_starts[None, :] <= rows_here[:, None], seq_starts[None, :], 0), axis=1)
        - group_start
    )
    start_column = starts[:, None]
    last_starts = starts[CHUNK - 1 :: CHUNK]

    gains = lax.all_gather(
        jnp.stack([norm_gain, forget_floor, group_gain, ffn_gain]), "fsdp", axis=1, tiled=True
    ).astype(f32)
    first_gain = gains[0:1]
    second_gain = gains[3:4]
    own_gains = lax.dynamic_slice_in_dim(gains, slot * own_width, own_width, 1)
    own_floor = own_gains[1:2]
    own_group_gain = own_gains[2:3]

    mixer_weight = own_columns(mixer_in, 3)
    out_lines = lax.all_gather(out_proj, "fsdp", axis=0, axis_index_groups=lines)
    ffn_weight = own_columns(gate_up, 2)
    down_weight = own_columns(down_proj, 1)

    inputs = tokens.astype(f32)
    first_inverse = inverse_rms(inputs)
    first_scaled = inputs * first_inverse
    first_normed = (first_scaled * first_gain).astype(bf16)
    first_all = group_gather(first_normed[None], 0).reshape(group_rows, width)
    tail_projected = dot_nn(first_all[group_rows - MAXLEN :], mixer_weight)
    edge = MAXLEN // CHUNK
    state_type = jax.ShapeDtypeStruct((heads, dim, dim), f32)
    last_state = local_call(
        last_state_kernel,
        heads,
        state_type,
        [],
        last_starts[-edge:] - (group_rows - MAXLEN),
        tail_projected,
        own_floor,
    )
    up_line = [(i, i + GROUP) for i in range(device_count - GROUP)]
    down_line = [(i + GROUP, i) for i in range(device_count - GROUP)]
    entering_state = lax.ppermute(last_state, "fsdp", up_line)
    projected = dot_nn(first_all, mixer_weight)
    chunks = group_rows // CHUNK
    mixed_heads, state_out, entering = local_call(
        forward_kernel,
        heads,
        (
            jax.ShapeDtypeStruct((group_rows, own_width), bf16),
            jax.ShapeDtypeStruct((group_rows, own_width), f32),
            jax.ShapeDtypeStruct((chunks, heads, dim, dim), f32),
        ),
        [pltpu.VMEM((heads, dim, dim), f32)],
        last_starts,
        projected,
        start_column,
        own_floor,
        own_group_gain,
        entering_state,
    )
    mixer_input = (
        swap(mixed_heads.reshape(GROUP, row_count, own_width))
        .transpose(1, 0, 2)
        .reshape(row_count, width)
    )
    out_weight = group_gather(out_lines, 1).reshape(width, width)
    residual = inputs + dot_nn(mixer_input, out_weight)
    second_inverse = inverse_rms(residual)
    second_scaled = residual * second_inverse
    second_normed = (second_scaled * second_gain).astype(bf16)
    second_all = group_gather(second_normed[None], 0).reshape(group_rows, width)
    cot_late, second_all = lax.optimization_barrier((cotangent, second_all))
    cot_all = group_gather(cot_late[None], 0).reshape(group_rows, width)
    gate_pre = dot_nn(second_all, ffn_weight)
    gate_part = gate_pre[:, :own_ffn]
    up_part = gate_pre[:, own_ffn:]
    gate_sigmoid = jax.nn.sigmoid(gate_part)
    gate_act = gate_part * gate_sigmoid
    hidden_act = (gate_act * up_part).astype(bf16)
    d_down_proj = home_rows(dot_tn(cot_all, hidden_act), 1)
    ffn_part = dot_nt(hidden_act, down_weight).astype(bf16)
    d_hidden = dot_nn(cot_all, down_weight)
    d_gate_pre = jnp.concatenate(
        [
            d_hidden * up_part * gate_sigmoid * (1.0 + gate_part * (1.0 - gate_sigmoid)),
            d_hidden * gate_act,
        ],
        axis=1,
    ).astype(bf16)
    d_gate_up = home_rows(dot_tn(second_all, d_gate_pre), 2)
    second_part = dot_nt(d_gate_pre, ffn_weight).astype(bf16)
    d_second = group_scatter(second_part.reshape(1, GROUP, row_count, width), 2, f32)[0]
    d_residual = cotangent.astype(f32) + rms_back(
        d_second * second_gain, second_scaled, second_inverse
    )
    d_mix_out = d_residual.astype(bf16)
    d_mixer_input = dot_nt(d_mix_out, out_weight).astype(bf16)
    d_mixed_heads = swap(
        d_mixer_input.reshape(row_count, GROUP, own_width).transpose(1, 0, 2)
    ).reshape(group_rows, own_width)
    first_grad = local_call(
        first_grad_kernel,
        heads,
        state_type,
        [],
        last_starts[:edge],
        projected[:MAXLEN],
        start_column[:MAXLEN],
        own_floor,
        own_group_gain,
        state_out[:MAXLEN],
        d_mixed_heads[:MAXLEN],
    )
    entering_grad = lax.ppermute(first_grad, "fsdp", down_line)
    d_projected, floor_grad, group_gain_grad = local_call(
        backward_kernel,
        heads,
        (
            jax.ShapeDtypeStruct((group_rows, 3 * own_width), bf16),
            jax.ShapeDtypeStruct((1, own_width), f32),
            jax.ShapeDtypeStruct((1, own_width), f32),
        ),
        [pltpu.VMEM((heads, dim, dim), f32)],
        last_starts,
        projected,
        start_column,
        own_floor,
        own_group_gain,
        state_out,
        d_mixed_heads,
        entering,
        entering_grad,
    )
    d_mixer_in = home_rows(dot_tn(first_all, d_projected), 3)
    first_part = dot_nt(d_projected, mixer_weight).astype(bf16)
    d_first = group_scatter(first_part.reshape(1, GROUP, row_count, width), 2, f32)[0]
    d_dealt = d_residual + rms_back(d_first * first_gain, first_scaled, first_inverse)

    ffn_out = group_scatter(ffn_part.reshape(1, GROUP, row_count, width), 2, f32)[0]
    layer_out = residual + ffn_out
    out_part = dot_tn(mixer_input, d_mix_out).astype(bf16)
    out_sum = group_scatter(out_part.reshape(groups, GROUP, weight_rows, width), 3, bf16)
    d_out_proj = line_scatter(out_sum.reshape(groups * weight_rows, width)).astype(f32)

    spread = jnp.zeros((2, width), f32)
    own_grads = jnp.concatenate([floor_grad, group_gain_grad])
    gain_grads = jnp.concatenate(
        [
            jnp.sum(d_first * first_scaled, axis=0, keepdims=True),
            lax.dynamic_update_slice_in_dim(spread, own_grads, slot * own_width, 1),
            jnp.sum(d_second * second_scaled, axis=0, keepdims=True),
        ]
    )
    gain_sums = lax.psum_scatter(gain_grads, "fsdp", scatter_dimension=1, tiled=True)
    return (
        layer_out,
        d_dealt,
        gain_sums[0],
        d_mixer_in,
        gain_sums[1],
        gain_sums[2],
        d_out_proj,
        gain_sums[3],
        d_gate_up,
        d_down_proj,
    )


def solution(mesh):
    by_rows = P("fsdp", None)
    by_one = P("fsdp")
    return jax.shard_map(
        body,
        mesh=mesh,
        in_specs=(
            by_rows,
            by_rows,
            P(),
            P(),
            by_one,
            by_rows,
            by_one,
            by_one,
            by_rows,
            by_one,
            by_rows,
            by_rows,
        ),
        out_specs=(
            by_rows,
            by_rows,
            by_one,
            by_rows,
            by_one,
            by_one,
            by_rows,
            by_one,
            by_rows,
            by_rows,
        ),
        check_vma=False,
    )
```

time: 3030 us -> 944 us (0.31)
  waiting for transfers between devices: 2260 us -> 180 us
  Pallas kernels: 0 us -> 406 us
  matrix products: 327 us -> 147 us
  other arithmetic: 102 us -> 13.2 us
  blocking collectives: 172 us -> 101 us
  local copies, waits for them, and re-layouts: 102 us -> 47.8 us
    reduce_scatter x4, waiting for transfers between devices: 1610 us -> 29.5 us  [line_scatter(): lax.psum_scatter(x, 'fsdp', scatter_dimension=0, axis_index_groups=lines,...]
    pallas_call x0 -> x12, Pallas kernels: none -> 406 us  [the longest x4 179 us: group_gather(): pl.pallas_call(group_gather_kernel, out_shape=jax.ShapeDtypeStruct((parts...]
    all_to_all x8 -> x5, waiting for transfers between devices: 363 us -> 12.6 us  [swap(): return lax.all_to_all(x, 'fsdp', 0, 0, axis_index_groups=planes, tiled=True)]
    all_gather x4, waiting for transfers between devices: 288 us -> 0.04 us  [the longest x3 0.02 us: line_gather(): lax.all_gather(x, 'fsdp', axis=0, axis_index_groups=lines, tiled=True)]
    dot_general x24 -> x13, matrix products: 327 us -> 147 us  [the longest x5 54.6 us: dot_nn(): lax.dot_general(left, right, (((1,), (0,)), ((), ())), preferred_element_...]
    unnamed x2 -> x0, blocking collectives: 172 us -> none
    unnamed x8 -> x10, waiting for transfers between devices: 2.65 us -> 132 us
    all_to_all x0 -> x3, blocking collectives: none -> 57.1 us  [swap(): return lax.all_to_all(x, 'fsdp', 0, 0, axis_index_groups=planes, tiled=True)]
  transfers between devices with their start and end apart: 16 -> 16, of which waited for: 11 -> 5; matrix products, arithmetic and copies ran while one was open for 15% -> 17% of each run, Pallas kernels for 0% -> 43%
where the time goes in v1:
time: 944 us; the launch traced here: 934 us
  Pallas kernels  406 us (43%)
  waiting for transfers between devices  180 us (19%)
  matrix products  147 us (16%)
  blocking collectives  101 us (11%)
  local copies, waits for them, and re-layouts  47.8 us (5%)
  starting transfers between devices  24.6 us (3%)
  between operations  14.8 us (2%)
  other arithmetic  13.2 us (1%)
    pallas_call x4, Pallas kernels, group_gather(): pl.pallas_call(group_gather_kernel, out_shape=jax.ShapeDtypeStruct((parts...  179 us
    pallas_call x4, Pallas kernels, group_scatter(): pl.pallas_call(functools.partial(group_scatter_kernel, min(32, rows)), ou...  178 us
    unnamed x10, waiting for transfers between devices  132 us
    all_to_all x3, blocking collectives, swap(): return lax.all_to_all(x, 'fsdp', 0, 0, axis_index_groups=planes, tiled=True)  57.1 us
    dot_general x5, matrix products, dot_nn(): lax.dot_general(left, right, (((1,), (0,)), ((), ())), preferred_element_...  54.6 us
    dot_general x4, matrix products, dot_tn(): lax.dot_general(left, right, (((0,), (0,)), ((), ())), preferred_element_...  49.8 us
    pallas_call x4, Pallas kernels, local_call(): pl.pallas_call(functools.partial(kernel, heads), out_shape=out_shape, in_...  49.8 us
    all_gather x1, blocking collectives, body(): lax.all_gather(jnp.stack([norm_gain, forget_floor, group_gain, ffn_gain])...  44.3 us
  transfers between devices with their start and end apart: 16, of which 5 were waited for; matrix products, arithmetic and copies ran while one was open for 17% of the time, Pallas kernels for 43%

profile of v1, /device:TPU:0, one launch (start us, length us, event | category | flops | bytes accessed | tf_op | source)
XLA Modules:
  0.0 934.3 jit_solution(11569861272876452306)
XLA Ops:
  9.9 17.6 %all_to_all.40 = bf16[8,64,768]{2,1,0:T(8,128)(2,1)} all-to-all(bf16[8,64,768]{2,1,0:T(8,128)(2,1)S(1)} %reshape.157), channel_id=1, replica_groups={{0,1,2,3,4,5,6,7},{8,9,10,11,12,13,14,15},{16,17,18,19,20,21,22,23},{24..., dimensions={0} | all-to-all | bytes 1572864 | tf_op jit(solution)/shard_map/all_to_all | solution.py:472
  34.0 22.7 %all_to_all.41 = bf16[8,64,1408]{2,1,0:T(8,128)(2,1)} all-to-all(bf16[8,64,1408]{2,1,0:T(8,128)(2,1)S(1)} %reshape.164), channel_id=1, replica_groups={{0,1,2,3,4,5,6,7},{8,9,10,11,12,13,14,15},{16,17,18,19,20,21,22,23},{24..., dimensions={0} | all-to-all | bytes 2883584 | tf_op jit(solution)/shard_map/all_to_all | solution.py:472
  64.0 44.3 %all-gather.1 = bf16[32,64,4]{1,2,0:T(4,128)(2,1)S(1)} all-gather(bf16[1,64,4]{1,2,0:T(4,128)(2,1)S(1)} %maximum_bitcast_fusion), channel_id=1, replica_groups=mesh['fsdp'=32] {'fsdp'}, dimensions={0}, use_global_device_ids=true | all-gather | bytes 16896 | tf_op jit(solution)/shard_map/all_gather | solution.py:510
  110.0 39.7 %shard_map.195 = bf16[1,8,256,2048]{3,2,1,0:T(8,128)(2,1)} custom-call(bf16[1,256,2048]{2,1,0:T(8,128)(2,1)} %fusion.14.x_ref), custom_call_target="tpu_custom_call" | custom-call | bytes 150000000 | tf_op jit(solution)/shard_map/pallas_call | solution.py:120
  155.2 10.6 %fusion.25.proj_ref = f32[2048,768]{1,0:T(8,128)} fusion(bf16[2048,2048]{1,0:T(8,128)(2,1)} %bitcast.142, bf16[2048,768]{1,0:T(8,128)(2,1)S(1)} %copy-done.9), kind=kOutput, calls=%fused_computation.73 | convolution fusion | flops 6442450944 | bytes 17825792 | tf_op jit(solution)/shard_map/dot_general | solution.py:38
  165.8 18.5 %shard_map.197 = (bf16[2048,256]{1,0:T(8,128)(2,1)S(1)}, f32[2048,256]{1,0:T(8,128)S(1)}, f32[32,2,128,128]{3,2,1,0:T(8,128)}) custom-call(s32[32]{0:T(128)S(1)} %slice.57.last_ref, f32[2048,768]{1,0:T(8,128)} %fusion.25.proj_ref, s32[2048,1]{1,0:T(8,128)S(1)} %copy.80.start_ref, f32[1,256]{1,0:T(1,128)S(1)} %get-tuple-element.42.floor_ref, ...), custom_call_target="tpu_custom_call" | custom-call | tf_op jit(solution)/shard_map/pallas_call | solution.py:431
  187.0 5.7 all-to-all-start.1
  193.5 53.6 %shard_map.198 = bf16[4,8,64,2048]{3,2,1,0:T(8,128)(2,1)} custom-call(bf16[4,64,2048]{2,1,0:T(8,128)(2,1)} %bitcast.165), custom_call_target="tpu_custom_call" | custom-call | bytes 150000000 | tf_op jit(solution)/shard_map/pallas_call | solution.py:120
  248.1 6.4 multiply_reduce_fusion.1
  255.7 42.6 %shard_map.199 = bf16[1,8,256,2048]{3,2,1,0:T(8,128)(2,1)} custom-call(bf16[1,256,2048]{2,1,0:T(8,128)(2,1)} %fusion.13.x_ref), custom_call_target="tpu_custom_call" | custom-call | bytes 150000000 | tf_op jit(solution)/shard_map/pallas_call | solution.py:120
  298.4 42.7 %shard_map.201 = bf16[1,8,256,2048]{3,2,1,0:T(8,128)(2,1)} custom-call(bf16[1,256,2048]{2,1,0:T(8,128)(2,1)} %bitcast.158), custom_call_target="tpu_custom_call" | custom-call | bytes 150000000 | tf_op jit(solution)/shard_map/pallas_call | solution.py:120
  341.1 18.8 %fusion.26 = f32[2048,1408]{0,1:T(8,128)} fusion(bf16[2048,2048]{1,0:T(8,128)(2,1)} %bitcast.147, bf16[2048,1408]{1,0:T(8,128)(2,1)} %all-gather.9.cloned.1.call-done), kind=kOutput, calls=%fused_computation.74 | convolution fusion | flops 11811160064 | bytes 25690112 | tf_op jit(solution)/shard_map/dot_general | solution.py:38
  359.9 16.0 %multiply_convert_fusion.1 = (bf16[2048,704]{0,1:T(8,128)(2,1)}, bf16[2048,704]{0,1:T(8,128)(2,1)}, bf16[2048,704]{0,1:T(8,128)(2,1)S(1)}) fusion(f32[2048,1408]{0,1:T(8,128)} %fusion.26, bf16[2048,2048]{1,0:T(8,128)(2,1)} %bitcast.149, bf16[2048,704]{1,0:T(8,128)(2,1)} %all-gather.11.cloned.1.call-done), kind=kOutput, calls=%fused_computation.7 | convolution fusion | flops 5927206912 | bytes 31457280 | tf_op jit(solution)/shard_map/dot_general | solution.py:38
  377.6 11.0 %convolution_convert_fusion.6 = bf16[2048,704]{0,1:T(8,128)(2,1)} fusion(bf16[2048,704]{0,1:T(8,128)(2,1)S(1)} %get-tuple-element.32, bf16[2048,2048]{1,0:T(8,128)(2,1)} %bitcast.150), kind=kOutput, calls=%fused_computation.12 | convolution fusion | flops 5907021824 | bytes 14155776 | tf_op jit(solution)/shard_map/dot_general | solution.py:42
  388.7 19.1 %convolution_convert_fusion.2 = bf16[2048,2048]{1,0:T(8,128)(2,1)} fusion(bf16[2048,1408]{1,0:T(8,128)(2,1)} %all-gather.9.cloned.1.call-done, bf16[2048,704]{0,1:T(8,128)(2,1)} %get-tuple-element.31, bf16[2048,704]{0,1:T(8,128)(2,1)} %get-tuple-element.30), kind=kOutput, calls=%fused_computation.2 | convolution fusion | flops 11826888704 | bytes 19922944 | tf_op jit(solution)/shard_map/dot_general | solution.py:34
  407.8 9.1 convolution_convert_fusion.3
  416.9 44.1 %shard_map.200 = f32[1,256,2048]{2,1,0:T(8,128)S(1)} custom-call(bf16[1,8,256,2048]{3,2,1,0:T(8,128)(2,1)} %bitcast.145), custom_call_target="tpu_custom_call" | custom-call | bytes 130000000 | tf_op jit(solution)/shard_map/pallas_call | solution.py:191
  461.1 43.8 %shard_map.202 = f32[1,256,2048]{2,1,0:T(8,128)S(1)} custom-call(bf16[1,8,256,2048]{3,2,1,0:T(8,128)(2,1)} %bitcast.144), custom_call_target="tpu_custom_call" | custom-call | bytes 130000000 | tf_op jit(solution)/shard_map/pallas_call | solution.py:191
  517.3 12.5 %all-to-all-done.4 = bf16[8,256,256]{2,1,0:T(8,128)(2,1)S(1)} async-done(((bf16[8,256,256]{2,1,0:T(8,128)(2,1)}), bf16[8,256,256]{2,1,0:T(8,128)(2,1)S(1)}, u32[]{:S(2)}, u32[]{:S(2)}) %all-to-all-start.4) | async-done | bytes 1048608 | tf_op jit(solution)/shard_map/all_to_all | solution.py:472
  532.2 5.6 collective-permute-done.1.in_ref
  539.3 29.5 %shard_map.204 = (bf16[2048,768]{1,0:T(8,128)(2,1)}, f32[1,256]{1,0:T(1,128)S(1)}, f32[1,256]{1,0:T(1,128)S(1)}) custom-call(s32[32]{0:T(128)S(1)} %slice.57.last_ref, f32[2048,768]{1,0:T(8,128)} %fusion.25.proj_ref, s32[2048,1]{1,0:T(8,128)S(1)} %copy.80.start_ref, f32[1,256]{1,0:T(1,128)S(1)} %get-tuple-element.42.floor_ref, ...), custom_call_target="tpu_custom_call" | custom-call | tf_op jit(solution)/shard_map/pallas_call | solution.py:431
  568.8 11.4 %convolution_convert_fusion.5 = bf16[2048,768]{1,0:T(8,128)(2,1)} fusion(bf16[2048,2048]{1,0:T(8,128)(2,1)} %bitcast.143, bf16[2048,768]{1,0:T(8,128)(2,1)} %get-tuple-element.23), kind=kOutput, calls=%fused_computation.11 | convolution fusion | flops 6444023808 | bytes 14680064 | tf_op jit(solution)/shard_map/dot_general | solution.py:42
  580.3 19.8 %convolution_convert_fusion.4 = bf16[2048,1408]{1,0:T(8,128)(2,1)} fusion(bf16[2048,2048]{1,0:T(8,128)(2,1)} %bitcast.148, bf16[2048,704]{0,1:T(8,128)(2,1)} %get-tuple-element.31, bf16[2048,704]{0,1:T(8,128)(2,1)} %get-tuple-element.30), kind=kOutput, calls=%fused_computation.4 | convolution fusion | flops 11825577984 | bytes 19922944 | tf_op jit(solution)/shard_map/dot_general | solution.py:42
  600.2 11.4 %convolution_convert_fusion.1 = bf16[2048,2048]{1,0:T(8,128)(2,1)} fusion(bf16[2048,768]{1,0:T(8,128)(2,1)} %get-tuple-element.23, bf16[2048,768]{1,0:T(8,128)(2,1)} %all-gather.7.cloned.1.call-done), kind=kOutput, calls=%fused_computation.1 | convolution fusion | flops 6446645248 | bytes 14680064 | tf_op jit(solution)/shard_map/dot_general | solution.py:34
  611.6 43.8 %shard_map.205 = f32[1,256,2048]{2,1,0:T(8,128)S(1)} custom-call(bf16[1,8,256,2048]{3,2,1,0:T(8,128)(2,1)} %bitcast.146), custom_call_target="tpu_custom_call" | custom-call | bytes 130000000 | tf_op jit(solution)/shard_map/pallas_call | solution.py:191
  664.3 7.6 convolution_convert_fusion
  672.0 46.0 %shard_map.206 = bf16[4,64,2048]{2,1,0:T(8,128)(2,1)} custom-call(bf16[4,8,64,2048]{3,2,1,0:T(8,128)(2,1)} %bitcast.137), custom_call_target="tpu_custom_call" | custom-call | bytes 130000000 | tf_op jit(solution)/shard_map/pallas_call | solution.py:191
  718.0 16.8 %all_to_all.42 = bf16[8,64,768]{2,1,0:T(8,128)(2,1)} all-to-all(bf16[8,64,768]{2,1,0:T(8,128)(2,1)} %bitcast.168), channel_id=1, replica_groups={{0,1,2,3,4,5,6,7},{8,9,10,11,12,13,14,15},{16,17,18,19,20,21,22,23},{24..., dimensions={0} | all-to-all | bytes 1572864 | tf_op jit(solution)/shard_map/all_to_all | solution.py:472
  734.8 7.3 reduce-scatter.12.cloned.1.call-done
  749.9 130.7 %reduce-scatter.16.cloned.1.call-done = f32[64,4]{1,0:T(8,128)} async-done(((f32[2048,4]{1,0:T(8,128)}), f32[64,4]{1,0:T(8,128)}) %reduce-scatter.16.cloned.1.call-update) | async-done | bytes 1040
  884.0 22.2 %reduce-scatter.10.cloned.1.call-done = bf16[64,2048]{1,0:T(8,128)(2,1)} async-done(((bf16[256,2048]{1,0:T(8,128)(2,1)}), bf16[64,2048]{1,0:T(8,128)(2,1)}) %reduce-scatter.10.cloned.1.call-update) | async-done | bytes 262160 | tf_op jit(solution)/shard_map/reduce_scatter | solution.py:478
  922.8 4.7 reshape.181
  (151 shorter events, 83.7 us)
Async XLA Ops:
  7.2 143.1 %all-gather.7.cloned.1.call-start = ((), (), s32[]{:S(2)}) async-start(), calls=%async_computation.13 | async-start | bytes 3932160 | tf_op jit(solution)/shard_map/all_gather | solution.py:475
  27.5 166.0 %all-gather.13.cloned.1.call-start = ((), (), s32[]{:S(2)}) async-start(), calls=%async_computation.20 | async-start | bytes 1310720 | tf_op jit(solution)/shard_map/all_gather | solution.py:520
  28.3 312.9 %all-gather.9.cloned.1.call-start = ((), (), s32[]{:S(2)}) async-start(), calls=%async_computation.14 | async-start | bytes 7208960 | tf_op jit(solution)/shard_map/all_gather | solution.py:475
  56.7 6.7 copy-start.21
  56.7 7.2 copy-start.15
  56.7 7.2 copy-start.16
  56.7 7.2 copy-start.17
  56.7 7.2 copy-start.18
  56.7 51.7 %copy-start.2 = (bf16[256,2048]{1,0:T(8,128)(2,1)S(1)}, bf16[256,2048]{1,0:T(8,128)(2,1)}, u32[]{:S(2)}) copy-start(bf16[256,2048]{1,0:T(8,128)(2,1)} %param.12) | copy-start | bytes 3145732
  59.8 127.2 %all-to-all-start.3 = ((bf16[8,64,704]{2,1,0:T(8,128)(2,1)}), bf16[8,64,704]{2,1,0:T(8,128)(2,1)S(1)}, u32[]{:S(2)}, u32[]{:S(2)}) async-start(bf16[8,64,704]{2,1,0:T(8,128)(2,1)} %bitcast.129), calls=%async_computation.3 | async-start | bytes 1572864 | tf_op jit(solution)/shard_map/all_to_all | solution.py:472
  63.8 86.0 %copy-start.12 = (s32[2048]{0:T(1024)}, s32[2048]{0:T(1024)S(1)}, u32[]{:S(2)}) copy-start(s32[2048]{0:T(1024)S(1)} %broadcast_subtract_fusion) | copy-start | bytes 24580
  108.7 41.1 %copy-start.13 = (f32[256]{0:T(256)}, f32[256]{0:T(256)S(1)}, u32[]{:S(2)}) copy-start(f32[256]{0:T(256)S(1)} %add_rsqrt_fusion.1) | copy-start | bytes 3076
  108.7 41.0 %copy-start.10 = (f32[1,2048]{1,0:T(1,128)}, f32[1,2048]{1,0:T(1,128)S(1)}, u32[]{:S(2)}) copy-start(f32[1,2048]{1,0:T(1,128)S(1)} %get-tuple-element.40) | copy-start | bytes 24580
  153.9 11.9 %collective-permute-start = (f32[2,128,128]{2,1,0:T(8,128)S(1)}, f32[2,128,128]{2,1,0:T(8,128)S(1)}, u32[]{:S(2)}, u32[]{:S(2)}) collective-permute-start(f32[2,128,128]{2,1,0:T(8,128)S(1)} %shard_map.196), channel_id=1, source_target_pairs={{0,8},{1,9},{2,10},{3,11},{4,12},{5,13},{6,14},{7,15},{8,16},{9,17... | collective-permute-start | bytes 393224 | tf_op jit(solution)/shard_map/ppermute | solution.py:543
  187.0 60.2 %all-to-all-start.1 = ((bf16[8,256,256]{1,2,0:T(8,128)(2,1)}), bf16[8,256,256]{1,2,0:T(8,128)(2,1)S(1)}, u32[]{:S(2)}, u32[]{:S(2)}) async-start(bf16[8,256,256]{1,2,0:T(8,128)(2,1)} %copy.81), calls=%async_computation.1 | async-start | bytes 2097152 | tf_op jit(solution)/shard_map/all_to_all | solution.py:472
  192.7 167.3 %all-gather.11.cloned.1.call-start = ((), (), s32[]{:S(2)}) async-start(), calls=%async_computation.15 | async-start | bytes 3932160 | tf_op jit(solution)/shard_map/all_gather | solution.py:475
  193.3 464.3 %reduce-scatter.14.cloned.1.call-start = ((), (), s32[]{:S(2)}) async-start(), calls=%async_computation.19 | async-start | bytes 3604480 | tf_op jit(solution)/shard_map/reduce_scatter | solution.py:478
  388.6 19.2 %copy-start.19 = (bf16[2048,704]{1,0:T(8,128)(2,1)S(1)}, bf16[2048,704]{1,0:T(8,128)(2,1)}, u32[]{:S(2)}) copy-start(bf16[2048,704]{1,0:T(8,128)(2,1)} %all-gather.11.cloned.1.call-done) | copy-start | bytes 8650756
  388.7 19.1 %copy-start.23 = (bf16[2048,704]{0,1:T(8,128)(2,1)S(1)}, bf16[2048,704]{0,1:T(8,128)(2,1)}, u32[]{:S(2)}) copy-start(bf16[2048,704]{0,1:T(8,128)(2,1)} %copy-done.22) | copy-start | bytes 8650756
  461.1 44.4 %copy-start.6 = (bf16[256,2048]{1,0:T(8,128)(2,1)S(1)}, bf16[256,2048]{1,0:T(8,128)(2,1)}, u32[]{:S(2)}) copy-start(bf16[256,2048]{1,0:T(8,128)(2,1)} %param.13) | copy-start | bytes 3145732
  461.1 46.4 %slice-start = ((s8[8388608]{0:T(1024)(128)(4,1)}), s8[4194304]{0:T(1024)(128)(4,1)S(1)}, s32[]{:S(2)}) async-start(s8[8388608]{0:T(1024)(128)(4,1)} %bitcast.134), calls=%async_computation.22 | async-start | bytes 8388608
  510.9 18.9 %all-to-all-start.4 = ((bf16[8,256,256]{2,1,0:T(8,128)(2,1)}), bf16[8,256,256]{2,1,0:T(8,128)(2,1)S(1)}, u32[]{:S(2)}, u32[]{:S(2)}) async-start(bf16[8,256,256]{2,1,0:T(8,128)(2,1)} %bitcast.157), calls=%async_computation.4 | async-start | bytes 2097152 | tf_op jit(solution)/shard_map/all_to_all | solution.py:472
  514.5 203.5 %reduce-scatter.8.cloned.1.call-start = ((), (), s32[]{:S(2)}) async-start(), calls=%async_computation.16 | async-start | bytes 3932160 | tf_op jit(solution)/shard_map/reduce_scatter | solution.py:478
  530.9 6.9 collective-permute-start.1
  580.2 161.8 %reduce-scatter.12.cloned.1.call-start = ((), (), s32[]{:S(2)}) async-start(), calls=%async_computation.18 | async-start | bytes 7208960 | tf_op jit(solution)/shard_map/reduce_scatter | solution.py:478
  600.1 280.5 %reduce-scatter.16.cloned.1.call-start = ((), (), s32[]{:S(2)}) async-start(), calls=%async_computation.21 | async-start | bytes 1081344
  611.6 43.8 %copy-start.3 = (bf16[256,2048]{1,0:T(8,128)(2,1)S(1)}, bf16[256,2048]{1,0:T(8,128)(2,1)}, u32[]{:S(2)}) copy-start(bf16[256,2048]{1,0:T(8,128)(2,1)} %param.12) | copy-start | bytes 3145732
  611.6 43.9 %copy-start.11 = (f32[1,2048]{1,0:T(1,128)S(1)}, f32[1,2048]{1,0:T(1,128)}, u32[]{:S(2)}) copy-start(f32[1,2048]{1,0:T(1,128)} %copy-done.10) | copy-start | bytes 24580
  611.6 43.9 %copy-start.14 = (f32[256]{0:T(256)S(1)}, f32[256]{0:T(256)}, u32[]{:S(2)}) copy-start(f32[256]{0:T(256)} %copy-done.13) | copy-start | bytes 3076
  659.8 58.1 %all-to-all-start.7 = ((bf16[8,64,704]{2,1,0:T(8,128)(2,1)}), bf16[8,64,704]{2,1,0:T(8,128)(2,1)}, u32[]{:S(2)}, u32[]{:S(2)}) async-start(bf16[8,64,704]{2,1,0:T(8,128)(2,1)} %bitcast.162), calls=%async_computation.11 | async-start | bytes 1572864 | tf_op jit(solution)/shard_map/all_to_all | solution.py:472
  664.1 242.1 %reduce-scatter.10.cloned.1.call-start = ((), (), s32[]{:S(2)}) async-start(), calls=%async_computation.17 | async-start | bytes 1310720 | tf_op jit(solution)/shard_map/reduce_scatter | solution.py:478
  742.1 173.1 %all-to-all-start.6 = ((bf16[8,64,1408]{2,1,0:T(8,128)(2,1)}), bf16[8,64,1408]{2,1,0:T(8,128)(2,1)}, u32[]{:S(2)}, u32[]{:S(2)}) async-start(bf16[8,64,1408]{2,1,0:T(8,128)(2,1)} %bitcast.164), calls=%async_computation.9 | async-start | bytes 2883584 | tf_op jit(solution)/shard_map/all_to_all | solution.py:472
  (10 other events, 30.5 us)
Sparse Core Ops, SparseCore 0:
  27.7 62.8 all-gather.6
  92.2 26.5 all-gather.12
  120.4 106.2 all-gather.8
  228.7 64.3 all-gather.10
  388.8 54.2 reduce-scatter.13
  580.4 57.0 reduce-scatter.7
  639.7 102.2 reduce-scatter.11
  744.9 135.6 reduce-scatter.15
  883.0 23.0 reduce-scatter.9

commit v2 on v1

--- a/solution.py
+++ b/solution.py
@@ -40,6 +40,10 @@
 
 def dot_tn(left, right):
     return lax.dot_general(left, right, (((0,), (0,)), ((), ())), preferred_element_type=f32)
+
+
+def cost(micros):
+    return pl.CostEstimate(flops=0, transcendentals=0, bytes_accessed=int(micros * 3_690_000))
 
 
 def places():
@@ -72,63 +76,199 @@
     )
 
 
-def group_gather_kernel(x_ref, out_ref, send_sem, recv_sem, own_sem):
+def plane_steps(step_core, step_low, step_high):
+    return [
+        (number, (number & 1) * step_core + ((number >> 1) & 1) * step_low + (number >> 2) * step_high)
+        for number in range(1, GROUP)
+    ]
+
+
+def exchange_kernel(plan, *refs):
+    count = len(plan)
+    ins, outs = refs[:count], refs[count : 2 * count]
+    send_sem, recv_sem, own_sem = refs[2 * count :]
     me, slot, step_core, first_step, second_step = places()
-    first, second, mate = me + first_step, me + second_step, me + step_core
-    greet((first, second, mate))
-
-    def block(place):
-        return out_ref.at[:, place]
-
-    own = pltpu.make_async_copy(x_ref, block(slot), own_sem)
+    core = lax.rem(slot, 2)
+    step_low = (1 - core) * first_step + core * second_step
+    step_high = core * first_step + (1 - core) * second_step
+    others = plane_steps(step_core, step_low, step_high)
+    group = me // GROUP
+    groups = lax.axis_size("fsdp") // GROUP
+    greeted = [me + first_step, me + second_step, me + step_core]
+    if set(plan) != {"gather"}:
+        greeted = [me + step for _, step in others]
+    line = []
+    if "all" in plan:
+        line = [
+            (
+                number,
+                lax.rem(group + number, groups) * GROUP + slot,
+                lax.rem(group + groups - number, groups),
+            )
+            for number in range(1, groups)
+        ]
+        greeted = greeted + [target for _, target, _ in line]
+    greet(greeted)
     sent = []
 
-    def send(source, place, number, target):
-        copy = remote(source, block(place), send_sem.at[number], recv_sem.at[number], target)
+    def copy_of(item, source, target, number, device):
+        return remote(source, target, send_sem.at[item, number], recv_sem.at[item, number], device)
+
+    def send(item, source, target, number, device):
+        copy = copy_of(item, source, target, number, device)
         copy.start()
         sent.append(copy)
 
-    def arrived(place, number, source):
-        remote(
-            block(place), block(place), send_sem.at[number], recv_sem.at[number], source
-        ).wait_recv()
-
-    from_first, from_second = slot + first_step, slot + second_step
-    corner = slot + first_step + second_step
-    send(x_ref, slot, 0, first)
-    send(x_ref, slot, 1, second)
-    send(x_ref, slot, 2, mate)
-    own.start()
-    arrived(from_first, 0, first)
-    send(block(from_first), from_first, 3, second)
-    send(block(from_first), from_first, 4, mate)
-    arrived(from_second, 1, second)
-    send(block(from_second), from_second, 5, mate)
-    arrived(corner, 3, second)
-    send(block(corner), corner, 6, mate)
-    arrived(slot + step_core, 2, mate)
-    arrived(slot + step_core + second_step, 4, mate)
-    arrived(slot + step_core + first_step, 5, mate)
-    arrived(corner + step_core, 6, mate)
+    def arrived(item, target, number):
+        copy_of(item, target, target, number, me).wait_recv()
+
+    def keep(item, source, target):
+        copy = pltpu.make_async_copy(source, target, own_sem.at[item])
+        copy.start()
+        return copy
+
+    def block(item, place):
+        kind, out = plan[item], outs[item]
+        if kind == "widen":
+            columns = out.shape[1] // GROUP
+            return out.at[:, pl.ds(pl.multiple_of(place * columns, columns), columns)]
+        if kind == "gather":
+            return out.at[:, place]
+        return out.at[place]
+
+    def piece(item, place):
+        if plan[item] == "narrow":
+            columns = ins[item].shape[1] // GROUP
+            return ins[item].at[:, pl.ds(pl.multiple_of(place * columns, columns), columns)]
+        return ins[item].at[place]
+
+    own = []
+    for item, kind in enumerate(plan):
+        if kind == "all":
+            own.append(keep(item, ins[item], outs[item].at[group, slot]))
+            for number, target, _ in line:
+                send(item, ins[item], outs[item].at[group, slot], GROUP - 1 + number, target)
+        elif kind == "gather":
+            for number, step in enumerate((first_step, second_step, step_core)):
+                send(item, ins[item], block(item, slot), number, me + step)
+            own.append(keep(item, ins[item], block(item, slot)))
+    for item, kind in enumerate(plan):
+        if kind in ("swap", "widen", "narrow"):
+            for number, step in others:
+                send(item, piece(item, slot + step), block(item, slot), number - 1, me + step)
+            own.append(keep(item, piece(item, slot), block(item, slot)))
+    for copy in own:
+        copy.wait()
+    for item, kind in enumerate(plan):
+        if kind == "all":
+            for number, _, sender in line:
+                arrived(item, outs[item].at[sender, slot], GROUP - 1 + number)
+            for number, step in others:
+                send(item, outs[item].at[:, slot], outs[item].at[:, slot], number - 1, me + step)
+    corner_step = first_step + second_step
+    for item, kind in enumerate(plan):
+        if kind == "gather":
+            for place, number, onward in (
+                (slot + first_step, 0, ((3, second_step), (4, step_core))),
+                (slot + second_step, 1, ((5, step_core),)),
+                (slot + corner_step, 3, ((6, step_core),)),
+            ):
+                arrived(item, block(item, place), number)
+                for then, step in onward:
+                    send(item, block(item, place), block(item, place), then, me + step)
+    for item, kind in enumerate(plan):
+        if kind == "gather":
+            for step, number in ((0, 2), (second_step, 4), (first_step, 5), (corner_step, 6)):
+                arrived(item, block(item, slot + step_core + step), number)
+        elif kind == "all":
+            for number, step in others:
+                arrived(item, outs[item].at[:, slot + step], number - 1)
+        else:
+            for number, step in others:
+                arrived(item, block(item, slot + step), number - 1)
     for copy in sent:
         copy.wait_send()
+
+
+def exchange(number, micros, *items):
+    groups = lax.axis_size("fsdp") // GROUP
+    kinds = [kind for kind, _ in items]
+    arrays = [array for _, array in items]
+    shapes = []
+    for kind, array in items:
+        if kind == "gather":
+            shape = (array.shape[0], GROUP) + array.shape[1:]
+        elif kind == "swap":
+            shape = array.shape
+        elif kind == "widen":
+            shape = (array.shape[1], GROUP * array.shape[2])
+        elif kind == "narrow":
+            shape = (GROUP, array.shape[0], array.shape[1] // GROUP)
+        else:
+            shape = (groups, GROUP) + array.shape
+        shapes.append(jax.ShapeDtypeStruct(shape, array.dtype))
+    numbers = GROUP - 1 + (groups if "all" in kinds else 0)
+    return pl.pallas_call(
+        functools.partial(exchange_kernel, kinds),
+        out_shape=tuple(shapes),
+        in_specs=[ANY] * len(items),
+        out_specs=tuple([ANY] * len(items)),
+        scratch_shapes=[
+            pltpu.SemaphoreType.DMA((len(items), numbers)),
+            pltpu.SemaphoreType.DMA((len(items), numbers)),
+            pltpu.SemaphoreType.DMA((len(items),)),
+        ],
+        compiler_params=pltpu.CompilerParams(collective_id=number, has_side_effects=True),
+        cost_estimate=cost(micros),
+    )(*arrays)
+
+
+def home_kernel(pieces, x_ref, out_ref, got, send_sem, recv_sem, own_sem):
+    me, slot, step_core, first_step, second_step = places()
+    core = lax.rem(slot, 2)
+    step_low = (1 - core) * first_step + core * second_step
+    step_high = core * first_step + (1 - core) * second_step
+    others = plane_steps(step_core, step_low, step_high)
+    greet([me + step for _, step in others])
+    sent = []
+    for number, step in others:
+        copy = remote(
+            x_ref.at[slot + step], got.at[slot], send_sem.at[number - 1], recv_sem.at[number - 1], me + step
+        )
+        copy.start()
+        sent.append(copy)
+    own = pltpu.make_async_copy(x_ref.at[slot], got.at[slot], own_sem)
+    own.start()
     own.wait()
-
-
-def group_gather(x, number):
-    parts, rows, columns = x.shape
+    for number, step in others:
+        target = got.at[slot + step]
+        remote(target, target, send_sem.at[number - 1], recv_sem.at[number - 1], me + step).wait_recv()
+    columns = x_ref.shape[2] // pieces
+    for piece in range(pieces):
+        for sender in range(GROUP):
+            lo = (piece * GROUP + sender) * columns
+            out_ref[:, lo : lo + columns] = got[sender, :, piece * columns : (piece + 1) * columns].astype(f32)
+    for copy in sent:
+        copy.wait_send()
+
+
+def home(x, pieces, number):
+    _, rows, columns = x.shape
     return pl.pallas_call(
-        group_gather_kernel,
-        out_shape=jax.ShapeDtypeStruct((parts, GROUP, rows, columns), x.dtype),
-        in_specs=[ANY],
-        out_specs=ANY,
+        functools.partial(home_kernel, pieces),
+        out_shape=jax.ShapeDtypeStruct((rows, GROUP * columns), f32),
+        in_specs=[VMEM],
+        out_specs=VMEM,
         scratch_shapes=[
-            pltpu.SemaphoreType.DMA((7,)),
-            pltpu.SemaphoreType.DMA((7,)),
+            pltpu.VMEM(x.shape, x.dtype),
+            pltpu.SemaphoreType.DMA((GROUP - 1,)),
+            pltpu.SemaphoreType.DMA((GROUP - 1,)),
             pltpu.SemaphoreType.DMA,
         ],
-        compiler_params=pltpu.CompilerParams(collective_id=number, has_side_effects=True),
-        cost_estimate=pl.CostEstimate(flops=0, transcendentals=0, bytes_accessed=150_000_000),
+        compiler_params=pltpu.CompilerParams(
+            collective_id=number, has_side_effects=True, vmem_limit_bytes=32 * 2**20
+        ),
+        cost_estimate=cost(20),
     )(x)
 
 
@@ -203,8 +343,78 @@
         compiler_params=pltpu.CompilerParams(
             collective_id=number, has_side_effects=True, vmem_limit_bytes=48 * 2**20
         ),
-        cost_estimate=pl.CostEstimate(flops=0, transcendentals=0, bytes_accessed=130_000_000),
+        cost_estimate=cost(43),
     )(x)
+
+
+def plane_permutes(device_count):
+    first, second, mate = [], [], []
+    for i in range(device_count):
+        low_bit, high_bit = (2, 4) if i % 2 == 0 else (4, 2)
+        first.append((i, i ^ low_bit))
+        second.append((i, i ^ high_bit))
+        mate.append((i, i ^ 1))
+    return first, second, mate
+
+
+def after(values, *earlier):
+    return lax.optimization_barrier((values, earlier))[0]
+
+
+def meet(*values):
+    return lax.optimization_barrier(values)
+
+
+def assemble_kernel(*refs):
+    blocks, out_ref = refs[:GROUP], refs[GROUP]
+    _, slot, step_core, first_step, second_step = places()
+    corner_step = first_step + second_step
+    here = (0, first_step, second_step, corner_step)
+    there = (step_core, step_core + second_step, step_core + first_step, step_core + corner_step)
+    for number, step in enumerate(here + there):
+        out_ref[:, slot + step] = blocks[number][...]
+
+
+def assemble(x, from_first, from_second, from_corner, mates):
+    parts, rows, columns = x.shape
+    return pl.pallas_call(
+        assemble_kernel,
+        out_shape=jax.ShapeDtypeStruct((parts, GROUP, rows, columns), x.dtype),
+        in_specs=[VMEM] * GROUP,
+        out_specs=VMEM,
+        compiler_params=pltpu.CompilerParams(vmem_limit_bytes=32 * 2**20),
+        cost_estimate=cost(8),
+    )(x, from_first, from_second, from_corner, *mates)
+
+
+class SlowScatter:
+    def __init__(self, x, moves, device_count):
+        self.x = x
+        self.slot, self.step_core, self.first_step, self.second_step = moves
+        self.first, self.second, self.mate = plane_permutes(device_count)
+
+    def block(self, step):
+        return lax.dynamic_index_in_dim(self.x, self.slot + step, 1, keepdims=False)
+
+    def pair(self, near, kind, step):
+        return self.block(step).astype(f32) + near[kind].astype(f32)
+
+    def to_mate(self):
+        steps = (self.first_step + self.second_step, self.second_step, self.first_step, 0)
+        away = jnp.stack([self.block(self.step_core + step) for step in steps])
+        return lax.ppermute(away, "fsdp", self.mate)
+
+    def to_second(self, near):
+        corner = self.pair(near, 0, self.first_step + self.second_step)
+        onward = jnp.stack([corner, self.pair(near, 2, self.second_step)]).astype(bf16)
+        return lax.ppermute(onward, "fsdp", self.second)
+
+    def to_first(self, near, far):
+        both = self.pair(near, 1, self.first_step) + far[0].astype(f32)
+        return lax.ppermute(both.astype(bf16), "fsdp", self.first)
+
+    def total(self, near, far, last):
+        return self.pair(near, 3, 0) + far[1].astype(f32) + last.astype(f32)
 
 
 def low(values):
@@ -315,8 +525,7 @@
     inverse = inverse_rms(out)
     scaled = out * inverse
     dmix = dmix_ref[rows, lo : lo + dim].astype(f32)
-    grad = rms_back(dmix * gain_ref[:, lo : lo + dim], scaled, inverse)
-    return grad, jnp.sum(dmix * scaled, axis=0, keepdims=True)
+    return rms_back(dmix * gain_ref[:, lo : lo + dim], scaled, inverse)
 
 
 def backward_kernel(
@@ -332,7 +541,6 @@
     in_ref,
     dproj_ref,
     dfloor_ref,
-    dgain_ref,
     later,
 ):
     dim = floor_ref.shape[1] // heads
@@ -340,7 +548,6 @@
     chunks = proj_ref.shape[0] // CHUNK
     later[...] = in_ref[...]
     dfloor_ref[...] = jnp.zeros_like(dfloor_ref)
-    dgain_ref[...] = jnp.zeros_like(dgain_ref)
 
     def step(i, _):
         n = chunks - 1 - i
@@ -355,7 +562,7 @@
         for head in range(heads):
             lo = head * dim
             g = gates(proj_ref, floor_ref, rows, head, heads)
-            grad, dgain = state_grad(out_ref, dmix_ref, gain_ref, rows, lo, dim)
+            grad = state_grad(out_ref, dmix_ref, gain_ref, rows, lo, dim)
             grad_hi = grad.astype(bf16)
             grad_lo = (grad - grad_hi.astype(f32)).astype(bf16)
             state = enter_ref[n, head]
@@ -403,7 +610,6 @@
             dproj_ref[rows, wide + lo : wide + lo + dim] = d_f_pre.astype(bf16)
             dproj_ref[rows, 2 * wide + lo : 2 * wide + lo + dim] = d_value.astype(bf16)
             dfloor_ref[:, lo : lo + dim] += jnp.sum(d_floor, axis=0, keepdims=True)
-            dgain_ref[:, lo : lo + dim] += dgain
             later[head] = after * fade + dot_tn(grad_hi, query_in)
         return 0
 
@@ -419,7 +625,7 @@
         for n in range(proj_ref.shape[0] // CHUNK - 1, -1, -1):
             rows = pl.ds(n * CHUNK, CHUNK)
             g = gates(proj_ref, floor_ref, rows, head, heads)
-            grad, _ = state_grad(out_ref, dmix_ref, gain_ref, rows, head * dim, dim)
+            grad = state_grad(out_ref, dmix_ref, gain_ref, rows, head * dim, dim)
             queries = entry_queries(g, start_ref[rows, :] < n * CHUNK)
             after = after * whole_fade(g, last_ref[n] - n * CHUNK) + dot_tn(
                 grad.astype(bf16), queries
@@ -427,7 +633,7 @@
         grad_ref[head] = after
 
 
-def local_call(kernel, heads, out_shape, scratch, *operands):
+def local_call(kernel, heads, micros, out_shape, scratch, *operands):
     return pl.pallas_call(
         functools.partial(kernel, heads),
         out_shape=out_shape,
@@ -435,6 +641,7 @@
         out_specs=jax.tree.map(lambda _: VMEM, out_shape),
         scratch_shapes=scratch,
         compiler_params=pltpu.CompilerParams(vmem_limit_bytes=48 * 2**20),
+        cost_estimate=cost(micros),
     )(*operands)
 
 
@@ -468,9 +675,6 @@
     planes = [[g * GROUP + s for s in range(GROUP)] for g in range(groups)]
     lines = [[g * GROUP + s for g in range(groups)] for s in range(GROUP)]
 
-    def swap(x):
-        return lax.all_to_all(x, "fsdp", 0, 0, axis_index_groups=planes, tiled=True)
-
     def line_gather(x):
         return lax.all_gather(x, "fsdp", axis=0, axis_index_groups=lines, tiled=True)
 
@@ -479,17 +683,26 @@
             x, "fsdp", scatter_dimension=0, axis_index_groups=lines, tiled=True
         )
 
-    def own_columns(weight, pieces):
+    def by_owner(weight, pieces):
         columns = weight.shape[1] // (pieces * GROUP)
         parted = weight.reshape(weight_rows, pieces, GROUP, columns).transpose(2, 0, 1, 3)
-        swapped = swap(parted.reshape(GROUP, weight_rows, pieces * columns))
-        return line_gather(swapped.reshape(GROUP * weight_rows, pieces * columns))
-
-    def home_rows(grad, pieces):
-        columns = grad.shape[1] // pieces
-        summed = line_scatter(grad.astype(bf16)).reshape(GROUP, weight_rows, pieces * columns)
-        swapped = swap(summed).reshape(GROUP, weight_rows, pieces, columns)
-        return swapped.transpose(1, 2, 0, 3).reshape(weight_rows, -1).astype(f32)
+        return parted.reshape(GROUP, weight_rows, pieces * columns)
+
+    def whole_rows(x):
+        return line_gather(x.reshape(GROUP * weight_rows, -1))
+
+    def home_rows(summed, pieces, number):
+        return home(summed.reshape(GROUP, weight_rows, -1), pieces, number)
+
+    low_step = 2 - 4 * (slot // 2 % 2)
+    high_step = 4 - 8 * (slot // 4)
+    odd = slot % 2
+    moves = (
+        slot,
+        1 - 2 * odd,
+        jnp.where(odd == 0, low_step, high_step),
+        jnp.where(odd == 0, high_step, low_step),
+    )
 
     seq_count = deal.shape[0]
     seq_ids = jnp.arange(seq_count, dtype=jnp.int32)
@@ -507,31 +720,47 @@
     start_column = starts[:, None]
     last_starts = starts[CHUNK - 1 :: CHUNK]
 
-    gains = lax.all_gather(
-        jnp.stack([norm_gain, forget_floor, group_gain, ffn_gain]), "fsdp", axis=1, tiled=True
-    ).astype(f32)
+    out_lines = lax.all_gather(out_proj, "fsdp", axis=0, axis_index_groups=lines)
+    gain_block = jnp.zeros((16, 128), bf16)
+    for number, gain in enumerate((norm_gain, forget_floor, group_gain, ffn_gain)):
+        gain_block = gain_block.at[number, :weight_rows].set(gain)
+    gain_blocks, mixer_swapped = exchange(
+        0, 15, ("all", gain_block), ("swap", by_owner(mixer_in, 3))
+    )
+    mixer_weight = whole_rows(mixer_swapped)
+    gains = (
+        gain_blocks[:, :, :4, :weight_rows].transpose(2, 0, 1, 3).reshape(4, width).astype(f32)
+    )
     first_gain = gains[0:1]
     second_gain = gains[3:4]
     own_gains = lax.dynamic_slice_in_dim(gains, slot * own_width, own_width, 1)
     own_floor = own_gains[1:2]
     own_group_gain = own_gains[2:3]
 
-    mixer_weight = own_columns(mixer_in, 3)
-    out_lines = lax.all_gather(out_proj, "fsdp", axis=0, axis_index_groups=lines)
-    ffn_weight = own_columns(gate_up, 2)
-    down_weight = own_columns(down_proj, 1)
-
     inputs = tokens.astype(f32)
     first_inverse = inverse_rms(inputs)
     first_scaled = inputs * first_inverse
     first_normed = (first_scaled * first_gain).astype(bf16)
-    first_all = group_gather(first_normed[None], 0).reshape(group_rows, width)
+    first_all, ffn_swapped, down_swapped = exchange(
+        1,
+        65,
+        ("gather", first_normed[None]),
+        ("swap", by_owner(gate_up, 2)),
+        ("swap", by_owner(down_proj, 1)),
+    )
+    first_all = first_all.reshape(group_rows, width)
+    ffn_weight = whole_rows(ffn_swapped)
+    first, second, mate = plane_permutes(device_count)
+    out_own = after(out_lines, first_all)
+    from_first = lax.ppermute(out_own, "fsdp", first)
+    from_second = lax.ppermute(out_own, "fsdp", second)
     tail_projected = dot_nn(first_all[group_rows - MAXLEN :], mixer_weight)
     edge = MAXLEN // CHUNK
     state_type = jax.ShapeDtypeStruct((heads, dim, dim), f32)
     last_state = local_call(
         last_state_kernel,
         heads,
+        3,
         state_type,
         [],
         last_starts[-edge:] - (group_rows - MAXLEN),
@@ -541,11 +770,13 @@
     up_line = [(i, i + GROUP) for i in range(device_count - GROUP)]
     down_line = [(i + GROUP, i) for i in range(device_count - GROUP)]
     entering_state = lax.ppermute(last_state, "fsdp", up_line)
-    projected = dot_nn(first_all, mixer_weight)
+    projected = dot_nn(after(first_all, last_state), mixer_weight)
+    projected, entering_state = meet(projected, entering_state)
     chunks = group_rows // CHUNK
     mixed_heads, state_out, entering = local_call(
         forward_kernel,
         heads,
+        18,
         (
             jax.ShapeDtypeStruct((group_rows, own_width), bf16),
             jax.ShapeDtypeStruct((group_rows, own_width), f32),
@@ -559,27 +790,31 @@
         own_group_gain,
         entering_state,
     )
-    mixer_input = (
-        swap(mixed_heads.reshape(GROUP, row_count, own_width))
-        .transpose(1, 0, 2)
-        .reshape(row_count, width)
-    )
-    out_weight = group_gather(out_lines, 1).reshape(width, width)
+    mixed_heads, from_first, from_second = meet(mixed_heads, from_first, from_second)
+    from_corner = lax.ppermute(from_first, "fsdp", second)
+    mates = [lax.ppermute(block, "fsdp", mate) for block in (out_own, from_first, from_second)]
+    [mixer_input] = exchange(
+        3, 15, ("widen", mixed_heads.reshape(GROUP, row_count, own_width))
+    )
+    mixer_input, from_corner, mates = meet(mixer_input, from_corner, mates)
+    mates = mates + [lax.ppermute(from_corner, "fsdp", mate)]
+    out_weight = assemble(out_own, from_first, from_second, from_corner, mates).reshape(width, width)
+    down_weight = whole_rows(after(down_swapped, mixed_heads))
     residual = inputs + dot_nn(mixer_input, out_weight)
     second_inverse = inverse_rms(residual)
     second_scaled = residual * second_inverse
     second_normed = (second_scaled * second_gain).astype(bf16)
-    second_all = group_gather(second_normed[None], 0).reshape(group_rows, width)
-    cot_late, second_all = lax.optimization_barrier((cotangent, second_all))
-    cot_all = group_gather(cot_late[None], 0).reshape(group_rows, width)
+    [second_all] = exchange(2, 43, ("gather", second_normed[None]))
+    second_all = second_all.reshape(group_rows, width)
+    [cot_all] = exchange(2, 43, ("gather", after(cotangent, second_all)[None]))
+    cot_all = cot_all.reshape(group_rows, width)
     gate_pre = dot_nn(second_all, ffn_weight)
     gate_part = gate_pre[:, :own_ffn]
     up_part = gate_pre[:, own_ffn:]
     gate_sigmoid = jax.nn.sigmoid(gate_part)
     gate_act = gate_part * gate_sigmoid
     hidden_act = (gate_act * up_part).astype(bf16)
-    d_down_proj = home_rows(dot_tn(cot_all, hidden_act), 1)
-    ffn_part = dot_nt(hidden_act, down_weight).astype(bf16)
+    down_summed = line_scatter(dot_tn(cot_all, hidden_act).astype(bf16))
     d_hidden = dot_nn(cot_all, down_weight)
     d_gate_pre = jnp.concatenate(
         [
@@ -588,20 +823,37 @@
         ],
         axis=1,
     ).astype(bf16)
-    d_gate_up = home_rows(dot_tn(second_all, d_gate_pre), 2)
-    second_part = dot_nt(d_gate_pre, ffn_weight).astype(bf16)
-    d_second = group_scatter(second_part.reshape(1, GROUP, row_count, width), 2, f32)[0]
+    ffn_part = dot_nt(hidden_act, after(down_weight, d_gate_pre)).astype(bf16)
+    ffn_sum = SlowScatter(ffn_part.reshape(1, GROUP, row_count, width), moves, device_count)
+    ffn_near = ffn_sum.to_mate()
+    ffn_grad = dot_tn(after(second_all, ffn_part), d_gate_pre).astype(bf16)
+    ffn_grad, ffn_near = meet(ffn_grad, ffn_near)
+    ffn_summed = line_scatter(ffn_grad)
+    ffn_far = ffn_sum.to_second(ffn_near)
+    second_part = dot_nt(d_gate_pre, after(ffn_weight, ffn_grad)).astype(bf16)
+    d_second = group_scatter(second_part.reshape(1, GROUP, row_count, width), 4, f32)[0]
+    d_second, ffn_far, down_summed = meet(d_second, ffn_far, down_summed)
+    ffn_last = ffn_sum.to_first(ffn_near, ffn_far)
     d_residual = cotangent.astype(f32) + rms_back(
         d_second * second_gain, second_scaled, second_inverse
     )
     d_mix_out = d_residual.astype(bf16)
-    d_mixer_input = dot_nt(d_mix_out, out_weight).astype(bf16)
-    d_mixed_heads = swap(
-        d_mixer_input.reshape(row_count, GROUP, own_width).transpose(1, 0, 2)
-    ).reshape(group_rows, own_width)
+    out_part = dot_tn(mixer_input, d_mix_out).astype(bf16)
+    out_sum = SlowScatter(
+        out_part.reshape(groups, GROUP, weight_rows, width), moves, device_count
+    )
+    out_near = out_sum.to_mate()
+    d_mixer_input = dot_nt(after(d_mix_out, out_part), out_weight).astype(bf16)
+    [d_mixed_heads] = exchange(5, 15, ("narrow", d_mixer_input))
+    d_mixed_heads, out_near, ffn_last = meet(
+        d_mixed_heads.reshape(group_rows, own_width), out_near, ffn_last
+    )
+    layer_out = residual + ffn_sum.total(ffn_near, ffn_far, ffn_last)[0]
+    out_far = out_sum.to_second(out_near)
     first_grad = local_call(
         first_grad_kernel,
         heads,
+        3,
         state_type,
         [],
         last_starts[:edge],
@@ -613,12 +865,12 @@
         d_mixed_heads[:MAXLEN],
     )
     entering_grad = lax.ppermute(first_grad, "fsdp", down_line)
-    d_projected, floor_grad, group_gain_grad = local_call(
+    d_projected, floor_grad = local_call(
         backward_kernel,
         heads,
+        30,
         (
             jax.ShapeDtypeStruct((group_rows, 3 * own_width), bf16),
-            jax.ShapeDtypeStruct((1, own_width), f32),
             jax.ShapeDtypeStruct((1, own_width), f32),
         ),
         [pltpu.VMEM((heads, dim, dim), f32)],
@@ -632,36 +884,41 @@
         entering,
         entering_grad,
     )
-    d_mixer_in = home_rows(dot_tn(first_all, d_projected), 3)
-    first_part = dot_nt(d_projected, mixer_weight).astype(bf16)
-    d_first = group_scatter(first_part.reshape(1, GROUP, row_count, width), 2, f32)[0]
+    d_projected, out_far = meet(d_projected, out_far)
+    out_last = out_sum.to_first(out_near, out_far)
+    mixer_grad = dot_tn(first_all, d_projected).astype(bf16)
+    mixer_summed = line_scatter(after(mixer_grad, ffn_summed))
+    first_part = dot_nt(d_projected, after(mixer_weight, mixer_grad)).astype(bf16)
+    first_part, out_last = meet(first_part, out_last)
+    out_total = out_sum.total(out_near, out_far, out_last).astype(bf16)
+    d_first = group_scatter(first_part.reshape(1, GROUP, row_count, width), 4, f32)[0]
+    d_first, mixer_summed = meet(d_first, mixer_summed)
+    d_out_proj = line_scatter(
+        after(out_total, mixer_summed).reshape(groups * weight_rows, width)
+    ).astype(f32)
+    d_down_proj = home_rows(after(down_summed, d_first), 1, 6)
+    d_gate_up = home_rows(after(ffn_summed, d_down_proj), 2, 7)
+    d_mixer_in = home_rows(after(mixer_summed, d_gate_up), 3, 8)
     d_dealt = d_residual + rms_back(d_first * first_gain, first_scaled, first_inverse)
 
-    ffn_out = group_scatter(ffn_part.reshape(1, GROUP, row_count, width), 2, f32)[0]
-    layer_out = residual + ffn_out
-    out_part = dot_tn(mixer_input, d_mix_out).astype(bf16)
-    out_sum = group_scatter(out_part.reshape(groups, GROUP, weight_rows, width), 3, bf16)
-    d_out_proj = line_scatter(out_sum.reshape(groups * weight_rows, width)).astype(f32)
-
-    spread = jnp.zeros((2, width), f32)
-    own_grads = jnp.concatenate([floor_grad, group_gain_grad])
-    gain_grads = jnp.concatenate(
-        [
-            jnp.sum(d_first * first_scaled, axis=0, keepdims=True),
-            lax.dynamic_update_slice_in_dim(spread, own_grads, slot * own_width, 1),
-            jnp.sum(d_second * second_scaled, axis=0, keepdims=True),
-        ]
-    )
-    gain_sums = lax.psum_scatter(gain_grads, "fsdp", scatter_dimension=1, tiled=True)
+    def gain_grad(weight, weight_grad, gain):
+        return jnp.sum(weight.astype(f32) * weight_grad, axis=1) / gain.astype(f32)
+
+    floor_block = jnp.zeros((8, 128), f32).at[: own_width // 128].set(
+        floor_grad.reshape(own_width // 128, 128)
+    )
+    [floor_blocks] = exchange(9, 8, ("all", after(floor_block, d_gate_up)))
+    floor_sums = jnp.sum(floor_blocks[:, :, : own_width // 128], axis=0).reshape(width)
+    d_forget_floor = lax.dynamic_slice_in_dim(floor_sums, own_index * weight_rows, weight_rows, 0)
     return (
         layer_out,
         d_dealt,
-        gain_sums[0],
+        gain_grad(mixer_in, d_mixer_in, norm_gain),
         d_mixer_in,
-        gain_sums[1],
-        gain_sums[2],
+        d_forget_floor,
+        gain_grad(out_proj, d_out_proj, group_gain),
         d_out_proj,
-        gain_sums[3],
+        gain_grad(gate_up, d_gate_up, ffn_gain),
         d_gate_up,
         d_down_proj,
     )

time: 944 us -> 702 us (0.74)
  waiting for transfers between devices: 180 us -> 12.5 us
  blocking collectives: 101 us -> 0 us
  other arithmetic: 13.2 us -> 43.1 us
  Pallas kernels: 406 us -> 421 us
  starting transfers between devices: 24.6 us -> 13.3 us
    unnamed x10 -> x8, waiting for transfers between devices: 132 us -> 0.8 us
    pallas_call x4 -> x11, Pallas kernels: 179 us -> 284 us  [the longest x7 237 us: exchange(): pl.pallas_call(functools.partial(exchange_kernel, kinds), out_shape=tuple...]
    pallas_call x4 -> x2, Pallas kernels: 178 us -> 87.4 us  [group_scatter(): pl.pallas_call(functools.partial(group_scatter_kernel, min(32, rows)), ou...]
    all_to_all x3 -> x0, blocking collectives: 57.1 us -> none  [swap(): return lax.all_to_all(x, 'fsdp', 0, 0, axis_index_groups=planes, tiled=True)]
    all_gather x1 -> x0, blocking collectives: 44.3 us -> none  [body(): lax.all_gather(jnp.stack([norm_gain, forget_floor, group_gain, ffn_gain])...]
    reduce_scatter x4, waiting for transfers between devices: 29.5 us -> 0.04 us  [line_scatter(): lax.psum_scatter(x, 'fsdp', scatter_dimension=0, axis_index_groups=lines,...]
    all_to_all x5 -> x0, starting transfers between devices: 21.3 us -> none  [swap(): return lax.all_to_all(x, 'fsdp', 0, 0, axis_index_groups=planes, tiled=True)]
    unnamed x59 -> x128, local copies, waits for them, and re-layouts: 12.2 us -> 29.1 us
  transfers between devices with their start and end apart: 16 -> 23, of which waited for: 5 -> 3; matrix products, arithmetic and copies ran while one was open for 17% -> 25% of each run, Pallas kernels for 43% -> 61%
where the time goes in v2:
time: 702 us; the launch traced here: 694 us
  Pallas kernels  421 us (60%)
  matrix products  140 us (20%)
  local copies, waits for them, and re-layouts  48.8 us (7%)
  other arithmetic  43.1 us (6%)
  between operations  15.5 us (2%)
  starting transfers between devices  13.3 us (2%)
  waiting for transfers between devices  12.5 us (2%)
    pallas_call x7, Pallas kernels, exchange(): pl.pallas_call(functools.partial(exchange_kernel, kinds), out_shape=tuple...  237 us
    pallas_call x2, Pallas kernels, group_scatter(): pl.pallas_call(functools.partial(group_scatter_kernel, min(32, rows)), ou...  87.4 us
    dot_general x5, matrix products, dot_nn(): lax.dot_general(left, right, (((1,), (0,)), ((), ())), preferred_element_...  51.1 us
    pallas_call x4, Pallas kernels, local_call(): pl.pallas_call(functools.partial(kernel, heads), out_shape=out_shape, in_...  49.7 us
    dot_general x4, matrix products, dot_nt(): lax.dot_general(left, right, (((1,), (1,)), ((), ())), preferred_element_...  46.3 us
    pallas_call x3, Pallas kernels, home(): pl.pallas_call(functools.partial(home_kernel, pieces), out_shape=jax.Shap...  43.8 us
    dot_general x4, matrix products, dot_tn(): lax.dot_general(left, right, (((0,), (0,)), ((), ())), preferred_element_...  42.9 us
    unnamed x128, local copies, waits for them, and re-layouts  29.1 us
  transfers between devices with their start and end apart: 23, of which 3 were waited for; matrix products, arithmetic and copies ran while one was open for 25% of the time, Pallas kernels for 61%

profile of v2, /device:TPU:0, one launch (start us, length us, event | category | flops | bytes accessed | tf_op | source)
XLA Modules:
  0.0 694.3 jit_solution(7241572270936018947)
XLA Ops:
  12.5 18.3 %shard_map.195 = (bf16[4,8,16,128]{3,2,1,0:T(8,128)(2,1)}, bf16[8,64,768]{2,1,0:T(8,128)(2,1)}) custom-call(bf16[16,128]{1,0:T(8,128)(2,1)} %copy-done.49, bf16[8,64,768]{2,1,0:T(8,128)(2,1)} %reshape.475.refs_1_), custom_call_target="tpu_custom_call" | custom-call | bytes 55350000 | tf_op jit(solution)/shard_map/pallas_call | solution.py:211
  42.8 64.1 %shard_map.196 = (bf16[1,8,256,2048]{3,2,1,0:T(8,128)(2,1)}, bf16[8,64,1408]{2,1,0:T(8,128)(2,1)}, bf16[8,64,704]{2,1,0:T(8,128)(2,1)}) custom-call(bf16[1,256,2048]{2,1,0:T(8,128)(2,1)} %fusion.17.refs_0_, bf16[8,64,1408]{2,1,0:T(8,128)(2,1)} %reshape.477.refs_1_, bf16[8,64,704]{2,1,0:T(8,128)(2,1)} %bitcast.159), custom_call_target="tpu_custom_call" | custom-call | bytes 239850000 | tf_op jit(solution)/shard_map/pallas_call | solution.py:211
  117.0 10.7 %fusion.23.proj_ref = f32[2048,768]{1,0:T(8,128)} fusion(bf16[2048,2048]{1,0:T(8,128)(2,1)} %bitcast.165, bf16[2048,768]{1,0:T(8,128)(2,1)S(1)} %copy-done.40), kind=kOutput, calls=%fused_computation.92 | convolution fusion | flops 6442450944 | bytes 17825792 | tf_op jit(solution)/shard_map/dot_general | solution.py:38
  127.7 18.4 %shard_map.198 = (bf16[2048,256]{1,0:T(8,128)(2,1)S(1)}, f32[2048,256]{1,0:T(8,128)S(1)}, f32[32,2,128,128]{3,2,1,0:T(8,128)}) custom-call(s32[32]{0:T(128)S(1)} %slice.178.last_ref, f32[2048,768]{1,0:T(8,128)} %fusion.23.proj_ref, s32[2048,1]{1,0:T(8,128)S(1)} %copy.45.start_ref, f32[1,256]{1,0:T(1,128)S(1)} %get-tuple-element.190.floor_ref, ...), custom_call_target="tpu_custom_call" | custom-call | bytes 66420000 | tf_op jit(solution)/shard_map/pallas_call | solution.py:637
  150.4 24.5 %shard_map.199 = bf16[256,2048]{1,0:T(8,128)(2,1)} custom-call(bf16[8,256,256]{2,1,0:T(8,128)(2,1)} %bitcast.136), custom_call_target="tpu_custom_call" | custom-call | bytes 55350000 | tf_op jit(solution)/shard_map/pallas_call | solution.py:211
  178.0 3.1 shard_map.200
  186.9 50.8 %shard_map.201 = bf16[1,8,256,2048]{3,2,1,0:T(8,128)(2,1)} custom-call(bf16[1,256,2048]{2,1,0:T(8,128)(2,1)} %fusion.15.refs_0_), custom_call_target="tpu_custom_call" | custom-call | bytes 158670000 | tf_op jit(solution)/shard_map/pallas_call | solution.py:211
  237.7 50.8 %shard_map.202 = bf16[1,8,256,2048]{3,2,1,0:T(8,128)(2,1)} custom-call(bf16[1,256,2048]{2,1,0:T(8,128)(2,1)} %bitcast.143), custom_call_target="tpu_custom_call" | custom-call | bytes 158670000 | tf_op jit(solution)/shard_map/pallas_call | solution.py:211
  288.5 19.0 %fusion.24 = f32[2048,1408]{0,1:T(8,128)} fusion(bf16[2048,2048]{1,0:T(8,128)(2,1)} %bitcast.150, bf16[2048,1408]{1,0:T(8,128)(2,1)} %all-gather.8.cloned.1.call-done), kind=kOutput, calls=%fused_computation.93 | convolution fusion | flops 11811160064 | bytes 25690112 | tf_op jit(solution)/shard_map/dot_general | solution.py:38
  307.5 16.0 %multiply_convert_fusion.1 = (bf16[2048,704]{0,1:T(8,128)(2,1)}, bf16[2048,704]{0,1:T(8,128)(2,1)}, bf16[2048,704]{0,1:T(8,128)(2,1)S(1)}) fusion(f32[2048,1408]{0,1:T(8,128)} %fusion.24, bf16[2048,2048]{1,0:T(8,128)(2,1)} %bitcast.152, bf16[2048,704]{1,0:T(8,128)(2,1)} %all-gather.10.cloned.1.call-done), kind=kOutput, calls=%fused_computation.7 | convolution fusion | flops 5927206912 | bytes 31457280 | tf_op jit(solution)/shard_map/dot_general | solution.py:38
  325.1 11.0 %convolution_convert_fusion.6 = bf16[2048,704]{0,1:T(8,128)(2,1)} fusion(bf16[2048,704]{0,1:T(8,128)(2,1)S(1)} %get-tuple-element.178, bf16[2048,2048]{1,0:T(8,128)(2,1)} %bitcast.153), kind=kOutput, calls=%fused_computation.14 | convolution fusion | flops 5907021824 | bytes 14155776 | tf_op jit(solution)/shard_map/dot_general | solution.py:42
  336.1 9.1 %convolution_convert_fusion.3 = bf16[2048,2048]{1,0:T(8,128)(2,1)S(1)} fusion(bf16[2048,704]{0,1:T(8,128)(2,1)} %copy-done.60, bf16[2048,704]{1,0:T(8,128)(2,1)S(1)} %copy-done.57), kind=kOutput, calls=%fused_computation.3 | convolution fusion | flops 5909774336 | bytes 14155776 | tf_op jit(solution)/shard_map/dot_general | solution.py:34
  351.9 18.2 %convolution_convert_fusion.4 = bf16[2048,1408]{1,0:T(8,128)(2,1)} fusion(bf16[2048,2048]{1,0:T(8,128)(2,1)} %bitcast.151, bf16[2048,704]{0,1:T(8,128)(2,1)} %get-tuple-element.173, bf16[2048,704]{0,1:T(8,128)(2,1)S(1)} %copy-done.61), kind=kOutput, calls=%fused_computation.4 | convolution fusion | flops 11825577984 | bytes 19922944 | tf_op jit(solution)/shard_map/dot_general | solution.py:42
  370.1 3.1 add_convert_fusion.2
  375.9 18.8 %convolution_convert_fusion.2 = bf16[2048,2048]{1,0:T(8,128)(2,1)} fusion(bf16[2048,1408]{1,0:T(8,128)(2,1)} %all-gather.8.cloned.1.call-done, bf16[2048,704]{0,1:T(8,128)(2,1)} %get-tuple-element.173, bf16[2048,704]{0,1:T(8,128)(2,1)S(1)} %copy-done.61), kind=kOutput, calls=%fused_computation.2 | convolution fusion | flops 11826888704 | bytes 19922944 | tf_op jit(solution)/shard_map/dot_general | solution.py:34
  394.7 43.6 %shard_map.203 = f32[1,256,2048]{2,1,0:T(8,128)S(1)} custom-call(bf16[1,8,256,2048]{3,2,1,0:T(8,128)(2,1)} %bitcast.149), custom_call_target="tpu_custom_call" | custom-call | bytes 158670000 | tf_op jit(solution)/shard_map/pallas_call | solution.py:331
  445.0 2.9 copy-done.24
  450.5 3.5 fusion.16
  455.0 6.7 convolution_convert_fusion.7.refs_0_
  461.8 17.8 %shard_map.204 = bf16[8,256,256]{2,1,0:T(8,128)(2,1)} custom-call(bf16[256,2048]{1,0:T(8,128)(2,1)} %convolution_convert_fusion.7.refs_0_), custom_call_target="tpu_custom_call" | custom-call | bytes 55350000 | tf_op jit(solution)/shard_map/pallas_call | solution.py:211
  479.6 3.2 fusion.14
  491.3 6.8 collective-permute-done.12.in_ref
  500.9 29.5 %shard_map.206 = (bf16[2048,768]{1,0:T(8,128)(2,1)}, f32[1,256]{1,0:T(1,128)S(1)}) custom-call(s32[32]{0:T(128)S(1)} %copy-done.23, f32[2048,768]{1,0:T(8,128)} %fusion.23.proj_ref, s32[2048,1]{1,0:T(8,128)S(1)} %copy-done.7, f32[1,256]{1,0:T(1,128)S(1)} %copy-done.19, f32[1,256]{1,0:T(1,128)S(1)} %copy-done.21, f32[2048,256]{1,0:T(8,128)S(1)} %copy-done.13, ...), custom_call_target="tpu_custom_call" | custom-call | bytes 110700000 | tf_op jit(solution)/shard_map/pallas_call | solution.py:637
  530.4 11.4 %convolution_convert_fusion.5 = bf16[2048,768]{1,0:T(8,128)(2,1)} fusion(bf16[2048,2048]{1,0:T(8,128)(2,1)} %bitcast.166, bf16[2048,768]{1,0:T(8,128)(2,1)} %get-tuple-element.153), kind=kOutput, calls=%fused_computation.13 | convolution fusion | flops 6444023808 | bytes 14680064 | tf_op jit(solution)/shard_map/dot_general | solution.py:42
  546.3 11.7 %convolution_convert_fusion = bf16[2048,2048]{1,0:T(8,128)(2,1)} fusion(bf16[2048,768]{1,0:T(8,128)(2,1)} %get-tuple-element.153, bf16[2048,768]{1,0:T(8,128)(2,1)S(1)} %copy-done.41), kind=kOutput, calls=%fused_computation | convolution fusion | flops 6446645248 | bytes 14680064 | tf_op jit(solution)/shard_map/dot_general | solution.py:34
  560.1 43.8 %shard_map.207 = f32[1,256,2048]{2,1,0:T(8,128)S(1)} custom-call(bf16[1,8,256,2048]{3,2,1,0:T(8,128)(2,1)} %bitcast.148), custom_call_target="tpu_custom_call" | custom-call | bytes 158670000 | tf_op jit(solution)/shard_map/pallas_call | solution.py:331
  605.2 3.6 fusion.11
  610.2 12.3 %shard_map.208 = f32[64,5632]{1,0:T(8,128)S(1)} custom-call(bf16[8,64,704]{2,1,0:T(8,128)(2,1)S(1)} %bitcast.130), custom_call_target="tpu_custom_call" | custom-call | bytes 73800000 | tf_op jit(solution)/shard_map/pallas_call | solution.py:257
  623.6 19.4 %shard_map.209 = f32[64,11264]{1,0:T(8,128)S(1)} custom-call(bf16[8,64,1408]{2,1,0:T(8,128)(2,1)S(1)} %bitcast.131), custom_call_target="tpu_custom_call" | custom-call | bytes 73800000 | tf_op jit(solution)/shard_map/pallas_call | solution.py:257
  644.6 10.4 %shard_map.211 = f32[4,8,8,128]{3,2,1,0:T(8,128)} custom-call(f32[8,128]{1,0:T(8,128)} %scatter.24.refs_0_), custom_call_target="tpu_custom_call" | custom-call | bytes 29520000 | tf_op jit(solution)/shard_map/pallas_call | solution.py:211
  656.1 12.2 %shard_map.210 = f32[64,6144]{1,0:T(8,128)S(1)} custom-call(bf16[8,64,768]{2,1,0:T(8,128)(2,1)S(1)} %bitcast.137), custom_call_target="tpu_custom_call" | custom-call | bytes 73800000 | tf_op jit(solution)/shard_map/pallas_call | solution.py:257
  673.6 4.9 fusion.8
  (242 shorter events, 99.4 us)
Async XLA Ops:
  7.2 101.0 %all-gather.12.cloned.1.call-start = ((), (), s32[]{:S(2)}) async-start(), calls=%async_computation.11 | async-start | bytes 1310720 | tf_op jit(solution)/shard_map/all_gather | solution.py:723
  8.0 102.4 %all-gather.6.cloned.1.call-start = ((), (), s32[]{:S(2)}) async-start(), calls=%async_computation.4 | async-start | bytes 3932160 | tf_op jit(solution)/shard_map/all_gather | solution.py:679
  9.3 22.7 %copy-start.34 = (bf16[64,11264]{1,0:T(8,128)(2,1)S(1)}, bf16[64,11264]{1,0:T(8,128)(2,1)}, u32[]{:S(2)}) copy-start(bf16[64,11264]{1,0:T(8,128)(2,1)} %param.32) | copy-start | bytes 4325380
  30.9 257.6 %all-gather.8.cloned.1.call-start = ((), (), s32[]{:S(2)}) async-start(), calls=%async_computation.5 | async-start | bytes 7208960 | tf_op jit(solution)/shard_map/all_gather | solution.py:679
  41.5 65.4 %copy-start.47 = (f32[256]{0:T(256)}, f32[256]{0:T(256)S(1)}, u32[]{:S(2)}) copy-start(f32[256]{0:T(256)S(1)} %add_rsqrt_fusion.1) | copy-start | bytes 3076
  42.8 64.3 %copy-start.58 = (s32[96]{0:T(128)S(1)}, s32[96]{0:T(128)}, u32[]{:S(2)}) copy-start(s32[96]{0:T(128)} %param.24) | copy-start | bytes 1156
  42.8 64.3 %copy-start.59 = (s32[96]{0:T(128)S(1)}, s32[96]{0:T(128)}, u32[]{:S(2)}) copy-start(s32[96]{0:T(128)} %param.25) | copy-start | bytes 1156
  106.9 200.5 %all-gather.10.cloned.1.call-start = ((), (), s32[]{:S(2)}) async-start(), calls=%async_computation.6 | async-start | bytes 3932160 | tf_op jit(solution)/shard_map/all_gather | solution.py:679
  107.6 20.1 %copy-start.22 = (s32[32]{0:T(128)}, s32[32]{0:T(128)S(1)}, u32[]{:S(2)}) copy-start(s32[32]{0:T(128)S(1)} %slice.178.last_ref) | copy-start | bytes 388
  108.3 40.2 %collective-permute-start.1 = (bf16[4,64,2048]{2,1,0:T(8,128)(2,1)}, bf16[4,64,2048]{2,1,0:T(8,128)(2,1)S(1)}, u32[]{:S(2)}, u32[]{:S(2)}) collective-permute-start(bf16[4,64,2048]{2,1,0:T(8,128)(2,1)} %bitcast.132), channel_id=1, source_target_pairs={{0,2},{1,5},{2,0},{3,7},{4,6},{5,1},{6,4},{7,3},{8,10},{9,13},{10,... | collective-permute-start | bytes 3145736 | tf_op jit(solution)/shard_map/ppermute | solution.py:755
  109.6 38.8 %collective-permute-start.2 = (bf16[4,64,2048]{2,1,0:T(8,128)(2,1)}, bf16[4,64,2048]{2,1,0:T(8,128)(2,1)S(1)}, u32[]{:S(2)}, u32[]{:S(2)}) collective-permute-start(bf16[4,64,2048]{2,1,0:T(8,128)(2,1)} %bitcast.133), channel_id=1, source_target_pairs={{0,4},{1,3},{2,6},{3,1},{4,0},{5,7},{6,2},{7,5},{8,12},{9,11},{10,... | collective-permute-start | bytes 3145736 | tf_op jit(solution)/shard_map/ppermute | solution.py:756
  110.4 64.5 %collective-permute-start.4 = (bf16[4,64,2048]{2,1,0:T(8,128)(2,1)}, bf16[4,64,2048]{2,1,0:T(8,128)(2,1)}, u32[]{:S(2)}, u32[]{:S(2)}) collective-permute-start(bf16[4,64,2048]{2,1,0:T(8,128)(2,1)} %bitcast.134), channel_id=1, source_target_pairs={{0,1},{1,0},{2,3},{3,2},{4,5},{5,4},{6,7},{7,6},{8,9},{9,8},{10,11... | collective-permute-start | bytes 3145736 | tf_op jit(solution)/shard_map/ppermute | solution.py:795
  114.1 13.6 %collective-permute-start = (f32[2,128,128]{2,1,0:T(8,128)S(1)}, f32[2,128,128]{2,1,0:T(8,128)S(1)}, u32[]{:S(2)}, u32[]{:S(2)}) collective-permute-start(f32[2,128,128]{2,1,0:T(8,128)S(1)} %shard_map.197), channel_id=1, source_target_pairs={{0,8},{1,9},{2,10},{3,11},{4,12},{5,13},{6,14},{7,15},{8,16},{9,17... | collective-permute-start | bytes 393224 | tf_op jit(solution)/shard_map/ppermute | solution.py:772
  148.4 29.6 %copy-start.15 = (bf16[256,2048]{1,0:T(8,128)(2,1)S(1)}, bf16[256,2048]{1,0:T(8,128)(2,1)}, u32[]{:S(2)}) copy-start(bf16[256,2048]{1,0:T(8,128)(2,1)} %all-gather.12.cloned.1.call-done) | copy-start | bytes 3145732
  148.5 26.5 %collective-permute-start.3 = (bf16[4,64,2048]{2,1,0:T(8,128)(2,1)S(1)}, bf16[4,64,2048]{2,1,0:T(8,128)(2,1)}, u32[]{:S(2)}, u32[]{:S(2)}) collective-permute-start(bf16[4,64,2048]{2,1,0:T(8,128)(2,1)S(1)} %collective-permute-done.1.refs_1_), channel_id=1, source_target_pairs={{0,4},{1,3},{2,6},{3,1},{4,0},{5,7},{6,2},{7,5},{8,12},{9,11},{10,... | collective-permute-start | bytes 3145736 | tf_op jit(solution)/shard_map/ppermute | solution.py:794
  149.9 25.0 %collective-permute-start.5 = (bf16[4,64,2048]{2,1,0:T(8,128)(2,1)S(1)}, bf16[4,64,2048]{2,1,0:T(8,128)(2,1)}, u32[]{:S(2)}, u32[]{:S(2)}) collective-permute-start(bf16[4,64,2048]{2,1,0:T(8,128)(2,1)S(1)} %collective-permute-done.1.refs_1_), channel_id=1, source_target_pairs={{0,1},{1,0},{2,3},{3,2},{4,5},{5,4},{6,7},{7,6},{8,9},{9,8},{10,11... | collective-permute-start | bytes 3145736 | tf_op jit(solution)/shard_map/ppermute | solution.py:795
  149.9 25.0 %collective-permute-start.6 = (bf16[4,64,2048]{2,1,0:T(8,128)(2,1)S(1)}, bf16[4,64,2048]{2,1,0:T(8,128)(2,1)}, u32[]{:S(2)}, u32[]{:S(2)}) collective-permute-start(bf16[4,64,2048]{2,1,0:T(8,128)(2,1)S(1)} %collective-permute-done.2.refs_2_), channel_id=1, source_target_pairs={{0,1},{1,0},{2,3},{3,2},{4,5},{5,4},{6,7},{7,6},{8,9},{9,8},{10,11... | collective-permute-start | bytes 3145736 | tf_op jit(solution)/shard_map/ppermute | solution.py:795
  174.9 3.1 collective-permute-start.7
  175.2 263.1 %reduce-scatter.5.cloned.1.call-start = ((), (), s32[]{:S(2)}) async-start(), calls=%async_computation.7 | async-start | bytes 3604480 | tf_op jit(solution)/shard_map/reduce_scatter | solution.py:682
  336.1 205.8 %reduce-scatter.7.cloned.1.call-start = ((), (), s32[]{:S(2)}) async-start(), calls=%async_computation.8 | async-start | bytes 7208960 | tf_op jit(solution)/shard_map/reduce_scatter | solution.py:682
  351.0 19.1 %collective-permute-start.8 = (bf16[4,1,256,2048]{3,2,1,0:T(8,128)(2,1)}, bf16[4,1,256,2048]{3,2,1,0:T(8,128)(2,1)}, u32[]{:S(2)}, u32[]{:S(2)}) collective-permute-start(bf16[4,1,256,2048]{3,2,1,0:T(8,128)(2,1)} %pad_maximum_fusion.1), channel_id=1, source_target_pairs={{0,1},{1,0},{2,3},{3,2},{4,5},{5,4},{6,7},{7,6},{8,9},{9,8},{10,11... | collective-permute-start | bytes 12582920 | tf_op jit(solution)/shard_map/ppermute | solution.py:405
  374.7 63.7 %collective-permute-start.9 = (bf16[2,1,256,2048]{3,2,1,0:T(8,128)(2,1)}, bf16[2,1,256,2048]{3,2,1,0:T(8,128)(2,1)}, u32[]{:S(2)}, u32[]{:S(2)}) collective-permute-start(bf16[2,1,256,2048]{3,2,1,0:T(8,128)(2,1)} %pad_maximum_fusion.3), channel_id=1, source_target_pairs={{0,4},{1,3},{2,6},{3,1},{4,0},{5,7},{6,2},{7,5},{8,12},{9,11},{10,... | collective-permute-start | bytes 6291464 | tf_op jit(solution)/shard_map/ppermute | solution.py:410
  375.8 233.0 %reduce-scatter.9.cloned.1.call-start = ((), (), s32[]{:S(2)}) async-start(), calls=%async_computation.9 | async-start | bytes 3932160 | tf_op jit(solution)/shard_map/reduce_scatter | solution.py:682
  450.4 29.2 %collective-permute-start.10 = (bf16[4,4,64,2048]{3,2,1,0:T(8,128)(2,1)}, bf16[4,4,64,2048]{3,2,1,0:T(8,128)(2,1)}, u32[]{:S(2)}, u32[]{:S(2)}) collective-permute-start(bf16[4,4,64,2048]{3,2,1,0:T(8,128)(2,1)} %pad_maximum_fusion.2), channel_id=1, source_target_pairs={{0,1},{1,0},{2,3},{3,2},{4,5},{5,4},{6,7},{7,6},{8,9},{9,8},{10,11... | collective-permute-start | bytes 12582920 | tf_op jit(solution)/shard_map/ppermute | solution.py:405
  454.1 25.5 %collective-permute-start.11 = (bf16[1,256,2048]{2,1,0:T(8,128)(2,1)}, bf16[1,256,2048]{2,1,0:T(8,128)(2,1)}, u32[]{:S(2)}, u32[]{:S(2)}) collective-permute-start(bf16[1,256,2048]{2,1,0:T(8,128)(2,1)} %fusion.16), channel_id=1, source_target_pairs={{0,2},{1,5},{2,0},{3,7},{4,6},{5,1},{6,4},{7,3},{8,10},{9,13},{10,... | collective-permute-start | bytes 3145736 | tf_op jit(solution)/shard_map/ppermute | solution.py:414
  484.4 46.0 %collective-permute-start.13 = (bf16[2,4,64,2048]{3,2,1,0:T(8,128)(2,1)}, bf16[2,4,64,2048]{3,2,1,0:T(8,128)(2,1)}, u32[]{:S(2)}, u32[]{:S(2)}) collective-permute-start(bf16[2,4,64,2048]{3,2,1,0:T(8,128)(2,1)} %pad_maximum_fusion.4), channel_id=1, source_target_pairs={{0,4},{1,3},{2,6},{3,1},{4,0},{5,7},{6,2},{7,5},{8,12},{9,11},{10,... | collective-permute-start | bytes 6291464 | tf_op jit(solution)/shard_map/ppermute | solution.py:410
  490.0 8.1 %collective-permute-start.12 = (f32[2,128,128]{2,1,0:T(8,128)S(1)}, f32[2,128,128]{2,1,0:T(8,128)S(1)}, u32[]{:S(2)}, u32[]{:S(2)}) collective-permute-start(f32[2,128,128]{2,1,0:T(8,128)S(1)} %shard_map.205), channel_id=1, source_target_pairs={{8,0},{9,1},{10,2},{11,3},{12,4},{13,5},{14,6},{15,7},{16,8},{17,9... | collective-permute-start | bytes 393224 | tf_op jit(solution)/shard_map/ppermute | solution.py:867
  541.9 136.6 %reduce-scatter.11.cloned.1.call-start = ((), (), s32[]{:S(2)}) async-start(), calls=%async_computation.10 | async-start | bytes 1310720 | tf_op jit(solution)/shard_map/reduce_scatter | solution.py:682
  545.2 14.9 %collective-permute-start.14 = (bf16[4,64,2048]{2,1,0:T(8,128)(2,1)S(1)}, bf16[4,64,2048]{2,1,0:T(8,128)(2,1)S(1)}, u32[]{:S(2)}, u32[]{:S(2)}) collective-permute-start(bf16[4,64,2048]{2,1,0:T(8,128)(2,1)S(1)} %fusion.12), channel_id=1, source_target_pairs={{0,2},{1,5},{2,0},{3,7},{4,6},{5,1},{6,4},{7,3},{8,10},{9,13},{10,... | collective-permute-start | bytes 3145736 | tf_op jit(solution)/shard_map/ppermute | solution.py:414
  623.6 32.5 %copy-start.17 = (bf16[512,768]{1,0:T(8,128)(2,1)S(1)}, bf16[512,768]{1,0:T(8,128)(2,1)}, u32[]{:S(2)}) copy-start(bf16[512,768]{1,0:T(8,128)(2,1)} %reduce-scatter.9.cloned.1.call-done) | copy-start | bytes 2359300
  644.6 26.6 %copy-start.45 = (f32[2048]{0:T(1024)S(1)}, f32[2048]{0:T(1024)}, u32[]{:S(2)}) copy-start(f32[2048]{0:T(1024)} %copy-done.44) | copy-start | bytes 24580
  644.6 26.6 %copy-start.48 = (f32[256]{0:T(256)S(1)}, f32[256]{0:T(256)}, u32[]{:S(2)}) copy-start(f32[256]{0:T(256)} %copy-done.47) | copy-start | bytes 3076
  (53 other events, 297.3 us)
Sparse Core Ops, SparseCore 0:
  9.6 30.6 all-gather.11
  41.9 62.9 all-gather.5
  107.0 105.5 all-gather.7
  214.0 64.3 all-gather.9
  336.2 55.5 reduce-scatter.4
  394.0 102.0 reduce-scatter.6
  542.0 59.9 reduce-scatter.8
  608.9 26.6 reduce-scatter.10

commit v3 on v2

--- a/solution.py
+++ b/solution.py
@@ -145,7 +145,7 @@
     own = []
     for item, kind in enumerate(plan):
         if kind == "all":
-            own.append(keep(item, ins[item], outs[item].at[group, slot]))
+            keep(item, ins[item], outs[item].at[group, slot]).wait()
             for number, target, _ in line:
                 send(item, ins[item], outs[item].at[group, slot], GROUP - 1 + number, target)
         elif kind == "gather":
@@ -157,8 +157,6 @@
             for number, step in others:
                 send(item, piece(item, slot + step), block(item, slot), number - 1, me + step)
             own.append(keep(item, piece(item, slot), block(item, slot)))
-    for copy in own:
-        copy.wait()
     for item, kind in enumerate(plan):
         if kind == "all":
             for number, _, sender in line:
@@ -188,6 +186,8 @@
                 arrived(item, block(item, slot + step), number - 1)
     for copy in sent:
         copy.wait_send()
+    for copy in own:
+        copy.wait()
 
 
 def exchange(number, micros, *items):
@@ -223,60 +223,39 @@
     )(*arrays)
 
 
-def home_kernel(pieces, x_ref, out_ref, got, send_sem, recv_sem, own_sem):
-    me, slot, step_core, first_step, second_step = places()
-    core = lax.rem(slot, 2)
-    step_low = (1 - core) * first_step + core * second_step
-    step_high = core * first_step + (1 - core) * second_step
-    others = plane_steps(step_core, step_low, step_high)
-    greet([me + step for _, step in others])
-    sent = []
-    for number, step in others:
-        copy = remote(
-            x_ref.at[slot + step], got.at[slot], send_sem.at[number - 1], recv_sem.at[number - 1], me + step
-        )
-        copy.start()
-        sent.append(copy)
-    own = pltpu.make_async_copy(x_ref.at[slot], got.at[slot], own_sem)
-    own.start()
-    own.wait()
-    for number, step in others:
-        target = got.at[slot + step]
-        remote(target, target, send_sem.at[number - 1], recv_sem.at[number - 1], me + step).wait_recv()
-    columns = x_ref.shape[2] // pieces
+def home_kernel(pieces, got_ref, weight_ref, out_ref, gain_ref):
+    columns = got_ref.shape[2] // pieces
     for piece in range(pieces):
         for sender in range(GROUP):
             lo = (piece * GROUP + sender) * columns
-            out_ref[:, lo : lo + columns] = got[sender, :, piece * columns : (piece + 1) * columns].astype(f32)
-    for copy in sent:
-        copy.wait_send()
-
-
-def home(x, pieces, number):
-    _, rows, columns = x.shape
+            out_ref[:, lo : lo + columns] = got_ref[
+                sender, :, piece * columns : (piece + 1) * columns
+            ].astype(f32)
+    gain_ref[...] = jnp.sum(out_ref[...] * weight_ref[...].astype(f32), axis=1, keepdims=True)
+
+
+def home(got, weight, pieces):
+    rows, columns = weight.shape
     return pl.pallas_call(
         functools.partial(home_kernel, pieces),
-        out_shape=jax.ShapeDtypeStruct((rows, GROUP * columns), f32),
-        in_specs=[VMEM],
-        out_specs=VMEM,
-        scratch_shapes=[
-            pltpu.VMEM(x.shape, x.dtype),
-            pltpu.SemaphoreType.DMA((GROUP - 1,)),
-            pltpu.SemaphoreType.DMA((GROUP - 1,)),
-            pltpu.SemaphoreType.DMA,
-        ],
-        compiler_params=pltpu.CompilerParams(
-            collective_id=number, has_side_effects=True, vmem_limit_bytes=32 * 2**20
+        out_shape=(
+            jax.ShapeDtypeStruct((rows, columns), f32),
+            jax.ShapeDtypeStruct((rows, 1), f32),
         ),
-        cost_estimate=cost(20),
-    )(x)
-
-
-def group_scatter_kernel(slab_rows, x_ref, out_ref, near, far, going, send_sem, recv_sem):
+        in_specs=[VMEM, VMEM],
+        out_specs=(VMEM, VMEM),
+        compiler_params=pltpu.CompilerParams(vmem_limit_bytes=32 * 2**20),
+        cost_estimate=cost(5),
+    )(got, weight)
+
+
+TILE = 256
+
+
+def product_scatter_kernel(a_ref, w_ref, out_ref, near, far, away, going, send_sem, recv_sem):
     me, slot, step_core, first_step, second_step = places()
     first, second, mate = me + first_step, me + second_step, me + step_core
     greet((first, second, mate))
-    parts, rows, _ = out_ref.shape
     corner_step = first_step + second_step
     steps = (corner_step, first_step, second_step, corner_step * 0)
     mate_steps = (corner_step, second_step, first_step, corner_step * 0)
@@ -290,61 +269,215 @@
     def arrived(ref, number, source):
         remote(ref, ref, send_sem.at[number], recv_sem.at[number], source).wait_recv()
 
-    def add(kind, extra, target):
-        place = slot + steps[kind]
-
-        def slab(i, _):
-            part = i // (rows // slab_rows)
-            at = pl.ds(
-                pl.multiple_of(lax.rem(i, rows // slab_rows) * slab_rows, slab_rows), slab_rows
-            )
-            total = x_ref[part, place, at, :].astype(f32) + near[kind, part, at, :].astype(f32)
+    def product(place, extra, target):
+        def tile(i, _):
+            at = pl.ds(pl.multiple_of(i * TILE, TILE), TILE)
+            total = dot_nt(a_ref[place], w_ref[at, :])
             for ref in extra:
-                total = total + ref[part, at, :].astype(f32)
-            target[part, at, :] = total.astype(target.dtype)
+                total = total + ref[:, at].astype(f32)
+            target[:, at] = total.astype(target.dtype)
             return 0
 
-        lax.fori_loop(0, parts * (rows // slab_rows), slab, 0)
-
-    for kind in (0, 2, 1, 3):
-        send(x_ref.at[:, slot + step_core + mate_steps[kind]], near.at[kind], kind, mate)
+        lax.fori_loop(0, out_ref.shape[1] // TILE, tile, 0)
+
+    def to_mate(kind):
+        product(slot + step_core + mate_steps[kind], (), away.at[kind])
+        send(away.at[kind], near.at[kind], kind, mate)
+
+    def add(ref):
+        def tile(i, _):
+            at = pl.ds(pl.multiple_of(i * TILE, TILE), TILE)
+            out_ref[:, at] = out_ref[:, at] + ref[:, at].astype(f32)
+            return 0
+
+        lax.fori_loop(0, out_ref.shape[1] // TILE, tile, 0)
+
+    to_mate(0)
+    to_mate(2)
     arrived(near.at[0], 0, mate)
-    add(0, (), going.at[0])
+    product(slot + steps[0], (near.at[0],), going.at[0])
     send(going.at[0], far.at[0], 4, second)
     arrived(near.at[2], 2, mate)
-    add(2, (), going.at[2])
+    product(slot + steps[2], (near.at[2],), going.at[2])
     send(going.at[2], far.at[2], 5, second)
+    to_mate(1)
+    to_mate(3)
+    arrived(near.at[3], 3, mate)
+    product(slot + steps[3], (near.at[3],), out_ref)
     arrived(near.at[1], 1, mate)
     arrived(far.at[0], 4, second)
-    add(1, (far.at[0],), going.at[1])
+    product(slot + steps[1], (near.at[1], far.at[0]), going.at[1])
     send(going.at[1], far.at[1], 6, first)
-    arrived(near.at[3], 3, mate)
     arrived(far.at[2], 5, second)
+    add(far.at[2])
     arrived(far.at[1], 6, first)
-    add(3, (far.at[1], far.at[2]), out_ref)
+    add(far.at[1])
     for copy in sent:
         copy.wait_send()
 
 
-def group_scatter(x, number, out_type):
-    parts, _, rows, columns = x.shape
+def product_scatter(a, w, number):
+    _, rows, depth = a.shape
+    columns = w.shape[0]
     return pl.pallas_call(
-        functools.partial(group_scatter_kernel, min(32, rows)),
-        out_shape=jax.ShapeDtypeStruct((parts, rows, columns), out_type),
-        in_specs=[VMEM],
+        product_scatter_kernel,
+        out_shape=jax.ShapeDtypeStruct((rows, columns), f32),
+        in_specs=[VMEM, VMEM],
         out_specs=VMEM,
         scratch_shapes=[
-            pltpu.VMEM((4, parts, rows, columns), x.dtype),
-            pltpu.VMEM((3, parts, rows, columns), x.dtype),
-            pltpu.VMEM((3, parts, rows, columns), x.dtype),
+            pltpu.VMEM((4, rows, columns), bf16),
+            pltpu.VMEM((3, rows, columns), bf16),
+            pltpu.VMEM((4, rows, columns), bf16),
+            pltpu.VMEM((3, rows, columns), bf16),
             pltpu.SemaphoreType.DMA((7,)),
             pltpu.SemaphoreType.DMA((7,)),
         ],
         compiler_params=pltpu.CompilerParams(
-            collective_id=number, has_side_effects=True, vmem_limit_bytes=48 * 2**20
+            collective_id=number, has_side_effects=True, vmem_limit_bytes=56 * 2**20
         ),
-        cost_estimate=cost(43),
-    )(x)
+        cost_estimate=cost(50),
+    )(a, w)
+
+
+def gate_gather_kernel(own_ref, x_ref, w_ref, all_ref, gate_ref, up_ref, hidden_ref, send_sem, recv_sem, own_sem):
+    me, slot, step_core, first_step, second_step = places()
+    first, second, mate = me + first_step, me + second_step, me + step_core
+    greet((first, second, mate))
+    sent = []
+
+    def send(source, place, number, device):
+        copy = remote(source, all_ref.at[place], send_sem.at[number], recv_sem.at[number], device)
+        copy.start()
+        sent.append(copy)
+
+    def arrived(place, number):
+        target = all_ref.at[place]
+        remote(target, target, send_sem.at[number], recv_sem.at[number], me).wait_recv()
+
+    own = pltpu.make_async_copy(own_ref, all_ref.at[slot], own_sem)
+    send(own_ref, slot, 0, first)
+    send(own_ref, slot, 1, second)
+    send(own_ref, slot, 2, mate)
+    own.start()
+    half = gate_ref.shape[1]
+    tile_rows = own_ref.shape[0]
+
+    def tile(i, _):
+        at = pl.ds(pl.multiple_of(i * tile_rows, tile_rows), tile_rows)
+        both = dot_nn(x_ref[at, :], w_ref[...])
+        gate = both[:, :half]
+        up = both[:, half:]
+        gate_ref[at, :] = gate
+        up_ref[at, :] = up
+        hidden_ref[at, :] = (gate * jax.nn.sigmoid(gate) * up).astype(bf16)
+        return 0
+
+    tiles = x_ref.shape[0] // tile_rows
+    lax.fori_loop(0, tiles // 2, tile, 0)
+    corner = slot + first_step + second_step
+    arrived(slot + first_step, 0)
+    send(all_ref.at[slot + first_step], slot + first_step, 3, second)
+    send(all_ref.at[slot + first_step], slot + first_step, 4, mate)
+    arrived(slot + second_step, 1)
+    send(all_ref.at[slot + second_step], slot + second_step, 5, mate)
+    lax.fori_loop(tiles // 2, tiles, tile, 0)
+    arrived(corner, 3)
+    send(all_ref.at[corner], corner, 6, mate)
+    arrived(slot + step_core, 2)
+    arrived(slot + step_core + second_step, 4)
+    arrived(slot + step_core + first_step, 5)
+    arrived(corner + step_core, 6)
+    for copy in sent:
+        copy.wait_send()
+    own.wait()
+
+
+def gate_gather(own, x, w, number):
+    rows, columns = own.shape
+    half = w.shape[1] // 2
+    wide = jax.ShapeDtypeStruct((x.shape[0], half), f32)
+    return pl.pallas_call(
+        gate_gather_kernel,
+        out_shape=(
+            jax.ShapeDtypeStruct((GROUP, rows, columns), own.dtype),
+            wide,
+            wide,
+            jax.ShapeDtypeStruct((x.shape[0], half), bf16),
+        ),
+        in_specs=[ANY, VMEM, VMEM],
+        out_specs=(ANY, VMEM, VMEM, VMEM),
+        scratch_shapes=[
+            pltpu.SemaphoreType.DMA((7,)),
+            pltpu.SemaphoreType.DMA((7,)),
+            pltpu.SemaphoreType.DMA,
+        ],
+        compiler_params=pltpu.CompilerParams(
+            collective_id=number, has_side_effects=True, vmem_limit_bytes=56 * 2**20
+        ),
+        cost_estimate=cost(45),
+    )(own, x, w)
+
+
+def hidden_back_kernel(cot_ref, gate_ref, up_ref, hidden_ref, w_ref, grad_ref, out_ref):
+    half = gate_ref.shape[1]
+    d_hidden = dot_nn(cot_ref[...], w_ref[...])
+    gate = gate_ref[...]
+    sigmoid = jax.nn.sigmoid(gate)
+    grad_ref[:, :half] = (
+        d_hidden * up_ref[...] * sigmoid * (1.0 + gate * (1.0 - sigmoid))
+    ).astype(bf16)
+    grad_ref[:, half:] = (d_hidden * gate * sigmoid).astype(bf16)
+    out_ref[...] = dot_nt(hidden_ref[...], w_ref[...]).astype(bf16)
+
+
+def hidden_back(cot, gate, up, hidden, w):
+    rows, columns = cot.shape
+    half = w.shape[1]
+    tile_rows = 256
+
+    def tiles(width):
+        return pl.BlockSpec((tile_rows, width), lambda i: (i, 0))
+
+    return pl.pallas_call(
+        hidden_back_kernel,
+        grid=(rows // tile_rows,),
+        in_specs=[
+            tiles(columns),
+            tiles(half),
+            tiles(half),
+            tiles(half),
+            pl.BlockSpec(w.shape, lambda i: (0, 0)),
+        ],
+        out_specs=(tiles(2 * half), tiles(columns)),
+        out_shape=(
+            jax.ShapeDtypeStruct((rows, 2 * half), bf16),
+            jax.ShapeDtypeStruct((rows, columns), bf16),
+        ),
+        compiler_params=pltpu.CompilerParams(vmem_limit_bytes=48 * 2**20),
+        cost_estimate=cost(20),
+    )(cot, gate, up, hidden, w)
+
+
+def rows_product_kernel(x_ref, y_ref, out_ref):
+    out_ref[...] = dot_tn(x_ref[...], y_ref[...]).astype(bf16)
+
+
+def rows_product(x, y, micros):
+    rows, columns = x.shape
+    wide = y.shape[1]
+    tile_columns = 512
+    return pl.pallas_call(
+        rows_product_kernel,
+        grid=(columns // tile_columns,),
+        in_specs=[
+            pl.BlockSpec((rows, tile_columns), lambda i: (0, i)),
+            pl.BlockSpec((rows, wide), lambda i: (0, 0)),
+        ],
+        out_specs=pl.BlockSpec((tile_columns, wide), lambda i: (i, 0)),
+        out_shape=jax.ShapeDtypeStruct((columns, wide), bf16),
+        compiler_params=pltpu.CompilerParams(vmem_limit_bytes=48 * 2**20),
+        cost_estimate=cost(micros),
+    )(x, y)
 
 
 def plane_permutes(device_count):
@@ -691,9 +824,6 @@
     def whole_rows(x):
         return line_gather(x.reshape(GROUP * weight_rows, -1))
 
-    def home_rows(summed, pieces, number):
-        return home(summed.reshape(GROUP, weight_rows, -1), pieces, number)
-
     low_step = 2 - 4 * (slot // 2 % 2)
     high_step = 4 - 8 * (slot // 4)
     odd = slot % 2
@@ -806,32 +936,24 @@
     second_normed = (second_scaled * second_gain).astype(bf16)
     [second_all] = exchange(2, 43, ("gather", second_normed[None]))
     second_all = second_all.reshape(group_rows, width)
-    [cot_all] = exchange(2, 43, ("gather", after(cotangent, second_all)[None]))
-    cot_all = cot_all.reshape(group_rows, width)
-    gate_pre = dot_nn(second_all, ffn_weight)
-    gate_part = gate_pre[:, :own_ffn]
-    up_part = gate_pre[:, own_ffn:]
-    gate_sigmoid = jax.nn.sigmoid(gate_part)
-    gate_act = gate_part * gate_sigmoid
-    hidden_act = (gate_act * up_part).astype(bf16)
-    down_summed = line_scatter(dot_tn(cot_all, hidden_act).astype(bf16))
-    d_hidden = dot_nn(cot_all, down_weight)
-    d_gate_pre = jnp.concatenate(
-        [
-            d_hidden * up_part * gate_sigmoid * (1.0 + gate_part * (1.0 - gate_sigmoid)),
-            d_hidden * gate_act,
-        ],
-        axis=1,
-    ).astype(bf16)
-    ffn_part = dot_nt(hidden_act, after(down_weight, d_gate_pre)).astype(bf16)
+    cot_blocks, gate_part, up_part, hidden_act = gate_gather(
+        cotangent, second_all, ffn_weight, 6
+    )
+    cot_all = cot_blocks.reshape(group_rows, width)
+    down_grad = rows_product(cot_all, hidden_act, 11)
+    down_summed = line_scatter(down_grad)
+    d_gate_pre, ffn_part = hidden_back(
+        after(cot_all, down_grad), gate_part, up_part, hidden_act, down_weight
+    )
     ffn_sum = SlowScatter(ffn_part.reshape(1, GROUP, row_count, width), moves, device_count)
     ffn_near = ffn_sum.to_mate()
-    ffn_grad = dot_tn(after(second_all, ffn_part), d_gate_pre).astype(bf16)
+    ffn_grad = rows_product(second_all, d_gate_pre, 18)
     ffn_grad, ffn_near = meet(ffn_grad, ffn_near)
     ffn_summed = line_scatter(ffn_grad)
     ffn_far = ffn_sum.to_second(ffn_near)
-    second_part = dot_nt(d_gate_pre, after(ffn_weight, ffn_grad)).astype(bf16)
-    d_second = group_scatter(second_part.reshape(1, GROUP, row_count, width), 4, f32)[0]
+    d_second = product_scatter(
+        d_gate_pre.reshape(GROUP, row_count, -1), after(ffn_weight, ffn_grad), 4
+    )
     d_second, ffn_far, down_summed = meet(d_second, ffn_far, down_summed)
     ffn_last = ffn_sum.to_first(ffn_near, ffn_far)
     d_residual = cotangent.astype(f32) + rms_back(
@@ -849,7 +971,6 @@
         d_mixed_heads.reshape(group_rows, own_width), out_near, ffn_last
     )
     layer_out = residual + ffn_sum.total(ffn_near, ffn_far, ffn_last)[0]
-    out_far = out_sum.to_second(out_near)
     first_grad = local_call(
         first_grad_kernel,
         heads,
@@ -865,6 +986,8 @@
         d_mixed_heads[:MAXLEN],
     )
     entering_grad = lax.ppermute(first_grad, "fsdp", down_line)
+    out_near = after(out_near, first_grad)
+    out_far = out_sum.to_second(out_near)
     d_projected, floor_grad = local_call(
         backward_kernel,
         heads,
@@ -888,37 +1011,46 @@
     out_last = out_sum.to_first(out_near, out_far)
     mixer_grad = dot_tn(first_all, d_projected).astype(bf16)
     mixer_summed = line_scatter(after(mixer_grad, ffn_summed))
-    first_part = dot_nt(d_projected, after(mixer_weight, mixer_grad)).astype(bf16)
-    first_part, out_last = meet(first_part, out_last)
+    d_first = product_scatter(
+        d_projected.reshape(GROUP, row_count, -1), after(mixer_weight, mixer_grad), 8
+    )
+    d_first, out_last = meet(d_first, out_last)
     out_total = out_sum.total(out_near, out_far, out_last).astype(bf16)
-    d_first = group_scatter(first_part.reshape(1, GROUP, row_count, width), 4, f32)[0]
-    d_first, mixer_summed = meet(d_first, mixer_summed)
     d_out_proj = line_scatter(
         after(out_total, mixer_summed).reshape(groups * weight_rows, width)
     ).astype(f32)
-    d_down_proj = home_rows(after(down_summed, d_first), 1, 6)
-    d_gate_up = home_rows(after(ffn_summed, d_down_proj), 2, 7)
-    d_mixer_in = home_rows(after(mixer_summed, d_gate_up), 3, 8)
-    d_dealt = d_residual + rms_back(d_first * first_gain, first_scaled, first_inverse)
-
-    def gain_grad(weight, weight_grad, gain):
-        return jnp.sum(weight.astype(f32) * weight_grad, axis=1) / gain.astype(f32)
-
     floor_block = jnp.zeros((8, 128), f32).at[: own_width // 128].set(
         floor_grad.reshape(own_width // 128, 128)
     )
-    [floor_blocks] = exchange(9, 8, ("all", after(floor_block, d_gate_up)))
+    down_summed, ffn_summed, floor_block = after((down_summed, ffn_summed, floor_block), d_first)
+    by_sender = (GROUP, weight_rows, -1)
+    down_swapped, ffn_swapped, floor_blocks = exchange(
+        7,
+        30,
+        ("swap", down_summed.reshape(by_sender)),
+        ("swap", ffn_summed.reshape(by_sender)),
+        ("all", floor_block),
+    )
+    d_down_proj, _ = home(down_swapped, down_proj, 1)
+    d_gate_up, ffn_gain_sum = home(ffn_swapped, gate_up, 2)
+    [mixer_swapped] = exchange(
+        9, 12, ("swap", after(mixer_summed, floor_blocks).reshape(by_sender))
+    )
+    d_mixer_in, norm_gain_sum = home(mixer_swapped, mixer_in, 3)
+    d_dealt = d_residual + rms_back(d_first * first_gain, first_scaled, first_inverse)
+
+    group_gain_sum = jnp.sum(out_proj.astype(f32) * d_out_proj, axis=1)
     floor_sums = jnp.sum(floor_blocks[:, :, : own_width // 128], axis=0).reshape(width)
     d_forget_floor = lax.dynamic_slice_in_dim(floor_sums, own_index * weight_rows, weight_rows, 0)
     return (
         layer_out,
         d_dealt,
-        gain_grad(mixer_in, d_mixer_in, norm_gain),
+        norm_gain_sum[:, 0] / norm_gain.astype(f32),
         d_mixer_in,
         d_forget_floor,
-        gain_grad(out_proj, d_out_proj, group_gain),
+        group_gain_sum / group_gain.astype(f32),
         d_out_proj,
-        gain_grad(gate_up, d_gate_up, ffn_gain),
+        ffn_gain_sum[:, 0] / ffn_gain.astype(f32),
         d_gate_up,
         d_down_proj,
     )

time: 702 us -> 650 us (0.926)
  matrix products: 140 us -> 37.1 us
  Pallas kernels: 421 us -> 481 us
  local copies, waits for them, and re-layouts: 48.8 us -> 34 us
    pallas_call x5 -> x9, Pallas kernels: 131 us -> 216 us  [the longest x2 110 us: product_scatter(): pl.pallas_call(product_scatter_kernel, out_shape=jax.ShapeDtypeStruct((ro...]
    dot_general x4 -> x1, matrix products: 46.3 us -> 7.08 us  [dot_nt(): lax.dot_general(left, right, (((1,), (1,)), ((), ())), preferred_element_...]
    dot_general x5 -> x3, matrix products: 51.1 us -> 16.3 us  [dot_nn(): lax.dot_general(left, right, (((1,), (0,)), ((), ())), preferred_element_...]
    dot_general x4 -> x2, matrix products: 42.9 us -> 13.8 us  [dot_tn(): lax.dot_general(left, right, (((0,), (0,)), ((), ())), preferred_element_...]
    pallas_call x7, Pallas kernels: 237 us -> 212 us  [exchange(): pl.pallas_call(functools.partial(exchange_kernel, kinds), out_shape=tuple...]
    unnamed x128 -> x81, local copies, waits for them, and re-layouts: 29.1 us -> 15.2 us
  transfers between devices with their start and end apart: 23 -> 23, of which waited for: 3 -> 3; matrix products, arithmetic and copies ran while one was open for 25% -> 14% of each run, Pallas kernels for 61% -> 72%
where the time goes in v3:
time: 650 us; the launch traced here: 641 us
  Pallas kernels  481 us (74%)
  other arithmetic  41.1 us (6%)
  matrix products  37.1 us (6%)
  local copies, waits for them, and re-layouts  34 us (5%)
  waiting for transfers between devices  18.6 us (3%)
  between operations  15.5 us (2%)
  starting transfers between devices  13.3 us (2%)
    pallas_call x7, Pallas kernels, exchange(): pl.pallas_call(functools.partial(exchange_kernel, kinds), out_shape=tuple...  212 us
    pallas_call x2, Pallas kernels, product_scatter(): pl.pallas_call(product_scatter_kernel, out_shape=jax.ShapeDtypeStruct((ro...  110 us
    pallas_call x1, Pallas kernels, gate_gather(): pl.pallas_call(gate_gather_kernel, out_shape=(jax.ShapeDtypeStruct((GROUP...  53.2 us
    pallas_call x4, Pallas kernels, local_call(): pl.pallas_call(functools.partial(kernel, heads), out_shape=out_shape, in_...  50 us
    pallas_call x2, Pallas kernels, rows_product(): pl.pallas_call(rows_product_kernel, grid=(columns // tile_columns,), in_s...  28.1 us
    pallas_call x1, Pallas kernels, hidden_back(): pl.pallas_call(hidden_back_kernel, grid=(rows // tile_rows,), in_specs=[t...  19.7 us
    dot_general x3, matrix products, dot_nn(): lax.dot_general(left, right, (((1,), (0,)), ((), ())), preferred_element_...  16.3 us
    unnamed x81, local copies, waits for them, and re-layouts  15.2 us
  transfers between devices with their start and end apart: 23, of which 3 were waited for; matrix products, arithmetic and copies ran while one was open for 14% of the time, Pallas kernels for 72%

profile of v3, /device:TPU:0, one launch (start us, length us, event | category | flops | bytes accessed | tf_op | source)
XLA Modules:
  0.0 640.7 jit_solution(1929966746852769047)
XLA Ops:
  12.5 19.5 %shard_map.195 = (bf16[4,8,16,128]{3,2,1,0:T(8,128)(2,1)}, bf16[8,64,768]{2,1,0:T(8,128)(2,1)}) custom-call(bf16[16,128]{1,0:T(8,128)(2,1)} %copy-done.33, bf16[8,64,768]{2,1,0:T(8,128)(2,1)} %reshape.475.refs_1_), custom_call_target="tpu_custom_call" | custom-call | bytes 55350000 | tf_op jit(solution)/shard_map/pallas_call | solution.py:211
  33.2 2.8 reshape.476
  36.0 2.6 copy.56
  43.9 64.0 %shard_map.196 = (bf16[1,8,256,2048]{3,2,1,0:T(8,128)(2,1)}, bf16[8,64,1408]{2,1,0:T(8,128)(2,1)}, bf16[8,64,704]{2,1,0:T(8,128)(2,1)}) custom-call(bf16[1,256,2048]{2,1,0:T(8,128)(2,1)} %fusion.16.refs_0_, bf16[8,64,1408]{2,1,0:T(8,128)(2,1)} %reshape.477.refs_1_, bf16[8,64,704]{2,1,0:T(8,128)(2,1)} %bitcast.134), custom_call_target="tpu_custom_call" | custom-call | bytes 239850000 | tf_op jit(solution)/shard_map/pallas_call | solution.py:211
  111.5 2.9 fusion.17.proj_ref
  117.4 10.9 %fusion.22.proj_ref = f32[2048,768]{1,0:T(8,128)} fusion(bf16[2048,2048]{1,0:T(8,128)(2,1)} %bitcast.144, bf16[2048,768]{1,0:T(8,128)(2,1)S(1)} %copy-done.27), kind=kOutput, calls=%fused_computation.79 | convolution fusion | flops 6442450944 | bytes 17825792 | tf_op jit(solution)/shard_map/dot_general | solution.py:38
  128.3 18.6 %shard_map.198 = (bf16[2048,256]{1,0:T(8,128)(2,1)S(1)}, f32[2048,256]{1,0:T(8,128)S(1)}, f32[32,2,128,128]{3,2,1,0:T(8,128)}) custom-call(s32[32]{0:T(128)S(1)} %slice.172.last_ref, f32[2048,768]{1,0:T(8,128)} %fusion.22.proj_ref, s32[2048,1]{1,0:T(8,128)S(1)} %copy.43.start_ref, f32[1,256]{1,0:T(1,128)S(1)} %get-tuple-element.209.floor_ref, ...), custom_call_target="tpu_custom_call" | custom-call | bytes 66420000 | tf_op jit(solution)/shard_map/pallas_call | solution.py:770
  151.6 24.7 %shard_map.199 = bf16[256,2048]{1,0:T(8,128)(2,1)} custom-call(bf16[8,256,256]{2,1,0:T(8,128)(2,1)} %bitcast.115), custom_call_target="tpu_custom_call" | custom-call | bytes 55350000 | tf_op jit(solution)/shard_map/pallas_call | solution.py:211
  176.6 2.8 collective-permute-done.7.refs_7_
  179.4 3.1 shard_map.200
  182.5 2.5 multiply_reduce_fusion.1
  188.3 42.5 %shard_map.201 = bf16[1,8,256,2048]{3,2,1,0:T(8,128)(2,1)} custom-call(bf16[1,256,2048]{2,1,0:T(8,128)(2,1)} %fusion.14.refs_0_), custom_call_target="tpu_custom_call" | custom-call | bytes 158670000 | tf_op jit(solution)/shard_map/pallas_call | solution.py:211
  230.8 53.2 %shard_map.202 = (bf16[8,256,2048]{2,1,0:T(8,128)(2,1)}, f32[2048,704]{1,0:T(8,128)}, f32[2048,704]{1,0:T(8,128)}, bf16[2048,704]{1,0:T(8,128)(2,1)}) custom-call(bf16[256,2048]{1,0:T(8,128)(2,1)} %own_ref.1, bf16[2048,2048]{1,0:T(8,128)(2,1)} %bitcast.117, bf16[2048,1408]{1,0:T(8,128)(2,1)} %all-gather.8.cloned.1.call-done.w_ref), custom_call_target="tpu_custom_call" | custom-call | bytes 166050000 | tf_op jit(solution)/shard_map/pallas_call | solution.py:399
  284.1 11.0 %shard_map.203 = bf16[2048,704]{1,0:T(8,128)(2,1)} custom-call(bf16[2048,2048]{1,0:T(8,128)(2,1)} %bitcast.123, bf16[2048,704]{1,0:T(8,128)(2,1)} %get-tuple-element.148.y_ref.hidden_ref), custom_call_target="tpu_custom_call" | custom-call | bytes 40590000 | tf_op jit(solution)/shard_map/pallas_call | solution.py:469
  295.1 19.7 %shard_map.204 = (bf16[2048,1408]{1,0:T(8,128)(2,1)}, bf16[2048,2048]{1,0:T(8,128)(2,1)}) custom-call(bf16[2048,2048]{1,0:T(8,128)(2,1)} %bitcast.124, f32[2048,704]{1,0:T(8,128)} %get-tuple-element.150.gate_ref, f32[2048,704]{1,0:T(8,128)} %get-tuple-element.151.up_ref, bf16[2048,704]{1,0:T(8,128)(2,1)S(1)} %copy-done.1, ...), custom_call_target="tpu_custom_call" | custom-call | bytes 73800000 | tf_op jit(solution)/shard_map/pallas_call | solution.py:441
  314.7 2.7 constant_dynamic-slice_fusion.3
  320.5 17.1 %shard_map.205 = bf16[2048,1408]{1,0:T(8,128)(2,1)S(1)} custom-call(bf16[2048,2048]{1,0:T(8,128)(2,1)} %bitcast.118, bf16[2048,1408]{1,0:T(8,128)(2,1)} %get-tuple-element.155.y_ref), custom_call_target="tpu_custom_call" | custom-call | bytes 66420000 | tf_op jit(solution)/shard_map/pallas_call | solution.py:469
  340.0 3.1 add_convert_fusion.2
  345.8 59.8 %shard_map.206 = f32[256,2048]{1,0:T(8,128)} custom-call(bf16[8,256,1408]{2,1,0:T(8,128)(2,1)} %bitcast.125, bf16[2048,1408]{1,0:T(8,128)(2,1)} %all-gather.8.cloned.1.call-done.w_ref), custom_call_target="tpu_custom_call" | custom-call | bytes 184500000 | tf_op jit(solution)/shard_map/pallas_call | solution.py:322
  412.2 2.9 copy-done.18
  418.4 3.6 fusion.15
  424.2 7.1 %convolution_convert_fusion.2.refs_0_ = bf16[256,2048]{1,0:T(8,128)(2,1)} fusion(bf16[256,2048]{1,0:T(8,128)(2,1)} %copy-done.31, bf16[2048,2048]{1,0:T(8,128)(2,1)} %bitcast.107), kind=kOutput, calls=%fused_computation.10 | convolution fusion | flops 2148007936 | bytes 10485760 | tf_op jit(solution)/shard_map/dot_general | solution.py:34
  431.3 16.3 %shard_map.207 = bf16[8,256,256]{2,1,0:T(8,128)(2,1)} custom-call(bf16[256,2048]{1,0:T(8,128)(2,1)} %convolution_convert_fusion.2.refs_0_), custom_call_target="tpu_custom_call" | custom-call | bytes 55350000 | tf_op jit(solution)/shard_map/pallas_call | solution.py:211
  449.4 3.2 fusion.13
  455.3 13.5 %collective-permute-done.12.in_ref = f32[2,128,128]{2,1,0:T(8,128)S(1)} collective-permute-done((f32[2,128,128]{2,1,0:T(8,128)S(1)}, f32[2,128,128]{2,1,0:T(8,128)S(1)}, u32[]{:S(2)}, u32[]{:S(2)}) %collective-permute-start.12) | collective-permute-done | bytes 131104 | tf_op jit(solution)/shard_map/ppermute | solution.py:988
  468.8 29.6 %shard_map.209 = (bf16[2048,768]{1,0:T(8,128)(2,1)}, f32[1,256]{1,0:T(1,128)S(1)}) custom-call(s32[32]{0:T(128)S(1)} %slice.172.last_ref, f32[2048,768]{1,0:T(8,128)} %fusion.22.proj_ref, s32[2048,1]{1,0:T(8,128)S(1)} %copy-done.3, f32[1,256]{1,0:T(1,128)S(1)} %get-tuple-element.209.floor_ref, f32[1,256]{1,0:T(1,128)S(1)} %get-tuple-element.208.gain_ref, ...), custom_call_target="tpu_custom_call" | custom-call | bytes 110700000 | tf_op jit(solution)/shard_map/pallas_call | solution.py:770
  498.4 11.4 %convolution_convert_fusion.1 = bf16[2048,768]{1,0:T(8,128)(2,1)} fusion(bf16[2048,2048]{1,0:T(8,128)(2,1)} %bitcast.145, bf16[2048,768]{1,0:T(8,128)(2,1)} %get-tuple-element.169), kind=kOutput, calls=%fused_computation.3 | convolution fusion | flops 6444023808 | bytes 14680064 | tf_op jit(solution)/shard_map/dot_general | solution.py:42
  512.3 50.3 %shard_map.210 = f32[256,2048]{1,0:T(8,128)} custom-call(bf16[8,256,768]{2,1,0:T(8,128)(2,1)} %bitcast.135, bf16[2048,768]{1,0:T(8,128)(2,1)} %all-gather.6.cloned.1.call-done.w_ref), custom_call_target="tpu_custom_call" | custom-call | bytes 184500000 | tf_op jit(solution)/shard_map/pallas_call | solution.py:322
  562.6 3.7 fusion.10
  570.8 5.4 fusion.7
  576.2 32.7 %shard_map.211 = (bf16[8,64,704]{2,1,0:T(8,128)(2,1)}, bf16[8,64,1408]{2,1,0:T(8,128)(2,1)}, f32[4,8,8,128]{3,2,1,0:T(8,128)}) custom-call(bf16[8,64,704]{2,1,0:T(8,128)(2,1)} %bitcast.139, bf16[8,64,1408]{2,1,0:T(8,128)(2,1)} %bitcast.137, f32[8,128]{1,0:T(8,128)} %scatter.24.refs_2_), custom_call_target="tpu_custom_call" | custom-call | bytes 110700000 | tf_op jit(solution)/shard_map/pallas_call | solution.py:211
  615.5 12.3 %shard_map.212.got_ref = bf16[8,64,768]{2,1,0:T(8,128)(2,1)} custom-call(bf16[8,64,768]{2,1,0:T(8,128)(2,1)} %bitcast.141), custom_call_target="tpu_custom_call" | custom-call | bytes 44280000 | tf_op jit(solution)/shard_map/pallas_call | solution.py:211
  (191 shorter events, 69.8 us)
Async XLA Ops:
  7.2 102.1 %all-gather.12.cloned.1.call-start = ((), (), s32[]{:S(2)}) async-start(), calls=%async_computation.11 | async-start | bytes 1310720 | tf_op jit(solution)/shard_map/all_gather | solution.py:853
  7.9 103.5 %all-gather.6.cloned.1.call-start = ((), (), s32[]{:S(2)}) async-start(), calls=%async_computation.4 | async-start | bytes 3932160 | tf_op jit(solution)/shard_map/all_gather | solution.py:812
  9.7 23.5 %copy-start.5 = (bf16[64,11264]{1,0:T(8,128)(2,1)S(1)}, bf16[64,11264]{1,0:T(8,128)(2,1)}, u32[]{:S(2)}) copy-start(bf16[64,11264]{1,0:T(8,128)(2,1)} %weight_ref.4) | copy-start | bytes 4325380
  32.1 198.7 %all-gather.8.cloned.1.call-start = ((), (), s32[]{:S(2)}) async-start(), calls=%async_computation.5 | async-start | bytes 7208960 | tf_op jit(solution)/shard_map/all_gather | solution.py:812
  43.9 64.2 %copy-start.38 = (s32[96]{0:T(128)S(1)}, s32[96]{0:T(128)}, u32[]{:S(2)}) copy-start(s32[96]{0:T(128)} %param.24) | copy-start | bytes 1156
  43.9 64.2 %copy-start.39 = (s32[96]{0:T(128)S(1)}, s32[96]{0:T(128)}, u32[]{:S(2)}) copy-start(s32[96]{0:T(128)} %param.25) | copy-start | bytes 1156
  108.0 187.1 %all-gather.10.cloned.1.call-start = ((), (), s32[]{:S(2)}) async-start(), calls=%async_computation.6 | async-start | bytes 3932160 | tf_op jit(solution)/shard_map/all_gather | solution.py:812
  109.1 19.2 %copy-start.2 = (s32[2048,1]{1,0:T(8,128)}, s32[2048,1]{1,0:T(8,128)S(1)}, u32[]{:S(2)}) copy-start(s32[2048,1]{1,0:T(8,128)S(1)} %copy.43.start_ref) | copy-start | bytes 24580
  109.3 39.9 %collective-permute-start.1 = (bf16[4,64,2048]{2,1,0:T(8,128)(2,1)}, bf16[4,64,2048]{2,1,0:T(8,128)(2,1)S(1)}, u32[]{:S(2)}, u32[]{:S(2)}) collective-permute-start(bf16[4,64,2048]{2,1,0:T(8,128)(2,1)} %bitcast.111), channel_id=1, source_target_pairs={{0,2},{1,5},{2,0},{3,7},{4,6},{5,1},{6,4},{7,3},{8,10},{9,13},{10,... | collective-permute-start | bytes 3145736 | tf_op jit(solution)/shard_map/ppermute | solution.py:885
  110.7 38.5 %collective-permute-start.2 = (bf16[4,64,2048]{2,1,0:T(8,128)(2,1)}, bf16[4,64,2048]{2,1,0:T(8,128)(2,1)}, u32[]{:S(2)}, u32[]{:S(2)}) collective-permute-start(bf16[4,64,2048]{2,1,0:T(8,128)(2,1)} %bitcast.112), channel_id=1, source_target_pairs={{0,4},{1,3},{2,6},{3,1},{4,0},{5,7},{6,2},{7,5},{8,12},{9,11},{10,... | collective-permute-start | bytes 3145736 | tf_op jit(solution)/shard_map/ppermute | solution.py:886
  115.2 13.1 %collective-permute-start = (f32[2,128,128]{2,1,0:T(8,128)S(1)}, f32[2,128,128]{2,1,0:T(8,128)S(1)}, u32[]{:S(2)}, u32[]{:S(2)}) collective-permute-start(f32[2,128,128]{2,1,0:T(8,128)S(1)} %shard_map.197), channel_id=1, source_target_pairs={{0,8},{1,9},{2,10},{3,11},{4,12},{5,13},{6,14},{7,15},{8,16},{9,17... | collective-permute-start | bytes 393224 | tf_op jit(solution)/shard_map/ppermute | solution.py:902
  128.3 21.1 %copy-start.15 = (bf16[256,2048]{1,0:T(8,128)(2,1)S(1)}, bf16[256,2048]{1,0:T(8,128)(2,1)}, u32[]{:S(2)}) copy-start(bf16[256,2048]{1,0:T(8,128)(2,1)} %all-gather.12.cloned.1.call-done) | copy-start | bytes 3145732
  149.2 256.4 %reduce-scatter.5.cloned.1.call-start = ((), (), s32[]{:S(2)}) async-start(), calls=%async_computation.7 | async-start | bytes 3932160 | tf_op jit(solution)/shard_map/reduce_scatter | solution.py:815
  149.4 26.9 %collective-permute-start.4 = (bf16[4,64,2048]{2,1,0:T(8,128)(2,1)S(1)}, bf16[4,64,2048]{2,1,0:T(8,128)(2,1)S(1)}, u32[]{:S(2)}, u32[]{:S(2)}) collective-permute-start(bf16[4,64,2048]{2,1,0:T(8,128)(2,1)S(1)} %bitcast.113), channel_id=1, source_target_pairs={{0,1},{1,0},{2,3},{3,2},{4,5},{5,4},{6,7},{7,6},{8,9},{9,8},{10,11... | collective-permute-start | bytes 3145736 | tf_op jit(solution)/shard_map/ppermute | solution.py:925
  149.5 26.8 %collective-permute-start.3 = (bf16[4,64,2048]{2,1,0:T(8,128)(2,1)S(1)}, bf16[4,64,2048]{2,1,0:T(8,128)(2,1)}, u32[]{:S(2)}, u32[]{:S(2)}) collective-permute-start(bf16[4,64,2048]{2,1,0:T(8,128)(2,1)S(1)} %collective-permute-done.1.refs_1_), channel_id=1, source_target_pairs={{0,4},{1,3},{2,6},{3,1},{4,0},{5,7},{6,2},{7,5},{8,12},{9,11},{10,... | collective-permute-start | bytes 3145736 | tf_op jit(solution)/shard_map/ppermute | solution.py:924
  151.1 25.2 %collective-permute-start.5 = (bf16[4,64,2048]{2,1,0:T(8,128)(2,1)S(1)}, bf16[4,64,2048]{2,1,0:T(8,128)(2,1)}, u32[]{:S(2)}, u32[]{:S(2)}) collective-permute-start(bf16[4,64,2048]{2,1,0:T(8,128)(2,1)S(1)} %collective-permute-done.1.refs_1_), channel_id=1, source_target_pairs={{0,1},{1,0},{2,3},{3,2},{4,5},{5,4},{6,7},{7,6},{8,9},{9,8},{10,11... | collective-permute-start | bytes 3145736 | tf_op jit(solution)/shard_map/ppermute | solution.py:925
  151.2 25.2 %collective-permute-start.6 = (bf16[4,64,2048]{2,1,0:T(8,128)(2,1)}, bf16[4,64,2048]{2,1,0:T(8,128)(2,1)}, u32[]{:S(2)}, u32[]{:S(2)}) collective-permute-start(bf16[4,64,2048]{2,1,0:T(8,128)(2,1)} %collective-permute-done.2.refs_2_), channel_id=1, source_target_pairs={{0,1},{1,0},{2,3},{3,2},{4,5},{5,4},{6,7},{7,6},{8,9},{9,8},{10,11... | collective-permute-start | bytes 3145736 | tf_op jit(solution)/shard_map/ppermute | solution.py:925
  176.3 3.1 collective-permute-start.7
  319.8 20.3 %collective-permute-start.8 = (bf16[4,1,256,2048]{3,2,1,0:T(8,128)(2,1)}, bf16[4,1,256,2048]{3,2,1,0:T(8,128)(2,1)}, u32[]{:S(2)}, u32[]{:S(2)}) collective-permute-start(bf16[4,1,256,2048]{3,2,1,0:T(8,128)(2,1)} %pad_maximum_fusion), channel_id=1, source_target_pairs={{0,1},{1,0},{2,3},{3,2},{4,5},{5,4},{6,7},{7,6},{8,9},{9,8},{10,11... | collective-permute-start | bytes 12582920 | tf_op jit(solution)/shard_map/ppermute | solution.py:538
  320.2 189.6 %reduce-scatter.7.cloned.1.call-start = ((), (), s32[]{:S(2)}) async-start(), calls=%async_computation.8 | async-start | bytes 7208960 | tf_op jit(solution)/shard_map/reduce_scatter | solution.py:815
  344.7 61.0 %collective-permute-start.9 = (bf16[2,1,256,2048]{3,2,1,0:T(8,128)(2,1)}, bf16[2,1,256,2048]{3,2,1,0:T(8,128)(2,1)}, u32[]{:S(2)}, u32[]{:S(2)}) collective-permute-start(bf16[2,1,256,2048]{3,2,1,0:T(8,128)(2,1)} %pad_maximum_fusion.2), channel_id=1, source_target_pairs={{0,4},{1,3},{2,6},{3,1},{4,0},{5,7},{6,2},{7,5},{8,12},{9,11},{10,... | collective-permute-start | bytes 6291464 | tf_op jit(solution)/shard_map/ppermute | solution.py:543
  345.8 222.0 %reduce-scatter.9.cloned.1.call-start = ((), (), s32[]{:S(2)}) async-start(), calls=%async_computation.9 | async-start | bytes 3932160 | tf_op jit(solution)/shard_map/reduce_scatter | solution.py:815
  345.8 59.9 %copy-start.20 = (f32[256,2048]{1,0:T(8,128)S(1)}, f32[256,2048]{1,0:T(8,128)}, u32[]{:S(2)}) copy-start(f32[256,2048]{1,0:T(8,128)} %copy-done.19) | copy-start | bytes 6291460
  417.4 30.2 %collective-permute-start.10 = (bf16[4,4,64,2048]{3,2,1,0:T(8,128)(2,1)}, bf16[4,4,64,2048]{3,2,1,0:T(8,128)(2,1)}, u32[]{:S(2)}, u32[]{:S(2)}) collective-permute-start(bf16[4,4,64,2048]{3,2,1,0:T(8,128)(2,1)} %pad_maximum_fusion.1), channel_id=1, source_target_pairs={{0,1},{1,0},{2,3},{3,2},{4,5},{5,4},{6,7},{7,6},{8,9},{9,8},{10,11... | collective-permute-start | bytes 12582920 | tf_op jit(solution)/shard_map/ppermute | solution.py:538
  421.9 25.6 %collective-permute-start.11 = (bf16[1,256,2048]{2,1,0:T(8,128)(2,1)}, bf16[1,256,2048]{2,1,0:T(8,128)(2,1)}, u32[]{:S(2)}, u32[]{:S(2)}) collective-permute-start(bf16[1,256,2048]{2,1,0:T(8,128)(2,1)} %fusion.15), channel_id=1, source_target_pairs={{0,2},{1,5},{2,0},{3,7},{4,6},{5,1},{6,4},{7,3},{8,10},{9,13},{10,... | collective-permute-start | bytes 3145736 | tf_op jit(solution)/shard_map/ppermute | solution.py:547
  452.9 45.5 %collective-permute-start.13 = (bf16[2,4,64,2048]{3,2,1,0:T(8,128)(2,1)S(1)}, bf16[2,4,64,2048]{3,2,1,0:T(8,128)(2,1)}, u32[]{:S(2)}, u32[]{:S(2)}) collective-permute-start(bf16[2,4,64,2048]{3,2,1,0:T(8,128)(2,1)S(1)} %pad_maximum_fusion.3), channel_id=1, source_target_pairs={{0,4},{1,3},{2,6},{3,1},{4,0},{5,7},{6,2},{7,5},{8,12},{9,11},{10,... | collective-permute-start | bytes 6291464 | tf_op jit(solution)/shard_map/ppermute | solution.py:543
  453.7 15.0 %collective-permute-start.12 = (f32[2,128,128]{2,1,0:T(8,128)S(1)}, f32[2,128,128]{2,1,0:T(8,128)S(1)}, u32[]{:S(2)}, u32[]{:S(2)}) collective-permute-start(f32[2,128,128]{2,1,0:T(8,128)S(1)} %shard_map.208), channel_id=1, source_target_pairs={{8,0},{9,1},{10,2},{11,3},{12,4},{13,5},{14,6},{15,7},{16,8},{17,9... | collective-permute-start | bytes 393224 | tf_op jit(solution)/shard_map/ppermute | solution.py:988
  509.8 121.2 %reduce-scatter.11.cloned.1.call-start = ((), (), s32[]{:S(2)}) async-start(), calls=%async_computation.10 | async-start | bytes 1310720 | tf_op jit(solution)/shard_map/reduce_scatter | solution.py:815
  512.2 50.4 %collective-permute-start.14 = (bf16[4,64,2048]{2,1,0:T(8,128)(2,1)S(1)}, bf16[4,64,2048]{2,1,0:T(8,128)(2,1)S(1)}, u32[]{:S(2)}, u32[]{:S(2)}) collective-permute-start(bf16[4,64,2048]{2,1,0:T(8,128)(2,1)S(1)} %fusion.11), channel_id=1, source_target_pairs={{0,2},{1,5},{2,0},{3,7},{4,6},{5,1},{6,4},{7,3},{8,10},{9,13},{10,... | collective-permute-start | bytes 3145736 | tf_op jit(solution)/shard_map/ppermute | solution.py:547
  576.2 32.7 %copy-start.6 = (bf16[64,11264]{1,0:T(8,128)(2,1)S(1)}, bf16[64,11264]{1,0:T(8,128)(2,1)}, u32[]{:S(2)}) copy-start(bf16[64,11264]{1,0:T(8,128)(2,1)} %weight_ref.4) | copy-start | bytes 4325380
  576.2 36.2 %copy-start.11 = (bf16[64,5632]{1,0:T(8,128)(2,1)S(1)}, bf16[64,5632]{1,0:T(8,128)(2,1)}, u32[]{:S(2)}) copy-start(bf16[64,5632]{1,0:T(8,128)(2,1)} %weight_ref.5) | copy-start | bytes 2162692
  612.5 18.5 %copy-start.32 = (bf16[64,2048]{1,0:T(8,128)(2,1)S(1)}, bf16[64,2048]{1,0:T(8,128)(2,1)}, u32[]{:S(2)}) copy-start(bf16[64,2048]{1,0:T(8,128)(2,1)} %param.30) | copy-start | bytes 786436
  (31 other events, 133.2 us)
Sparse Core Ops, SparseCore 0:
  9.6 30.6 all-gather.11
  41.8 62.9 all-gather.5
  108.1 105.5 all-gather.7
  215.1 64.0 all-gather.9
  320.3 59.5 reduce-scatter.4
  382.0 105.0 reduce-scatter.6
  509.9 57.7 reduce-scatter.8
  570.0 27.4 reduce-scatter.10

commit v4 on v3

v4 whole, which is shorter than its diff:
```python
import functools

import jax
import jax.numpy as jnp
from jax import lax
from jax.experimental import pallas as pl
from jax.experimental.pallas import tpu as pltpu
from jax.sharding import PartitionSpec as P

HEADS = 16
CHUNK = 64
HALF = 32
TILE_ROWS = 512
UNROLL = 2
MAXLEN = 128
GROUP = 8
MESH_ID = pl.DeviceIdType.MESH
VMEM = pl.BlockSpec(memory_space=pltpu.VMEM)
SMEM = pl.BlockSpec(memory_space=pltpu.SMEM)
ANY = pl.BlockSpec(memory_space=pl.ANY)

norm_eps = 1e-05
f32 = jnp.float32
bf16 = jnp.bfloat16


def inverse_rms(values):
    return lax.rsqrt(jnp.mean(values * values, axis=-1, keepdims=True) + norm_eps)


def rms_back(grad_scaled, scaled, inverse):
    return inverse * (grad_scaled - scaled * jnp.mean(grad_scaled * scaled, axis=-1, keepdims=True))


def dot_nt(left, right):
    return lax.dot_general(left, right, (((1,), (1,)), ((), ())), preferred_element_type=f32)


def dot_nn(left, right):
    return lax.dot_general(left, right, (((1,), (0,)), ((), ())), preferred_element_type=f32)


def dot_tn(left, right):
    return lax.dot_general(left, right, (((0,), (0,)), ((), ())), preferred_element_type=f32)


def cost(micros):
    return pl.CostEstimate(flops=0, transcendentals=0, bytes_accessed=int(micros * 36_900))


def places():
    me = lax.axis_index("fsdp")
    slot = lax.rem(me, GROUP)
    core = lax.rem(slot, 2)
    step_low = 2 - 4 * lax.rem(slot // 2, 2)
    step_high = 4 - 8 * (slot // 4)
    step_core = 1 - 2 * core
    first_step = (1 - core) * step_low + core * step_high
    second_step = core * step_low + (1 - core) * step_high
    return me, slot, step_core, first_step, second_step


def greet(others):
    barrier = pltpu.get_barrier_semaphore()
    for other in others:
        pl.semaphore_signal(barrier, inc=1, device_id=(other,), device_id_type=MESH_ID)
    pl.semaphore_wait(barrier, len(others))


def remote(source, target, send_sem, recv_sem, device):
    return pltpu.make_async_remote_copy(
        src_ref=source,
        dst_ref=target,
        send_sem=send_sem,
        recv_sem=recv_sem,
        device_id=(device,),
        device_id_type=MESH_ID,
    )


def plane_steps(step_core, step_low, step_high):
    return [
        (number, (number & 1) * step_core + ((number >> 1) & 1) * step_low + (number >> 2) * step_high)
        for number in range(1, GROUP)
    ]


AROUND = (1, 2, 4, 3, 5, 6, 7)


def exchange_kernel(plan, *refs):
    count = len(plan)
    ins, outs = refs[:count], refs[count : 2 * count]
    send_sem, recv_sem, own_sem = refs[2 * count :]
    me, slot, step_core, first_step, second_step = places()
    core = lax.rem(slot, 2)
    step_low = (1 - core) * first_step + core * second_step
    step_high = core * first_step + (1 - core) * second_step
    others = plane_steps(step_core, step_low, step_high)
    group = me // GROUP
    groups = lax.axis_size("fsdp") // GROUP
    greeted = [me + first_step, me + second_step, me + step_core]
    if not set(plan) <= {"gather", "around"}:
        greeted = [me + step for _, step in others]
    line = []
    if "all" in plan:
        line = [
            (
                number,
                lax.rem(group + number, groups) * GROUP + slot,
                lax.rem(group + groups - number, groups),
            )
            for number in range(1, groups)
        ]
        greeted = greeted + [target for _, target, _ in line]
    greet(greeted)
    sent = []

    def copy_of(item, source, target, number, device):
        return remote(source, target, send_sem.at[item, number], recv_sem.at[item, number], device)

    def send(item, source, target, number, device):
        copy = copy_of(item, source, target, number, device)
        copy.start()
        sent.append(copy)

    def arrived(item, target, number):
        copy_of(item, target, target, number, me).wait_recv()

    def keep(item, source, target):
        copy = pltpu.make_async_copy(source, target, own_sem.at[item])
        copy.start()
        return copy

    def block(item, place):
        kind, out = plan[item], outs[item]
        if kind == "widen":
            columns = out.shape[1] // GROUP
            return out.at[:, pl.ds(pl.multiple_of(place * columns, columns), columns)]
        if kind in ("gather", "around"):
            return out.at[:, place]
        return out.at[place]

    def landing(item, place, number):
        return block(item, AROUND[number] if plan[item] == "around" else place)

    def piece(item, place):
        if plan[item] == "narrow":
            columns = ins[item].shape[1] // GROUP
            return ins[item].at[:, pl.ds(pl.multiple_of(place * columns, columns), columns)]
        return ins[item].at[place]

    own = []
    for item, kind in enumerate(plan):
        if kind == "all":
            keep(item, ins[item], outs[item].at[group, slot]).wait()
            for number, target, _ in line:
                send(item, ins[item], outs[item].at[group, slot], GROUP - 1 + number, target)
        elif kind in ("gather", "around"):
            for number, step in enumerate((first_step, second_step, step_core)):
                send(item, ins[item], landing(item, slot, number), number, me + step)
            own.append(keep(item, ins[item], block(item, 0 if kind == "around" else slot)))
    for item, kind in enumerate(plan):
        if kind in ("swap", "widen", "narrow"):
            for number, step in others:
                send(item, piece(item, slot + step), block(item, slot), number - 1, me + step)
            own.append(keep(item, piece(item, slot), block(item, slot)))
    for item, kind in enumerate(plan):
        if kind == "all":
            for number, _, sender in line:
                arrived(item, outs[item].at[sender, slot], GROUP - 1 + number)
            for number, step in others:
                send(item, outs[item].at[:, slot], outs[item].at[:, slot], number - 1, me + step)
    corner_step = first_step + second_step
    for item, kind in enumerate(plan):
        if kind in ("gather", "around"):
            for place, number, onward in (
                (slot + first_step, 0, ((3, second_step), (4, step_core))),
                (slot + second_step, 1, ((5, step_core),)),
                (slot + corner_step, 3, ((6, step_core),)),
            ):
                here = landing(item, place, number)
                arrived(item, here, number)
                for then, step in onward:
                    send(item, here, landing(item, place, then), then, me + step)
    for item, kind in enumerate(plan):
        if kind in ("gather", "around"):
            for step, number in ((0, 2), (second_step, 4), (first_step, 5), (corner_step, 6)):
                arrived(item, landing(item, slot + step_core + step, number), number)
        elif kind == "all":
            for number, step in others:
                arrived(item, outs[item].at[:, slot + step], number - 1)
        else:
            for number, step in others:
                arrived(item, block(item, slot + step), number - 1)
    for copy in sent:
        copy.wait_send()
    for copy in own:
        copy.wait()


def exchange(number, micros, *items):
    groups = lax.axis_size("fsdp") // GROUP
    kinds = [kind for kind, _ in items]
    arrays = [array for _, array in items]
    shapes = []
    for kind, array in items:
        if kind in ("gather", "around"):
            shape = (array.shape[0], GROUP) + array.shape[1:]
        elif kind == "swap":
            shape = array.shape
        elif kind == "widen":
            shape = (array.shape[1], GROUP * array.shape[2])
        elif kind == "narrow":
            shape = (GROUP, array.shape[0], array.shape[1] // GROUP)
        else:
            shape = (groups, GROUP) + array.shape
        shapes.append(jax.ShapeDtypeStruct(shape, array.dtype))
    numbers = GROUP - 1 + (groups if "all" in kinds else 0)
    return pl.pallas_call(
        functools.partial(exchange_kernel, kinds),
        out_shape=tuple(shapes),
        in_specs=[ANY] * len(items),
        out_specs=tuple([ANY] * len(items)),
        scratch_shapes=[
            pltpu.SemaphoreType.DMA((len(items), numbers)),
            pltpu.SemaphoreType.DMA((len(items), numbers)),
            pltpu.SemaphoreType.DMA((len(items),)),
        ],
        compiler_params=pltpu.CompilerParams(collective_id=number, has_side_effects=True),
        cost_estimate=cost(micros),
    )(*arrays)


def owners_kernel(pieces, in_ref, out_ref):
    columns = out_ref.shape[2] // pieces
    for piece in range(pieces):
        for owner in range(GROUP):
            lo = (piece * GROUP + owner) * columns
            out_ref[owner, :, piece * columns : (piece + 1) * columns] = in_ref[:, lo : lo + columns]


def by_owner(weight, pieces):
    rows, columns = weight.shape
    return pl.pallas_call(
        functools.partial(owners_kernel, pieces),
        out_shape=jax.ShapeDtypeStruct((GROUP, rows, columns // GROUP), weight.dtype),
        in_specs=[VMEM],
        out_specs=VMEM,
        compiler_params=pltpu.CompilerParams(vmem_limit_bytes=32 * 2**20),
        cost_estimate=cost(3),
    )(weight)


def dealt_columns_kernel(piece, in_ref, out_ref):
    for owner in range(GROUP):
        for part in range(out_ref.shape[2] // piece):
            lo = (part * GROUP + owner) * piece
            out_ref[owner, :, part * piece : (part + 1) * piece] = in_ref[:, lo : lo + piece]


def dealt_columns(x, piece):
    rows, columns = x.shape
    return pl.pallas_call(
        functools.partial(dealt_columns_kernel, piece),
        out_shape=jax.ShapeDtypeStruct((GROUP, rows, columns // GROUP), x.dtype),
        in_specs=[VMEM],
        out_specs=VMEM,
        compiler_params=pltpu.CompilerParams(vmem_limit_bytes=32 * 2**20),
        cost_estimate=cost(2),
    )(x)


def home_kernel(pieces, got_ref, weight_ref, out_ref, gain_ref, more_ref):
    columns = weight_ref.shape[1] // GROUP // pieces
    more_ref[...] = jnp.zeros_like(more_ref)
    for sender in range(GROUP):
        for piece in range(pieces):
            lo = (piece * GROUP + sender) * columns
            out_ref[:, lo : lo + columns] = got_ref[
                sender, :, piece * columns : (piece + 1) * columns
            ].astype(f32)
        if got_ref.shape[2] > pieces * columns:
            more_ref[...] += got_ref[sender, :, pieces * columns :].astype(f32)
    gain_ref[...] = jnp.sum(out_ref[...] * weight_ref[...].astype(f32), axis=1, keepdims=True)


def home(got, weight, pieces):
    rows, columns = weight.shape
    return pl.pallas_call(
        functools.partial(home_kernel, pieces),
        out_shape=(
            jax.ShapeDtypeStruct((rows, columns), f32),
            jax.ShapeDtypeStruct((rows, 1), f32),
            jax.ShapeDtypeStruct((rows, 128), f32),
        ),
        in_specs=[VMEM, VMEM],
        out_specs=(VMEM, VMEM, VMEM),
        compiler_params=pltpu.CompilerParams(vmem_limit_bytes=32 * 2**20),
        cost_estimate=cost(5),
    )(got, weight)


TILE = 1024


def product_scatter_kernel(swaps, around, a_far, w_far, *refs):
    swap_refs, out_ref, swapped_refs = refs[:swaps], refs[swaps], refs[swaps + 1 : 2 * swaps + 1]
    near, far, away, going, send_sem, recv_sem, a_ref, w_ref, a_sem, w_sem = refs[
        2 * swaps + 1 : 2 * swaps + 11
    ]
    me, slot, step_core, first_step, second_step = places()
    first, second, mate = me + first_step, me + second_step, me + step_core
    core = lax.rem(slot, 2)
    others = plane_steps(
        step_core,
        (1 - core) * first_step + core * second_step,
        core * first_step + (1 - core) * second_step,
    )
    corner_step = first_step + second_step
    if around:
        own_places, mate_places = (3, 1, 2, 0), (7, 5, 6, 4)
    else:
        own_places = (slot + corner_step, slot + first_step, slot + second_step, slot)
        mate_slot = slot + step_core
        mate_places = (
            mate_slot + corner_step,
            mate_slot + second_step,
            mate_slot + first_step,
            mate_slot,
        )

    def a_load(place):
        return pltpu.make_async_copy(a_far.at[place], a_ref.at[place], a_sem.at[place])

    def w_load(i):
        at = pl.ds(i * TILE, TILE)
        return pltpu.make_async_copy(w_far.at[at, :], w_ref.at[at, :], w_sem.at[i])

    a_load(mate_places[0]).start()
    for i in range(out_ref.shape[1] // TILE):
        w_load(i).start()
    for place in (
        mate_places[2],
        own_places[0],
        own_places[2],
        mate_places[1],
        mate_places[3],
        own_places[3],
        own_places[1],
    ):
        a_load(place).start()
    greet([me + step for _, step in others] if swaps else (first, second, mate))
    sent = []

    def send(source, target, number, device):
        copy = remote(source, target, send_sem.at[number], recv_sem.at[number], device)
        copy.start()
        sent.append(copy)

    def arrived(ref, number, source):
        remote(ref, ref, send_sem.at[number], recv_sem.at[number], source).wait_recv()

    def product(place, extra, target):
        a_load(place).wait()

        def tile(i, _):
            at = pl.ds(pl.multiple_of(i * TILE, TILE), TILE)
            total = dot_nt(a_ref[place], w_ref[at, :])
            for ref in extra:
                total = total + ref[:, at].astype(f32)
            target[:, at] = total.astype(target.dtype)
            return 0

        lax.fori_loop(0, out_ref.shape[1] // TILE, tile, 0)

    def to_mate(kind):
        product(mate_places[kind], (), away.at[kind])
        send(away.at[kind], near.at[kind], kind, mate)

    def add(ref):
        def tile(i, _):
            at = pl.ds(pl.multiple_of(i * TILE, TILE), TILE)
            out_ref[:, at] = out_ref[:, at] + ref[:, at].astype(f32)
            return 0

        lax.fori_loop(0, out_ref.shape[1] // TILE, tile, 0)

    swapping, kept = [], []
    if swaps:
        swap_send, swap_recv, swap_own = refs[2 * swaps + 11 :]

    def start_swaps():
        for item in range(swaps):
            for number, step in others:
                copy = remote(
                    swap_refs[item].at[slot + step],
                    swapped_refs[item].at[slot],
                    swap_send.at[item, number - 1],
                    swap_recv.at[item, number - 1],
                    me + step,
                )
                copy.start()
                swapping.append(copy)
            copy = pltpu.make_async_copy(
                swap_refs[item].at[slot], swapped_refs[item].at[slot], swap_own.at[item]
            )
            copy.start()
            kept.append(copy)

    for i in range(out_ref.shape[1] // TILE):
        w_load(i).wait()
    to_mate(0)
    to_mate(2)
    arrived(near.at[0], 0, mate)
    product(own_places[0], (near.at[0],), going.at[0])
    send(going.at[0], far.at[0], 4, second)
    arrived(near.at[2], 2, mate)
    product(own_places[2], (near.at[2],), going.at[2])
    send(going.at[2], far.at[2], 5, second)
    start_swaps()
    to_mate(1)
    to_mate(3)
    arrived(near.at[3], 3, mate)
    product(own_places[3], (near.at[3],), out_ref)
    arrived(near.at[1], 1, mate)
    arrived(far.at[0], 4, second)
    product(own_places[1], (near.at[1], far.at[0]), going.at[1])
    send(going.at[1], far.at[1], 6, first)
    arrived(far.at[2], 5, second)
    add(far.at[2])
    arrived(far.at[1], 6, first)
    add(far.at[1])
    for item in range(swaps):
        for number, step in others:
            target = swapped_refs[item].at[slot + step]
            remote(
                target,
                target,
                swap_send.at[item, number - 1],
                swap_recv.at[item, number - 1],
                me + step,
            ).wait_recv()
    for copy in sent + swapping:
        copy.wait_send()
    for copy in kept:
        copy.wait()


def product_scatter(a, w, number, around, *swaps):
    _, rows, depth = a.shape
    columns = w.shape[0]
    count = len(swaps)
    swap_sems = [
        pltpu.SemaphoreType.DMA((count, GROUP - 1)),
        pltpu.SemaphoreType.DMA((count, GROUP - 1)),
        pltpu.SemaphoreType.DMA((count,)),
    ]
    return pl.pallas_call(
        functools.partial(product_scatter_kernel, count, around),
        out_shape=(jax.ShapeDtypeStruct((rows, columns), f32),)
        + tuple(jax.ShapeDtypeStruct(x.shape, x.dtype) for x in swaps),
        in_specs=[ANY, ANY] + [ANY] * count,
        out_specs=(VMEM,) + (ANY,) * count,
        scratch_shapes=[
            pltpu.VMEM((4, rows, columns), bf16),
            pltpu.VMEM((3, rows, columns), bf16),
            pltpu.VMEM((4, rows, columns), bf16),
            pltpu.VMEM((3, rows, columns), bf16),
            pltpu.SemaphoreType.DMA((7,)),
            pltpu.SemaphoreType.DMA((7,)),
            pltpu.VMEM(a.shape, bf16),
            pltpu.VMEM(w.shape, bf16),
            pltpu.SemaphoreType.DMA((GROUP,)),
            pltpu.SemaphoreType.DMA((columns // TILE,)),
        ]
        + (swap_sems if swaps else []),
        compiler_params=pltpu.CompilerParams(
            collective_id=number, has_side_effects=True, vmem_limit_bytes=56 * 2**20
        ),
        cost_estimate=cost(50),
    )(a, w, *swaps)


def gate_gather_kernel(
    own_ref,
    x_far,
    w_far,
    all_ref,
    gate_far,
    up_far,
    hidden_far,
    x_ref,
    w_ref,
    gate_ref,
    up_ref,
    hidden_ref,
    send_sem,
    recv_sem,
    own_sem,
    x_sem,
    w_sem,
    store_sem,
):
    me, slot, step_core, first_step, second_step = places()
    first, second, mate = me + first_step, me + second_step, me + step_core
    w_load = pltpu.make_async_copy(w_far, w_ref, w_sem)
    w_load.start()
    tiles, tile_rows = x_ref.shape[:2]
    half = gate_ref.shape[2]

    def rows_of(i):
        return pl.ds(pl.multiple_of(i * tile_rows, tile_rows), tile_rows)

    def x_load(i):
        return pltpu.make_async_copy(x_far.at[rows_of(i), :], x_ref.at[i], x_sem.at[i])

    for i in range(tiles):
        x_load(i).start()
    greet((first, second, mate))
    sent = []

    def send(source, number, device):
        copy = remote(
            source, all_ref.at[AROUND[number]], send_sem.at[number], recv_sem.at[number], device
        )
        copy.start()
        sent.append(copy)

    def arrived(number):
        target = all_ref.at[AROUND[number]]
        remote(target, target, send_sem.at[number], recv_sem.at[number], me).wait_recv()
        return target

    own = pltpu.make_async_copy(own_ref, all_ref.at[0], own_sem)
    send(own_ref, 0, first)
    send(own_ref, 1, second)
    send(own_ref, 2, mate)
    own.start()

    def stores(i, spot):
        return [
            pltpu.make_async_copy(near.at[spot], far.at[rows_of(i), :], store_sem.at[spot, number])
            for number, (near, far) in enumerate(
                ((gate_ref, gate_far), (up_ref, up_far), (hidden_ref, hidden_far))
            )
        ]

    def tile(i, _):
        spot = lax.rem(i, 2)
        x_load(i).wait()

        @pl.when(i >= 2)
        def _():
            for copy in stores(i - 2, spot):
                copy.wait()

        both = dot_nn(x_ref[i], w_ref[...])
        gate = both[:, :half]
        up = both[:, half:]
        gate_ref[spot] = gate
        up_ref[spot] = up
        hidden_ref[spot] = (gate * jax.nn.sigmoid(gate) * up).astype(bf16)
        for copy in stores(i, spot):
            copy.start()
        return 0

    w_load.wait()
    lax.fori_loop(0, tiles // 2, tile, 0)
    block = arrived(0)
    send(block, 3, second)
    send(block, 4, mate)
    send(arrived(1), 5, mate)
    lax.fori_loop(tiles // 2, tiles, tile, 0)
    for i in (tiles - 2, tiles - 1):
        for copy in stores(i, i % 2):
            copy.wait()
    send(arrived(3), 6, mate)
    for number in (2, 4, 5, 6):
        arrived(number)
    for copy in sent:
        copy.wait_send()
    own.wait()


def gate_gather(own, x, w, number):
    rows, columns = own.shape
    half = w.shape[1] // 2
    tiles = x.shape[0] // rows
    wide = jax.ShapeDtypeStruct((x.shape[0], half), f32)
    return pl.pallas_call(
        gate_gather_kernel,
        out_shape=(
            jax.ShapeDtypeStruct((GROUP, rows, columns), own.dtype),
            wide,
            wide,
            jax.ShapeDtypeStruct((x.shape[0], half), bf16),
        ),
        in_specs=[ANY, ANY, ANY],
        out_specs=(ANY, ANY, ANY, ANY),
        scratch_shapes=[
            pltpu.VMEM((tiles, rows, x.shape[1]), bf16),
            pltpu.VMEM(w.shape, bf16),
            pltpu.VMEM((2, rows, half), f32),
            pltpu.VMEM((2, rows, half), f32),
            pltpu.VMEM((2, rows, half), bf16),
            pltpu.SemaphoreType.DMA((7,)),
            pltpu.SemaphoreType.DMA((7,)),
            pltpu.SemaphoreType.DMA,
            pltpu.SemaphoreType.DMA((tiles,)),
            pltpu.SemaphoreType.DMA,
            pltpu.SemaphoreType.DMA((2, 3)),
        ],
        compiler_params=pltpu.CompilerParams(
            collective_id=number, has_side_effects=True, vmem_limit_bytes=56 * 2**20
        ),
        cost_estimate=cost(45),
    )(own, x, w)


def hidden_back_kernel(cot_ref, gate_ref, up_ref, w_ref, grad_ref):
    half = gate_ref.shape[1]
    d_hidden = dot_nn(cot_ref[...], w_ref[...])
    gate = gate_ref[...]
    sigmoid = jax.nn.sigmoid(gate)
    grad_ref[:, :half] = (
        d_hidden * up_ref[...] * sigmoid * (1.0 + gate * (1.0 - sigmoid))
    ).astype(bf16)
    grad_ref[:, half:] = (d_hidden * gate * sigmoid).astype(bf16)


def hidden_back(cot, gate, up, w):
    rows, columns = cot.shape
    half = w.shape[1]
    tile_rows = 256

    def tiles(width):
        return pl.BlockSpec((tile_rows, width), lambda i: (i, 0))

    return pl.pallas_call(
        hidden_back_kernel,
        grid=(rows // tile_rows,),
        in_specs=[
            tiles(columns),
            tiles(half),
            tiles(half),
            pl.BlockSpec(w.shape, lambda i: (0, 0)),
        ],
        out_specs=tiles(2 * half),
        out_shape=jax.ShapeDtypeStruct((rows, 2 * half), bf16),
        compiler_params=pltpu.CompilerParams(vmem_limit_bytes=56 * 2**20),
        cost_estimate=cost(20),
    )(cot, gate, up, w)


def away_product_kernel(x_ref, w_ref, out_ref):
    out_ref[...] = dot_nt(x_ref[...], w_ref[...]).astype(bf16)


def away_product(x, w, tile_rows):
    rows, depth = x.shape
    tiles = rows // tile_rows // 2
    return pl.pallas_call(
        away_product_kernel,
        grid=(tiles,),
        in_specs=[
            pl.BlockSpec((tile_rows, depth), lambda i: (tiles + i, 0)),
            pl.BlockSpec(w.shape, lambda i: (0, 0)),
        ],
        out_specs=pl.BlockSpec((tile_rows, w.shape[0]), lambda i: (i, 0)),
        out_shape=jax.ShapeDtypeStruct((rows // 2, w.shape[0]), bf16),
        compiler_params=pltpu.CompilerParams(vmem_limit_bytes=56 * 2**20),
        cost_estimate=cost(6),
    )(x, w)


def rows_product_kernel(x_ref, y_ref, *refs):
    out_ref = refs[-1]
    wide = y_ref.shape[1]
    out_ref[:, :wide] = dot_tn(x_ref[...], y_ref[...]).astype(bf16)
    for more_ref in refs[:-1]:
        out_ref[:, wide:] = more_ref[...]


def rows_product(x, y, micros, *more):
    rows, columns = x.shape
    wide = y.shape[1]
    tile_columns = 512
    more_wide = sum(m.shape[1] for m in more)
    return pl.pallas_call(
        rows_product_kernel,
        grid=(columns // tile_columns,),
        in_specs=[
            pl.BlockSpec((rows, tile_columns), lambda i: (0, i)),
            pl.BlockSpec((rows, wide), lambda i: (0, 0)),
        ]
        + [pl.BlockSpec((tile_columns, m.shape[1]), lambda i: (i, 0)) for m in more],
        out_specs=pl.BlockSpec((tile_columns, wide + more_wide), lambda i: (i, 0)),
        out_shape=jax.ShapeDtypeStruct((columns, wide + more_wide), bf16),
        compiler_params=pltpu.CompilerParams(vmem_limit_bytes=56 * 2**20),
        cost_estimate=cost(micros),
    )(x, y, *more)


def plane_permutes(device_count):
    first, second, mate = [], [], []
    for i in range(device_count):
        low_bit, high_bit = (2, 4) if i % 2 == 0 else (4, 2)
        first.append((i, i ^ low_bit))
        second.append((i, i ^ high_bit))
        mate.append((i, i ^ 1))
    return first, second, mate


def after(values, *earlier):
    return lax.optimization_barrier((values, earlier))[0]


def meet(*values):
    return lax.optimization_barrier(values)


def assemble_kernel(*refs):
    blocks, out_ref = refs[:GROUP], refs[GROUP]
    _, slot, step_core, first_step, second_step = places()
    corner_step = first_step + second_step
    here = (0, first_step, second_step, corner_step)
    there = (step_core, step_core + second_step, step_core + first_step, step_core + corner_step)
    for number, step in enumerate(here + there):
        out_ref[:, slot + step] = blocks[number][...]


def assemble(x, from_first, from_second, from_corner, mates):
    parts, rows, columns = x.shape
    return pl.pallas_call(
        assemble_kernel,
        out_shape=jax.ShapeDtypeStruct((parts, GROUP, rows, columns), x.dtype),
        in_specs=[VMEM] * GROUP,
        out_specs=VMEM,
        compiler_params=pltpu.CompilerParams(vmem_limit_bytes=32 * 2**20),
        cost_estimate=cost(8),
    )(x, from_first, from_second, from_corner, *mates)


class SlowScatter:
    def __init__(self, keep, away, device_count):
        self.keep = keep
        self.away = away
        self.first, self.second, self.mate = plane_permutes(device_count)

    def to_mate(self):
        return lax.ppermute(self.away, "fsdp", self.mate)

    def onward(self, near):
        return (self.keep(2, 2) + near[2:].astype(f32)).astype(bf16)

    def to_second(self, sums):
        return lax.ppermute(sums, "fsdp", self.second)

    def both(self, near, far):
        return (self.keep(1, 1)[0] + near[1].astype(f32) + far[1].astype(f32)).astype(bf16)

    def to_first(self, both):
        return lax.ppermute(both, "fsdp", self.first)

    def total(self, near, far, last):
        own = self.keep(0, 1)[0] + near[0].astype(f32)
        return own + far[0].astype(f32) + last.astype(f32)


def low(values):
    return values.astype(bf16).astype(f32)


def gates(proj_ref, floor_ref, rows, head, heads):
    dim = floor_ref.shape[1] // heads
    wide = heads * dim
    lo = head * dim
    q_pre = proj_ref[rows, lo : lo + dim]
    f_pre = proj_ref[rows, wide + lo : wide + lo + dim]
    value = proj_ref[rows, 2 * wide + lo : 2 * wide + lo + dim].astype(bf16)
    floor = floor_ref[:, lo : lo + dim]
    q_sigmoid = jax.nn.sigmoid(q_pre)
    query = low(q_pre * q_sigmoid)
    f_sigmoid = jax.nn.sigmoid(f_pre)
    forget = floor + (1.0 - floor) * f_sigmoid
    key = low(1.0 - forget)
    row = lax.broadcasted_iota(jnp.int32, (CHUNK, dim), 0)
    in_half = lax.rem(row, HALF)
    product = forget
    step = 1
    while step < HALF:
        product = jnp.where(in_half >= step, product * pltpu.roll(product, step, 0), product)
        step *= 2
    middle = product[HALF - 1 : HALF, :]
    end = product[CHUNK - 1 : CHUNK, :]
    ratio = jnp.where(row < HALF, product / middle, product)
    inverse = 1.0 / ratio
    return {
        "q_pre": q_pre,
        "q_sigmoid": q_sigmoid,
        "f_sigmoid": f_sigmoid,
        "forget": forget,
        "value": value,
        "floor": floor,
        "middle": middle,
        "end": end,
        "ratio": ratio,
        "inverse": inverse,
        "row": row,
        "query_mid": query * ratio,
        "key_mid": key * inverse,
    }


def whole_fade(g, last):
    return g["middle"] * g["end"] * jnp.where(last < 0, 1.0, 0.0)


def tail_keys(g, last):
    return jnp.where(g["row"] >= last, g["key_mid"] * g["end"], 0.0).astype(bf16)


def entry_queries(g, carried):
    return jnp.where(carried, g["query_mid"] * g["middle"], 0.0).astype(bf16)


def next_state(g, last, state):
    return state * whole_fade(g, last) + dot_tn(g["value"], tail_keys(g, last))


def forward_kernel(
    heads, last_ref, proj_ref, start_ref, floor_ref, gain_ref, in_ref, mix_ref, out_ref, enter_ref, state
):
    dim = floor_ref.shape[1] // heads
    chunks = proj_ref.shape[0] // CHUNK
    tile = pl.program_id(0)

    @pl.when(tile == 0)
    def _():
        state[...] = in_ref[...]

    def step(n, _):
        base = pl.multiple_of(n * CHUNK, CHUNK)
        rows = pl.ds(base, CHUNK)
        place = (tile * chunks + n) * CHUNK
        starts = start_ref[rows, :] - place
        last = last_ref[tile * chunks + n] - place
        column = lax.broadcasted_iota(jnp.int32, (CHUNK, CHUNK), 1)
        line = lax.broadcasted_iota(jnp.int32, (CHUNK, CHUNK), 0)
        within = (column <= line) & (column >= starts)
        carried = starts < 0
        for head in range(heads):
            lo = head * dim
            g = gates(proj_ref, floor_ref, rows, head, heads)
            now = state[head]
            enter_ref[n, head] = now
            scores = dot_nt(g["query_mid"].astype(bf16), g["key_mid"].astype(bf16))
            scores = jnp.where(within, scores, 0.0).astype(bf16)
            out = dot_nn(scores, g["value"]) + dot_nt(entry_queries(g, carried), now.astype(bf16))
            state[head] = next_state(g, last, now)
            out_ref[rows, lo : lo + dim] = out
            mix_ref[rows, lo : lo + dim] = (
                out * inverse_rms(out) * gain_ref[:, lo : lo + dim]
            ).astype(bf16)
        return 0

    lax.fori_loop(0, chunks, step, 0, unroll=UNROLL)


def last_state_kernel(heads, last_ref, proj_ref, floor_ref, out_ref):
    for head in range(heads):
        state = jnp.zeros(out_ref.shape[1:], f32)
        for n in range(proj_ref.shape[0] // CHUNK):
            g = gates(proj_ref, floor_ref, pl.ds(n * CHUNK, CHUNK), head, heads)
            state = next_state(g, last_ref[n] - n * CHUNK, state)
        out_ref[head] = state


def state_grad(out_ref, dmix_ref, gain_ref, rows, lo, dim):
    out = out_ref[rows, lo : lo + dim]
    inverse = inverse_rms(out)
    scaled = out * inverse
    dmix = dmix_ref[rows, lo : lo + dim].astype(f32)
    return rms_back(dmix * gain_ref[:, lo : lo + dim], scaled, inverse)


def backward_chunk(heads, n, at, refs, outs, later, before=0):
    last_ref, proj_ref, start_ref, floor_ref, gain_ref, out_ref, dmix_ref, enter_ref = refs
    dproj_ref, dfloor_ref = outs
    dim = floor_ref.shape[1] // heads
    wide = heads * dim
    base = n * CHUNK
    rows = pl.ds(base, CHUNK)
    place = (before + n) * CHUNK
    starts = start_ref[rows, :] - place
    last = last_ref[before + n] - place
    column = lax.broadcasted_iota(jnp.int32, (CHUNK, CHUNK), 1)
    line = lax.broadcasted_iota(jnp.int32, (CHUNK, CHUNK), 0)
    within = (column <= line) & (column >= starts)
    carried = starts < 0
    for head in range(heads):
        lo = head * dim
        g = gates(proj_ref, floor_ref, rows, head, heads)
        grad = state_grad(out_ref, dmix_ref, gain_ref, rows, lo, dim)
        grad_hi = grad.astype(bf16)
        grad_lo = (grad - grad_hi.astype(f32)).astype(bf16)
        state = enter_ref[n, head]
        after = later[head]
        after_low = after.astype(bf16)
        query_mid = g["query_mid"].astype(bf16)
        key_mid = g["key_mid"].astype(bf16)
        scores = jnp.where(within, dot_nt(query_mid, key_mid), 0.0).astype(bf16)
        d_scores = dot_nt(grad_hi, g["value"]) + dot_nt(grad_lo, g["value"])
        d_scores = jnp.where(within, d_scores, 0.0).astype(bf16)
        query_in = entry_queries(g, carried)
        key_out = tail_keys(g, last)
        d_query_mid = dot_nn(d_scores, key_mid)
        d_query_in = jnp.where(carried, dot_nn(grad_hi, state.astype(bf16)), 0.0)
        d_key_mid = dot_tn(d_scores, query_mid)
        d_key_out = jnp.where(g["row"] >= last, dot_nn(g["value"], after_low), 0.0)
        d_value = dot_tn(scores, grad_hi) + dot_nt(key_out, after_low)
        d_query = (d_query_mid + d_query_in * g["middle"]) * g["ratio"]
        d_key = (d_key_mid + d_key_out * g["end"]) * g["inverse"]
        tail = d_key_out * key_out.astype(f32)
        term = (
            d_query_mid * query_mid.astype(f32)
            + d_query_in * query_in.astype(f32)
            - d_key_mid * key_mid.astype(f32)
            - tail
        )
        fade = whole_fade(g, last)
        final = jnp.sum(tail, axis=0, keepdims=True) + fade * jnp.sum(
            state * after, axis=0, keepdims=True
        )
        step_rows = 1
        while step_rows < CHUNK:
            term = jnp.where(
                g["row"] < CHUNK - step_rows,
                term + pltpu.roll(term, CHUNK - step_rows, 0),
                term,
            )
            step_rows *= 2
        d_forget = (term + final) / g["forget"] - d_key
        q_sigmoid, f_sigmoid = g["q_sigmoid"], g["f_sigmoid"]
        d_q_pre = d_query * q_sigmoid * (1.0 + g["q_pre"] * (1.0 - q_sigmoid))
        d_floor = d_forget * (1.0 - f_sigmoid)
        d_f_pre = d_floor * (1.0 - g["floor"]) * f_sigmoid
        dproj_ref[at, lo : lo + dim] = d_q_pre.astype(bf16)
        dproj_ref[at, wide + lo : wide + lo + dim] = d_f_pre.astype(bf16)
        dproj_ref[at, 2 * wide + lo : 2 * wide + lo + dim] = d_value.astype(bf16)
        dfloor_ref[:, lo : lo + dim] += jnp.sum(d_floor, axis=0, keepdims=True)
        later[head] = after * fade + dot_tn(grad_hi, query_in)


def backward_rest(heads, n, refs, later, before=0):
    last_ref, proj_ref, start_ref, floor_ref, gain_ref, out_ref, dmix_ref = refs
    dim = floor_ref.shape[1] // heads
    rows = pl.ds(n * CHUNK, CHUNK)
    for head in range(heads):
        g = gates(proj_ref, floor_ref, rows, head, heads)
        grad = state_grad(out_ref, dmix_ref, gain_ref, rows, head * dim, dim)
        place = (before + n) * CHUNK
        queries = entry_queries(g, start_ref[rows, :] < place)
        fade = whole_fade(g, last_ref[before + n] - place)
        later[head] = later[head] * fade + dot_tn(grad.astype(bf16), queries)


def backward_kernel(heads, *refs):
    ins, outs, later = refs[:8], refs[8:10], refs[10]
    chunks = ins[1].shape[0] // CHUNK
    edge = MAXLEN // CHUNK
    tile = pl.num_programs(0) - 1 - pl.program_id(0)
    before = tile * chunks

    def step(i, first):
        n = first - i
        at = pl.ds(pl.multiple_of(n * CHUNK, CHUNK), CHUNK)
        backward_chunk(heads, n, at, ins, outs, later, before)
        return first

    @pl.when(pl.program_id(0) == 0)
    def _():
        later[...] = jnp.zeros_like(later)
        outs[1][...] = jnp.zeros_like(outs[1])
        for n in range(chunks - 1, chunks - 1 - edge, -1):
            backward_rest(heads, n, ins[:7], later, before)
        lax.fori_loop(0, chunks - edge, step, chunks - 1 - edge, unroll=UNROLL)

    @pl.when(pl.program_id(0) != 0)
    def _():
        lax.fori_loop(0, chunks, step, chunks - 1, unroll=UNROLL)


def backward_edge_kernel(heads, *refs):
    ins, in_ref, _, outs, later = refs[:8], refs[8], refs[9], refs[10:12], refs[12]
    later[...] = in_ref[...]
    outs[1][...] = jnp.zeros_like(outs[1])
    edge = MAXLEN // CHUNK
    before = ins[0].shape[0] - edge
    for n in range(edge - 1, -1, -1):
        backward_chunk(heads, n, pl.ds(n * CHUNK, CHUNK), ins, outs, later, before)


def first_grad_kernel(heads, *refs):
    ins, grad_ref = refs[:7], refs[7]
    grad_ref[...] = jnp.zeros_like(grad_ref)
    for n in range(ins[1].shape[0] // CHUNK - 1, -1, -1):
        backward_rest(heads, n, ins, grad_ref)


def local_call(kernel, heads, micros, out_shape, scratch, *operands):
    return pl.pallas_call(
        functools.partial(kernel, heads),
        out_shape=out_shape,
        in_specs=[SMEM] + [VMEM] * (len(operands) - 1),
        out_specs=jax.tree.map(lambda _: VMEM, out_shape),
        scratch_shapes=scratch,
        compiler_params=pltpu.CompilerParams(vmem_limit_bytes=56 * 2**20),
        cost_estimate=cost(micros),
    )(*operands)


def body(
    tokens,
    cotangent,
    dealt_lengths,
    deal,
    norm_gain,
    mixer_in,
    forget_floor,
    group_gain,
    out_proj,
    ffn_gain,
    gate_up,
    down_proj,
):
    row_count, width = tokens.shape
    weight_rows = mixer_in.shape[0]
    device_count = lax.axis_size("fsdp")
    groups = device_count // GROUP
    own_index = lax.axis_index("fsdp")
    slot = lax.rem(own_index, GROUP)
    group = own_index // GROUP
    group_rows = GROUP * row_count
    heads = HEADS // GROUP
    own_width = width // GROUP
    dim = width // HEADS
    ffn_width = down_proj.shape[1]
    own_ffn = ffn_width // GROUP
    planes = [[g * GROUP + s for s in range(GROUP)] for g in range(groups)]
    lines = [[g * GROUP + s for g in range(groups)] for s in range(GROUP)]

    def line_gather(x):
        return lax.all_gather(x, "fsdp", axis=0, axis_index_groups=lines, tiled=True)

    def line_scatter(x):
        return lax.psum_scatter(
            x, "fsdp", scatter_dimension=0, axis_index_groups=lines, tiled=True
        )

    def whole_rows(x):
        return line_gather(x.reshape(GROUP * weight_rows, -1))

    low_step = 2 - 4 * (slot // 2 % 2)
    high_step = 4 - 8 * (slot // 4)
    odd = slot % 2
    moves = (
        slot,
        1 - 2 * odd,
        jnp.where(odd == 0, low_step, high_step),
        jnp.where(odd == 0, high_step, low_step),
    )

    seq_count = deal.shape[0]
    seq_ids = jnp.arange(seq_count, dtype=jnp.int32)
    matches = deal[:, None] == seq_ids[None, :]
    lengths = jnp.sum(jnp.where(matches, dealt_lengths[:, None], 0), axis=0)
    seq_starts = jnp.sum(
        jnp.where(seq_ids[:, None] < seq_ids[None, :], lengths[:, None], 0), axis=0
    )
    group_start = group * group_rows
    rows_here = group_start + jnp.arange(group_rows, dtype=jnp.int32)
    starts = (
        jnp.max(jnp.where(seq_starts[None, :] <= rows_here[:, None], seq_starts[None, :], 0), axis=1)
        - group_start
    )
    start_column = starts[:, None]
    last_starts = starts[CHUNK - 1 :: CHUNK]

    out_lines = lax.all_gather(out_proj, "fsdp", axis=0, axis_index_groups=lines)
    gain_block = jnp.zeros((16, 128), bf16)
    for number, gain in enumerate((norm_gain, forget_floor, group_gain, ffn_gain)):
        gain_block = gain_block.at[number, :weight_rows].set(gain)
    gain_blocks, mixer_swapped = exchange(
        0, 15, ("all", gain_block), ("swap", by_owner(mixer_in, 3))
    )
    mixer_weight = whole_rows(mixer_swapped)
    gains = (
        gain_blocks[:, :, :4, :weight_rows].transpose(2, 0, 1, 3).reshape(4, width).astype(f32)
    )
    first_gain = gains[0:1]
    second_gain = gains[3:4]
    own_gains = lax.dynamic_slice_in_dim(gains, slot * own_width, own_width, 1)
    own_floor = own_gains[1:2]
    own_group_gain = own_gains[2:3]

    inputs = tokens.astype(f32)
    first_inverse = inverse_rms(inputs)
    first_scaled = inputs * first_inverse
    first_normed = (first_scaled * first_gain).astype(bf16)
    late_gate_up, late_down = after((gate_up, down_proj), mixer_swapped)
    first_all, ffn_swapped, down_swapped = exchange(
        1,
        58,
        ("gather", first_normed[None]),
        ("swap", by_owner(late_gate_up, 2)),
        ("swap", by_owner(late_down, 1)),
    )
    first_all = first_all.reshape(group_rows, width)
    ffn_weight = whole_rows(ffn_swapped)
    first, second, mate = plane_permutes(device_count)
    out_own = after(out_lines, first_all)
    from_first = lax.ppermute(out_own, "fsdp", first)
    from_second = lax.ppermute(out_own, "fsdp", second)
    tail_projected = dot_nn(first_all[group_rows - MAXLEN :], mixer_weight)
    edge = MAXLEN // CHUNK
    state_type = jax.ShapeDtypeStruct((heads, dim, dim), f32)
    last_state = local_call(
        last_state_kernel,
        heads,
        3,
        state_type,
        [],
        last_starts[-edge:] - (group_rows - MAXLEN),
        tail_projected,
        own_floor,
    )
    up_line = [(i, i + GROUP) for i in range(device_count - GROUP)]
    down_line = [(i + GROUP, i) for i in range(device_count - GROUP)]
    entering_state = lax.ppermute(last_state, "fsdp", up_line)
    projected = dot_nn(after(first_all, last_state), mixer_weight)
    projected, entering_state, from_first, from_second = meet(
        projected, entering_state, from_first, from_second
    )
    from_corner = lax.ppermute(from_first, "fsdp", second)
    mates = [lax.ppermute(block, "fsdp", mate) for block in (out_own, from_first, from_second)]
    chunks = group_rows // CHUNK
    tile_count = group_rows // TILE_ROWS

    def row_tiles(columns, turned=False):
        return pl.BlockSpec(
            (TILE_ROWS, columns), lambda i: (tile_count - 1 - i if turned else i, 0)
        )

    def state_tiles(turned=False):
        return pl.BlockSpec(
            (TILE_ROWS // CHUNK, heads, dim, dim),
            lambda i: (tile_count - 1 - i if turned else i, 0, 0, 0),
        )

    state_scratch = pltpu.VMEM((heads, dim, dim), f32)
    mixed_heads, state_out, entering = pl.pallas_call(
        functools.partial(forward_kernel, heads),
        grid=(tile_count,),
        out_shape=(
            jax.ShapeDtypeStruct((group_rows, own_width), bf16),
            jax.ShapeDtypeStruct((group_rows, own_width), f32),
            jax.ShapeDtypeStruct((chunks, heads, dim, dim), f32),
        ),
        in_specs=[SMEM, row_tiles(3 * own_width), row_tiles(1), VMEM, VMEM, VMEM],
        out_specs=(row_tiles(own_width), row_tiles(own_width), state_tiles()),
        scratch_shapes=[state_scratch],
        compiler_params=pltpu.CompilerParams(vmem_limit_bytes=56 * 2**20),
        cost_estimate=cost(18),
    )(last_starts, projected, start_column, own_floor, own_group_gain, entering_state)
    mixed_heads, from_corner = meet(mixed_heads, from_corner)
    mates = mates + [lax.ppermute(from_corner, "fsdp", mate)]
    [mixer_input] = exchange(
        3, 15, ("widen", mixed_heads.reshape(GROUP, row_count, own_width))
    )
    mixer_input, mates = meet(mixer_input, mates)
    _, step_core, first_step, second_step = moves
    steps = (0, first_step, second_step, first_step + second_step)
    mate_steps = [step_core + steps[kind] for kind in (0, 2, 1, 3)]
    mixer_blocks = dealt_columns(mixer_input, weight_rows)
    mixer_around = [
        lax.dynamic_index_in_dim(mixer_blocks, slot + step, 0) for step in (*steps, *mate_steps)
    ]
    mixer_keep = jnp.concatenate(mixer_around[:4])
    mixer_away = jnp.concatenate(mixer_around[4:])
    out_weight = assemble(out_own, from_first, from_second, from_corner, mates).reshape(width, width)
    down_weight = whole_rows(after(down_swapped, mixed_heads))
    residual = inputs + dot_nn(mixer_input, out_weight)
    second_inverse = inverse_rms(residual)
    second_scaled = residual * second_inverse
    second_normed = (second_scaled * second_gain).astype(bf16)
    second_normed, mixer_keep, mixer_away = meet(second_normed, mixer_keep, mixer_away)
    [second_all] = exchange(2, 43, ("around", second_normed[None]))
    second_all = second_all.reshape(group_rows, width)
    cot_blocks, gate_part, up_part, hidden_act = gate_gather(
        cotangent, second_all, ffn_weight, 6
    )
    cot_all = cot_blocks.reshape(group_rows, width)
    down_grad = rows_product(cot_all, hidden_act, 11)
    down_summed = line_scatter(down_grad)
    hidden_act = after(hidden_act, down_grad)

    def ffn_blocks(begin, number):
        rows = hidden_act[begin * row_count : (begin + number) * row_count]
        return dot_nt(rows, down_weight).reshape(number, row_count, width)

    ffn_away = away_product(hidden_act, down_weight, row_count).reshape(4, row_count, width)
    ffn_sum = SlowScatter(ffn_blocks, ffn_away, device_count)
    ffn_near = ffn_sum.to_mate()
    d_gate_pre = hidden_back(after(cot_all, ffn_away), gate_part, up_part, down_weight)
    d_gate_pre, ffn_near = meet(d_gate_pre, ffn_near)
    ffn_sums = ffn_sum.onward(ffn_near)
    ffn_grad = rows_product(after(second_all, ffn_sums), d_gate_pre, 18)
    ffn_grad, ffn_far = meet(ffn_grad, ffn_sum.to_second(ffn_sums))
    ffn_both = ffn_sum.both(ffn_near, ffn_far)
    ffn_summed = line_scatter(ffn_grad)
    [d_second] = product_scatter(
        d_gate_pre.reshape(GROUP, row_count, -1), after(ffn_weight, ffn_grad, ffn_both), 4, True
    )
    d_second, ffn_last, down_summed = meet(d_second, ffn_sum.to_first(ffn_both), down_summed)

    d_residual = cotangent.astype(f32) + rms_back(
        d_second * second_gain, second_scaled, second_inverse
    )
    d_mix_out = d_residual.astype(bf16)

    def out_blocks(blocks):
        return lax.dot_general(
            blocks, d_mix_out, (((1,), (0,)), ((), ())), preferred_element_type=f32
        )

    out_away = out_blocks(mixer_away).astype(bf16)
    out_sum = SlowScatter(
        lambda begin, number: out_blocks(mixer_keep[begin : begin + number]), out_away, device_count
    )
    out_near = out_sum.to_mate()
    d_mixer_input = dot_nt(after(d_mix_out, out_away), out_weight).astype(bf16)
    [d_mixed_heads] = exchange(5, 15, ("narrow", d_mixer_input))
    d_mixed_heads, out_near = meet(d_mixed_heads.reshape(group_rows, own_width), out_near)
    operands = (projected, start_column, own_floor, own_group_gain, state_out, d_mixed_heads)

    def edge_specs(place):
        def rows(columns):
            return pl.BlockSpec((MAXLEN, columns), lambda i: (place, 0))

        return [rows(3 * own_width), rows(1), VMEM, VMEM, rows(own_width), rows(own_width)]

    first_grad = pl.pallas_call(
        functools.partial(first_grad_kernel, heads),
        grid=(1,),
        out_shape=state_type,
        in_specs=[SMEM] + edge_specs(0),
        out_specs=VMEM,
        compiler_params=pltpu.CompilerParams(vmem_limit_bytes=56 * 2**20),
        cost_estimate=cost(3),
    )(last_starts, *operands)
    entering_grad = lax.ppermute(first_grad, "fsdp", down_line)
    out_near = after(out_near, first_grad)
    out_far = out_sum.to_second(out_sum.onward(out_near))
    dproj_type = jax.ShapeDtypeStruct((group_rows, 3 * own_width), bf16)
    dfloor_type = jax.ShapeDtypeStruct((1, own_width), f32)
    d_projected, floor_most = pl.pallas_call(
        functools.partial(backward_kernel, heads),
        grid=(tile_count,),
        out_shape=(dproj_type, dfloor_type),
        in_specs=[
            SMEM,
            row_tiles(3 * own_width, True),
            row_tiles(1, True),
            VMEM,
            VMEM,
            row_tiles(own_width, True),
            row_tiles(own_width, True),
            state_tiles(True),
        ],
        out_specs=(row_tiles(3 * own_width, True), VMEM),
        scratch_shapes=[state_scratch],
        compiler_params=pltpu.CompilerParams(vmem_limit_bytes=56 * 2**20),
        cost_estimate=cost(30),
    )(last_starts, *operands, entering)
    d_projected, entering_grad = meet(d_projected, entering_grad)
    last_tile = group_rows // MAXLEN - 1
    d_projected, floor_rest = pl.pallas_call(
        functools.partial(backward_edge_kernel, heads),
        grid=(1,),
        out_shape=(dproj_type, dfloor_type),
        in_specs=[SMEM]
        + edge_specs(last_tile)
        + [pl.BlockSpec((edge, heads, dim, dim), lambda i: (last_tile, 0, 0, 0)), VMEM, ANY],
        out_specs=(
            pl.BlockSpec((MAXLEN, 3 * own_width), lambda i: (last_tile, 0)),
            VMEM,
        ),
        scratch_shapes=[state_scratch],
        input_output_aliases={9: 0},
        compiler_params=pltpu.CompilerParams(vmem_limit_bytes=56 * 2**20),
        cost_estimate=cost(4),
    )(last_starts, *operands, entering, entering_grad, d_projected)
    d_projected, out_far = meet(d_projected, out_far)
    out_both = out_sum.both(out_near, out_far)
    d_projected = after(d_projected, out_both)
    floor_grad = floor_most + floor_rest
    by_sender = (GROUP, weight_rows, -1)
    floor_column = lax.dynamic_update_slice_in_dim(
        jnp.zeros((width, 128), f32), jnp.pad(floor_grad.T, ((0, 0), (0, 127))), slot * own_width, 0
    ).astype(bf16)
    mixer_grad = rows_product(first_all, d_projected, 11, floor_column)
    mixer_summed = line_scatter(mixer_grad)
    d_first, ffn_swapped = product_scatter(
        d_projected.reshape(GROUP, row_count, -1),
        after(mixer_weight, mixer_grad),
        8,
        False,
        ffn_summed.reshape(by_sender),
    )
    d_first, mixer_summed, out_last = meet(d_first, mixer_summed, out_sum.to_first(out_both))
    out_total = out_sum.total(out_near, out_far, out_last).astype(bf16)
    out_summed = line_scatter(out_total.reshape(groups * weight_rows, width))

    def swap(x):
        x = x.reshape(by_sender)
        return lax.all_to_all(x, "fsdp", 0, 0, axis_index_groups=planes, tiled=True)

    mixer_swapped = swap(mixer_summed)
    down_swapped = swap(after(down_summed, d_first))
    layer_out = residual + ffn_sum.total(ffn_near, ffn_far, after(ffn_last, d_first))
    d_gate_up, ffn_gain_sum, _ = home(ffn_swapped, gate_up, 2)
    d_mixer_in, norm_gain_sum, d_forget_floor = home(mixer_swapped, mixer_in, 3)
    d_down_proj, _, _ = home(down_swapped, down_proj, 1)
    d_out_proj = out_summed.astype(f32)
    d_dealt = d_residual + rms_back(d_first * first_gain, first_scaled, first_inverse)

    group_gain_sum = jnp.sum(out_proj.astype(f32) * d_out_proj, axis=1)
    return (
        layer_out,
        d_dealt,
        norm_gain_sum[:, 0] / norm_gain.astype(f32),
        d_mixer_in,
        d_forget_floor[:, 0],
        group_gain_sum / group_gain.astype(f32),
        d_out_proj,
        ffn_gain_sum[:, 0] / ffn_gain.astype(f32),
        d_gate_up,
        d_down_proj,
    )


def solution(mesh):
    by_rows = P("fsdp", None)
    by_one = P("fsdp")
    return jax.shard_map(
        body,
        mesh=mesh,
        in_specs=(
            by_rows,
            by_rows,
            P(),
            P(),
            by_one,
            by_rows,
            by_one,
            by_one,
            by_rows,
            by_one,
            by_rows,
            by_rows,
        ),
        out_specs=(
            by_rows,
            by_rows,
            by_one,
            by_rows,
            by_one,
            by_one,
            by_rows,
            by_one,
            by_rows,
            by_rows,
        ),
        check_vma=False,
    )
```

time: 650 us -> 592 us (0.911)
  Pallas kernels: 481 us -> 425 us
  local copies, waits for them, and re-layouts: 34 us -> 17.6 us
  matrix products: 37.1 us -> 48.5 us
  other arithmetic: 41.1 us -> 29.9 us
  starting transfers between devices: 13.3 us -> 22.9 us
  waiting for transfers between devices: 18.6 us -> 26 us
    pallas_call x7 -> x5, Pallas kernels: 212 us -> 157 us  [exchange(): pl.pallas_call(functools.partial(exchange_kernel, kinds), out_shape=tuple...]
    pallas_call x2 -> x11, Pallas kernels: 110 us -> 159 us  [the longest x2 114 us: product_scatter(): pl.pallas_call(functools.partial(product_scatter_kernel, count, around),...]
    pallas_call x4 -> x1, Pallas kernels: 50 us -> 1.93 us  [local_call(): pl.pallas_call(functools.partial(kernel, heads), out_shape=out_shape, in_...]
    ppermute x1, waiting for transfers between devices: 13.5 us -> 0.01 us  [body(): entering_grad = lax.ppermute(first_grad, 'fsdp', down_line)]
    another operation x6 -> x0, other arithmetic: 12.5 us -> none
    pallas_call x2 -> x3, Pallas kernels: 28.1 us -> 40.2 us  [rows_product(): pl.pallas_call(rows_product_kernel, grid=(columns // tile_columns,), in_s...]
    reshape x7 -> x0, local copies, waits for them, and re-layouts: 11.2 us -> none  [the longest x5 7.5 us: by_owner(): weight.reshape(weight_rows, pieces, GROUP, columns).transpose(2, 0, 1, 3)]
    all_to_all x0 -> x2, waiting for transfers between devices: none -> 10.9 us  [swap(): return lax.all_to_all(x, 'fsdp', 0, 0, axis_index_groups=planes, tiled=True)]
  transfers between devices with their start and end apart: 23 -> 25, of which waited for: 3 -> 6; matrix products, arithmetic and copies ran while one was open for 14% -> 13% of each run, Pallas kernels for 72% -> 71%
where the time goes in v4:
time: 592 us; the launch traced here: 585 us
  Pallas kernels  425 us (72%)
  matrix products  48.5 us (8%)
  other arithmetic  29.9 us (5%)
  waiting for transfers between devices  26 us (4%)
  starting transfers between devices  22.9 us (4%)
  local copies, waits for them, and re-layouts  17.6 us (3%)
  between operations  15 us (3%)
    pallas_call x5, Pallas kernels, exchange(): pl.pallas_call(functools.partial(exchange_kernel, kinds), out_shape=tuple...  157 us
    pallas_call x2, Pallas kernels, product_scatter(): pl.pallas_call(functools.partial(product_scatter_kernel, count, around),...  114 us
    pallas_call x1, Pallas kernels, gate_gather(): pl.pallas_call(gate_gather_kernel, out_shape=(jax.ShapeDtypeStruct((GROUP...  42.8 us
    pallas_call x3, Pallas kernels, rows_product(): pl.pallas_call(rows_product_kernel, grid=(columns // tile_columns,), in_s...  40.2 us
    dot_general x3, matrix products, dot_nn(): lax.dot_general(left, right, (((1,), (0,)), ((), ())), preferred_element_...  18.3 us
    pallas_call x1, Pallas kernels, body(): pl.pallas_call(functools.partial(backward_kernel, heads), grid=(tile_coun...  18.1 us
    pallas_call x1, Pallas kernels, hidden_back(): pl.pallas_call(hidden_back_kernel, grid=(rows // tile_rows,), in_specs=[t...  16.3 us
    dot_general x4, matrix products, dot_nt(): lax.dot_general(left, right, (((1,), (1,)), ((), ())), preferred_element_...  16.2 us
  transfers between devices with their start and end apart: 25, of which 6 were waited for; matrix products, arithmetic and copies ran while one was open for 13% of the time, Pallas kernels for 71%

profile of v4, /device:TPU:0, one launch (start us, length us, event | category | flops | bytes accessed | tf_op | source)
XLA Modules:
  0.0 584.8 jit_solution(15456107863495363058)
XLA Ops:
  13.7 19.5 %shard_map.196 = (bf16[4,8,16,128]{3,2,1,0:T(8,128)(2,1)}, bf16[8,64,768]{2,1,0:T(8,128)(2,1)}) custom-call(bf16[16,128]{1,0:T(8,128)(2,1)} %copy-done.30, bf16[8,64,768]{2,1,0:T(8,128)(2,1)} %copy-done.5), custom_call_target="tpu_custom_call" | custom-call | bytes 553500 | tf_op jit(solution)/shard_map/pallas_call | solution.py:220
  38.4 64.1 %shard_map.199 = (bf16[1,8,256,2048]{3,2,1,0:T(8,128)(2,1)}, bf16[8,64,1408]{2,1,0:T(8,128)(2,1)}, bf16[8,64,704]{2,1,0:T(8,128)(2,1)}) custom-call(bf16[1,256,2048]{2,1,0:T(8,128)(2,1)} %fusion.17.refs_0_, bf16[8,64,1408]{2,1,0:T(8,128)(2,1)} %copy-done.2, bf16[8,64,704]{2,1,0:T(8,128)(2,1)} %copy-done.8), custom_call_target="tpu_custom_call" | custom-call | bytes 2140200 | tf_op jit(solution)/shard_map/pallas_call | solution.py:220
  106.6 3.5 fusion.22.proj_ref
  114.6 11.1 %fusion.32.proj_ref.refs_1_ = f32[2048,768]{1,0:T(8,128)} fusion(bf16[2048,2048]{1,0:T(8,128)(2,1)} %bitcast.100, bf16[2048,768]{1,0:T(8,128)(2,1)S(1)} %copy-done.19), kind=kOutput, calls=%fused_computation.80 | convolution fusion | flops 6442450944 | bytes 17825792 | tf_op jit(solution)/shard_map/dot_general | solution.py:40
  125.6 5.0 collective-permute-done.1.refs_1_
  133.4 12.7 %shard_map.201 = (bf16[2048,256]{1,0:T(8,128)(2,1)}, f32[2048,256]{1,0:T(8,128)}, f32[32,2,128,128]{3,2,1,0:T(8,128)}) custom-call(s32[32]{0:T(128)} %copy-done.31, f32[2048,768]{1,0:T(8,128)} %fusion.32.proj_ref.refs_1_, s32[2048,1]{1,0:T(8,128)} %copy.35.start_ref.refs_2_, f32[1,256]{1,0:T(1,128)} %get-tuple-element.209.floor_ref.refs_3_, ...), custom_call_target="tpu_custom_call" | custom-call | bytes 664200 | tf_op jit(solution)/shard_map/pallas_call | solution.py:1163
  147.6 15.1 %shard_map.202.in_ref = bf16[256,2048]{1,0:T(8,128)(2,1)} custom-call(bf16[8,256,256]{2,1,0:T(8,128)(2,1)} %bitcast.107), custom_call_target="tpu_custom_call" | custom-call | bytes 553500 | tf_op jit(solution)/shard_map/pallas_call | solution.py:220
  165.2 3.4 shard_map.203
  171.7 3.7 multiply_reduce_fusion.1
  178.3 42.9 %shard_map.205 = bf16[1,8,256,2048]{3,2,1,0:T(8,128)(2,1)} custom-call(bf16[1,256,2048]{2,1,0:T(8,128)(2,1)} %bitcast.102), custom_call_target="tpu_custom_call" | custom-call | bytes 1586700 | tf_op jit(solution)/shard_map/pallas_call | solution.py:220
  221.3 42.8 %shard_map.206 = (bf16[8,256,2048]{2,1,0:T(8,128)(2,1)}, f32[2048,704]{1,0:T(8,128)}, f32[2048,704]{1,0:T(8,128)}, bf16[2048,704]{1,0:T(8,128)(2,1)}) custom-call(bf16[256,2048]{1,0:T(8,128)(2,1)} %own_ref.1, bf16[2048,2048]{1,0:T(8,128)(2,1)} %bitcast.90, bf16[2048,1408]{1,0:T(8,128)(2,1)} %all-gather.8.cloned.1.call-done.w_far), custom_call_target="tpu_custom_call" | custom-call | bytes 1660500 | tf_op jit(solution)/shard_map/pallas_call | solution.py:591
  264.0 10.9 %shard_map.207 = bf16[2048,704]{1,0:T(8,128)(2,1)} custom-call(bf16[2048,2048]{1,0:T(8,128)(2,1)} %bitcast.93, bf16[2048,704]{1,0:T(8,128)(2,1)} %get-tuple-element.150.y_ref.x_ref), custom_call_target="tpu_custom_call" | custom-call | bytes 405900 | tf_op jit(solution)/shard_map/pallas_call | solution.py:690
  276.4 7.4 %shard_map.208 = bf16[1024,2048]{1,0:T(8,128)(2,1)} custom-call(bf16[2048,704]{1,0:T(8,128)(2,1)} %get-tuple-element.150.y_ref.x_ref, bf16[2048,704]{1,0:T(8,128)(2,1)} %all-gather.10.cloned.1.call-done.w_ref), custom_call_target="tpu_custom_call" | custom-call | bytes 221400 | tf_op jit(solution)/shard_map/pallas_call | solution.py:663
  284.2 16.3 %shard_map.209.y_ref = bf16[2048,1408]{1,0:T(8,128)(2,1)} custom-call(bf16[2048,2048]{1,0:T(8,128)(2,1)} %bitcast.94, f32[2048,704]{1,0:T(8,128)} %get-tuple-element.154.gate_ref, f32[2048,704]{1,0:T(8,128)} %get-tuple-element.155.up_ref, bf16[2048,704]{1,0:T(8,128)(2,1)} %all-gather.10.cloned.1.call-done.w_ref), custom_call_target="tpu_custom_call" | custom-call | bytes 738000 | tf_op jit(solution)/shard_map/pallas_call | solution.py:640
  303.5 3.7 add_convert_fusion.1
  309.0 18.2 %shard_map.210 = bf16[2048,1408]{1,0:T(8,128)(2,1)} custom-call(bf16[2048,2048]{1,0:T(8,128)(2,1)} %bitcast.91, bf16[2048,1408]{1,0:T(8,128)(2,1)} %shard_map.209.y_ref), custom_call_target="tpu_custom_call" | custom-call | bytes 664200 | tf_op jit(solution)/shard_map/pallas_call | solution.py:690
  327.3 6.3 %collective-permute-done.9 = bf16[2,256,2048]{2,1,0:T(8,128)(2,1)} collective-permute-done((bf16[2,256,2048]{2,1,0:T(8,128)(2,1)}, bf16[2,256,2048]{2,1,0:T(8,128)(2,1)}, u32[]{:S(2)}, u32[]{:S(2)}) %collective-permute-start.9) | collective-permute-done | bytes 2097184 | tf_op jit(solution)/shard_map/ppermute | solution.py:758
  333.6 4.7 fusion.9
  340.1 48.7 %shard_map.211 = f32[256,2048]{1,0:T(8,128)} custom-call(bf16[8,256,1408]{2,1,0:T(8,128)(2,1)} %bitcast.92, bf16[2048,1408]{1,0:T(8,128)(2,1)} %all-gather.8.cloned.1.call-done.w_far), custom_call_target="tpu_custom_call" | custom-call | bytes 1845000 | tf_op jit(solution)/shard_map/pallas_call | solution.py:459
  399.3 3.3 convolution_convert_fusion.1.refs_0_
  402.6 15.1 %shard_map.212 = bf16[8,256,256]{2,1,0:T(8,128)(2,1)} custom-call(bf16[256,2048]{1,0:T(8,128)(2,1)} %convolution_convert_fusion.1.refs_0_), custom_call_target="tpu_custom_call" | custom-call | bytes 553500 | tf_op jit(solution)/shard_map/pallas_call | solution.py:220
  420.0 3.7 add_convert_fusion
  426.1 18.1 %shard_map.213 = (bf16[2048,768]{1,0:T(8,128)(2,1)}, f32[1,256]{1,0:T(1,128)}) custom-call(s32[32]{0:T(128)} %copy-done.31, f32[2048,768]{1,0:T(8,128)} %fusion.32.proj_ref.refs_1_, s32[2048,1]{1,0:T(8,128)} %copy.35.start_ref.refs_2_, f32[1,256]{1,0:T(1,128)} %get-tuple-element.209.floor_ref.refs_3_, f32[1,256]{1,0:T(1,128)} %get-tuple-element.208.gain_ref.refs_4_, ...), custom_call_target="tpu_custom_call" | custom-call | bytes 1107000 | tf_op jit(solution)/shard_map/pallas_call | solution.py:1268
  453.2 11.1 %shard_map.216 = bf16[2048,896]{1,0:T(8,128)(2,1)} custom-call(bf16[2048,2048]{1,0:T(8,128)(2,1)} %bitcast.101, bf16[2048,768]{1,0:T(8,128)(2,1)} %get-tuple-element.178.y_ref, bf16[2048,128]{1,0:T(8,128)(2,1)} %copy-done.22), custom_call_target="tpu_custom_call" | custom-call | bytes 405900 | tf_op jit(solution)/shard_map/pallas_call | solution.py:690
  465.5 65.5 %shard_map.217 = (f32[256,2048]{1,0:T(8,128)}, bf16[8,64,1408]{2,1,0:T(8,128)(2,1)}) custom-call(bf16[8,256,768]{2,1,0:T(8,128)(2,1)} %bitcast.95, bf16[2048,768]{1,0:T(8,128)(2,1)} %all-gather.6.cloned.1.call-done.w_far, bf16[8,64,1408]{2,1,0:T(8,128)(2,1)} %bitcast.106), custom_call_target="tpu_custom_call" | custom-call | bytes 1845000 | tf_op jit(solution)/shard_map/pallas_call | solution.py:459
  535.2 3.9 add_convert_fusion.2
  539.1 3.6 all-to-all-start.1
  545.7 5.2 fusion.8
  550.9 4.3 all-to-all-done.1.got_ref
  555.2 3.6 all-to-all-start
  558.8 5.9 %fusion.15 = f32[256,2048]{1,0:T(8,128)} fusion(bf16[256,2048]{1,0:T(8,128)(2,1)} %param.20, f32[256,2048]{1,0:T(8,128)} %get-tuple-element.183, f32[256]{0:T(256)S(1)} %broadcast_multiply_fusion, f32[2048]{0:T(1024)S(1)} %mul.111, f32[256]{0:T(256)S(1)} %add_rsqrt_fusion.1, f32[256]{0:T(256)S(1)} %broadcast_multiply_fusion.1, ...), kind=kLoop, calls=%fused_computation.26 | loop fusion | flops 7340032 | bytes 10506240 | tf_op jit(solution)/shard_map/add | solution.py:1337
  566.1 6.6 %all-to-all-done.got_ref = bf16[8,64,896]{2,1,0:T(8,128)(2,1)S(1)} async-done(((bf16[8,64,896]{2,1,0:T(8,128)(2,1)}), bf16[8,64,896]{2,1,0:T(8,128)(2,1)S(1)}, u32[]{:S(2)}, u32[]{:S(2)}) %all-to-all-start) | async-done | bytes 917536 | tf_op jit(solution)/shard_map/all_to_all | solution.py:1328
  (188 shorter events, 79.8 us)
Async XLA Ops:
  7.2 27.2 %copy-start.1 = (bf16[64,11264]{1,0:T(8,128)(2,1)S(1)}, bf16[64,11264]{1,0:T(8,128)(2,1)}, u32[]{:S(2)}) copy-start(bf16[64,11264]{1,0:T(8,128)(2,1)} %weight_ref.4) | copy-start | bytes 4325380
  7.2 97.4 %all-gather.12.cloned.1.call-start = ((), (), s32[]{:S(2)}) async-start(), calls=%async_computation.13 | async-start | bytes 1310720 | tf_op jit(solution)/shard_map/all_gather | solution.py:1091
  7.9 98.7 %all-gather.6.cloned.1.call-start = ((), (), s32[]{:S(2)}) async-start(), calls=%async_computation.6 | async-start | bytes 3932160 | tf_op jit(solution)/shard_map/all_gather | solution.py:1055
  33.3 188.0 %all-gather.8.cloned.1.call-start = ((), (), s32[]{:S(2)}) async-start(), calls=%async_computation.7 | async-start | bytes 7208960 | tf_op jit(solution)/shard_map/all_gather | solution.py:1055
  38.4 64.3 %copy-start.36 = (s32[96]{0:T(128)S(1)}, s32[96]{0:T(128)}, u32[]{:S(2)}) copy-start(s32[96]{0:T(128)} %param.22) | copy-start | bytes 1156
  38.4 64.3 %copy-start.37 = (s32[96]{0:T(128)S(1)}, s32[96]{0:T(128)}, u32[]{:S(2)}) copy-start(s32[96]{0:T(128)} %param.23) | copy-start | bytes 1156
  102.6 173.8 %all-gather.10.cloned.1.call-start = ((), (), s32[]{:S(2)}) async-start(), calls=%async_computation.8 | async-start | bytes 3932160 | tf_op jit(solution)/shard_map/all_gather | solution.py:1055
  104.6 26.0 %collective-permute-start.1 = (bf16[4,64,2048]{2,1,0:T(8,128)(2,1)}, bf16[4,64,2048]{2,1,0:T(8,128)(2,1)}, u32[]{:S(2)}, u32[]{:S(2)}) collective-permute-start(bf16[4,64,2048]{2,1,0:T(8,128)(2,1)} %bitcast.86), channel_id=1, source_target_pairs={{0,2},{1,5},{2,0},{3,7},{4,6},{5,1},{6,4},{7,3},{8,10},{9,13},{10,... | collective-permute-start | bytes 3145736 | tf_op jit(solution)/shard_map/ppermute | solution.py:1124
  105.9 24.7 %collective-permute-start.2 = (bf16[4,64,2048]{2,1,0:T(8,128)(2,1)}, bf16[4,64,2048]{2,1,0:T(8,128)(2,1)S(1)}, u32[]{:S(2)}, u32[]{:S(2)}) collective-permute-start(bf16[4,64,2048]{2,1,0:T(8,128)(2,1)} %bitcast.87), channel_id=1, source_target_pairs={{0,4},{1,3},{2,6},{3,1},{4,0},{5,7},{6,2},{7,5},{8,12},{9,11},{10,... | collective-permute-start | bytes 3145736 | tf_op jit(solution)/shard_map/ppermute | solution.py:1125
  112.1 18.5 %collective-permute-start = (f32[2,128,128]{2,1,0:T(8,128)}, f32[2,128,128]{2,1,0:T(8,128)S(1)}, u32[]{:S(2)}, u32[]{:S(2)}) collective-permute-start(f32[2,128,128]{2,1,0:T(8,128)} %shard_map.200), channel_id=1, source_target_pairs={{0,8},{1,9},{2,10},{3,11},{4,12},{5,13},{6,14},{7,15},{8,16},{9,17... | collective-permute-start | bytes 393224 | tf_op jit(solution)/shard_map/ppermute | solution.py:1141
  130.6 15.5 %collective-permute-start.3 = (bf16[4,64,2048]{2,1,0:T(8,128)(2,1)}, bf16[4,64,2048]{2,1,0:T(8,128)(2,1)}, u32[]{:S(2)}, u32[]{:S(2)}) collective-permute-start(bf16[4,64,2048]{2,1,0:T(8,128)(2,1)} %collective-permute-done.1.refs_1_), channel_id=1, source_target_pairs={{0,4},{1,3},{2,6},{3,1},{4,0},{5,7},{6,2},{7,5},{8,12},{9,11},{10,... | collective-permute-start | bytes 3145736 | tf_op jit(solution)/shard_map/ppermute | solution.py:1146
  133.4 13.0 %copy-start.11 = (bf16[256,2048]{1,0:T(8,128)(2,1)S(1)}, bf16[256,2048]{1,0:T(8,128)(2,1)}, u32[]{:S(2)}) copy-start(bf16[256,2048]{1,0:T(8,128)(2,1)} %all-gather.12.cloned.1.call-done) | copy-start | bytes 3145732
  146.1 242.7 %reduce-scatter.5.cloned.1.call-start = ((), (), s32[]{:S(2)}) async-start(), calls=%async_computation.9 | async-start | bytes 3932160 | tf_op jit(solution)/shard_map/reduce_scatter | solution.py:1058
  146.4 16.3 %collective-permute-start.4 = (bf16[4,64,2048]{2,1,0:T(8,128)(2,1)S(1)}, bf16[4,64,2048]{2,1,0:T(8,128)(2,1)}, u32[]{:S(2)}, u32[]{:S(2)}) collective-permute-start(bf16[4,64,2048]{2,1,0:T(8,128)(2,1)S(1)} %bitcast.88), channel_id=1, source_target_pairs={{0,1},{1,0},{2,3},{3,2},{4,5},{5,4},{6,7},{7,6},{8,9},{9,8},{10,11... | collective-permute-start | bytes 3145736 | tf_op jit(solution)/shard_map/ppermute | solution.py:1147
  146.5 16.2 %collective-permute-start.5 = (bf16[4,64,2048]{2,1,0:T(8,128)(2,1)}, bf16[4,64,2048]{2,1,0:T(8,128)(2,1)}, u32[]{:S(2)}, u32[]{:S(2)}) collective-permute-start(bf16[4,64,2048]{2,1,0:T(8,128)(2,1)} %collective-permute-done.1.refs_1_), channel_id=1, source_target_pairs={{0,1},{1,0},{2,3},{3,2},{4,5},{5,4},{6,7},{7,6},{8,9},{9,8},{10,11... | collective-permute-start | bytes 3145736 | tf_op jit(solution)/shard_map/ppermute | solution.py:1147
  147.0 15.8 %collective-permute-start.6 = (bf16[4,64,2048]{2,1,0:T(8,128)(2,1)}, bf16[4,64,2048]{2,1,0:T(8,128)(2,1)}, u32[]{:S(2)}, u32[]{:S(2)}) collective-permute-start(bf16[4,64,2048]{2,1,0:T(8,128)(2,1)} %copy-done.12), channel_id=1, source_target_pairs={{0,1},{1,0},{2,3},{3,2},{4,5},{5,4},{6,7},{7,6},{8,9},{9,8},{10,11... | collective-permute-start | bytes 3145736 | tf_op jit(solution)/shard_map/ppermute | solution.py:1147
  147.1 15.7 %collective-permute-start.7 = (bf16[4,64,2048]{2,1,0:T(8,128)(2,1)}, bf16[4,64,2048]{2,1,0:T(8,128)(2,1)}, u32[]{:S(2)}, u32[]{:S(2)}) collective-permute-start(bf16[4,64,2048]{2,1,0:T(8,128)(2,1)} %collective-permute-done.3.refs_3_), channel_id=1, source_target_pairs={{0,1},{1,0},{2,3},{3,2},{4,5},{5,4},{6,7},{7,6},{8,9},{9,8},{10,11... | collective-permute-start | bytes 3145736 | tf_op jit(solution)/shard_map/ppermute | solution.py:1178
  283.8 19.7 %collective-permute-start.8 = (bf16[4,256,2048]{2,1,0:T(8,128)(2,1)}, bf16[4,256,2048]{2,1,0:T(8,128)(2,1)}, u32[]{:S(2)}, u32[]{:S(2)}) collective-permute-start(bf16[4,256,2048]{2,1,0:T(8,128)(2,1)} %bitcast.103), channel_id=1, source_target_pairs={{0,1},{1,0},{2,3},{3,2},{4,5},{5,4},{6,7},{7,6},{8,9},{9,8},{10,11... | collective-permute-start | bytes 12582920 | tf_op jit(solution)/shard_map/ppermute | solution.py:752
  283.8 181.7 %reduce-scatter.7.cloned.1.call-start = ((), (), s32[]{:S(2)}) async-start(), calls=%async_computation.10 | async-start | bytes 7208960 | tf_op jit(solution)/shard_map/reduce_scatter | solution.py:1058
  284.1 16.3 %copy-start.15 = (bf16[2048,704]{1,0:T(8,128)(2,1)S(1)}, bf16[2048,704]{1,0:T(8,128)(2,1)}, u32[]{:S(2)}) copy-start(bf16[2048,704]{1,0:T(8,128)(2,1)} %all-gather.10.cloned.1.call-done.w_ref) | copy-start | bytes 8650756
  307.2 26.4 %collective-permute-start.9 = (bf16[2,256,2048]{2,1,0:T(8,128)(2,1)}, bf16[2,256,2048]{2,1,0:T(8,128)(2,1)}, u32[]{:S(2)}, u32[]{:S(2)}) collective-permute-start(bf16[2,256,2048]{2,1,0:T(8,128)(2,1)} %add_convert_fusion.1), channel_id=1, source_target_pairs={{0,4},{1,3},{2,6},{3,1},{4,0},{5,7},{6,2},{7,5},{8,12},{9,11},{10,... | collective-permute-start | bytes 6291464 | tf_op jit(solution)/shard_map/ppermute | solution.py:758
  333.6 201.6 %reduce-scatter.9.cloned.1.call-start = ((), (), s32[]{:S(2)}) async-start(), calls=%async_computation.11 | async-start | bytes 4587520 | tf_op jit(solution)/shard_map/reduce_scatter | solution.py:1058
  338.3 50.5 %collective-permute-start.10 = (bf16[256,2048]{1,0:T(8,128)(2,1)}, bf16[256,2048]{1,0:T(8,128)(2,1)S(1)}, u32[]{:S(2)}, u32[]{:S(2)}) collective-permute-start(bf16[256,2048]{1,0:T(8,128)(2,1)} %fusion.9), channel_id=1, source_target_pairs={{0,2},{1,5},{2,0},{3,7},{4,6},{5,1},{6,4},{7,3},{8,10},{9,13},{10,... | collective-permute-start | bytes 3145736 | tf_op jit(solution)/shard_map/ppermute | solution.py:764
  395.2 54.9 %copy-start.20 = (bf16[256,2048]{1,0:T(8,128)(2,1)}, bf16[256,2048]{1,0:T(8,128)(2,1)S(1)}, u32[]{:S(2)}) copy-start(bf16[256,2048]{1,0:T(8,128)(2,1)S(1)} %fusion.30) | copy-start | bytes 3145732
  398.5 19.3 %collective-permute-start.11 = (bf16[4,256,2048]{2,1,0:T(8,128)(2,1)}, bf16[4,256,2048]{2,1,0:T(8,128)(2,1)}, u32[]{:S(2)}, u32[]{:S(2)}) collective-permute-start(bf16[4,256,2048]{2,1,0:T(8,128)(2,1)} %convolution_convert_fusion), channel_id=1, source_target_pairs={{0,1},{1,0},{2,3},{3,2},{4,5},{5,4},{6,7},{7,6},{8,9},{9,8},{10,11... | collective-permute-start | bytes 12582920 | tf_op jit(solution)/shard_map/ppermute | solution.py:752
  423.7 26.4 %collective-permute-start.13 = (bf16[2,256,2048]{2,1,0:T(8,128)(2,1)}, bf16[2,256,2048]{2,1,0:T(8,128)(2,1)}, u32[]{:S(2)}, u32[]{:S(2)}) collective-permute-start(bf16[2,256,2048]{2,1,0:T(8,128)(2,1)} %add_convert_fusion), channel_id=1, source_target_pairs={{0,4},{1,3},{2,6},{3,1},{4,0},{5,7},{6,2},{7,5},{8,12},{9,11},{10,... | collective-permute-start | bytes 6291464 | tf_op jit(solution)/shard_map/ppermute | solution.py:758
  424.8 19.4 %collective-permute-start.12 = (f32[2,128,128]{2,1,0:T(8,128)S(1)}, f32[2,128,128]{2,1,0:T(8,128)S(1)}, u32[]{:S(2)}, u32[]{:S(2)}) collective-permute-start(f32[2,128,128]{2,1,0:T(8,128)S(1)} %copy-done.29), channel_id=1, source_target_pairs={{8,0},{9,1},{10,2},{11,3},{12,4},{13,5},{14,6},{15,7},{16,8},{17,9... | collective-permute-start | bytes 393224 | tf_op jit(solution)/shard_map/ppermute | solution.py:1263
  464.3 111.0 %reduce-scatter.11.cloned.1.call-start = ((), (), s32[]{:S(2)}) async-start(), calls=%async_computation.12 | async-start | bytes 1310720 | tf_op jit(solution)/shard_map/reduce_scatter | solution.py:1058
  464.3 70.8 %collective-permute-start.14 = (bf16[256,2048]{1,0:T(8,128)(2,1)}, bf16[256,2048]{1,0:T(8,128)(2,1)}, u32[]{:S(2)}, u32[]{:S(2)}) collective-permute-start(bf16[256,2048]{1,0:T(8,128)(2,1)} %fusion.10), channel_id=1, source_target_pairs={{0,2},{1,5},{2,0},{3,7},{4,6},{5,1},{6,4},{7,3},{8,10},{9,13},{10,... | collective-permute-start | bytes 3145736 | tf_op jit(solution)/shard_map/ppermute | solution.py:764
  539.1 16.1 %all-to-all-start.1 = ((bf16[8,64,704]{2,1,0:T(8,128)(2,1)}), bf16[8,64,704]{2,1,0:T(8,128)(2,1)S(1)}, u32[]{:S(2)}, u32[]{:S(2)}) async-start(bf16[8,64,704]{2,1,0:T(8,128)(2,1)} %bitcast.36), calls=%async_computation.5 | async-start | bytes 1572864 | tf_op jit(solution)/shard_map/all_to_all | solution.py:1328
  555.2 17.5 %all-to-all-start = ((bf16[8,64,896]{2,1,0:T(8,128)(2,1)}), bf16[8,64,896]{2,1,0:T(8,128)(2,1)S(1)}, u32[]{:S(2)}, u32[]{:S(2)}) async-start(bf16[8,64,896]{2,1,0:T(8,128)(2,1)} %bitcast.108), calls=%async_computation.3 | async-start | bytes 1835008 | tf_op jit(solution)/shard_map/all_to_all | solution.py:1328
  558.8 13.9 %copy-start.7 = (bf16[64,6144]{1,0:T(8,128)(2,1)S(1)}, bf16[64,6144]{1,0:T(8,128)(2,1)}, u32[]{:S(2)}) copy-start(bf16[64,6144]{1,0:T(8,128)(2,1)} %weight_ref.3) | copy-start | bytes 2359300
  (33 other events, 136.4 us)
Sparse Core Ops, SparseCore 0:
  9.6 31.2 all-gather.11
  42.4 62.4 all-gather.5
  106.5 105.3 all-gather.7
  213.3 63.0 all-gather.9
  284.0 59.0 reduce-scatter.4
  345.2 105.1 reduce-scatter.6
  464.4 66.8 reduce-scatter.8
  539.2 25.8 reduce-scatter.10

commit v5 on v4

--- a/solution.py
+++ b/solution.py
@@ -271,17 +271,14 @@
     )(x)
 
 
-def home_kernel(pieces, got_ref, weight_ref, out_ref, gain_ref, more_ref):
-    columns = weight_ref.shape[1] // GROUP // pieces
-    more_ref[...] = jnp.zeros_like(more_ref)
+def home_kernel(pieces, got_ref, weight_ref, out_ref, gain_ref):
+    columns = got_ref.shape[2] // pieces
     for sender in range(GROUP):
         for piece in range(pieces):
             lo = (piece * GROUP + sender) * columns
             out_ref[:, lo : lo + columns] = got_ref[
                 sender, :, piece * columns : (piece + 1) * columns
             ].astype(f32)
-        if got_ref.shape[2] > pieces * columns:
-            more_ref[...] += got_ref[sender, :, pieces * columns :].astype(f32)
     gain_ref[...] = jnp.sum(out_ref[...] * weight_ref[...].astype(f32), axis=1, keepdims=True)
 
 
@@ -292,10 +289,9 @@
         out_shape=(
             jax.ShapeDtypeStruct((rows, columns), f32),
             jax.ShapeDtypeStruct((rows, 1), f32),
-            jax.ShapeDtypeStruct((rows, 128), f32),
         ),
         in_specs=[VMEM, VMEM],
-        out_specs=(VMEM, VMEM, VMEM),
+        out_specs=(VMEM, VMEM),
         compiler_params=pltpu.CompilerParams(vmem_limit_bytes=32 * 2**20),
         cost_estimate=cost(5),
     )(got, weight)
@@ -482,6 +478,129 @@
     )(a, w, *swaps)
 
 
+def residual_back_kernel(
+    d_second_ref,
+    residual_ref,
+    cot_ref,
+    gain_ref,
+    w_far,
+    mixer_ref,
+    down_ref,
+    d_residual_ref,
+    d_mix_ref,
+    heads_ref,
+    near_ref,
+    swapped_ref,
+    w_ref,
+    parts_ref,
+    away_ref,
+    send_sem,
+    recv_sem,
+    own_sem,
+    w_sem,
+):
+    me, slot, step_core, first_step, second_step = places()
+    core = lax.rem(slot, 2)
+    others = plane_steps(
+        step_core,
+        (1 - core) * first_step + core * second_step,
+        core * first_step + (1 - core) * second_step,
+    )
+    mate = me + step_core
+    width = parts_ref.shape[2]
+
+    def w_load(i):
+        at = pl.ds(i * width, width)
+        return pltpu.make_async_copy(w_far.at[at, :], w_ref.at[i], w_sem.at[i])
+
+    for i in range(GROUP):
+        w_load(i).start()
+    greet([me + step for _, step in others])
+    sent = []
+
+    def send(source, target, item, number, device):
+        copy = remote(source, target, send_sem.at[item, number], recv_sem.at[item, number], device)
+        copy.start()
+        sent.append(copy)
+
+    def arrived(target, item, number):
+        remote(target, target, send_sem.at[item, number], recv_sem.at[item, number], me).wait_recv()
+
+    for number, step in others:
+        send(down_ref.at[slot + step], swapped_ref.at[slot], 2, number - 1, me + step)
+    own_down = pltpu.make_async_copy(down_ref.at[slot], swapped_ref.at[slot], own_sem.at[0])
+    own_down.start()
+    rows = d_residual_ref.shape[0]
+    slab_rows = 32
+
+    def slab(i, _):
+        at = pl.ds(pl.multiple_of(i * slab_rows, slab_rows), slab_rows)
+        residual = residual_ref[at, :]
+        inverse = inverse_rms(residual)
+        grad = rms_back(d_second_ref[at, :] * gain_ref[...], residual * inverse, inverse)
+        total = cot_ref[at, :].astype(f32) + grad
+        d_residual_ref[at, :] = total
+        d_mix_ref[at, :] = total.astype(bf16)
+        return 0
+
+    lax.fori_loop(0, rows // slab_rows, slab, 0)
+    for i in range(GROUP):
+        w_load(i).wait()
+
+    def part(place):
+        parts_ref[place] = dot_nt(d_mix_ref[...], w_ref[place]).astype(bf16)
+
+    for number, step in reversed(others):
+        part(slot + step)
+        send(parts_ref.at[slot + step], heads_ref.at[slot], 0, number - 1, me + step)
+    part(slot)
+    own_part = pltpu.make_async_copy(parts_ref.at[slot], heads_ref.at[slot], own_sem.at[1])
+    own_part.start()
+    for kind in (3, 2, 1, 0):
+        away_ref[kind] = dot_tn(mixer_ref[kind], d_mix_ref[...]).astype(bf16)
+        send(away_ref.at[kind], near_ref.at[kind], 1, kind, mate)
+    for number, step in others:
+        arrived(heads_ref.at[slot + step], 0, number - 1)
+        arrived(swapped_ref.at[slot + step], 2, number - 1)
+    for kind in range(4):
+        arrived(near_ref.at[kind], 1, kind)
+    for copy in sent:
+        copy.wait_send()
+    own_down.wait()
+    own_part.wait()
+
+
+def residual_back(d_second, residual, cot, gain, w, mixer_away, down, number):
+    rows, columns = residual.shape
+    width = columns // GROUP
+    blocks = mixer_away.shape[0]
+    return pl.pallas_call(
+        residual_back_kernel,
+        out_shape=(
+            jax.ShapeDtypeStruct((rows, columns), f32),
+            jax.ShapeDtypeStruct((rows, columns), bf16),
+            jax.ShapeDtypeStruct((GROUP, rows, width), bf16),
+            jax.ShapeDtypeStruct((blocks, mixer_away.shape[2], columns), bf16),
+            jax.ShapeDtypeStruct(down.shape, down.dtype),
+        ),
+        in_specs=[VMEM, VMEM, VMEM, VMEM, ANY, VMEM, ANY],
+        out_specs=(VMEM, VMEM, ANY, ANY, ANY),
+        scratch_shapes=[
+            pltpu.VMEM((GROUP, width, columns), bf16),
+            pltpu.VMEM((GROUP, rows, width), bf16),
+            pltpu.VMEM((blocks, mixer_away.shape[2], columns), bf16),
+            pltpu.SemaphoreType.DMA((3, GROUP - 1)),
+            pltpu.SemaphoreType.DMA((3, GROUP - 1)),
+            pltpu.SemaphoreType.DMA((2,)),
+            pltpu.SemaphoreType.DMA((GROUP,)),
+        ],
+        compiler_params=pltpu.CompilerParams(
+            collective_id=number, has_side_effects=True, vmem_limit_bytes=48 * 2**20
+        ),
+        cost_estimate=cost(20),
+    )(d_second, residual, cot, gain, w, mixer_away, down)
+
+
 def gate_gather_kernel(
     own_ref,
     x_far,
@@ -674,32 +793,48 @@
     )(x, w)
 
 
-def rows_product_kernel(x_ref, y_ref, *refs):
-    out_ref = refs[-1]
-    wide = y_ref.shape[1]
-    out_ref[:, :wide] = dot_tn(x_ref[...], y_ref[...]).astype(bf16)
-    for more_ref in refs[:-1]:
-        out_ref[:, wide:] = more_ref[...]
-
-
-def rows_product(x, y, micros, *more):
+def keep_product_kernel(x_ref, w_ref, near_ref, out_ref):
+    total = dot_nt(x_ref[...], w_ref[...]) + near_ref[0].astype(f32)
+    out_ref[0] = total.astype(out_ref.dtype)
+
+
+def keep_product(x, w, near, begin, number, out_type):
+    _, rows, columns = near.shape
+    return pl.pallas_call(
+        keep_product_kernel,
+        grid=(number,),
+        in_specs=[
+            pl.BlockSpec((rows, x.shape[1]), lambda i: (begin + i, 0)),
+            pl.BlockSpec(w.shape, lambda i: (0, 0)),
+            pl.BlockSpec((1, rows, columns), lambda i: (begin + i, 0, 0)),
+        ],
+        out_specs=pl.BlockSpec((1, rows, columns), lambda i: (i, 0, 0)),
+        out_shape=jax.ShapeDtypeStruct((number, rows, columns), out_type),
+        compiler_params=pltpu.CompilerParams(vmem_limit_bytes=56 * 2**20),
+        cost_estimate=cost(5),
+    )(x, w, near)
+
+
+def rows_product_kernel(x_ref, y_ref, out_ref):
+    out_ref[...] = dot_tn(x_ref[...], y_ref[...]).astype(bf16)
+
+
+def rows_product(x, y, micros):
     rows, columns = x.shape
     wide = y.shape[1]
     tile_columns = 512
-    more_wide = sum(m.shape[1] for m in more)
     return pl.pallas_call(
         rows_product_kernel,
         grid=(columns // tile_columns,),
         in_specs=[
             pl.BlockSpec((rows, tile_columns), lambda i: (0, i)),
             pl.BlockSpec((rows, wide), lambda i: (0, 0)),
-        ]
-        + [pl.BlockSpec((tile_columns, m.shape[1]), lambda i: (i, 0)) for m in more],
-        out_specs=pl.BlockSpec((tile_columns, wide + more_wide), lambda i: (i, 0)),
-        out_shape=jax.ShapeDtypeStruct((columns, wide + more_wide), bf16),
+        ],
+        out_specs=pl.BlockSpec((tile_columns, wide), lambda i: (i, 0)),
+        out_shape=jax.ShapeDtypeStruct((columns, wide), bf16),
         compiler_params=pltpu.CompilerParams(vmem_limit_bytes=56 * 2**20),
         cost_estimate=cost(micros),
-    )(x, y, *more)
+    )(x, y)
 
 
 def plane_permutes(device_count):
@@ -757,8 +892,11 @@
     def to_second(self, sums):
         return lax.ppermute(sums, "fsdp", self.second)
 
-    def both(self, near, far):
-        return (self.keep(1, 1)[0] + near[1].astype(f32) + far[1].astype(f32)).astype(bf16)
+    def half(self, near):
+        return self.keep(1, 1)[0] + near[1].astype(f32)
+
+    def both(self, half, far):
+        return (half + far[1].astype(f32)).astype(bf16)
 
     def to_first(self, both):
         return lax.ppermute(both, "fsdp", self.first)
@@ -1206,43 +1344,43 @@
     down_summed = line_scatter(down_grad)
     hidden_act = after(hidden_act, down_grad)
 
-    def ffn_blocks(begin, number):
-        rows = hidden_act[begin * row_count : (begin + number) * row_count]
-        return dot_nt(rows, down_weight).reshape(number, row_count, width)
-
     ffn_away = away_product(hidden_act, down_weight, row_count).reshape(4, row_count, width)
-    ffn_sum = SlowScatter(ffn_blocks, ffn_away, device_count)
-    ffn_near = ffn_sum.to_mate()
+    ffn_near = lax.ppermute(ffn_away, "fsdp", mate)
     d_gate_pre = hidden_back(after(cot_all, ffn_away), gate_part, up_part, down_weight)
     d_gate_pre, ffn_near = meet(d_gate_pre, ffn_near)
-    ffn_sums = ffn_sum.onward(ffn_near)
+    ffn_sums = keep_product(hidden_act, down_weight, ffn_near, 2, 2, bf16)
     ffn_grad = rows_product(after(second_all, ffn_sums), d_gate_pre, 18)
-    ffn_grad, ffn_far = meet(ffn_grad, ffn_sum.to_second(ffn_sums))
-    ffn_both = ffn_sum.both(ffn_near, ffn_far)
+    ffn_rest = keep_product(hidden_act, down_weight, after(ffn_near, ffn_grad), 0, 2, f32)
+    ffn_grad, ffn_rest, ffn_far = meet(ffn_grad, ffn_rest, lax.ppermute(ffn_sums, "fsdp", second))
+    ffn_both = (ffn_rest[1] + ffn_far[1].astype(f32)).astype(bf16)
     ffn_summed = line_scatter(ffn_grad)
     [d_second] = product_scatter(
         d_gate_pre.reshape(GROUP, row_count, -1), after(ffn_weight, ffn_grad, ffn_both), 4, True
     )
-    d_second, ffn_last, down_summed = meet(d_second, ffn_sum.to_first(ffn_both), down_summed)
-
-    d_residual = cotangent.astype(f32) + rms_back(
-        d_second * second_gain, second_scaled, second_inverse
-    )
-    d_mix_out = d_residual.astype(bf16)
+    d_second, ffn_last, down_summed = meet(
+        d_second, lax.ppermute(ffn_both, "fsdp", first), down_summed
+    )
+
+    d_residual, d_mix_out, d_mixed_heads, out_near, down_swapped = residual_back(
+        d_second,
+        residual,
+        cotangent,
+        second_gain,
+        out_weight,
+        mixer_away,
+        down_summed.reshape(GROUP, weight_rows, -1),
+        5,
+    )
+    d_mixed_heads = d_mixed_heads.reshape(group_rows, own_width)
 
     def out_blocks(blocks):
         return lax.dot_general(
             blocks, d_mix_out, (((1,), (0,)), ((), ())), preferred_element_type=f32
         )
 
-    out_away = out_blocks(mixer_away).astype(bf16)
     out_sum = SlowScatter(
-        lambda begin, number: out_blocks(mixer_keep[begin : begin + number]), out_away, device_count
-    )
-    out_near = out_sum.to_mate()
-    d_mixer_input = dot_nt(after(d_mix_out, out_away), out_weight).astype(bf16)
-    [d_mixed_heads] = exchange(5, 15, ("narrow", d_mixer_input))
-    d_mixed_heads, out_near = meet(d_mixed_heads.reshape(group_rows, own_width), out_near)
+        lambda begin, number: out_blocks(mixer_keep[begin : begin + number]), None, device_count
+    )
     operands = (projected, start_column, own_floor, own_group_gain, state_out, d_mixed_heads)
 
     def edge_specs(place):
@@ -1303,38 +1441,42 @@
         cost_estimate=cost(4),
     )(last_starts, *operands, entering, entering_grad, d_projected)
     d_projected, out_far = meet(d_projected, out_far)
-    out_both = out_sum.both(out_near, out_far)
+    out_both = out_sum.both(out_sum.half(out_near), out_far)
     d_projected = after(d_projected, out_both)
     floor_grad = floor_most + floor_rest
     by_sender = (GROUP, weight_rows, -1)
-    floor_column = lax.dynamic_update_slice_in_dim(
-        jnp.zeros((width, 128), f32), jnp.pad(floor_grad.T, ((0, 0), (0, 127))), slot * own_width, 0
-    ).astype(bf16)
-    mixer_grad = rows_product(first_all, d_projected, 11, floor_column)
+    floor_parts = lax.dynamic_update_slice_in_dim(
+        jnp.zeros((width,), f32), floor_grad[0], slot * own_width, 0
+    ).reshape(device_count, weight_rows)
+    floor_parts = lax.all_to_all(floor_parts, "fsdp", 0, 0, tiled=True)
+    mixer_grad = rows_product(first_all, d_projected, 11)
+    mixer_grad, out_last = meet(mixer_grad, out_sum.to_first(out_both))
     mixer_summed = line_scatter(mixer_grad)
+    out_total = out_sum.total(after(out_near, mixer_grad), out_far, out_last).astype(bf16)
+    out_summed = line_scatter(out_total.reshape(groups * weight_rows, width))
     d_first, ffn_swapped = product_scatter(
         d_projected.reshape(GROUP, row_count, -1),
-        after(mixer_weight, mixer_grad),
+        after(mixer_weight, out_total),
         8,
         False,
         ffn_summed.reshape(by_sender),
     )
-    d_first, mixer_summed, out_last = meet(d_first, mixer_summed, out_sum.to_first(out_both))
-    out_total = out_sum.total(out_near, out_far, out_last).astype(bf16)
-    out_summed = line_scatter(out_total.reshape(groups * weight_rows, width))
+    d_first, mixer_summed, floor_parts = meet(d_first, mixer_summed, floor_parts)
+    d_forget_floor = jnp.sum(floor_parts, axis=0)
 
     def swap(x):
         x = x.reshape(by_sender)
         return lax.all_to_all(x, "fsdp", 0, 0, axis_index_groups=planes, tiled=True)
 
     mixer_swapped = swap(mixer_summed)
-    down_swapped = swap(after(down_summed, d_first))
-    layer_out = residual + ffn_sum.total(ffn_near, ffn_far, after(ffn_last, d_first))
-    d_gate_up, ffn_gain_sum, _ = home(ffn_swapped, gate_up, 2)
-    d_mixer_in, norm_gain_sum, d_forget_floor = home(mixer_swapped, mixer_in, 3)
-    d_down_proj, _, _ = home(down_swapped, down_proj, 1)
-    d_out_proj = out_summed.astype(f32)
+    ffn_last = after(ffn_last, d_first)
+    layer_out = residual + (ffn_rest[0] + ffn_far[0].astype(f32) + ffn_last.astype(f32))
+    d_gate_up, ffn_gain_sum = home(ffn_swapped, gate_up, 2)
+    d_mixer_in, norm_gain_sum = home(mixer_swapped, mixer_in, 3)
+    d_down_proj, _ = home(down_swapped, down_proj, 1)
     d_dealt = d_residual + rms_back(d_first * first_gain, first_scaled, first_inverse)
+
+    d_out_proj = after(out_summed, d_dealt, mixer_swapped).astype(f32)
 
     group_gain_sum = jnp.sum(out_proj.astype(f32) * d_out_proj, axis=1)
     return (
@@ -1342,7 +1484,7 @@
         d_dealt,
         norm_gain_sum[:, 0] / norm_gain.astype(f32),
         d_mixer_in,
-        d_forget_floor[:, 0],
+        d_forget_floor,
         group_gain_sum / group_gain.astype(f32),
         d_out_proj,
         ffn_gain_sum[:, 0] / ffn_gain.astype(f32),

time: 592 us -> 577 us (0.975)
  matrix products: 48.5 us -> 26.2 us
  Pallas kernels: 425 us -> 445 us
  waiting for transfers between devices: 26 us -> 14.3 us
  local copies, waits for them, and re-layouts: 17.6 us -> 23.7 us
    pallas_call x0 -> x3, Pallas kernels: none -> 39.1 us  [the longest x1 27.8 us: residual_back(): pl.pallas_call(residual_back_kernel, out_shape=(jax.ShapeDtypeStruct((row...]
    dot_general x4 -> x0, matrix products: 16.2 us -> none  [dot_nt(): lax.dot_general(left, right, (((1,), (1,)), ((), ())), preferred_element_...]
    pallas_call x5 -> x4, Pallas kernels: 157 us -> 142 us  [exchange(): pl.pallas_call(functools.partial(exchange_kernel, kinds), out_shape=tuple...]
    all_to_all x2 -> x1, waiting for transfers between devices: 10.9 us -> 0.01 us  [swap(): return lax.all_to_all(x, 'fsdp', 0, 0, axis_index_groups=planes, tiled=True)]
    unnamed x80 -> x84, local copies, waits for them, and re-layouts: 11.2 us -> 17.2 us
    dot_general x4 -> x3, matrix products: 14 us -> 9.1 us  [out_blocks(): lax.dot_general(blocks, d_mix_out, (((1,), (0,)), ((), ())), preferred_el...]
  transfers between devices with their start and end apart: 25 -> 24, of which waited for: 6 -> 5; matrix products, arithmetic and copies ran while one was open for 13% -> 9% of each run, Pallas kernels for 71% -> 76%
where the time goes in v5:
time: 577 us; the launch traced here: 570 us
  Pallas kernels  445 us (77%)
  matrix products  26.2 us (5%)
  other arithmetic  24.1 us (4%)
  local copies, waits for them, and re-layouts  23.7 us (4%)
  starting transfers between devices  21.9 us (4%)
  between operations  15 us (3%)
  waiting for transfers between devices  14.3 us (2%)
    pallas_call x4, Pallas kernels, exchange(): pl.pallas_call(functools.partial(exchange_kernel, kinds), out_shape=tuple...  142 us
    pallas_call x2, Pallas kernels, product_scatter(): pl.pallas_call(functools.partial(product_scatter_kernel, count, around),...  110 us
    pallas_call x1, Pallas kernels, gate_gather(): pl.pallas_call(gate_gather_kernel, out_shape=(jax.ShapeDtypeStruct((GROUP...  42.8 us
    pallas_call x3, Pallas kernels, rows_product(): pl.pallas_call(rows_product_kernel, grid=(columns // tile_columns,), in_s...  39.9 us
    pallas_call x1, Pallas kernels, residual_back(): pl.pallas_call(residual_back_kernel, out_shape=(jax.ShapeDtypeStruct((row...  27.8 us
    pallas_call x1, Pallas kernels, body(): pl.pallas_call(functools.partial(backward_kernel, heads), grid=(tile_coun...  17.9 us
    unnamed x84, local copies, waits for them, and re-layouts  17.2 us
    dot_general x3, matrix products, dot_nn(): lax.dot_general(left, right, (((1,), (0,)), ((), ())), preferred_element_...  17.1 us
  transfers between devices with their start and end apart: 24, of which 5 were waited for; matrix products, arithmetic and copies ran while one was open for 9% of the time, Pallas kernels for 76%

profile of v5, /device:TPU:0, one launch (start us, length us, event | category | flops | bytes accessed | tf_op | source)
XLA Modules:
  0.0 570.3 jit_solution(5500132683985643418)
XLA Ops:
  13.8 19.5 %shard_map.196 = (bf16[4,8,16,128]{3,2,1,0:T(8,128)(2,1)}, bf16[8,64,768]{2,1,0:T(8,128)(2,1)}) custom-call(bf16[16,128]{1,0:T(8,128)(2,1)} %copy-done.33, bf16[8,64,768]{2,1,0:T(8,128)(2,1)} %copy-done.9), custom_call_target="tpu_custom_call" | custom-call | bytes 553500 | tf_op jit(solution)/shard_map/pallas_call | solution.py:220
  38.5 64.1 %shard_map.199 = (bf16[1,8,256,2048]{3,2,1,0:T(8,128)(2,1)}, bf16[8,64,1408]{2,1,0:T(8,128)(2,1)}, bf16[8,64,704]{2,1,0:T(8,128)(2,1)}) custom-call(bf16[1,256,2048]{2,1,0:T(8,128)(2,1)} %fusion.14.refs_0_, bf16[8,64,1408]{2,1,0:T(8,128)(2,1)} %copy-done.3, bf16[8,64,704]{2,1,0:T(8,128)(2,1)} %copy-done.10), custom_call_target="tpu_custom_call" | custom-call | bytes 2140200 | tf_op jit(solution)/shard_map/pallas_call | solution.py:220
  106.6 3.5 fusion.16.proj_ref
  114.6 11.1 %fusion.23.proj_ref.refs_1_ = f32[2048,768]{1,0:T(8,128)} fusion(bf16[2048,2048]{1,0:T(8,128)(2,1)} %bitcast.85, bf16[2048,768]{1,0:T(8,128)(2,1)S(1)} %copy-done.26), kind=kOutput, calls=%fused_computation.62 | convolution fusion | flops 6442450944 | bytes 17825792 | tf_op jit(solution)/shard_map/dot_general | solution.py:40
  125.6 4.8 collective-permute-done.2.refs_2_
  133.3 12.7 %shard_map.201 = (bf16[2048,256]{1,0:T(8,128)(2,1)}, f32[2048,256]{1,0:T(8,128)}, f32[32,2,128,128]{3,2,1,0:T(8,128)}) custom-call(s32[32]{0:T(128)} %copy-done.34, f32[2048,768]{1,0:T(8,128)} %fusion.23.proj_ref.refs_1_, s32[2048,1]{1,0:T(8,128)} %copy.32.start_ref.refs_2_, f32[1,256]{1,0:T(1,128)} %get-tuple-element.222.floor_ref.refs_3_, ...), custom_call_target="tpu_custom_call" | custom-call | bytes 664200 | tf_op jit(solution)/shard_map/pallas_call | solution.py:1301
  147.4 15.1 %shard_map.202.in_ref = bf16[256,2048]{1,0:T(8,128)(2,1)} custom-call(bf16[8,256,256]{2,1,0:T(8,128)(2,1)} %bitcast.91), custom_call_target="tpu_custom_call" | custom-call | bytes 553500 | tf_op jit(solution)/shard_map/pallas_call | solution.py:220
  165.0 3.4 shard_map.203
  176.6 43.0 %shard_map.205 = bf16[1,8,256,2048]{3,2,1,0:T(8,128)(2,1)} custom-call(bf16[1,256,2048]{2,1,0:T(8,128)(2,1)} %bitcast.87), custom_call_target="tpu_custom_call" | custom-call | bytes 1586700 | tf_op jit(solution)/shard_map/pallas_call | solution.py:220
  219.6 42.8 %shard_map.206 = (bf16[8,256,2048]{2,1,0:T(8,128)(2,1)}, f32[2048,704]{1,0:T(8,128)}, f32[2048,704]{1,0:T(8,128)}, bf16[2048,704]{1,0:T(8,128)(2,1)}) custom-call(bf16[256,2048]{1,0:T(8,128)(2,1)} %cot_ref.1, bf16[2048,2048]{1,0:T(8,128)(2,1)} %bitcast.78, bf16[2048,1408]{1,0:T(8,128)(2,1)} %all-gather.8.cloned.1.call-done.w_far), custom_call_target="tpu_custom_call" | custom-call | bytes 1660500 | tf_op jit(solution)/shard_map/pallas_call | solution.py:710
  262.4 10.9 %shard_map.207 = bf16[2048,704]{1,0:T(8,128)(2,1)} custom-call(bf16[2048,2048]{1,0:T(8,128)(2,1)} %bitcast.81, bf16[2048,704]{1,0:T(8,128)(2,1)} %get-tuple-element.156.y_ref.x_ref), custom_call_target="tpu_custom_call" | custom-call | bytes 405900 | tf_op jit(solution)/shard_map/pallas_call | solution.py:826
  273.2 3.2 all-gather.10.cloned.1.call-done.w_ref
  276.4 7.4 %shard_map.208 = bf16[1024,2048]{1,0:T(8,128)(2,1)} custom-call(bf16[2048,704]{1,0:T(8,128)(2,1)} %get-tuple-element.156.y_ref.x_ref, bf16[2048,704]{1,0:T(8,128)(2,1)} %all-gather.10.cloned.1.call-done.w_ref), custom_call_target="tpu_custom_call" | custom-call | bytes 221400 | tf_op jit(solution)/shard_map/pallas_call | solution.py:782
  283.9 16.6 %shard_map.209.y_ref = bf16[2048,1408]{1,0:T(8,128)(2,1)} custom-call(bf16[2048,2048]{1,0:T(8,128)(2,1)} %bitcast.82, f32[2048,704]{1,0:T(8,128)} %get-tuple-element.160.gate_ref, f32[2048,704]{1,0:T(8,128)} %get-tuple-element.161.up_ref, bf16[2048,704]{1,0:T(8,128)(2,1)} %all-gather.10.cloned.1.call-done.w_ref), custom_call_target="tpu_custom_call" | custom-call | bytes 738000 | tf_op jit(solution)/shard_map/pallas_call | solution.py:759
  300.5 5.5 shard_map.210
  307.6 18.2 %shard_map.211 = bf16[2048,1408]{1,0:T(8,128)(2,1)} custom-call(bf16[2048,2048]{1,0:T(8,128)(2,1)} %bitcast.79, bf16[2048,1408]{1,0:T(8,128)(2,1)} %shard_map.209.y_ref), custom_call_target="tpu_custom_call" | custom-call | bytes 664200 | tf_op jit(solution)/shard_map/pallas_call | solution.py:826
  325.8 5.7 %shard_map.212 = f32[2,256,2048]{2,1,0:T(8,128)} custom-call(bf16[2048,704]{1,0:T(8,128)(2,1)} %get-tuple-element.156.y_ref.x_ref, bf16[2048,704]{1,0:T(8,128)(2,1)} %all-gather.10.cloned.1.call-done.w_ref, bf16[4,256,2048]{2,1,0:T(8,128)(2,1)} %collective-permute-done.8.near_ref), custom_call_target="tpu_custom_call" | custom-call | bytes 184500 | tf_op jit(solution)/shard_map/pallas_call | solution.py:803
  332.8 3.1 fusion.13
  337.7 48.7 %shard_map.213.d_second_ref = f32[256,2048]{1,0:T(8,128)} custom-call(bf16[8,256,1408]{2,1,0:T(8,128)(2,1)} %bitcast.80, bf16[2048,1408]{1,0:T(8,128)(2,1)} %all-gather.8.cloned.1.call-done.w_far), custom_call_target="tpu_custom_call" | custom-call | bytes 1845000 | tf_op jit(solution)/shard_map/pallas_call | solution.py:455
  388.6 27.8 %shard_map.214 = (f32[256,2048]{1,0:T(8,128)}, bf16[256,2048]{1,0:T(8,128)(2,1)S(1)}, bf16[8,256,256]{2,1,0:T(8,128)(2,1)S(1)}, bf16[4,256,2048]{2,1,0:T(8,128)(2,1)}, bf16[8,64,704]{2,1,0:T(8,128)(2,1)S(1)}) custom-call(f32[256,2048]{1,0:T(8,128)} %shard_map.213.d_second_ref, f32[256,2048]{1,0:T(8,128)} %copy-done.22, bf16[256,2048]{1,0:T(8,128)(2,1)S(1)} %copy-done.6, ...), custom_call_target="tpu_custom_call" | custom-call | bytes 738000 | tf_op jit(solution)/shard_map/pallas_call | solution.py:577
  418.4 2.6 shard_map.216
  426.3 17.9 %shard_map.215 = (bf16[2048,768]{1,0:T(8,128)(2,1)}, f32[1,256]{1,0:T(1,128)}) custom-call(s32[32]{0:T(128)} %copy-done.34, f32[2048,768]{1,0:T(8,128)} %fusion.23.proj_ref.refs_1_, s32[2048,1]{1,0:T(8,128)} %copy.32.start_ref.refs_2_, f32[1,256]{1,0:T(1,128)} %get-tuple-element.222.floor_ref.refs_3_, f32[1,256]{1,0:T(1,128)} %get-tuple-element.221.gain_ref.refs_4_, ...), custom_call_target="tpu_custom_call" | custom-call | bytes 1107000 | tf_op jit(solution)/shard_map/pallas_call | solution.py:1406
  444.9 2.9 shard_map.217
  449.6 3.2 fusion.5
  454.2 10.8 %shard_map.218 = bf16[2048,768]{1,0:T(8,128)(2,1)} custom-call(bf16[2048,2048]{1,0:T(8,128)(2,1)} %bitcast.86, bf16[2048,768]{1,0:T(8,128)(2,1)} %get-tuple-element.187.y_ref), custom_call_target="tpu_custom_call" | custom-call | bytes 405900 | tf_op jit(solution)/shard_map/pallas_call | solution.py:826
  465.0 2.8 collective-permute-done.13
  467.9 3.6 add_convert_fusion.1
  477.6 61.4 %shard_map.219 = (f32[256,2048]{1,0:T(8,128)}, bf16[8,64,1408]{2,1,0:T(8,128)(2,1)}) custom-call(bf16[8,256,768]{2,1,0:T(8,128)(2,1)} %bitcast.83, bf16[2048,768]{1,0:T(8,128)(2,1)} %all-gather.6.cloned.1.call-done.w_far, bf16[8,64,1408]{2,1,0:T(8,128)(2,1)} %bitcast.90), custom_call_target="tpu_custom_call" | custom-call | bytes 1845000 | tf_op jit(solution)/shard_map/pallas_call | solution.py:455
  539.0 3.8 all-to-all-start.1
  546.4 2.6 fusion.7
  549.3 3.5 fusion.10
  553.8 4.9 fusion.12
  (185 shorter events, 68.1 us)
Async XLA Ops:
  7.2 97.4 %all-gather.12.cloned.1.call-start = ((), (), s32[]{:S(2)}) async-start(), calls=%async_computation.13 | async-start | bytes 1310720 | tf_op jit(solution)/shard_map/all_gather | solution.py:1229
  7.9 27.6 %copy-start.2 = (bf16[64,11264]{1,0:T(8,128)(2,1)S(1)}, bf16[64,11264]{1,0:T(8,128)(2,1)}, u32[]{:S(2)}) copy-start(bf16[64,11264]{1,0:T(8,128)(2,1)} %weight_ref.4) | copy-start | bytes 4325380
  7.9 98.7 %all-gather.6.cloned.1.call-start = ((), (), s32[]{:S(2)}) async-start(), calls=%async_computation.6 | async-start | bytes 3932160 | tf_op jit(solution)/shard_map/all_gather | solution.py:1193
  9.2 25.2 %copy-start.11 = (bf16[64,5632]{1,0:T(8,128)(2,1)S(1)}, bf16[64,5632]{1,0:T(8,128)(2,1)}, u32[]{:S(2)}) copy-start(bf16[64,5632]{1,0:T(8,128)(2,1)} %weight_ref.5) | copy-start | bytes 2162692
  33.4 186.3 %all-gather.8.cloned.1.call-start = ((), (), s32[]{:S(2)}) async-start(), calls=%async_computation.7 | async-start | bytes 7208960 | tf_op jit(solution)/shard_map/all_gather | solution.py:1193
  38.4 64.3 %copy-start.40 = (s32[96]{0:T(128)S(1)}, s32[96]{0:T(128)}, u32[]{:S(2)}) copy-start(s32[96]{0:T(128)} %param.22) | copy-start | bytes 1156
  38.5 64.3 %copy-start.41 = (s32[96]{0:T(128)S(1)}, s32[96]{0:T(128)}, u32[]{:S(2)}) copy-start(s32[96]{0:T(128)} %param.23) | copy-start | bytes 1156
  102.6 173.8 %all-gather.10.cloned.1.call-start = ((), (), s32[]{:S(2)}) async-start(), calls=%async_computation.8 | async-start | bytes 3932160 | tf_op jit(solution)/shard_map/all_gather | solution.py:1193
  103.3 8.8 %copy-start.34 = (s32[32]{0:T(128)}, s32[32]{0:T(128)S(1)}, u32[]{:S(2)}) copy-start(s32[32]{0:T(128)S(1)} %slice.137.last_ref.refs_0_) | copy-start | bytes 388
  104.6 25.8 %collective-permute-start.2 = (bf16[4,64,2048]{2,1,0:T(8,128)(2,1)}, bf16[4,64,2048]{2,1,0:T(8,128)(2,1)S(1)}, u32[]{:S(2)}, u32[]{:S(2)}) collective-permute-start(bf16[4,64,2048]{2,1,0:T(8,128)(2,1)} %bitcast.73), channel_id=1, source_target_pairs={{0,4},{1,3},{2,6},{3,1},{4,0},{5,7},{6,2},{7,5},{8,12},{9,11},{10,... | collective-permute-start | bytes 3145736 | tf_op jit(solution)/shard_map/ppermute | solution.py:1263
  106.0 24.4 %collective-permute-start.1 = (bf16[4,64,2048]{2,1,0:T(8,128)(2,1)}, bf16[4,64,2048]{2,1,0:T(8,128)(2,1)}, u32[]{:S(2)}, u32[]{:S(2)}) collective-permute-start(bf16[4,64,2048]{2,1,0:T(8,128)(2,1)} %bitcast.74), channel_id=1, source_target_pairs={{0,2},{1,5},{2,0},{3,7},{4,6},{5,1},{6,4},{7,3},{8,10},{9,13},{10,... | collective-permute-start | bytes 3145736 | tf_op jit(solution)/shard_map/ppermute | solution.py:1262
  112.1 18.3 %collective-permute-start = (f32[2,128,128]{2,1,0:T(8,128)}, f32[2,128,128]{2,1,0:T(8,128)S(1)}, u32[]{:S(2)}, u32[]{:S(2)}) collective-permute-start(f32[2,128,128]{2,1,0:T(8,128)} %shard_map.200), channel_id=1, source_target_pairs={{0,8},{1,9},{2,10},{3,11},{4,12},{5,13},{6,14},{7,15},{8,16},{9,17... | collective-permute-start | bytes 393224 | tf_op jit(solution)/shard_map/ppermute | solution.py:1279
  130.4 15.5 %collective-permute-start.3 = (bf16[4,64,2048]{2,1,0:T(8,128)(2,1)}, bf16[4,64,2048]{2,1,0:T(8,128)(2,1)}, u32[]{:S(2)}, u32[]{:S(2)}) collective-permute-start(bf16[4,64,2048]{2,1,0:T(8,128)(2,1)} %collective-permute-done.1.refs_1_), channel_id=1, source_target_pairs={{0,4},{1,3},{2,6},{3,1},{4,0},{5,7},{6,2},{7,5},{8,12},{9,11},{10,... | collective-permute-start | bytes 3145736 | tf_op jit(solution)/shard_map/ppermute | solution.py:1284
  133.3 12.9 %copy-start.14 = (bf16[256,2048]{1,0:T(8,128)(2,1)S(1)}, bf16[256,2048]{1,0:T(8,128)(2,1)}, u32[]{:S(2)}) copy-start(bf16[256,2048]{1,0:T(8,128)(2,1)} %all-gather.12.cloned.1.call-done) | copy-start | bytes 3145732
  146.0 240.4 %reduce-scatter.5.cloned.1.call-start = ((), (), s32[]{:S(2)}) async-start(), calls=%async_computation.9 | async-start | bytes 3932160 | tf_op jit(solution)/shard_map/reduce_scatter | solution.py:1196
  146.2 16.3 %collective-permute-start.4 = (bf16[4,64,2048]{2,1,0:T(8,128)(2,1)S(1)}, bf16[4,64,2048]{2,1,0:T(8,128)(2,1)}, u32[]{:S(2)}, u32[]{:S(2)}) collective-permute-start(bf16[4,64,2048]{2,1,0:T(8,128)(2,1)S(1)} %bitcast.75), channel_id=1, source_target_pairs={{0,1},{1,0},{2,3},{3,2},{4,5},{5,4},{6,7},{7,6},{8,9},{9,8},{10,11... | collective-permute-start | bytes 3145736 | tf_op jit(solution)/shard_map/ppermute | solution.py:1285
  146.3 16.3 %collective-permute-start.5 = (bf16[4,64,2048]{2,1,0:T(8,128)(2,1)}, bf16[4,64,2048]{2,1,0:T(8,128)(2,1)}, u32[]{:S(2)}, u32[]{:S(2)}) collective-permute-start(bf16[4,64,2048]{2,1,0:T(8,128)(2,1)} %collective-permute-done.1.refs_1_), channel_id=1, source_target_pairs={{0,1},{1,0},{2,3},{3,2},{4,5},{5,4},{6,7},{7,6},{8,9},{9,8},{10,11... | collective-permute-start | bytes 3145736 | tf_op jit(solution)/shard_map/ppermute | solution.py:1285
  146.8 15.7 %collective-permute-start.6 = (bf16[4,64,2048]{2,1,0:T(8,128)(2,1)}, bf16[4,64,2048]{2,1,0:T(8,128)(2,1)}, u32[]{:S(2)}, u32[]{:S(2)}) collective-permute-start(bf16[4,64,2048]{2,1,0:T(8,128)(2,1)} %copy-done.15), channel_id=1, source_target_pairs={{0,1},{1,0},{2,3},{3,2},{4,5},{5,4},{6,7},{7,6},{8,9},{9,8},{10,11... | collective-permute-start | bytes 3145736 | tf_op jit(solution)/shard_map/ppermute | solution.py:1285
  146.9 15.7 %collective-permute-start.7 = (bf16[4,64,2048]{2,1,0:T(8,128)(2,1)}, bf16[4,64,2048]{2,1,0:T(8,128)(2,1)}, u32[]{:S(2)}, u32[]{:S(2)}) collective-permute-start(bf16[4,64,2048]{2,1,0:T(8,128)(2,1)} %collective-permute-done.3.refs_3_), channel_id=1, source_target_pairs={{0,1},{1,0},{2,3},{3,2},{4,5},{5,4},{6,7},{7,6},{8,9},{9,8},{10,11... | collective-permute-start | bytes 3145736 | tf_op jit(solution)/shard_map/ppermute | solution.py:1316
  283.8 16.7 %collective-permute-start.8 = (bf16[4,256,2048]{2,1,0:T(8,128)(2,1)}, bf16[4,256,2048]{2,1,0:T(8,128)(2,1)}, u32[]{:S(2)}, u32[]{:S(2)}) collective-permute-start(bf16[4,256,2048]{2,1,0:T(8,128)(2,1)} %bitcast.88), channel_id=1, source_target_pairs={{0,1},{1,0},{2,3},{3,2},{4,5},{5,4},{6,7},{7,6},{8,9},{9,8},{10,11... | collective-permute-start | bytes 12582920 | tf_op jit(solution)/shard_map/ppermute | solution.py:1348
  283.8 193.8 %reduce-scatter.7.cloned.1.call-start = ((), (), s32[]{:S(2)}) async-start(), calls=%async_computation.10 | async-start | bytes 7208960 | tf_op jit(solution)/shard_map/reduce_scatter | solution.py:1196
  306.0 26.4 %collective-permute-start.9 = (bf16[2,256,2048]{2,1,0:T(8,128)(2,1)}, bf16[2,256,2048]{2,1,0:T(8,128)(2,1)}, u32[]{:S(2)}, u32[]{:S(2)}) collective-permute-start(bf16[2,256,2048]{2,1,0:T(8,128)(2,1)} %shard_map.210), channel_id=1, source_target_pairs={{0,4},{1,3},{2,6},{3,1},{4,0},{5,7},{6,2},{7,5},{8,12},{9,11},{10,... | collective-permute-start | bytes 6291464 | tf_op jit(solution)/shard_map/ppermute | solution.py:1354
  332.4 206.7 %reduce-scatter.9.cloned.1.call-start = ((), (), s32[]{:S(2)}) async-start(), calls=%async_computation.11 | async-start | bytes 3932160 | tf_op jit(solution)/shard_map/reduce_scatter | solution.py:1196
  336.0 50.5 %collective-permute-start.10 = (bf16[256,2048]{1,0:T(8,128)(2,1)}, bf16[256,2048]{1,0:T(8,128)(2,1)}, u32[]{:S(2)}, u32[]{:S(2)}) collective-permute-start(bf16[256,2048]{1,0:T(8,128)(2,1)} %fusion.13), channel_id=1, source_target_pairs={{0,2},{1,5},{2,0},{3,7},{4,6},{5,1},{6,4},{7,3},{8,10},{9,13},{10,... | collective-permute-start | bytes 3145736 | tf_op jit(solution)/shard_map/ppermute | solution.py:1361
  337.7 48.8 %copy-start.6 = (bf16[256,2048]{1,0:T(8,128)(2,1)S(1)}, bf16[256,2048]{1,0:T(8,128)(2,1)}, u32[]{:S(2)}) copy-start(bf16[256,2048]{1,0:T(8,128)(2,1)} %cot_ref.1) | copy-start | bytes 3145732
  418.4 31.2 %copy-start.17 = (bf16[256,2048]{1,0:T(8,128)(2,1)}, bf16[256,2048]{1,0:T(8,128)(2,1)S(1)}, u32[]{:S(2)}) copy-start(bf16[256,2048]{1,0:T(8,128)(2,1)S(1)} %get-tuple-element.182) | copy-start | bytes 3145732
  423.3 26.2 %collective-permute-start.12 = (bf16[2,256,2048]{2,1,0:T(8,128)(2,1)S(1)}, bf16[2,256,2048]{2,1,0:T(8,128)(2,1)}, u32[]{:S(2)}, u32[]{:S(2)}) collective-permute-start(bf16[2,256,2048]{2,1,0:T(8,128)(2,1)S(1)} %add_convert_fusion), channel_id=1, source_target_pairs={{0,4},{1,3},{2,6},{3,1},{4,0},{5,7},{6,2},{7,5},{8,12},{9,11},{10,... | collective-permute-start | bytes 6291464 | tf_op jit(solution)/shard_map/ppermute | solution.py:893
  424.8 19.4 %collective-permute-start.11 = (f32[2,128,128]{2,1,0:T(8,128)S(1)}, f32[2,128,128]{2,1,0:T(8,128)S(1)}, u32[]{:S(2)}, u32[]{:S(2)}) collective-permute-start(f32[2,128,128]{2,1,0:T(8,128)S(1)} %copy-done.32), channel_id=1, source_target_pairs={{8,0},{9,1},{10,2},{11,3},{12,4},{13,5},{14,6},{15,7},{16,8},{17,9... | collective-permute-start | bytes 393224 | tf_op jit(solution)/shard_map/ppermute | solution.py:1401
  452.7 15.1 %collective-permute-start.13 = (bf16[256,2048]{1,0:T(8,128)(2,1)}, bf16[256,2048]{1,0:T(8,128)(2,1)}, u32[]{:S(2)}, u32[]{:S(2)}) collective-permute-start(bf16[256,2048]{1,0:T(8,128)(2,1)} %fusion.5), channel_id=1, source_target_pairs={{0,2},{1,5},{2,0},{3,7},{4,6},{5,1},{6,4},{7,3},{8,10},{9,13},{10,... | collective-permute-start | bytes 3145736 | tf_op jit(solution)/shard_map/ppermute | solution.py:902
  467.9 90.9 %reduce-scatter.11.cloned.1.call-start = ((), (), s32[]{:S(2)}) async-start(), calls=%async_computation.12 | async-start | bytes 1310720 | tf_op jit(solution)/shard_map/reduce_scatter | solution.py:1196
  472.6 66.5 %all-to-all-start = ((f32[32,1,64]{2,1,0:T(1,128)}), f32[32,1,64]{2,1,0:T(1,128)S(1)}, u32[]{:S(2)}, u32[]{:S(2)}) async-start(f32[32,1,64]{2,1,0:T(1,128)} %all_to_all.11), calls=%async_computation.3 | async-start | bytes 32768 | tf_op jit(solution)/shard_map/all_to_all | solution.py:1451
  539.0 19.7 %all-to-all-start.1 = ((bf16[8,64,768]{2,1,0:T(8,128)(2,1)}), bf16[8,64,768]{2,1,0:T(8,128)(2,1)S(1)}, u32[]{:S(2)}, u32[]{:S(2)}) async-start(bf16[8,64,768]{2,1,0:T(8,128)(2,1)} %bitcast.94), calls=%async_computation.4 | async-start | bytes 1572864 | tf_op jit(solution)/shard_map/all_to_all | solution.py:1469
  (34 other events, 91.4 us)
Sparse Core Ops, SparseCore 0:
  9.6 31.2 all-gather.11
  42.4 62.4 all-gather.5
  106.5 105.3 all-gather.7
  213.3 63.0 all-gather.9
  284.0 59.0 reduce-scatter.4
  345.2 105.1 reduce-scatter.6
  468.0 58.2 reduce-scatter.8
  529.1 27.1 reduce-scatter.10

commit v6 on v5

--- a/solution.py
+++ b/solution.py
@@ -404,6 +404,7 @@
             copy.start()
             kept.append(copy)
 
+    start_swaps()
     for i in range(out_ref.shape[1] // TILE):
         w_load(i).wait()
     to_mate(0)
@@ -414,7 +415,6 @@
     arrived(near.at[2], 2, mate)
     product(own_places[2], (near.at[2],), going.at[2])
     send(going.at[2], far.at[2], 5, second)
-    start_swaps()
     to_mate(1)
     to_mate(3)
     arrived(near.at[3], 3, mate)

time: 577 us -> 575 us (level)
  Pallas kernels: 445 us -> 439 us
    pallas_call x2, Pallas kernels: 110 us -> 104 us  [product_scatter(): pl.pallas_call(functools.partial(product_scatter_kernel, count, around),...]
  transfers between devices with their start and end apart: 24 -> 24, of which waited for: 5 -> 6; matrix products, arithmetic and copies ran while one was open for 9% -> 9% of each run, Pallas kernels for 76% -> 76%
where the time goes in v6:
time: 575 us; the launch traced here: 568 us
  Pallas kernels  439 us (76%)
  matrix products  26.2 us (5%)
  other arithmetic  24.1 us (4%)
  local copies, waits for them, and re-layouts  23.7 us (4%)
  starting transfers between devices  21.9 us (4%)
  waiting for transfers between devices  17.8 us (3%)
  between operations  15 us (3%)
    pallas_call x4, Pallas kernels, exchange(): pl.pallas_call(functools.partial(exchange_kernel, kinds), out_shape=tuple...  142 us
    pallas_call x2, Pallas kernels, product_scatter(): pl.pallas_call(functools.partial(product_scatter_kernel, count, around),...  104 us
    pallas_call x1, Pallas kernels, gate_gather(): pl.pallas_call(gate_gather_kernel, out_shape=(jax.ShapeDtypeStruct((GROUP...  42.8 us
    pallas_call x3, Pallas kernels, rows_product(): pl.pallas_call(rows_product_kernel, grid=(columns // tile_columns,), in_s...  39.9 us
    pallas_call x1, Pallas kernels, residual_back(): pl.pallas_call(residual_back_kernel, out_shape=(jax.ShapeDtypeStruct((row...  27.8 us
    pallas_call x1, Pallas kernels, body(): pl.pallas_call(functools.partial(backward_kernel, heads), grid=(tile_coun...  17.9 us
    unnamed x84, local copies, waits for them, and re-layouts  17.2 us
    dot_general x3, matrix products, dot_nn(): lax.dot_general(left, right, (((1,), (0,)), ((), ())), preferred_element_...  17.1 us
  transfers between devices with their start and end apart: 24, of which 6 were waited for; matrix products, arithmetic and copies ran while one was open for 9% of the time, Pallas kernels for 76%

profile of v6, /device:TPU:0, one launch (start us, length us, event | category | flops | bytes accessed | tf_op | source)
XLA Modules:
  0.0 567.9 jit_solution(7176972007308672886)
XLA Ops:
  13.8 19.5 %shard_map.196 = (bf16[4,8,16,128]{3,2,1,0:T(8,128)(2,1)}, bf16[8,64,768]{2,1,0:T(8,128)(2,1)}) custom-call(bf16[16,128]{1,0:T(8,128)(2,1)} %copy-done.33, bf16[8,64,768]{2,1,0:T(8,128)(2,1)} %copy-done.9), custom_call_target="tpu_custom_call" | custom-call | bytes 553500 | tf_op jit(solution)/shard_map/pallas_call | solution.py:220
  38.5 64.1 %shard_map.199 = (bf16[1,8,256,2048]{3,2,1,0:T(8,128)(2,1)}, bf16[8,64,1408]{2,1,0:T(8,128)(2,1)}, bf16[8,64,704]{2,1,0:T(8,128)(2,1)}) custom-call(bf16[1,256,2048]{2,1,0:T(8,128)(2,1)} %fusion.14.refs_0_, bf16[8,64,1408]{2,1,0:T(8,128)(2,1)} %copy-done.3, bf16[8,64,704]{2,1,0:T(8,128)(2,1)} %copy-done.10), custom_call_target="tpu_custom_call" | custom-call | bytes 2140200 | tf_op jit(solution)/shard_map/pallas_call | solution.py:220
  106.6 3.5 fusion.16.proj_ref
  114.6 11.1 %fusion.23.proj_ref.refs_1_ = f32[2048,768]{1,0:T(8,128)} fusion(bf16[2048,2048]{1,0:T(8,128)(2,1)} %bitcast.85, bf16[2048,768]{1,0:T(8,128)(2,1)S(1)} %copy-done.26), kind=kOutput, calls=%fused_computation.62 | convolution fusion | flops 6442450944 | bytes 17825792 | tf_op jit(solution)/shard_map/dot_general | solution.py:40
  125.6 4.8 collective-permute-done.2.refs_2_
  133.3 12.7 %shard_map.201 = (bf16[2048,256]{1,0:T(8,128)(2,1)}, f32[2048,256]{1,0:T(8,128)}, f32[32,2,128,128]{3,2,1,0:T(8,128)}) custom-call(s32[32]{0:T(128)} %copy-done.34, f32[2048,768]{1,0:T(8,128)} %fusion.23.proj_ref.refs_1_, s32[2048,1]{1,0:T(8,128)} %copy.32.start_ref.refs_2_, f32[1,256]{1,0:T(1,128)} %get-tuple-element.222.floor_ref.refs_3_, ...), custom_call_target="tpu_custom_call" | custom-call | bytes 664200 | tf_op jit(solution)/shard_map/pallas_call | solution.py:1301
  147.4 15.1 %shard_map.202.in_ref = bf16[256,2048]{1,0:T(8,128)(2,1)} custom-call(bf16[8,256,256]{2,1,0:T(8,128)(2,1)} %bitcast.91), custom_call_target="tpu_custom_call" | custom-call | bytes 553500 | tf_op jit(solution)/shard_map/pallas_call | solution.py:220
  165.0 3.4 shard_map.203
  176.6 43.0 %shard_map.205 = bf16[1,8,256,2048]{3,2,1,0:T(8,128)(2,1)} custom-call(bf16[1,256,2048]{2,1,0:T(8,128)(2,1)} %bitcast.87), custom_call_target="tpu_custom_call" | custom-call | bytes 1586700 | tf_op jit(solution)/shard_map/pallas_call | solution.py:220
  219.6 42.8 %shard_map.206 = (bf16[8,256,2048]{2,1,0:T(8,128)(2,1)}, f32[2048,704]{1,0:T(8,128)}, f32[2048,704]{1,0:T(8,128)}, bf16[2048,704]{1,0:T(8,128)(2,1)}) custom-call(bf16[256,2048]{1,0:T(8,128)(2,1)} %cot_ref.1, bf16[2048,2048]{1,0:T(8,128)(2,1)} %bitcast.78, bf16[2048,1408]{1,0:T(8,128)(2,1)} %all-gather.8.cloned.1.call-done.w_far), custom_call_target="tpu_custom_call" | custom-call | bytes 1660500 | tf_op jit(solution)/shard_map/pallas_call | solution.py:710
  262.4 10.9 %shard_map.207 = bf16[2048,704]{1,0:T(8,128)(2,1)} custom-call(bf16[2048,2048]{1,0:T(8,128)(2,1)} %bitcast.81, bf16[2048,704]{1,0:T(8,128)(2,1)} %get-tuple-element.156.y_ref.x_ref), custom_call_target="tpu_custom_call" | custom-call | bytes 405900 | tf_op jit(solution)/shard_map/pallas_call | solution.py:826
  273.2 3.2 all-gather.10.cloned.1.call-done.w_ref
  276.4 7.4 %shard_map.208 = bf16[1024,2048]{1,0:T(8,128)(2,1)} custom-call(bf16[2048,704]{1,0:T(8,128)(2,1)} %get-tuple-element.156.y_ref.x_ref, bf16[2048,704]{1,0:T(8,128)(2,1)} %all-gather.10.cloned.1.call-done.w_ref), custom_call_target="tpu_custom_call" | custom-call | bytes 221400 | tf_op jit(solution)/shard_map/pallas_call | solution.py:782
  283.9 16.6 %shard_map.209.y_ref = bf16[2048,1408]{1,0:T(8,128)(2,1)} custom-call(bf16[2048,2048]{1,0:T(8,128)(2,1)} %bitcast.82, f32[2048,704]{1,0:T(8,128)} %get-tuple-element.160.gate_ref, f32[2048,704]{1,0:T(8,128)} %get-tuple-element.161.up_ref, bf16[2048,704]{1,0:T(8,128)(2,1)} %all-gather.10.cloned.1.call-done.w_ref), custom_call_target="tpu_custom_call" | custom-call | bytes 738000 | tf_op jit(solution)/shard_map/pallas_call | solution.py:759
  300.5 5.5 shard_map.210
  307.6 18.2 %shard_map.211 = bf16[2048,1408]{1,0:T(8,128)(2,1)} custom-call(bf16[2048,2048]{1,0:T(8,128)(2,1)} %bitcast.79, bf16[2048,1408]{1,0:T(8,128)(2,1)} %shard_map.209.y_ref), custom_call_target="tpu_custom_call" | custom-call | bytes 664200 | tf_op jit(solution)/shard_map/pallas_call | solution.py:826
  325.8 5.7 %shard_map.212 = f32[2,256,2048]{2,1,0:T(8,128)} custom-call(bf16[2048,704]{1,0:T(8,128)(2,1)} %get-tuple-element.156.y_ref.x_ref, bf16[2048,704]{1,0:T(8,128)(2,1)} %all-gather.10.cloned.1.call-done.w_ref, bf16[4,256,2048]{2,1,0:T(8,128)(2,1)} %collective-permute-done.8.near_ref), custom_call_target="tpu_custom_call" | custom-call | bytes 184500 | tf_op jit(solution)/shard_map/pallas_call | solution.py:803
  332.8 3.1 fusion.13
  337.7 48.7 %shard_map.213.d_second_ref = f32[256,2048]{1,0:T(8,128)} custom-call(bf16[8,256,1408]{2,1,0:T(8,128)(2,1)} %bitcast.80, bf16[2048,1408]{1,0:T(8,128)(2,1)} %all-gather.8.cloned.1.call-done.w_far), custom_call_target="tpu_custom_call" | custom-call | bytes 1845000 | tf_op jit(solution)/shard_map/pallas_call | solution.py:455
  388.6 27.8 %shard_map.214 = (f32[256,2048]{1,0:T(8,128)}, bf16[256,2048]{1,0:T(8,128)(2,1)S(1)}, bf16[8,256,256]{2,1,0:T(8,128)(2,1)S(1)}, bf16[4,256,2048]{2,1,0:T(8,128)(2,1)}, bf16[8,64,704]{2,1,0:T(8,128)(2,1)S(1)}) custom-call(f32[256,2048]{1,0:T(8,128)} %shard_map.213.d_second_ref, f32[256,2048]{1,0:T(8,128)} %copy-done.22, bf16[256,2048]{1,0:T(8,128)(2,1)S(1)} %copy-done.6, ...), custom_call_target="tpu_custom_call" | custom-call | bytes 738000 | tf_op jit(solution)/shard_map/pallas_call | solution.py:577
  418.4 2.6 shard_map.216
  426.3 17.9 %shard_map.215 = (bf16[2048,768]{1,0:T(8,128)(2,1)}, f32[1,256]{1,0:T(1,128)}) custom-call(s32[32]{0:T(128)} %copy-done.34, f32[2048,768]{1,0:T(8,128)} %fusion.23.proj_ref.refs_1_, s32[2048,1]{1,0:T(8,128)} %copy.32.start_ref.refs_2_, f32[1,256]{1,0:T(1,128)} %get-tuple-element.222.floor_ref.refs_3_, f32[1,256]{1,0:T(1,128)} %get-tuple-element.221.gain_ref.refs_4_, ...), custom_call_target="tpu_custom_call" | custom-call | bytes 1107000 | tf_op jit(solution)/shard_map/pallas_call | solution.py:1406
  444.9 2.9 shard_map.217
  449.6 3.2 fusion.5
  454.2 10.8 %shard_map.218 = bf16[2048,768]{1,0:T(8,128)(2,1)} custom-call(bf16[2048,2048]{1,0:T(8,128)(2,1)} %bitcast.86, bf16[2048,768]{1,0:T(8,128)(2,1)} %get-tuple-element.187.y_ref), custom_call_target="tpu_custom_call" | custom-call | bytes 405900 | tf_op jit(solution)/shard_map/pallas_call | solution.py:826
  465.0 2.8 collective-permute-done.13
  467.9 3.6 add_convert_fusion.1
  477.6 55.4 %shard_map.219 = (f32[256,2048]{1,0:T(8,128)}, bf16[8,64,1408]{2,1,0:T(8,128)(2,1)}) custom-call(bf16[8,256,768]{2,1,0:T(8,128)(2,1)} %bitcast.83, bf16[2048,768]{1,0:T(8,128)(2,1)} %all-gather.6.cloned.1.call-done.w_far, bf16[8,64,1408]{2,1,0:T(8,128)(2,1)} %bitcast.90), custom_call_target="tpu_custom_call" | custom-call | bytes 1845000 | tf_op jit(solution)/shard_map/pallas_call | solution.py:455
  533.1 3.8 all-to-all-start.1
  543.3 3.5 fusion.10
  547.9 4.9 fusion.12
  552.8 3.5 reduce-scatter.11.cloned.1.call-done
  (185 shorter events, 70.7 us)
Async XLA Ops:
  7.2 97.4 %all-gather.12.cloned.1.call-start = ((), (), s32[]{:S(2)}) async-start(), calls=%async_computation.13 | async-start | bytes 1310720 | tf_op jit(solution)/shard_map/all_gather | solution.py:1229
  7.9 27.6 %copy-start.2 = (bf16[64,11264]{1,0:T(8,128)(2,1)S(1)}, bf16[64,11264]{1,0:T(8,128)(2,1)}, u32[]{:S(2)}) copy-start(bf16[64,11264]{1,0:T(8,128)(2,1)} %weight_ref.4) | copy-start | bytes 4325380
  7.9 98.7 %all-gather.6.cloned.1.call-start = ((), (), s32[]{:S(2)}) async-start(), calls=%async_computation.6 | async-start | bytes 3932160 | tf_op jit(solution)/shard_map/all_gather | solution.py:1193
  9.2 25.2 %copy-start.11 = (bf16[64,5632]{1,0:T(8,128)(2,1)S(1)}, bf16[64,5632]{1,0:T(8,128)(2,1)}, u32[]{:S(2)}) copy-start(bf16[64,5632]{1,0:T(8,128)(2,1)} %weight_ref.5) | copy-start | bytes 2162692
  33.4 186.3 %all-gather.8.cloned.1.call-start = ((), (), s32[]{:S(2)}) async-start(), calls=%async_computation.7 | async-start | bytes 7208960 | tf_op jit(solution)/shard_map/all_gather | solution.py:1193
  38.4 64.3 %copy-start.40 = (s32[96]{0:T(128)S(1)}, s32[96]{0:T(128)}, u32[]{:S(2)}) copy-start(s32[96]{0:T(128)} %param.22) | copy-start | bytes 1156
  38.5 64.3 %copy-start.41 = (s32[96]{0:T(128)S(1)}, s32[96]{0:T(128)}, u32[]{:S(2)}) copy-start(s32[96]{0:T(128)} %param.23) | copy-start | bytes 1156
  102.6 173.8 %all-gather.10.cloned.1.call-start = ((), (), s32[]{:S(2)}) async-start(), calls=%async_computation.8 | async-start | bytes 3932160 | tf_op jit(solution)/shard_map/all_gather | solution.py:1193
  104.6 25.8 %collective-permute-start.2 = (bf16[4,64,2048]{2,1,0:T(8,128)(2,1)}, bf16[4,64,2048]{2,1,0:T(8,128)(2,1)S(1)}, u32[]{:S(2)}, u32[]{:S(2)}) collective-permute-start(bf16[4,64,2048]{2,1,0:T(8,128)(2,1)} %bitcast.73), channel_id=1, source_target_pairs={{0,4},{1,3},{2,6},{3,1},{4,0},{5,7},{6,2},{7,5},{8,12},{9,11},{10,... | collective-permute-start | bytes 3145736 | tf_op jit(solution)/shard_map/ppermute | solution.py:1263
  106.0 24.4 %collective-permute-start.1 = (bf16[4,64,2048]{2,1,0:T(8,128)(2,1)}, bf16[4,64,2048]{2,1,0:T(8,128)(2,1)}, u32[]{:S(2)}, u32[]{:S(2)}) collective-permute-start(bf16[4,64,2048]{2,1,0:T(8,128)(2,1)} %bitcast.74), channel_id=1, source_target_pairs={{0,2},{1,5},{2,0},{3,7},{4,6},{5,1},{6,4},{7,3},{8,10},{9,13},{10,... | collective-permute-start | bytes 3145736 | tf_op jit(solution)/shard_map/ppermute | solution.py:1262
  112.1 18.3 %collective-permute-start = (f32[2,128,128]{2,1,0:T(8,128)}, f32[2,128,128]{2,1,0:T(8,128)S(1)}, u32[]{:S(2)}, u32[]{:S(2)}) collective-permute-start(f32[2,128,128]{2,1,0:T(8,128)} %shard_map.200), channel_id=1, source_target_pairs={{0,8},{1,9},{2,10},{3,11},{4,12},{5,13},{6,14},{7,15},{8,16},{9,17... | collective-permute-start | bytes 393224 | tf_op jit(solution)/shard_map/ppermute | solution.py:1279
  130.4 15.5 %collective-permute-start.3 = (bf16[4,64,2048]{2,1,0:T(8,128)(2,1)}, bf16[4,64,2048]{2,1,0:T(8,128)(2,1)}, u32[]{:S(2)}, u32[]{:S(2)}) collective-permute-start(bf16[4,64,2048]{2,1,0:T(8,128)(2,1)} %collective-permute-done.1.refs_1_), channel_id=1, source_target_pairs={{0,4},{1,3},{2,6},{3,1},{4,0},{5,7},{6,2},{7,5},{8,12},{9,11},{10,... | collective-permute-start | bytes 3145736 | tf_op jit(solution)/shard_map/ppermute | solution.py:1284
  133.3 12.9 %copy-start.14 = (bf16[256,2048]{1,0:T(8,128)(2,1)S(1)}, bf16[256,2048]{1,0:T(8,128)(2,1)}, u32[]{:S(2)}) copy-start(bf16[256,2048]{1,0:T(8,128)(2,1)} %all-gather.12.cloned.1.call-done) | copy-start | bytes 3145732
  146.0 240.4 %reduce-scatter.5.cloned.1.call-start = ((), (), s32[]{:S(2)}) async-start(), calls=%async_computation.9 | async-start | bytes 3932160 | tf_op jit(solution)/shard_map/reduce_scatter | solution.py:1196
  146.2 16.3 %collective-permute-start.4 = (bf16[4,64,2048]{2,1,0:T(8,128)(2,1)S(1)}, bf16[4,64,2048]{2,1,0:T(8,128)(2,1)}, u32[]{:S(2)}, u32[]{:S(2)}) collective-permute-start(bf16[4,64,2048]{2,1,0:T(8,128)(2,1)S(1)} %bitcast.75), channel_id=1, source_target_pairs={{0,1},{1,0},{2,3},{3,2},{4,5},{5,4},{6,7},{7,6},{8,9},{9,8},{10,11... | collective-permute-start | bytes 3145736 | tf_op jit(solution)/shard_map/ppermute | solution.py:1285
  146.3 16.3 %collective-permute-start.5 = (bf16[4,64,2048]{2,1,0:T(8,128)(2,1)}, bf16[4,64,2048]{2,1,0:T(8,128)(2,1)}, u32[]{:S(2)}, u32[]{:S(2)}) collective-permute-start(bf16[4,64,2048]{2,1,0:T(8,128)(2,1)} %collective-permute-done.1.refs_1_), channel_id=1, source_target_pairs={{0,1},{1,0},{2,3},{3,2},{4,5},{5,4},{6,7},{7,6},{8,9},{9,8},{10,11... | collective-permute-start | bytes 3145736 | tf_op jit(solution)/shard_map/ppermute | solution.py:1285
  146.8 15.7 %collective-permute-start.6 = (bf16[4,64,2048]{2,1,0:T(8,128)(2,1)}, bf16[4,64,2048]{2,1,0:T(8,128)(2,1)}, u32[]{:S(2)}, u32[]{:S(2)}) collective-permute-start(bf16[4,64,2048]{2,1,0:T(8,128)(2,1)} %copy-done.15), channel_id=1, source_target_pairs={{0,1},{1,0},{2,3},{3,2},{4,5},{5,4},{6,7},{7,6},{8,9},{9,8},{10,11... | collective-permute-start | bytes 3145736 | tf_op jit(solution)/shard_map/ppermute | solution.py:1285
  146.9 15.7 %collective-permute-start.7 = (bf16[4,64,2048]{2,1,0:T(8,128)(2,1)}, bf16[4,64,2048]{2,1,0:T(8,128)(2,1)}, u32[]{:S(2)}, u32[]{:S(2)}) collective-permute-start(bf16[4,64,2048]{2,1,0:T(8,128)(2,1)} %collective-permute-done.3.refs_3_), channel_id=1, source_target_pairs={{0,1},{1,0},{2,3},{3,2},{4,5},{5,4},{6,7},{7,6},{8,9},{9,8},{10,11... | collective-permute-start | bytes 3145736 | tf_op jit(solution)/shard_map/ppermute | solution.py:1316
  283.8 16.7 %collective-permute-start.8 = (bf16[4,256,2048]{2,1,0:T(8,128)(2,1)}, bf16[4,256,2048]{2,1,0:T(8,128)(2,1)}, u32[]{:S(2)}, u32[]{:S(2)}) collective-permute-start(bf16[4,256,2048]{2,1,0:T(8,128)(2,1)} %bitcast.88), channel_id=1, source_target_pairs={{0,1},{1,0},{2,3},{3,2},{4,5},{5,4},{6,7},{7,6},{8,9},{9,8},{10,11... | collective-permute-start | bytes 12582920 | tf_op jit(solution)/shard_map/ppermute | solution.py:1348
  283.8 193.8 %reduce-scatter.7.cloned.1.call-start = ((), (), s32[]{:S(2)}) async-start(), calls=%async_computation.10 | async-start | bytes 7208960 | tf_op jit(solution)/shard_map/reduce_scatter | solution.py:1196
  306.0 26.4 %collective-permute-start.9 = (bf16[2,256,2048]{2,1,0:T(8,128)(2,1)}, bf16[2,256,2048]{2,1,0:T(8,128)(2,1)}, u32[]{:S(2)}, u32[]{:S(2)}) collective-permute-start(bf16[2,256,2048]{2,1,0:T(8,128)(2,1)} %shard_map.210), channel_id=1, source_target_pairs={{0,4},{1,3},{2,6},{3,1},{4,0},{5,7},{6,2},{7,5},{8,12},{9,11},{10,... | collective-permute-start | bytes 6291464 | tf_op jit(solution)/shard_map/ppermute | solution.py:1354
  332.4 200.7 %reduce-scatter.9.cloned.1.call-start = ((), (), s32[]{:S(2)}) async-start(), calls=%async_computation.11 | async-start | bytes 3932160 | tf_op jit(solution)/shard_map/reduce_scatter | solution.py:1196
  336.0 50.5 %collective-permute-start.10 = (bf16[256,2048]{1,0:T(8,128)(2,1)}, bf16[256,2048]{1,0:T(8,128)(2,1)}, u32[]{:S(2)}, u32[]{:S(2)}) collective-permute-start(bf16[256,2048]{1,0:T(8,128)(2,1)} %fusion.13), channel_id=1, source_target_pairs={{0,2},{1,5},{2,0},{3,7},{4,6},{5,1},{6,4},{7,3},{8,10},{9,13},{10,... | collective-permute-start | bytes 3145736 | tf_op jit(solution)/shard_map/ppermute | solution.py:1361
  337.7 48.8 %copy-start.6 = (bf16[256,2048]{1,0:T(8,128)(2,1)S(1)}, bf16[256,2048]{1,0:T(8,128)(2,1)}, u32[]{:S(2)}) copy-start(bf16[256,2048]{1,0:T(8,128)(2,1)} %cot_ref.1) | copy-start | bytes 3145732
  418.4 31.2 %copy-start.17 = (bf16[256,2048]{1,0:T(8,128)(2,1)}, bf16[256,2048]{1,0:T(8,128)(2,1)S(1)}, u32[]{:S(2)}) copy-start(bf16[256,2048]{1,0:T(8,128)(2,1)S(1)} %get-tuple-element.182) | copy-start | bytes 3145732
  423.3 26.2 %collective-permute-start.12 = (bf16[2,256,2048]{2,1,0:T(8,128)(2,1)S(1)}, bf16[2,256,2048]{2,1,0:T(8,128)(2,1)}, u32[]{:S(2)}, u32[]{:S(2)}) collective-permute-start(bf16[2,256,2048]{2,1,0:T(8,128)(2,1)S(1)} %add_convert_fusion), channel_id=1, source_target_pairs={{0,4},{1,3},{2,6},{3,1},{4,0},{5,7},{6,2},{7,5},{8,12},{9,11},{10,... | collective-permute-start | bytes 6291464 | tf_op jit(solution)/shard_map/ppermute | solution.py:893
  424.8 19.4 %collective-permute-start.11 = (f32[2,128,128]{2,1,0:T(8,128)S(1)}, f32[2,128,128]{2,1,0:T(8,128)S(1)}, u32[]{:S(2)}, u32[]{:S(2)}) collective-permute-start(f32[2,128,128]{2,1,0:T(8,128)S(1)} %copy-done.32), channel_id=1, source_target_pairs={{8,0},{9,1},{10,2},{11,3},{12,4},{13,5},{14,6},{15,7},{16,8},{17,9... | collective-permute-start | bytes 393224 | tf_op jit(solution)/shard_map/ppermute | solution.py:1401
  452.7 15.1 %collective-permute-start.13 = (bf16[256,2048]{1,0:T(8,128)(2,1)}, bf16[256,2048]{1,0:T(8,128)(2,1)}, u32[]{:S(2)}, u32[]{:S(2)}) collective-permute-start(bf16[256,2048]{1,0:T(8,128)(2,1)} %fusion.5), channel_id=1, source_target_pairs={{0,2},{1,5},{2,0},{3,7},{4,6},{5,1},{6,4},{7,3},{8,10},{9,13},{10,... | collective-permute-start | bytes 3145736 | tf_op jit(solution)/shard_map/ppermute | solution.py:902
  467.9 88.5 %reduce-scatter.11.cloned.1.call-start = ((), (), s32[]{:S(2)}) async-start(), calls=%async_computation.12 | async-start | bytes 1310720 | tf_op jit(solution)/shard_map/reduce_scatter | solution.py:1196
  472.6 60.5 %all-to-all-start = ((f32[32,1,64]{2,1,0:T(1,128)}), f32[32,1,64]{2,1,0:T(1,128)S(1)}, u32[]{:S(2)}, u32[]{:S(2)}) async-start(f32[32,1,64]{2,1,0:T(1,128)} %all_to_all.11), calls=%async_computation.3 | async-start | bytes 32768 | tf_op jit(solution)/shard_map/all_to_all | solution.py:1451
  533.1 23.3 %all-to-all-start.1 = ((bf16[8,64,768]{2,1,0:T(8,128)(2,1)}), bf16[8,64,768]{2,1,0:T(8,128)(2,1)S(1)}, u32[]{:S(2)}, u32[]{:S(2)}) async-start(bf16[8,64,768]{2,1,0:T(8,128)(2,1)} %bitcast.94), calls=%async_computation.4 | async-start | bytes 1572864 | tf_op jit(solution)/shard_map/all_to_all | solution.py:1469
  547.9 10.9 %copy-start.8 = (bf16[64,6144]{1,0:T(8,128)(2,1)S(1)}, bf16[64,6144]{1,0:T(8,128)(2,1)}, u32[]{:S(2)}) copy-start(bf16[64,6144]{1,0:T(8,128)(2,1)} %weight_ref.3) | copy-start | bytes 2359300
  (34 other events, 103.4 us)
Sparse Core Ops, SparseCore 0:
  9.6 31.2 all-gather.11
  42.4 62.4 all-gather.5
  106.5 105.3 all-gather.7
  213.3 63.0 all-gather.9
  284.0 59.0 reduce-scatter.4
  345.2 105.1 reduce-scatter.6
  468.0 58.2 reduce-scatter.8
  529.1 27.1 reduce-scatter.10

commit v7 on v6

--- a/solution.py
+++ b/solution.py
@@ -1127,7 +1127,7 @@
 
     @pl.when(pl.program_id(0) != 0)
     def _():
-        lax.fori_loop(0, chunks, step, chunks - 1, unroll=UNROLL)
+        lax.fori_loop(0, chunks, step, chunks - 1, unroll=2 * UNROLL)
 
 
 def backward_edge_kernel(heads, *refs):
@@ -1381,6 +1381,9 @@
     out_sum = SlowScatter(
         lambda begin, number: out_blocks(mixer_keep[begin : begin + number]), None, device_count
     )
+    out_sums = out_sum.onward(out_near)
+    d_mixed_heads = after(d_mixed_heads, out_sums)
+    out_far = out_sum.to_second(out_sums)
     operands = (projected, start_column, own_floor, own_group_gain, state_out, d_mixed_heads)
 
     def edge_specs(place):
@@ -1399,8 +1402,6 @@
         cost_estimate=cost(3),
     )(last_starts, *operands)
     entering_grad = lax.ppermute(first_grad, "fsdp", down_line)
-    out_near = after(out_near, first_grad)
-    out_far = out_sum.to_second(out_sum.onward(out_near))
     dproj_type = jax.ShapeDtypeStruct((group_rows, 3 * own_width), bf16)
     dfloor_type = jax.ShapeDtypeStruct((1, own_width), f32)
     d_projected, floor_most = pl.pallas_call(

time: 575 us -> 571 us (level)
    unnamed x84 -> x82, local copies, waits for them, and re-layouts: 17.2 us -> 15.3 us
  transfers between devices with their start and end apart: 24 -> 24, of which waited for: 6 -> 6; matrix products, arithmetic and copies ran while one was open for 9% -> 10% of each run, Pallas kernels for 76% -> 76%
where the time goes in v7:
time: 571 us; the launch traced here: 565 us
  Pallas kernels  437 us (77%)
  matrix products  27.1 us (5%)
  other arithmetic  24.1 us (4%)
  starting transfers between devices  22 us (4%)
  local copies, waits for them, and re-layouts  21.9 us (4%)
  waiting for transfers between devices  17.7 us (3%)
  between operations  15.1 us (3%)
    pallas_call x4, Pallas kernels, exchange(): pl.pallas_call(functools.partial(exchange_kernel, kinds), out_shape=tuple...  142 us
    pallas_call x2, Pallas kernels, product_scatter(): pl.pallas_call(functools.partial(product_scatter_kernel, count, around),...  104 us
    pallas_call x1, Pallas kernels, gate_gather(): pl.pallas_call(gate_gather_kernel, out_shape=(jax.ShapeDtypeStruct((GROUP...  42.8 us
    pallas_call x3, Pallas kernels, rows_product(): pl.pallas_call(rows_product_kernel, grid=(columns // tile_columns,), in_s...  39.9 us
    pallas_call x1, Pallas kernels, residual_back(): pl.pallas_call(residual_back_kernel, out_shape=(jax.ShapeDtypeStruct((row...  27.9 us
    dot_general x3, matrix products, dot_nn(): lax.dot_general(left, right, (((1,), (0,)), ((), ())), preferred_element_...  17.1 us
    pallas_call x1, Pallas kernels, hidden_back(): pl.pallas_call(hidden_back_kernel, grid=(rows // tile_rows,), in_specs=[t...  16.6 us
    pallas_call x1, Pallas kernels, body(): pl.pallas_call(functools.partial(backward_kernel, heads), grid=(tile_coun...  15.9 us
  transfers between devices with their start and end apart: 24, of which 6 were waited for; matrix products, arithmetic and copies ran while one was open for 10% of the time, Pallas kernels for 76%

profile of v7, /device:TPU:0, one launch (start us, length us, event | category | flops | bytes accessed | tf_op | source)
XLA Modules:
  0.0 564.7 jit_solution(6101742491010929835)
XLA Ops:
  13.8 19.5 %shard_map.196 = (bf16[4,8,16,128]{3,2,1,0:T(8,128)(2,1)}, bf16[8,64,768]{2,1,0:T(8,128)(2,1)}) custom-call(bf16[16,128]{1,0:T(8,128)(2,1)} %copy-done.32, bf16[8,64,768]{2,1,0:T(8,128)(2,1)} %copy-done.9), custom_call_target="tpu_custom_call" | custom-call | bytes 553500 | tf_op jit(solution)/shard_map/pallas_call | solution.py:220
  38.5 64.1 %shard_map.199 = (bf16[1,8,256,2048]{3,2,1,0:T(8,128)(2,1)}, bf16[8,64,1408]{2,1,0:T(8,128)(2,1)}, bf16[8,64,704]{2,1,0:T(8,128)(2,1)}) custom-call(bf16[1,256,2048]{2,1,0:T(8,128)(2,1)} %fusion.14.refs_0_, bf16[8,64,1408]{2,1,0:T(8,128)(2,1)} %copy-done.3, bf16[8,64,704]{2,1,0:T(8,128)(2,1)} %copy-done.10), custom_call_target="tpu_custom_call" | custom-call | bytes 2140200 | tf_op jit(solution)/shard_map/pallas_call | solution.py:220
  106.6 3.5 fusion.16.proj_ref
  114.6 11.1 %fusion.23.proj_ref.refs_1_ = f32[2048,768]{1,0:T(8,128)} fusion(bf16[2048,2048]{1,0:T(8,128)(2,1)} %bitcast.85, bf16[2048,768]{1,0:T(8,128)(2,1)S(1)} %copy-done.26), kind=kOutput, calls=%fused_computation.62 | convolution fusion | flops 6442450944 | bytes 17825792 | tf_op jit(solution)/shard_map/dot_general | solution.py:40
  125.6 4.8 collective-permute-done.2.refs_2_
  133.3 12.7 %shard_map.201 = (bf16[2048,256]{1,0:T(8,128)(2,1)}, f32[2048,256]{1,0:T(8,128)}, f32[32,2,128,128]{3,2,1,0:T(8,128)}) custom-call(s32[32]{0:T(128)} %copy-done.33, f32[2048,768]{1,0:T(8,128)} %fusion.23.proj_ref.refs_1_, s32[2048,1]{1,0:T(8,128)} %copy.32.start_ref.refs_2_, f32[1,256]{1,0:T(1,128)} %get-tuple-element.222.floor_ref.refs_3_, ...), custom_call_target="tpu_custom_call" | custom-call | bytes 664200 | tf_op jit(solution)/shard_map/pallas_call | solution.py:1301
  147.4 15.1 %shard_map.202.in_ref = bf16[256,2048]{1,0:T(8,128)(2,1)} custom-call(bf16[8,256,256]{2,1,0:T(8,128)(2,1)} %bitcast.91), custom_call_target="tpu_custom_call" | custom-call | bytes 553500 | tf_op jit(solution)/shard_map/pallas_call | solution.py:220
  165.1 3.4 shard_map.203
  176.6 43.0 %shard_map.205 = bf16[1,8,256,2048]{3,2,1,0:T(8,128)(2,1)} custom-call(bf16[1,256,2048]{2,1,0:T(8,128)(2,1)} %bitcast.87), custom_call_target="tpu_custom_call" | custom-call | bytes 1586700 | tf_op jit(solution)/shard_map/pallas_call | solution.py:220
  219.6 42.8 %shard_map.206 = (bf16[8,256,2048]{2,1,0:T(8,128)(2,1)}, f32[2048,704]{1,0:T(8,128)}, f32[2048,704]{1,0:T(8,128)}, bf16[2048,704]{1,0:T(8,128)(2,1)}) custom-call(bf16[256,2048]{1,0:T(8,128)(2,1)} %cot_ref.1, bf16[2048,2048]{1,0:T(8,128)(2,1)} %bitcast.78, bf16[2048,1408]{1,0:T(8,128)(2,1)} %all-gather.8.cloned.1.call-done.w_far), custom_call_target="tpu_custom_call" | custom-call | bytes 1660500 | tf_op jit(solution)/shard_map/pallas_call | solution.py:710
  262.4 10.9 %shard_map.207 = bf16[2048,704]{1,0:T(8,128)(2,1)} custom-call(bf16[2048,2048]{1,0:T(8,128)(2,1)} %bitcast.81, bf16[2048,704]{1,0:T(8,128)(2,1)} %get-tuple-element.156.y_ref.x_ref), custom_call_target="tpu_custom_call" | custom-call | bytes 405900 | tf_op jit(solution)/shard_map/pallas_call | solution.py:826
  273.3 3.1 all-gather.10.cloned.1.call-done.w_ref
  276.4 7.4 %shard_map.208 = bf16[1024,2048]{1,0:T(8,128)(2,1)} custom-call(bf16[2048,704]{1,0:T(8,128)(2,1)} %get-tuple-element.156.y_ref.x_ref, bf16[2048,704]{1,0:T(8,128)(2,1)} %all-gather.10.cloned.1.call-done.w_ref), custom_call_target="tpu_custom_call" | custom-call | bytes 221400 | tf_op jit(solution)/shard_map/pallas_call | solution.py:782
  283.9 16.6 %shard_map.209.y_ref = bf16[2048,1408]{1,0:T(8,128)(2,1)} custom-call(bf16[2048,2048]{1,0:T(8,128)(2,1)} %bitcast.82, f32[2048,704]{1,0:T(8,128)} %get-tuple-element.160.gate_ref, f32[2048,704]{1,0:T(8,128)} %get-tuple-element.161.up_ref, bf16[2048,704]{1,0:T(8,128)(2,1)} %all-gather.10.cloned.1.call-done.w_ref), custom_call_target="tpu_custom_call" | custom-call | bytes 738000 | tf_op jit(solution)/shard_map/pallas_call | solution.py:759
  300.5 5.5 shard_map.210
  307.6 18.2 %shard_map.211 = bf16[2048,1408]{1,0:T(8,128)(2,1)} custom-call(bf16[2048,2048]{1,0:T(8,128)(2,1)} %bitcast.79, bf16[2048,1408]{1,0:T(8,128)(2,1)} %shard_map.209.y_ref), custom_call_target="tpu_custom_call" | custom-call | bytes 664200 | tf_op jit(solution)/shard_map/pallas_call | solution.py:826
  325.8 5.7 %shard_map.212 = f32[2,256,2048]{2,1,0:T(8,128)} custom-call(bf16[2048,704]{1,0:T(8,128)(2,1)} %get-tuple-element.156.y_ref.x_ref, bf16[2048,704]{1,0:T(8,128)(2,1)} %all-gather.10.cloned.1.call-done.w_ref, bf16[4,256,2048]{2,1,0:T(8,128)(2,1)} %collective-permute-done.8.near_ref), custom_call_target="tpu_custom_call" | custom-call | bytes 184500 | tf_op jit(solution)/shard_map/pallas_call | solution.py:803
  332.8 3.1 fusion.13
  337.7 48.7 %shard_map.213.d_second_ref = f32[256,2048]{1,0:T(8,128)} custom-call(bf16[8,256,1408]{2,1,0:T(8,128)(2,1)} %bitcast.80, bf16[2048,1408]{1,0:T(8,128)(2,1)} %all-gather.8.cloned.1.call-done.w_far), custom_call_target="tpu_custom_call" | custom-call | bytes 1845000 | tf_op jit(solution)/shard_map/pallas_call | solution.py:455
  388.6 27.9 %shard_map.214 = (f32[256,2048]{1,0:T(8,128)}, bf16[256,2048]{1,0:T(8,128)(2,1)S(1)}, bf16[8,256,256]{2,1,0:T(8,128)(2,1)S(1)}, bf16[4,256,2048]{2,1,0:T(8,128)(2,1)}, bf16[8,64,704]{2,1,0:T(8,128)(2,1)S(1)}) custom-call(f32[256,2048]{1,0:T(8,128)} %shard_map.213.d_second_ref, f32[256,2048]{1,0:T(8,128)} %copy-done.22, bf16[256,2048]{1,0:T(8,128)(2,1)S(1)} %copy-done.6, ...), custom_call_target="tpu_custom_call" | custom-call | bytes 738000 | tf_op jit(solution)/shard_map/pallas_call | solution.py:577
  416.6 3.3 add_convert_fusion
  425.1 15.9 %shard_map.215 = (bf16[2048,768]{1,0:T(8,128)(2,1)}, f32[1,256]{1,0:T(1,128)}) custom-call(s32[32]{0:T(128)} %copy-done.33, f32[2048,768]{1,0:T(8,128)} %fusion.23.proj_ref.refs_1_, s32[2048,1]{1,0:T(8,128)} %copy.32.start_ref.refs_2_, f32[1,256]{1,0:T(1,128)} %get-tuple-element.222.floor_ref.refs_3_, f32[1,256]{1,0:T(1,128)} %get-tuple-element.221.gain_ref.refs_4_, ...), custom_call_target="tpu_custom_call" | custom-call | bytes 1107000 | tf_op jit(solution)/shard_map/pallas_call | solution.py:1407
  441.6 2.9 shard_map.217
  446.2 3.1 fusion.5
  450.7 10.8 %shard_map.218 = bf16[2048,768]{1,0:T(8,128)(2,1)} custom-call(bf16[2048,2048]{1,0:T(8,128)(2,1)} %bitcast.86, bf16[2048,768]{1,0:T(8,128)(2,1)} %get-tuple-element.187.y_ref), custom_call_target="tpu_custom_call" | custom-call | bytes 405900 | tf_op jit(solution)/shard_map/pallas_call | solution.py:826
  461.6 2.8 collective-permute-done.13
  464.5 3.6 add_convert_fusion.1
  474.2 55.5 %shard_map.219 = (f32[256,2048]{1,0:T(8,128)}, bf16[8,64,1408]{2,1,0:T(8,128)(2,1)}) custom-call(bf16[8,256,768]{2,1,0:T(8,128)(2,1)} %bitcast.83, bf16[2048,768]{1,0:T(8,128)(2,1)} %all-gather.6.cloned.1.call-done.w_far, bf16[8,64,1408]{2,1,0:T(8,128)(2,1)} %bitcast.90), custom_call_target="tpu_custom_call" | custom-call | bytes 1845000 | tf_op jit(solution)/shard_map/pallas_call | solution.py:455
  529.8 3.8 all-to-all-start.1
  540.0 3.5 fusion.10
  544.6 4.9 fusion.12
  549.5 3.6 reduce-scatter.11.cloned.1.call-done
  (183 shorter events, 68.6 us)
Async XLA Ops:
  7.2 97.4 %all-gather.12.cloned.1.call-start = ((), (), s32[]{:S(2)}) async-start(), calls=%async_computation.13 | async-start | bytes 1310720 | tf_op jit(solution)/shard_map/all_gather | solution.py:1229
  7.9 27.6 %copy-start.2 = (bf16[64,11264]{1,0:T(8,128)(2,1)S(1)}, bf16[64,11264]{1,0:T(8,128)(2,1)}, u32[]{:S(2)}) copy-start(bf16[64,11264]{1,0:T(8,128)(2,1)} %weight_ref.4) | copy-start | bytes 4325380
  7.9 98.7 %all-gather.6.cloned.1.call-start = ((), (), s32[]{:S(2)}) async-start(), calls=%async_computation.6 | async-start | bytes 3932160 | tf_op jit(solution)/shard_map/all_gather | solution.py:1193
  9.2 25.2 %copy-start.11 = (bf16[64,5632]{1,0:T(8,128)(2,1)S(1)}, bf16[64,5632]{1,0:T(8,128)(2,1)}, u32[]{:S(2)}) copy-start(bf16[64,5632]{1,0:T(8,128)(2,1)} %weight_ref.5) | copy-start | bytes 2162692
  33.4 186.3 %all-gather.8.cloned.1.call-start = ((), (), s32[]{:S(2)}) async-start(), calls=%async_computation.7 | async-start | bytes 7208960 | tf_op jit(solution)/shard_map/all_gather | solution.py:1193
  38.4 64.3 %copy-start.39 = (s32[96]{0:T(128)S(1)}, s32[96]{0:T(128)}, u32[]{:S(2)}) copy-start(s32[96]{0:T(128)} %param.22) | copy-start | bytes 1156
  38.5 64.3 %copy-start.40 = (s32[96]{0:T(128)S(1)}, s32[96]{0:T(128)}, u32[]{:S(2)}) copy-start(s32[96]{0:T(128)} %param.23) | copy-start | bytes 1156
  102.6 173.8 %all-gather.10.cloned.1.call-start = ((), (), s32[]{:S(2)}) async-start(), calls=%async_computation.8 | async-start | bytes 3932160 | tf_op jit(solution)/shard_map/all_gather | solution.py:1193
  104.6 25.8 %collective-permute-start.2 = (bf16[4,64,2048]{2,1,0:T(8,128)(2,1)}, bf16[4,64,2048]{2,1,0:T(8,128)(2,1)S(1)}, u32[]{:S(2)}, u32[]{:S(2)}) collective-permute-start(bf16[4,64,2048]{2,1,0:T(8,128)(2,1)} %bitcast.73), channel_id=1, source_target_pairs={{0,4},{1,3},{2,6},{3,1},{4,0},{5,7},{6,2},{7,5},{8,12},{9,11},{10,... | collective-permute-start | bytes 3145736 | tf_op jit(solution)/shard_map/ppermute | solution.py:1263
  106.0 24.4 %collective-permute-start.1 = (bf16[4,64,2048]{2,1,0:T(8,128)(2,1)}, bf16[4,64,2048]{2,1,0:T(8,128)(2,1)}, u32[]{:S(2)}, u32[]{:S(2)}) collective-permute-start(bf16[4,64,2048]{2,1,0:T(8,128)(2,1)} %bitcast.74), channel_id=1, source_target_pairs={{0,2},{1,5},{2,0},{3,7},{4,6},{5,1},{6,4},{7,3},{8,10},{9,13},{10,... | collective-permute-start | bytes 3145736 | tf_op jit(solution)/shard_map/ppermute | solution.py:1262
  112.1 18.3 %collective-permute-start = (f32[2,128,128]{2,1,0:T(8,128)}, f32[2,128,128]{2,1,0:T(8,128)S(1)}, u32[]{:S(2)}, u32[]{:S(2)}) collective-permute-start(f32[2,128,128]{2,1,0:T(8,128)} %shard_map.200), channel_id=1, source_target_pairs={{0,8},{1,9},{2,10},{3,11},{4,12},{5,13},{6,14},{7,15},{8,16},{9,17... | collective-permute-start | bytes 393224 | tf_op jit(solution)/shard_map/ppermute | solution.py:1279
  130.4 15.5 %collective-permute-start.3 = (bf16[4,64,2048]{2,1,0:T(8,128)(2,1)}, bf16[4,64,2048]{2,1,0:T(8,128)(2,1)}, u32[]{:S(2)}, u32[]{:S(2)}) collective-permute-start(bf16[4,64,2048]{2,1,0:T(8,128)(2,1)} %collective-permute-done.1.refs_1_), channel_id=1, source_target_pairs={{0,4},{1,3},{2,6},{3,1},{4,0},{5,7},{6,2},{7,5},{8,12},{9,11},{10,... | collective-permute-start | bytes 3145736 | tf_op jit(solution)/shard_map/ppermute | solution.py:1284
  133.3 12.9 %copy-start.14 = (bf16[256,2048]{1,0:T(8,128)(2,1)S(1)}, bf16[256,2048]{1,0:T(8,128)(2,1)}, u32[]{:S(2)}) copy-start(bf16[256,2048]{1,0:T(8,128)(2,1)} %all-gather.12.cloned.1.call-done) | copy-start | bytes 3145732
  146.0 240.4 %reduce-scatter.5.cloned.1.call-start = ((), (), s32[]{:S(2)}) async-start(), calls=%async_computation.9 | async-start | bytes 3932160 | tf_op jit(solution)/shard_map/reduce_scatter | solution.py:1196
  146.3 16.3 %collective-permute-start.4 = (bf16[4,64,2048]{2,1,0:T(8,128)(2,1)S(1)}, bf16[4,64,2048]{2,1,0:T(8,128)(2,1)}, u32[]{:S(2)}, u32[]{:S(2)}) collective-permute-start(bf16[4,64,2048]{2,1,0:T(8,128)(2,1)S(1)} %bitcast.75), channel_id=1, source_target_pairs={{0,1},{1,0},{2,3},{3,2},{4,5},{5,4},{6,7},{7,6},{8,9},{9,8},{10,11... | collective-permute-start | bytes 3145736 | tf_op jit(solution)/shard_map/ppermute | solution.py:1285
  146.3 16.3 %collective-permute-start.5 = (bf16[4,64,2048]{2,1,0:T(8,128)(2,1)}, bf16[4,64,2048]{2,1,0:T(8,128)(2,1)}, u32[]{:S(2)}, u32[]{:S(2)}) collective-permute-start(bf16[4,64,2048]{2,1,0:T(8,128)(2,1)} %collective-permute-done.1.refs_1_), channel_id=1, source_target_pairs={{0,1},{1,0},{2,3},{3,2},{4,5},{5,4},{6,7},{7,6},{8,9},{9,8},{10,11... | collective-permute-start | bytes 3145736 | tf_op jit(solution)/shard_map/ppermute | solution.py:1285
  146.8 15.7 %collective-permute-start.6 = (bf16[4,64,2048]{2,1,0:T(8,128)(2,1)}, bf16[4,64,2048]{2,1,0:T(8,128)(2,1)}, u32[]{:S(2)}, u32[]{:S(2)}) collective-permute-start(bf16[4,64,2048]{2,1,0:T(8,128)(2,1)} %copy-done.15), channel_id=1, source_target_pairs={{0,1},{1,0},{2,3},{3,2},{4,5},{5,4},{6,7},{7,6},{8,9},{9,8},{10,11... | collective-permute-start | bytes 3145736 | tf_op jit(solution)/shard_map/ppermute | solution.py:1285
  146.9 15.7 %collective-permute-start.7 = (bf16[4,64,2048]{2,1,0:T(8,128)(2,1)}, bf16[4,64,2048]{2,1,0:T(8,128)(2,1)}, u32[]{:S(2)}, u32[]{:S(2)}) collective-permute-start(bf16[4,64,2048]{2,1,0:T(8,128)(2,1)} %collective-permute-done.3.refs_3_), channel_id=1, source_target_pairs={{0,1},{1,0},{2,3},{3,2},{4,5},{5,4},{6,7},{7,6},{8,9},{9,8},{10,11... | collective-permute-start | bytes 3145736 | tf_op jit(solution)/shard_map/ppermute | solution.py:1316
  283.8 16.7 %collective-permute-start.8 = (bf16[4,256,2048]{2,1,0:T(8,128)(2,1)}, bf16[4,256,2048]{2,1,0:T(8,128)(2,1)}, u32[]{:S(2)}, u32[]{:S(2)}) collective-permute-start(bf16[4,256,2048]{2,1,0:T(8,128)(2,1)} %bitcast.88), channel_id=1, source_target_pairs={{0,1},{1,0},{2,3},{3,2},{4,5},{5,4},{6,7},{7,6},{8,9},{9,8},{10,11... | collective-permute-start | bytes 12582920 | tf_op jit(solution)/shard_map/ppermute | solution.py:1348
  283.8 190.4 %reduce-scatter.7.cloned.1.call-start = ((), (), s32[]{:S(2)}) async-start(), calls=%async_computation.10 | async-start | bytes 7208960 | tf_op jit(solution)/shard_map/reduce_scatter | solution.py:1196
  306.0 26.4 %collective-permute-start.9 = (bf16[2,256,2048]{2,1,0:T(8,128)(2,1)}, bf16[2,256,2048]{2,1,0:T(8,128)(2,1)}, u32[]{:S(2)}, u32[]{:S(2)}) collective-permute-start(bf16[2,256,2048]{2,1,0:T(8,128)(2,1)} %shard_map.210), channel_id=1, source_target_pairs={{0,4},{1,3},{2,6},{3,1},{4,0},{5,7},{6,2},{7,5},{8,12},{9,11},{10,... | collective-permute-start | bytes 6291464 | tf_op jit(solution)/shard_map/ppermute | solution.py:1354
  332.4 197.4 %reduce-scatter.9.cloned.1.call-start = ((), (), s32[]{:S(2)}) async-start(), calls=%async_computation.11 | async-start | bytes 3932160 | tf_op jit(solution)/shard_map/reduce_scatter | solution.py:1196
  336.0 50.5 %collective-permute-start.10 = (bf16[256,2048]{1,0:T(8,128)(2,1)}, bf16[256,2048]{1,0:T(8,128)(2,1)}, u32[]{:S(2)}, u32[]{:S(2)}) collective-permute-start(bf16[256,2048]{1,0:T(8,128)(2,1)} %fusion.13), channel_id=1, source_target_pairs={{0,2},{1,5},{2,0},{3,7},{4,6},{5,1},{6,4},{7,3},{8,10},{9,13},{10,... | collective-permute-start | bytes 3145736 | tf_op jit(solution)/shard_map/ppermute | solution.py:1361
  337.7 48.8 %copy-start.6 = (bf16[256,2048]{1,0:T(8,128)(2,1)S(1)}, bf16[256,2048]{1,0:T(8,128)(2,1)}, u32[]{:S(2)}) copy-start(bf16[256,2048]{1,0:T(8,128)(2,1)} %cot_ref.1) | copy-start | bytes 3145732
  388.6 27.9 %copy-start.28 = (bf16[4,256,256]{2,1,0:T(8,128)(2,1)S(1)}, bf16[4,256,256]{2,1,0:T(8,128)(2,1)}, u32[]{:S(2)}) copy-start(bf16[4,256,256]{2,1,0:T(8,128)(2,1)} %get-tuple-element.176) | copy-start | bytes 1572868
  416.6 29.6 %copy-start.17 = (bf16[256,2048]{1,0:T(8,128)(2,1)}, bf16[256,2048]{1,0:T(8,128)(2,1)S(1)}, u32[]{:S(2)}) copy-start(bf16[256,2048]{1,0:T(8,128)(2,1)S(1)} %get-tuple-element.177) | copy-start | bytes 3145732
  419.9 26.2 %collective-permute-start.12 = (bf16[2,256,2048]{2,1,0:T(8,128)(2,1)S(1)}, bf16[2,256,2048]{2,1,0:T(8,128)(2,1)}, u32[]{:S(2)}, u32[]{:S(2)}) collective-permute-start(bf16[2,256,2048]{2,1,0:T(8,128)(2,1)S(1)} %add_convert_fusion), channel_id=1, source_target_pairs={{0,4},{1,3},{2,6},{3,1},{4,0},{5,7},{6,2},{7,5},{8,12},{9,11},{10,... | collective-permute-start | bytes 6291464 | tf_op jit(solution)/shard_map/ppermute | solution.py:893
  423.6 17.3 %collective-permute-start.11 = (f32[2,128,128]{2,1,0:T(8,128)}, f32[2,128,128]{2,1,0:T(8,128)S(1)}, u32[]{:S(2)}, u32[]{:S(2)}) collective-permute-start(f32[2,128,128]{2,1,0:T(8,128)} %shard_map.216), channel_id=1, source_target_pairs={{8,0},{9,1},{10,2},{11,3},{12,4},{13,5},{14,6},{15,7},{16,8},{17,9... | collective-permute-start | bytes 393224 | tf_op jit(solution)/shard_map/ppermute | solution.py:1404
  449.3 15.1 %collective-permute-start.13 = (bf16[256,2048]{1,0:T(8,128)(2,1)}, bf16[256,2048]{1,0:T(8,128)(2,1)}, u32[]{:S(2)}, u32[]{:S(2)}) collective-permute-start(bf16[256,2048]{1,0:T(8,128)(2,1)} %fusion.5), channel_id=1, source_target_pairs={{0,2},{1,5},{2,0},{3,7},{4,6},{5,1},{6,4},{7,3},{8,10},{9,13},{10,... | collective-permute-start | bytes 3145736 | tf_op jit(solution)/shard_map/ppermute | solution.py:902
  464.4 88.7 %reduce-scatter.11.cloned.1.call-start = ((), (), s32[]{:S(2)}) async-start(), calls=%async_computation.12 | async-start | bytes 1310720 | tf_op jit(solution)/shard_map/reduce_scatter | solution.py:1196
  469.1 60.7 %all-to-all-start = ((f32[32,1,64]{2,1,0:T(1,128)}), f32[32,1,64]{2,1,0:T(1,128)S(1)}, u32[]{:S(2)}, u32[]{:S(2)}) async-start(f32[32,1,64]{2,1,0:T(1,128)} %all_to_all.11), calls=%async_computation.3 | async-start | bytes 32768 | tf_op jit(solution)/shard_map/all_to_all | solution.py:1452
  529.8 23.3 %all-to-all-start.1 = ((bf16[8,64,768]{2,1,0:T(8,128)(2,1)}), bf16[8,64,768]{2,1,0:T(8,128)(2,1)S(1)}, u32[]{:S(2)}, u32[]{:S(2)}) async-start(bf16[8,64,768]{2,1,0:T(8,128)(2,1)} %bitcast.94), calls=%async_computation.4 | async-start | bytes 1572864 | tf_op jit(solution)/shard_map/all_to_all | solution.py:1470
  (33 other events, 113.1 us)
Sparse Core Ops, SparseCore 0:
  9.6 31.2 all-gather.11
  42.4 62.4 all-gather.5
  106.5 105.3 all-gather.7
  213.3 63.0 all-gather.9
  284.0 59.0 reduce-scatter.4
  345.2 105.1 reduce-scatter.6
  464.5 58.5 reduce-scatter.8
  525.9 27.1 reduce-scatter.10

commit v8 on v7

--- a/solution.py
+++ b/solution.py
@@ -485,12 +485,10 @@
     gain_ref,
     w_far,
     mixer_ref,
-    down_ref,
     d_residual_ref,
     d_mix_ref,
     heads_ref,
     near_ref,
-    swapped_ref,
     w_ref,
     parts_ref,
     away_ref,
@@ -526,10 +524,6 @@
     def arrived(target, item, number):
         remote(target, target, send_sem.at[item, number], recv_sem.at[item, number], me).wait_recv()
 
-    for number, step in others:
-        send(down_ref.at[slot + step], swapped_ref.at[slot], 2, number - 1, me + step)
-    own_down = pltpu.make_async_copy(down_ref.at[slot], swapped_ref.at[slot], own_sem.at[0])
-    own_down.start()
     rows = d_residual_ref.shape[0]
     slab_rows = 32
 
@@ -554,23 +548,21 @@
         part(slot + step)
         send(parts_ref.at[slot + step], heads_ref.at[slot], 0, number - 1, me + step)
     part(slot)
-    own_part = pltpu.make_async_copy(parts_ref.at[slot], heads_ref.at[slot], own_sem.at[1])
+    own_part = pltpu.make_async_copy(parts_ref.at[slot], heads_ref.at[slot], own_sem)
     own_part.start()
     for kind in (3, 2, 1, 0):
         away_ref[kind] = dot_tn(mixer_ref[kind], d_mix_ref[...]).astype(bf16)
         send(away_ref.at[kind], near_ref.at[kind], 1, kind, mate)
     for number, step in others:
         arrived(heads_ref.at[slot + step], 0, number - 1)
-        arrived(swapped_ref.at[slot + step], 2, number - 1)
     for kind in range(4):
         arrived(near_ref.at[kind], 1, kind)
     for copy in sent:
         copy.wait_send()
-    own_down.wait()
     own_part.wait()
 
 
-def residual_back(d_second, residual, cot, gain, w, mixer_away, down, number):
+def residual_back(d_second, residual, cot, gain, w, mixer_away, number):
     rows, columns = residual.shape
     width = columns // GROUP
     blocks = mixer_away.shape[0]
@@ -581,24 +573,23 @@
             jax.ShapeDtypeStruct((rows, columns), bf16),
             jax.ShapeDtypeStruct((GROUP, rows, width), bf16),
             jax.ShapeDtypeStruct((blocks, mixer_away.shape[2], columns), bf16),
-            jax.ShapeDtypeStruct(down.shape, down.dtype),
         ),
-        in_specs=[VMEM, VMEM, VMEM, VMEM, ANY, VMEM, ANY],
-        out_specs=(VMEM, VMEM, ANY, ANY, ANY),
+        in_specs=[VMEM, VMEM, VMEM, VMEM, ANY, VMEM],
+        out_specs=(VMEM, VMEM, ANY, ANY),
         scratch_shapes=[
             pltpu.VMEM((GROUP, width, columns), bf16),
             pltpu.VMEM((GROUP, rows, width), bf16),
             pltpu.VMEM((blocks, mixer_away.shape[2], columns), bf16),
-            pltpu.SemaphoreType.DMA((3, GROUP - 1)),
-            pltpu.SemaphoreType.DMA((3, GROUP - 1)),
-            pltpu.SemaphoreType.DMA((2,)),
+            pltpu.SemaphoreType.DMA((2, GROUP - 1)),
+            pltpu.SemaphoreType.DMA((2, GROUP - 1)),
+            pltpu.SemaphoreType.DMA,
             pltpu.SemaphoreType.DMA((GROUP,)),
         ],
         compiler_params=pltpu.CompilerParams(
             collective_id=number, has_side_effects=True, vmem_limit_bytes=48 * 2**20
         ),
         cost_estimate=cost(20),
-    )(d_second, residual, cot, gain, w, mixer_away, down)
+    )(d_second, residual, cot, gain, w, mixer_away)
 
 
 def gate_gather_kernel(
@@ -1354,21 +1345,21 @@
     ffn_grad, ffn_rest, ffn_far = meet(ffn_grad, ffn_rest, lax.ppermute(ffn_sums, "fsdp", second))
     ffn_both = (ffn_rest[1] + ffn_far[1].astype(f32)).astype(bf16)
     ffn_summed = line_scatter(ffn_grad)
-    [d_second] = product_scatter(
-        d_gate_pre.reshape(GROUP, row_count, -1), after(ffn_weight, ffn_grad, ffn_both), 4, True
-    )
-    d_second, ffn_last, down_summed = meet(
-        d_second, lax.ppermute(ffn_both, "fsdp", first), down_summed
-    )
-
-    d_residual, d_mix_out, d_mixed_heads, out_near, down_swapped = residual_back(
+    d_second, down_swapped = product_scatter(
+        d_gate_pre.reshape(GROUP, row_count, -1),
+        after(ffn_weight, ffn_grad, ffn_both),
+        4,
+        True,
+        down_summed.reshape(GROUP, weight_rows, -1),
+    )
+    d_second, ffn_last = meet(d_second, lax.ppermute(ffn_both, "fsdp", first))
+    d_residual, d_mix_out, d_mixed_heads, out_near = residual_back(
         d_second,
         residual,
         cotangent,
         second_gain,
         out_weight,
         mixer_away,
-        down_summed.reshape(GROUP, weight_rows, -1),
         5,
     )
     d_mixed_heads = d_mixed_heads.reshape(group_rows, own_width)

time: 571 us -> 580 us (1.016)
  starting transfers between devices: 22 us -> 32.1 us
    reduce_scatter x4, starting transfers between devices: 0.75 us -> 11 us  [line_scatter(): lax.psum_scatter(x, 'fsdp', scatter_dimension=0, axis_index_groups=lines,...]
    pallas_call x1, Pallas kernels: 27.9 us -> 20.5 us  [residual_back(): pl.pallas_call(residual_back_kernel, out_shape=(jax.ShapeDtypeStruct((row...]
    unnamed x82 -> x76, local copies, waits for them, and re-layouts: 15.3 us -> 12.7 us
  transfers between devices with their start and end apart: 24 -> 24, of which waited for: 6 -> 6; matrix products, arithmetic and copies ran while one was open for 10% -> 10% of each run, Pallas kernels for 76% -> 74%
where the time goes in v8:
time: 580 us; the launch traced here: 574 us
  Pallas kernels  433 us (75%)
  starting transfers between devices  32.1 us (6%)
  matrix products  28.8 us (5%)
  other arithmetic  24.7 us (4%)
  waiting for transfers between devices  21 us (4%)
  local copies, waits for them, and re-layouts  19.4 us (3%)
  between operations  15 us (3%)
    pallas_call x4, Pallas kernels, exchange(): pl.pallas_call(functools.partial(exchange_kernel, kinds), out_shape=tuple...  142 us
    pallas_call x2, Pallas kernels, product_scatter(): pl.pallas_call(functools.partial(product_scatter_kernel, count, around),...  108 us
    pallas_call x1, Pallas kernels, gate_gather(): pl.pallas_call(gate_gather_kernel, out_shape=(jax.ShapeDtypeStruct((GROUP...  42.8 us
    pallas_call x3, Pallas kernels, rows_product(): pl.pallas_call(rows_product_kernel, grid=(columns // tile_columns,), in_s...  39.9 us
    pallas_call x1, Pallas kernels, residual_back(): pl.pallas_call(residual_back_kernel, out_shape=(jax.ShapeDtypeStruct((row...  20.5 us
    dot_general x3, matrix products, dot_nn(): lax.dot_general(left, right, (((1,), (0,)), ((), ())), preferred_element_...  18.3 us
    pallas_call x1, Pallas kernels, hidden_back(): pl.pallas_call(hidden_back_kernel, grid=(rows // tile_rows,), in_specs=[t...  16.5 us
    pallas_call x1, Pallas kernels, body(): pl.pallas_call(functools.partial(backward_kernel, heads), grid=(tile_coun...  15.9 us
  transfers between devices with their start and end apart: 24, of which 6 were waited for; matrix products, arithmetic and copies ran while one was open for 10% of the time, Pallas kernels for 74%

profile of v8, /device:TPU:0, one launch (start us, length us, event | category | flops | bytes accessed | tf_op | source)
XLA Modules:
  0.0 573.6 jit_solution(476250479099878210)
XLA Ops:
  13.8 19.5 %shard_map.196 = (bf16[4,8,16,128]{3,2,1,0:T(8,128)(2,1)}, bf16[8,64,768]{2,1,0:T(8,128)(2,1)}) custom-call(bf16[16,128]{1,0:T(8,128)(2,1)} %copy-done.29, bf16[8,64,768]{2,1,0:T(8,128)(2,1)} %copy-done.9), custom_call_target="tpu_custom_call" | custom-call | bytes 553500 | tf_op jit(solution)/shard_map/pallas_call | solution.py:220
  38.5 64.1 %shard_map.199 = (bf16[1,8,256,2048]{3,2,1,0:T(8,128)(2,1)}, bf16[8,64,1408]{2,1,0:T(8,128)(2,1)}, bf16[8,64,704]{2,1,0:T(8,128)(2,1)}) custom-call(bf16[1,256,2048]{2,1,0:T(8,128)(2,1)} %fusion.14.refs_0_, bf16[8,64,1408]{2,1,0:T(8,128)(2,1)} %copy-done.3, bf16[8,64,704]{2,1,0:T(8,128)(2,1)} %copy-done.10), custom_call_target="tpu_custom_call" | custom-call | bytes 2140200 | tf_op jit(solution)/shard_map/pallas_call | solution.py:220
  106.7 3.5 fusion.16.proj_ref
  114.6 11.1 %fusion.23.proj_ref.refs_1_ = f32[2048,768]{1,0:T(8,128)} fusion(bf16[2048,2048]{1,0:T(8,128)(2,1)} %bitcast.84, bf16[2048,768]{1,0:T(8,128)(2,1)S(1)} %copy-done.24), kind=kOutput, calls=%fused_computation.62 | convolution fusion | flops 6442450944 | bytes 17825792 | tf_op jit(solution)/shard_map/dot_general | solution.py:40
  125.7 4.8 collective-permute-done.2.refs_2_
  133.4 12.7 %shard_map.201 = (bf16[2048,256]{1,0:T(8,128)(2,1)}, f32[2048,256]{1,0:T(8,128)}, f32[32,2,128,128]{3,2,1,0:T(8,128)}) custom-call(s32[32]{0:T(128)} %copy-done.30, f32[2048,768]{1,0:T(8,128)} %fusion.23.proj_ref.refs_1_, s32[2048,1]{1,0:T(8,128)} %copy.32.start_ref.refs_2_, f32[1,256]{1,0:T(1,128)} %get-tuple-element.222.floor_ref.refs_3_, ...), custom_call_target="tpu_custom_call" | custom-call | bytes 664200 | tf_op jit(solution)/shard_map/pallas_call | solution.py:1292
  146.1 10.5 %reduce-scatter.5.cloned.1.call-start = ((), (), s32[]{:S(2)}) async-start(), calls=%async_computation.9 | async-start | bytes 3932160 | tf_op jit(solution)/shard_map/reduce_scatter | solution.py:1187
  157.7 15.1 %shard_map.202.in_ref = bf16[256,2048]{1,0:T(8,128)(2,1)} custom-call(bf16[8,256,256]{2,1,0:T(8,128)(2,1)} %bitcast.90), custom_call_target="tpu_custom_call" | custom-call | bytes 553500 | tf_op jit(solution)/shard_map/pallas_call | solution.py:220
  175.4 3.4 shard_map.203
  181.9 3.8 multiply_reduce_fusion
  188.5 42.9 %shard_map.205 = bf16[1,8,256,2048]{3,2,1,0:T(8,128)(2,1)} custom-call(bf16[1,256,2048]{2,1,0:T(8,128)(2,1)} %bitcast.86), custom_call_target="tpu_custom_call" | custom-call | bytes 1586700 | tf_op jit(solution)/shard_map/pallas_call | solution.py:220
  231.5 42.8 %shard_map.206 = (bf16[8,256,2048]{2,1,0:T(8,128)(2,1)}, f32[2048,704]{1,0:T(8,128)}, f32[2048,704]{1,0:T(8,128)}, bf16[2048,704]{1,0:T(8,128)(2,1)}) custom-call(bf16[256,2048]{1,0:T(8,128)(2,1)} %cot_ref.1, bf16[2048,2048]{1,0:T(8,128)(2,1)} %bitcast.77, bf16[2048,1408]{1,0:T(8,128)(2,1)} %all-gather.8.cloned.1.call-done.w_far), custom_call_target="tpu_custom_call" | custom-call | bytes 1660500 | tf_op jit(solution)/shard_map/pallas_call | solution.py:701
  274.3 10.9 %shard_map.207 = bf16[2048,704]{1,0:T(8,128)(2,1)} custom-call(bf16[2048,2048]{1,0:T(8,128)(2,1)} %bitcast.80, bf16[2048,704]{1,0:T(8,128)(2,1)} %get-tuple-element.156.y_ref.x_ref), custom_call_target="tpu_custom_call" | custom-call | bytes 405900 | tf_op jit(solution)/shard_map/pallas_call | solution.py:817
  285.1 7.4 %shard_map.208 = bf16[1024,2048]{1,0:T(8,128)(2,1)} custom-call(bf16[2048,704]{1,0:T(8,128)(2,1)} %get-tuple-element.156.y_ref.x_ref, bf16[2048,704]{1,0:T(8,128)(2,1)} %all-gather.10.cloned.1.call-done.w_ref), custom_call_target="tpu_custom_call" | custom-call | bytes 221400 | tf_op jit(solution)/shard_map/pallas_call | solution.py:773
  293.0 16.5 %shard_map.209.y_ref = bf16[2048,1408]{1,0:T(8,128)(2,1)} custom-call(bf16[2048,2048]{1,0:T(8,128)(2,1)} %bitcast.81, f32[2048,704]{1,0:T(8,128)} %get-tuple-element.160.gate_ref, f32[2048,704]{1,0:T(8,128)} %get-tuple-element.161.up_ref, bf16[2048,704]{1,0:T(8,128)(2,1)} %all-gather.10.cloned.1.call-done.w_ref), custom_call_target="tpu_custom_call" | custom-call | bytes 738000 | tf_op jit(solution)/shard_map/pallas_call | solution.py:750
  309.5 5.5 shard_map.210
  316.3 18.2 %shard_map.211 = bf16[2048,1408]{1,0:T(8,128)(2,1)} custom-call(bf16[2048,2048]{1,0:T(8,128)(2,1)} %bitcast.78, bf16[2048,1408]{1,0:T(8,128)(2,1)} %shard_map.209.y_ref), custom_call_target="tpu_custom_call" | custom-call | bytes 664200 | tf_op jit(solution)/shard_map/pallas_call | solution.py:817
  334.5 5.7 shard_map.212
  341.9 3.1 fusion.13
  346.4 5.7 reduce-scatter.5.cloned.1.call-done
  352.1 52.0 %shard_map.213 = (f32[256,2048]{1,0:T(8,128)}, bf16[8,64,704]{2,1,0:T(8,128)(2,1)}) custom-call(bf16[8,256,1408]{2,1,0:T(8,128)(2,1)} %bitcast.79, bf16[2048,1408]{1,0:T(8,128)(2,1)} %all-gather.8.cloned.1.call-done.w_far, bf16[8,64,704]{2,1,0:T(8,128)(2,1)} %bitcast.91), custom_call_target="tpu_custom_call" | custom-call | bytes 1845000 | tf_op jit(solution)/shard_map/pallas_call | solution.py:455
  404.1 20.5 %shard_map.214 = (f32[256,2048]{1,0:T(8,128)S(1)}, bf16[256,2048]{1,0:T(8,128)(2,1)S(1)}, bf16[8,256,256]{2,1,0:T(8,128)(2,1)S(1)}, bf16[4,256,2048]{2,1,0:T(8,128)(2,1)}) custom-call(f32[256,2048]{1,0:T(8,128)} %get-tuple-element.173.d_second_ref, f32[256,2048]{1,0:T(8,128)} %get-tuple-element.224.residual_ref, bf16[256,2048]{1,0:T(8,128)(2,1)S(1)} %copy-done.6, ...), custom_call_target="tpu_custom_call" | custom-call | bytes 738000 | tf_op jit(solution)/shard_map/pallas_call | solution.py:569
  424.6 3.8 add_convert_fusion
  433.5 15.9 %shard_map.215 = (bf16[2048,768]{1,0:T(8,128)(2,1)}, f32[1,256]{1,0:T(1,128)}) custom-call(s32[32]{0:T(128)} %copy-done.30, f32[2048,768]{1,0:T(8,128)} %fusion.23.proj_ref.refs_1_, s32[2048,1]{1,0:T(8,128)} %copy.32.start_ref.refs_2_, f32[1,256]{1,0:T(1,128)} %get-tuple-element.222.floor_ref.refs_3_, f32[1,256]{1,0:T(1,128)} %get-tuple-element.221.gain_ref.refs_4_, ...), custom_call_target="tpu_custom_call" | custom-call | bytes 1107000 | tf_op jit(solution)/shard_map/pallas_call | solution.py:1398
  454.7 3.1 fusion.5
  459.1 10.9 %shard_map.218 = bf16[2048,768]{1,0:T(8,128)(2,1)} custom-call(bf16[2048,2048]{1,0:T(8,128)(2,1)} %bitcast.85, bf16[2048,768]{1,0:T(8,128)(2,1)} %get-tuple-element.187.y_ref), custom_call_target="tpu_custom_call" | custom-call | bytes 405900 | tf_op jit(solution)/shard_map/pallas_call | solution.py:817
  473.0 3.6 add_convert_fusion.1
  483.2 55.6 %shard_map.219 = (f32[256,2048]{1,0:T(8,128)}, bf16[8,64,1408]{2,1,0:T(8,128)(2,1)}) custom-call(bf16[8,256,768]{2,1,0:T(8,128)(2,1)} %bitcast.82, bf16[2048,768]{1,0:T(8,128)(2,1)} %all-gather.6.cloned.1.call-done.w_far, bf16[8,64,1408]{2,1,0:T(8,128)(2,1)} %bitcast.89), custom_call_target="tpu_custom_call" | custom-call | bytes 1845000 | tf_op jit(solution)/shard_map/pallas_call | solution.py:455
  538.8 3.8 all-to-all-start.1
  548.9 3.5 fusion.10
  553.5 4.9 fusion.12
  558.4 3.7 reduce-scatter.11.cloned.1.call-done
  (177 shorter events, 70.2 us)
Async XLA Ops:
  7.2 97.5 %all-gather.12.cloned.1.call-start = ((), (), s32[]{:S(2)}) async-start(), calls=%async_computation.13 | async-start | bytes 1310720 | tf_op jit(solution)/shard_map/all_gather | solution.py:1220
  7.9 27.6 %copy-start.2 = (bf16[64,11264]{1,0:T(8,128)(2,1)S(1)}, bf16[64,11264]{1,0:T(8,128)(2,1)}, u32[]{:S(2)}) copy-start(bf16[64,11264]{1,0:T(8,128)(2,1)} %weight_ref.4) | copy-start | bytes 4325380
  7.9 98.8 %all-gather.6.cloned.1.call-start = ((), (), s32[]{:S(2)}) async-start(), calls=%async_computation.6 | async-start | bytes 3932160 | tf_op jit(solution)/shard_map/all_gather | solution.py:1184
  9.2 25.2 %copy-start.11 = (bf16[64,5632]{1,0:T(8,128)(2,1)S(1)}, bf16[64,5632]{1,0:T(8,128)(2,1)}, u32[]{:S(2)}) copy-start(bf16[64,5632]{1,0:T(8,128)(2,1)} %weight_ref.5) | copy-start | bytes 2162692
  33.4 198.1 %all-gather.8.cloned.1.call-start = ((), (), s32[]{:S(2)}) async-start(), calls=%async_computation.7 | async-start | bytes 7208960 | tf_op jit(solution)/shard_map/all_gather | solution.py:1184
  38.5 64.3 %copy-start.36 = (s32[96]{0:T(128)S(1)}, s32[96]{0:T(128)}, u32[]{:S(2)}) copy-start(s32[96]{0:T(128)} %param.22) | copy-start | bytes 1156
  38.5 64.3 %copy-start.37 = (s32[96]{0:T(128)S(1)}, s32[96]{0:T(128)}, u32[]{:S(2)}) copy-start(s32[96]{0:T(128)} %param.23) | copy-start | bytes 1156
  102.6 182.5 %all-gather.10.cloned.1.call-start = ((), (), s32[]{:S(2)}) async-start(), calls=%async_computation.8 | async-start | bytes 3932160 | tf_op jit(solution)/shard_map/all_gather | solution.py:1184
  104.6 25.8 %collective-permute-start.2 = (bf16[4,64,2048]{2,1,0:T(8,128)(2,1)}, bf16[4,64,2048]{2,1,0:T(8,128)(2,1)S(1)}, u32[]{:S(2)}, u32[]{:S(2)}) collective-permute-start(bf16[4,64,2048]{2,1,0:T(8,128)(2,1)} %bitcast.73), channel_id=1, source_target_pairs={{0,4},{1,3},{2,6},{3,1},{4,0},{5,7},{6,2},{7,5},{8,12},{9,11},{10,... | collective-permute-start | bytes 3145736 | tf_op jit(solution)/shard_map/ppermute | solution.py:1254
  106.1 24.4 %collective-permute-start.1 = (bf16[4,64,2048]{2,1,0:T(8,128)(2,1)}, bf16[4,64,2048]{2,1,0:T(8,128)(2,1)}, u32[]{:S(2)}, u32[]{:S(2)}) collective-permute-start(bf16[4,64,2048]{2,1,0:T(8,128)(2,1)} %bitcast.74), channel_id=1, source_target_pairs={{0,2},{1,5},{2,0},{3,7},{4,6},{5,1},{6,4},{7,3},{8,10},{9,13},{10,... | collective-permute-start | bytes 3145736 | tf_op jit(solution)/shard_map/ppermute | solution.py:1253
  112.1 18.3 %collective-permute-start = (f32[2,128,128]{2,1,0:T(8,128)}, f32[2,128,128]{2,1,0:T(8,128)S(1)}, u32[]{:S(2)}, u32[]{:S(2)}) collective-permute-start(f32[2,128,128]{2,1,0:T(8,128)} %shard_map.200), channel_id=1, source_target_pairs={{0,8},{1,9},{2,10},{3,11},{4,12},{5,13},{6,14},{7,15},{8,16},{9,17... | collective-permute-start | bytes 393224 | tf_op jit(solution)/shard_map/ppermute | solution.py:1270
  130.5 15.5 %collective-permute-start.3 = (bf16[4,64,2048]{2,1,0:T(8,128)(2,1)}, bf16[4,64,2048]{2,1,0:T(8,128)(2,1)}, u32[]{:S(2)}, u32[]{:S(2)}) collective-permute-start(bf16[4,64,2048]{2,1,0:T(8,128)(2,1)} %collective-permute-done.1.refs_1_), channel_id=1, source_target_pairs={{0,4},{1,3},{2,6},{3,1},{4,0},{5,7},{6,2},{7,5},{8,12},{9,11},{10,... | collective-permute-start | bytes 3145736 | tf_op jit(solution)/shard_map/ppermute | solution.py:1275
  133.4 23.2 %copy-start.15 = (bf16[256,2048]{1,0:T(8,128)(2,1)S(1)}, bf16[256,2048]{1,0:T(8,128)(2,1)}, u32[]{:S(2)}) copy-start(bf16[256,2048]{1,0:T(8,128)(2,1)} %all-gather.12.cloned.1.call-done) | copy-start | bytes 3145732
  146.1 206.0 %reduce-scatter.5.cloned.1.call-start = ((), (), s32[]{:S(2)}) async-start(), calls=%async_computation.9 | async-start | bytes 3932160 | tf_op jit(solution)/shard_map/reduce_scatter | solution.py:1187
  156.6 16.3 %collective-permute-start.4 = (bf16[4,64,2048]{2,1,0:T(8,128)(2,1)S(1)}, bf16[4,64,2048]{2,1,0:T(8,128)(2,1)}, u32[]{:S(2)}, u32[]{:S(2)}) collective-permute-start(bf16[4,64,2048]{2,1,0:T(8,128)(2,1)S(1)} %bitcast.75), channel_id=1, source_target_pairs={{0,1},{1,0},{2,3},{3,2},{4,5},{5,4},{6,7},{7,6},{8,9},{9,8},{10,11... | collective-permute-start | bytes 3145736 | tf_op jit(solution)/shard_map/ppermute | solution.py:1276
  156.6 16.3 %collective-permute-start.5 = (bf16[4,64,2048]{2,1,0:T(8,128)(2,1)}, bf16[4,64,2048]{2,1,0:T(8,128)(2,1)}, u32[]{:S(2)}, u32[]{:S(2)}) collective-permute-start(bf16[4,64,2048]{2,1,0:T(8,128)(2,1)} %collective-permute-done.1.refs_1_), channel_id=1, source_target_pairs={{0,1},{1,0},{2,3},{3,2},{4,5},{5,4},{6,7},{7,6},{8,9},{9,8},{10,11... | collective-permute-start | bytes 3145736 | tf_op jit(solution)/shard_map/ppermute | solution.py:1276
  157.1 15.7 %collective-permute-start.6 = (bf16[4,64,2048]{2,1,0:T(8,128)(2,1)}, bf16[4,64,2048]{2,1,0:T(8,128)(2,1)}, u32[]{:S(2)}, u32[]{:S(2)}) collective-permute-start(bf16[4,64,2048]{2,1,0:T(8,128)(2,1)} %copy-done.16), channel_id=1, source_target_pairs={{0,1},{1,0},{2,3},{3,2},{4,5},{5,4},{6,7},{7,6},{8,9},{9,8},{10,11... | collective-permute-start | bytes 3145736 | tf_op jit(solution)/shard_map/ppermute | solution.py:1276
  157.2 15.7 %collective-permute-start.7 = (bf16[4,64,2048]{2,1,0:T(8,128)(2,1)}, bf16[4,64,2048]{2,1,0:T(8,128)(2,1)}, u32[]{:S(2)}, u32[]{:S(2)}) collective-permute-start(bf16[4,64,2048]{2,1,0:T(8,128)(2,1)} %collective-permute-done.3.refs_3_), channel_id=1, source_target_pairs={{0,1},{1,0},{2,3},{3,2},{4,5},{5,4},{6,7},{7,6},{8,9},{9,8},{10,11... | collective-permute-start | bytes 3145736 | tf_op jit(solution)/shard_map/ppermute | solution.py:1307
  179.1 275.6 %copy-start.25 = (bf16[4,256,256]{2,1,0:T(8,128)(2,1)}, bf16[4,256,256]{2,1,0:T(8,128)(2,1)S(1)}, u32[]{:S(2)}) copy-start(bf16[4,256,256]{2,1,0:T(8,128)(2,1)S(1)} %get-tuple-element.176) | copy-start | bytes 1572868
  292.5 17.0 %collective-permute-start.8 = (bf16[4,256,2048]{2,1,0:T(8,128)(2,1)}, bf16[4,256,2048]{2,1,0:T(8,128)(2,1)}, u32[]{:S(2)}, u32[]{:S(2)}) collective-permute-start(bf16[4,256,2048]{2,1,0:T(8,128)(2,1)} %bitcast.87), channel_id=1, source_target_pairs={{0,1},{1,0},{2,3},{3,2},{4,5},{5,4},{6,7},{7,6},{8,9},{9,8},{10,11... | collective-permute-start | bytes 12582920 | tf_op jit(solution)/shard_map/ppermute | solution.py:1339
  293.0 190.2 %reduce-scatter.7.cloned.1.call-start = ((), (), s32[]{:S(2)}) async-start(), calls=%async_computation.10 | async-start | bytes 7208960 | tf_op jit(solution)/shard_map/reduce_scatter | solution.py:1187
  315.1 26.4 %collective-permute-start.9 = (bf16[2,256,2048]{2,1,0:T(8,128)(2,1)}, bf16[2,256,2048]{2,1,0:T(8,128)(2,1)}, u32[]{:S(2)}, u32[]{:S(2)}) collective-permute-start(bf16[2,256,2048]{2,1,0:T(8,128)(2,1)} %shard_map.210), channel_id=1, source_target_pairs={{0,4},{1,3},{2,6},{3,1},{4,0},{5,7},{6,2},{7,5},{8,12},{9,11},{10,... | collective-permute-start | bytes 6291464 | tf_op jit(solution)/shard_map/ppermute | solution.py:1345
  341.4 197.4 %reduce-scatter.9.cloned.1.call-start = ((), (), s32[]{:S(2)}) async-start(), calls=%async_computation.11 | async-start | bytes 3932160 | tf_op jit(solution)/shard_map/reduce_scatter | solution.py:1187
  345.0 59.0 %collective-permute-start.10 = (bf16[256,2048]{1,0:T(8,128)(2,1)}, bf16[256,2048]{1,0:T(8,128)(2,1)}, u32[]{:S(2)}, u32[]{:S(2)}) collective-permute-start(bf16[256,2048]{1,0:T(8,128)(2,1)} %fusion.13), channel_id=1, source_target_pairs={{0,2},{1,5},{2,0},{3,7},{4,6},{5,1},{6,4},{7,3},{8,10},{9,13},{10,... | collective-permute-start | bytes 3145736 | tf_op jit(solution)/shard_map/ppermute | solution.py:1355
  352.1 52.0 %copy-start.6 = (bf16[256,2048]{1,0:T(8,128)(2,1)S(1)}, bf16[256,2048]{1,0:T(8,128)(2,1)}, u32[]{:S(2)}) copy-start(bf16[256,2048]{1,0:T(8,128)(2,1)} %cot_ref.1) | copy-start | bytes 3145732
  424.6 30.1 %copy-start.18 = (bf16[256,2048]{1,0:T(8,128)(2,1)}, bf16[256,2048]{1,0:T(8,128)(2,1)S(1)}, u32[]{:S(2)}) copy-start(bf16[256,2048]{1,0:T(8,128)(2,1)S(1)} %get-tuple-element.177) | copy-start | bytes 3145732
  428.5 26.2 %collective-permute-start.12 = (bf16[2,256,2048]{2,1,0:T(8,128)(2,1)S(1)}, bf16[2,256,2048]{2,1,0:T(8,128)(2,1)}, u32[]{:S(2)}, u32[]{:S(2)}) collective-permute-start(bf16[2,256,2048]{2,1,0:T(8,128)(2,1)S(1)} %add_convert_fusion), channel_id=1, source_target_pairs={{0,4},{1,3},{2,6},{3,1},{4,0},{5,7},{6,2},{7,5},{8,12},{9,11},{10,... | collective-permute-start | bytes 6291464 | tf_op jit(solution)/shard_map/ppermute | solution.py:884
  432.0 17.3 %collective-permute-start.11 = (f32[2,128,128]{2,1,0:T(8,128)}, f32[2,128,128]{2,1,0:T(8,128)S(1)}, u32[]{:S(2)}, u32[]{:S(2)}) collective-permute-start(f32[2,128,128]{2,1,0:T(8,128)} %shard_map.216), channel_id=1, source_target_pairs={{8,0},{9,1},{10,2},{11,3},{12,4},{13,5},{14,6},{15,7},{16,8},{17,9... | collective-permute-start | bytes 393224 | tf_op jit(solution)/shard_map/ppermute | solution.py:1395
  457.8 15.1 %collective-permute-start.13 = (bf16[256,2048]{1,0:T(8,128)(2,1)}, bf16[256,2048]{1,0:T(8,128)(2,1)}, u32[]{:S(2)}, u32[]{:S(2)}) collective-permute-start(bf16[256,2048]{1,0:T(8,128)(2,1)} %fusion.5), channel_id=1, source_target_pairs={{0,2},{1,5},{2,0},{3,7},{4,6},{5,1},{6,4},{7,3},{8,10},{9,13},{10,... | collective-permute-start | bytes 3145736 | tf_op jit(solution)/shard_map/ppermute | solution.py:893
  472.9 89.2 %reduce-scatter.11.cloned.1.call-start = ((), (), s32[]{:S(2)}) async-start(), calls=%async_computation.12 | async-start | bytes 1310720 | tf_op jit(solution)/shard_map/reduce_scatter | solution.py:1187
  477.6 61.2 %all-to-all-start = ((f32[32,1,64]{2,1,0:T(1,128)}), f32[32,1,64]{2,1,0:T(1,128)S(1)}, u32[]{:S(2)}, u32[]{:S(2)}) async-start(f32[32,1,64]{2,1,0:T(1,128)} %all_to_all.11), calls=%async_computation.3 | async-start | bytes 32768 | tf_op jit(solution)/shard_map/all_to_all | solution.py:1443
  538.8 23.3 %all-to-all-start.1 = ((bf16[8,64,768]{2,1,0:T(8,128)(2,1)}), bf16[8,64,768]{2,1,0:T(8,128)(2,1)S(1)}, u32[]{:S(2)}, u32[]{:S(2)}) async-start(bf16[8,64,768]{2,1,0:T(8,128)(2,1)} %bitcast.94), calls=%async_computation.4 | async-start | bytes 1572864 | tf_op jit(solution)/shard_map/all_to_all | solution.py:1461
  (30 other events, 112.2 us)
Sparse Core Ops, SparseCore 0:
  9.6 31.2 all-gather.11
  42.4 62.4 all-gather.5
  106.5 105.3 all-gather.7
  213.3 63.0 all-gather.9
  293.1 58.9 reduce-scatter.4
  354.2 105.1 reduce-scatter.6
  473.0 58.9 reduce-scatter.8
  534.9 27.1 reduce-scatter.10
